TPU v7x, 128 devices: a whole 4x4x4 slice. The times are simulated.
128 devices in a mesh: dp: 4 (over x), expert: 32 (over y, z, core).
Axes of the slice: x: 4, y: 4, z: 4, core: 2. Of those that a mesh axis runs over, the one named last changes fastest.
Arguments:
- tokens: bfloat16 [32768, 2048], P(('dp', 'expert')), may hold values from -6 to 6
- out_grad: bfloat16 [32768, 2048], P(('dp', 'expert')), may hold values from -6 to 6
- token_picks: int32 [128, 64, 8], P(('dp', 'expert')), may hold values from 0 to 255, as said below
- router: bfloat16 [2048, 64], P(None, 'expert'), may hold values from -0.125 to 0.125
- kept_blocks: int32 [64, 3, 128], P('expert'), may hold values from 0 to 384, as said below
- masters: float32 [64, 3, 128, 4096], P('expert', None, 'dp'), may hold values from -0.25 to 0.25
- scores: float32 [64, 3, 128], P('expert', None, 'dp'), may hold values from -6 to 6
Outputs:
- layer_out: bfloat16 [32768, 2048], P(('dp', 'expert'))
- input_grad: bfloat16 [32768, 2048], P(('dp', 'expert'))
- master_new: float32 [64, 3, 128, 4096], P('expert', None, 'dp')
- score_new: float32 [64, 3, 128], P('expert', None, 'dp')
- router_grad: float32 [2048, 64], P('dp', 'expert')
Inputs may be any that keep to these rules, and one draw needn't show every extreme that they name: `token_picks`: within one source block and one expert the 8 picks are distinct tokens. `kept_blocks`: each list of 128 slots holds, in ascending order, between 64 and 128 distinct block numbers below 384, then 384 in the remaining slots; for each of the three matrices the list of some expert is full.
All inputs are finite; a program needn't handle non-finite values.
Results may differ from a plain program's by a relative error of at most 0.0081.
Values may be sent and summed in bfloat16 or wider, within the bound.
No kernel may reach another device: no remote copies, remote signals or barrier semaphores. Data moves between devices by JAX's collectives and lax.ppermute only.
A program may use at most 192 MiB of HBM per device.

v0:
```python
import jax
import jax.numpy as jnp
from jax import lax
from jax.sharding import PartitionSpec as P

FF = 768
BS = 64


LEARN_RATE = 0.005
SCORE_RATE = 0.05


def layouts(kept_rows, in_blocks, hid_blocks):
    blocks_total = in_blocks * hid_blocks
    plan_list = []
    for matrix, col_count in ((0, hid_blocks), (1, hid_blocks), (2, in_blocks)):
        usable = kept_rows[matrix] < blocks_total
        safe_index = jnp.where(usable, kept_rows[matrix], 0)
        plan_list.append((safe_index // col_count, safe_index % col_count, usable, safe_index))
    return plan_list


def masked_tiles(tile_stack, plan_list):
    return [
        jnp.where(
            plan_list[matrix][2][:, None, None],
            tile_stack[matrix],
            jnp.zeros_like(tile_stack[matrix]),
        )
        for matrix in range(3)
    ]


def block_matrix(tile_set, block_plan, row_blocks, col_blocks):
    tile_width = tile_set.shape[-1]
    slot_count = tile_set.shape[0]
    numbers = jnp.arange(row_blocks * col_blocks, dtype=jnp.int32)
    hits = (block_plan[3][None, :] == numbers[:, None]) & block_plan[2][None, :]
    slot_of = jnp.sum(jnp.where(hits, jnp.arange(slot_count, dtype=jnp.int32)[None, :], 0), axis=1)
    present = jnp.any(hits, axis=1)
    slot_of = jnp.where(present, slot_of, slot_count)
    padded = jnp.concatenate(
        [tile_set, jnp.zeros((1, tile_width, tile_width), tile_set.dtype)], axis=0
    )
    placed = jnp.take(padded, slot_of, axis=0).reshape(
        row_blocks, col_blocks, tile_width, tile_width
    )
    return placed.transpose(0, 2, 1, 3).reshape(row_blocks * tile_width, col_blocks * tile_width)


def project(operand, weight, flipped):
    tile_set, block_plan, matrix_full = weight
    if flipped:
        return lax.dot_general(
            operand, matrix_full, (((1,), (1,)), ((), ())), preferred_element_type=jnp.float32
        )
    return jnp.dot(operand, matrix_full, preferred_element_type=jnp.float32)


def weight_grad(operand, cotangent, weight):
    tile_set, block_plan, matrix_full = weight
    tile_width = tile_set.shape[-1]
    grid_rows = matrix_full.shape[0] // tile_width
    grid_cols = matrix_full.shape[1] // tile_width
    full_grad = lax.dot_general(
        operand, cotangent, (((0,), (0,)), ((), ())), preferred_element_type=jnp.float32
    )
    full_grad = full_grad.reshape(grid_rows, tile_width, grid_cols, tile_width).transpose(
        0, 2, 1, 3
    )
    gradient = jnp.take(full_grad.reshape(-1, tile_width, tile_width), block_plan[3], axis=0)
    gradient = jnp.where(block_plan[2][:, None, None], gradient, jnp.zeros_like(gradient))
    return gradient.reshape(-1, tile_width * tile_width)


def expert_forward(rows_in, weights, router_col):
    gate_pre = project(rows_in, weights[0], False)
    up_pre = project(rows_in, weights[1], False)
    hidden = (jax.nn.silu(gate_pre) * up_pre).astype(jnp.bfloat16)
    output = project(hidden, weights[2], False)
    gating = jax.nn.sigmoid(jnp.dot(rows_in, router_col, preferred_element_type=jnp.float32))
    part_out = (gating[:, None] * output).astype(jnp.bfloat16)
    return (part_out, (gate_pre, up_pre, hidden, output, gating))


def expert_down_grad(grad_rows, saved_state, weights):
    gate_pre, up_pre, hidden, output, gating = saved_state
    grad_float = grad_rows.astype(jnp.float32)
    logit_grad = jnp.sum(grad_float * output, axis=1) * gating * (1.0 - gating)
    scaled = (gating[:, None] * grad_float).astype(jnp.bfloat16)
    down_grad = weight_grad(hidden, scaled, weights[2])
    hidden_grad = project(scaled, weights[2], True)
    return (down_grad, (hidden_grad, logit_grad))


def expert_rest_grad(rows_in, carried, saved_state, weights, router_col):
    hidden_grad, logit_grad = carried
    gate_pre, up_pre = (saved_state[0], saved_state[1])
    sigmoid = jax.nn.sigmoid(gate_pre)
    gate_grad = (hidden_grad * up_pre * sigmoid * (1.0 + gate_pre * (1.0 - sigmoid))).astype(
        jnp.bfloat16
    )
    up_grad = (hidden_grad * gate_pre * sigmoid).astype(jnp.bfloat16)
    gate_weight = weight_grad(rows_in, gate_grad, weights[0])
    up_weight = weight_grad(rows_in, up_grad, weights[1])
    input_part = project(gate_grad, weights[0], True) + project(up_grad, weights[1], True)
    input_part = input_part + logit_grad[:, None] * router_col.astype(jnp.float32)[None, :]
    router_part = jnp.dot(logit_grad, rows_in.astype(jnp.float32), precision=lax.Precision.HIGHEST)
    return (input_part.astype(jnp.bfloat16), gate_weight, up_weight, router_part)


def body(tokens, out_grad, token_picks, router, kept_blocks, masters, scores):
    local_count = kept_blocks.shape[0]
    peer_count = lax.axis_size("expert")
    capacity = token_picks.shape[2]
    model_width = tokens.shape[1]
    in_blocks = model_width // BS
    hid_blocks = FF // BS
    copies = lax.all_gather(masters.astype(jnp.bfloat16), "dp", axis=2, tiled=True)
    copies = copies.reshape(local_count, 3, -1, BS, BS)
    slot_order = (
        token_picks[0].reshape(peer_count, local_count, capacity).transpose(1, 0, 2).reshape(-1)
    )
    experts = []
    for member in range(local_count):
        plan_list = layouts(kept_blocks[member], in_blocks, hid_blocks)
        tile_list = masked_tiles(copies[member], plan_list)
        extents = ((in_blocks, hid_blocks), (in_blocks, hid_blocks), (hid_blocks, in_blocks))
        matrix_list = [
            block_matrix(
                tile_list[matrix], plan_list[matrix], extents[matrix][0], extents[matrix][1]
            )
            for matrix in range(3)
        ]
        experts.append(
            [(tile_list[matrix], plan_list[matrix], matrix_list[matrix]) for matrix in range(3)]
        )

    def outbound(source):
        return jnp.take(source, slot_order, axis=0).reshape(
            local_count, peer_count, capacity, model_width
        )

    arrived = lax.all_to_all(outbound(tokens), "expert", split_axis=1, concat_axis=1, tiled=True)
    parts_out = []
    saved_list = []
    for member in range(local_count):
        rows_in = arrived[member].reshape(-1, model_width)
        part_out, saved_state = expert_forward(rows_in, experts[member], router[:, member])
        parts_out.append(part_out.reshape(peer_count, capacity, model_width))
        saved_list.append(saved_state)
    parts_out, saved_list = (jnp.stack(parts_out), saved_list)
    returned_out, arrived_grad = (
        lax.all_to_all(parts_out, "expert", split_axis=1, concat_axis=1, tiled=True),
        lax.all_to_all(outbound(out_grad), "expert", split_axis=1, concat_axis=1, tiled=True),
    )
    down_list = []
    inner_list = []
    for member in range(local_count):
        grad_rows = arrived_grad[member].reshape(-1, model_width)
        down_grad, inner_state = expert_down_grad(grad_rows, saved_list[member], experts[member])
        down_list.append(down_grad)
        inner_list.append(inner_state)
    parts_in = []
    gate_list = []
    up_list = []
    router_list = []
    for member in range(local_count):
        rows_in = arrived[member].reshape(-1, model_width)
        input_part, gate_weight, up_weight, router_part = expert_rest_grad(
            rows_in, inner_list[member], saved_list[member], experts[member], router[:, member]
        )
        parts_in.append(input_part.reshape(peer_count, capacity, model_width))
        gate_list.append(gate_weight)
        up_list.append(up_weight)
        router_list.append(router_part)
    router_terms = jnp.stack(router_list, axis=1)
    all_terms = jnp.stack([jnp.stack(gate_list), jnp.stack(up_list), jnp.stack(down_list)], axis=1)
    summed = lax.psum_scatter(all_terms, "dp", scatter_dimension=2, tiled=True)
    router_sum = lax.psum_scatter(router_terms, "dp", scatter_dimension=0, tiled=True)
    parts_in, summed, router_sum = (jnp.stack(parts_in), summed, router_sum)
    returned_in = lax.all_to_all(parts_in, "expert", split_axis=1, concat_axis=1, tiled=True)

    def combine(returned):
        totals = jnp.zeros((tokens.shape[0], model_width), jnp.float32)
        totals = totals.at[slot_order].add(returned.reshape(-1, model_width).astype(jnp.float32))
        return totals.astype(jnp.bfloat16)

    master_new = masters - LEARN_RATE * summed
    score_new = scores - SCORE_RATE * jnp.sum(masters * summed, axis=-1)
    return (combine(returned_out), combine(returned_in), master_new, score_new, router_sum)


def solution(mesh):
    return jax.shard_map(
        body,
        mesh=mesh,
        in_specs=(
            P(("dp", "expert"), None),
            P(("dp", "expert"), None),
            P(("dp", "expert"), None, None),
            P(None, "expert"),
            P("expert", None, None),
            P("expert", None, "dp", None),
            P("expert", None, "dp"),
        ),
        out_specs=(
            P(("dp", "expert"), None),
            P(("dp", "expert"), None),
            P("expert", None, "dp", None),
            P("expert", None, "dp"),
            P("dp", "expert"),
        ),
        check_vma=False,
    )
```

profile of v0, /device:TPU:1, one launch (start us, length us, event | category | flops | bytes accessed | tf_op | source)
XLA Modules:
  0.0 861.9 jit_solution(17191262523541266474)
XLA Ops:
  25.7 9.7 %all-to-all-start = ((bf16[2,32,8,2048]{3,2,0,1:T(8,128)(2,1)}), bf16[2,32,8,2048]{3,2,0,1:T(8,128)(2,1)S(1)}, u32[]{:S(2)}, u32[]{:S(2)}) async-start(bf16[2,32,8,2048]{3,2,0,1:T(8,128)(2,1)} %copy.239), calls=%async_computation | async-start | bytes 4194304 | tf_op jit(solution)/shard_map/all_to_all | solution.py:145
  44.9 18.9 %all-to-all-done = bf16[2,32,8,2048]{3,2,0,1:T(8,128)(2,1)S(1)} async-done(((bf16[2,32,8,2048]{3,2,0,1:T(8,128)(2,1)}), bf16[2,32,8,2048]{3,2,0,1:T(8,128)(2,1)S(1)}, u32[]{:S(2)}, u32[]{:S(2)}) %all-to-all-start) | async-done | bytes 2097184 | tf_op jit(solution)/shard_map/all_to_all | solution.py:145
  74.7 7.1 all-gather.2.cloned.1.call-done
  81.8 19.7 %fusion.110 = (bf16[1,1,128,4096]{3,0,1,2:T(2,128)(2,1)}, bf16[1,1,128,4096]{3,0,1,2:T(2,128)(2,1)S(1)}, bf16[1,1,128,4096]{3,0,1,2:T(2,128)(2,1)}, bf16[1,1,128...) fusion(bf16[2,3,128,4096]{3,0,1,2:T(2,128)(2,1)} %all-gather.2.cloned.1.call-done), kind=kLoop, calls=%fused_computation.255 | loop fusion | bytes 12582912 | tf_op jit(solution)/shard_map/slice | solution.py:28
  180.3 6.9 broadcast_select_fusion
  187.2 13.0 %gather_fusion.5 = bf16[384,64,64]{2,1,0:T(8,128)(2,1)} fusion(bf16[129,64,64]{2,1,0:T(8,128)(2,1)S(1)} %concatenate.22, s32[1024]{0:T(1024)S(1)} %pad_clamp_fusion.7), kind=kCustom, calls=%fused_computation.7.clone | custom fusion | bytes 6292992 | tf_op jit(solution)/shard_map/jit(_take)/gather | solution.py:46
  200.2 7.4 broadcast_select_fusion.1
  207.6 13.0 %gather_fusion.4 = bf16[384,64,64]{2,1,0:T(8,128)(2,1)} fusion(bf16[129,64,64]{2,1,0:T(8,128)(2,1)S(1)} %copy-done.3, s32[1024]{0:T(1024)S(1)} %pad_clamp_fusion.8), kind=kCustom, calls=%fused_computation.6.clone | custom fusion | bytes 6292992 | tf_op jit(solution)/shard_map/jit(_take)/gather | solution.py:46
  220.6 7.1 broadcast_select_fusion.2
  227.8 13.0 %gather_fusion.3 = bf16[384,64,64]{2,1,0:T(8,128)(2,1)} fusion(bf16[129,64,64]{2,1,0:T(8,128)(2,1)S(1)} %copy-done.4, s32[1024]{0:T(1024)S(1)} %pad_clamp_fusion.9), kind=kCustom, calls=%fused_computation.5.clone | custom fusion | bytes 6292992 | tf_op jit(solution)/shard_map/jit(_take)/gather | solution.py:46
  240.8 7.2 broadcast_select_fusion.3
  248.0 13.2 %gather_fusion.2 = bf16[384,64,64]{2,1,0:T(8,128)(2,1)} fusion(bf16[129,64,64]{2,1,0:T(8,128)(2,1)S(1)} %copy-done.5, s32[1024]{0:T(1024)S(1)} %pad_clamp_fusion.10), kind=kCustom, calls=%fused_computation.4.clone | custom fusion | bytes 6292992 | tf_op jit(solution)/shard_map/jit(_take)/gather | solution.py:46
  261.2 7.2 broadcast_select_fusion.4
  268.4 13.0 %gather_fusion.1 = bf16[384,64,64]{2,1,0:T(8,128)(2,1)} fusion(bf16[129,64,64]{2,1,0:T(8,128)(2,1)S(1)} %copy-done.6, s32[1024]{0:T(1024)S(1)} %pad_clamp_fusion.11), kind=kCustom, calls=%fused_computation.1.clone | custom fusion | bytes 6292992 | tf_op jit(solution)/shard_map/jit(_take)/gather | solution.py:46
  281.4 7.4 broadcast_select_fusion.5
  288.8 10.3 %copy.260 = bf16[12,64,32,64]{3,2,1,0:T(8,128)(2,1)} copy(bf16[12,64,32,64]{3,1,2,0:T(8,128)(2,1)} %bitcast.362) | data formatting | bytes 6291456 | tf_op jit(solution)/shard_map/transpose | solution.py:49
  299.0 9.7 %reshape.319 = bf16[768,2048]{1,0:T(8,128)(2,1)} reshape(bf16[12,64,32,64]{3,2,1,0:T(8,128)(2,1)} %copy.260) | data formatting | bytes 6291456 | tf_op jit(solution)/shard_map/reshape | solution.py:49
  308.8 9.4 %copy.257 = bf16[32,64,12,64]{1,0,3,2:T(8,128)(2,1)} copy(bf16[32,64,12,64]{3,1,2,0:T(8,128)(2,1)} %bitcast.363) | data formatting | bytes 6291456 | tf_op jit(solution)/shard_map/transpose | solution.py:49
  318.2 9.7 %reshape.317 = bf16[2048,768]{0,1:T(8,128)(2,1)} reshape(bf16[32,64,12,64]{1,0,3,2:T(8,128)(2,1)} %copy.257) | data formatting | bytes 6291456 | tf_op jit(solution)/shard_map/reshape | solution.py:49
  327.9 9.4 %copy.254 = bf16[32,64,12,64]{1,0,3,2:T(8,128)(2,1)} copy(bf16[32,64,12,64]{3,1,2,0:T(8,128)(2,1)} %bitcast.364) | data formatting | bytes 6291456 | tf_op jit(solution)/shard_map/transpose | solution.py:49
  337.3 9.9 %reshape.315 = bf16[2048,768]{0,1:T(8,128)(2,1)} reshape(bf16[32,64,12,64]{1,0,3,2:T(8,128)(2,1)} %copy.254) | data formatting | bytes 6291456 | tf_op jit(solution)/shard_map/reshape | solution.py:49
  347.2 10.2 %copy.250 = bf16[12,64,32,64]{3,2,1,0:T(8,128)(2,1)} copy(bf16[12,64,32,64]{3,1,2,0:T(8,128)(2,1)} %bitcast.365) | data formatting | bytes 6291456 | tf_op jit(solution)/shard_map/transpose | solution.py:49
  357.5 9.7 %reshape.313 = bf16[768,2048]{1,0:T(8,128)(2,1)} reshape(bf16[12,64,32,64]{3,2,1,0:T(8,128)(2,1)} %copy.250) | data formatting | bytes 6291456 | tf_op jit(solution)/shard_map/reshape | solution.py:49
  367.2 9.5 %copy.247 = bf16[32,64,12,64]{1,0,3,2:T(8,128)(2,1)} copy(bf16[32,64,12,64]{3,1,2,0:T(8,128)(2,1)} %bitcast.366) | data formatting | bytes 6291456 | tf_op jit(solution)/shard_map/transpose | solution.py:49
  376.6 9.7 %reshape.311 = bf16[2048,768]{0,1:T(8,128)(2,1)} reshape(bf16[32,64,12,64]{1,0,3,2:T(8,128)(2,1)} %copy.247) | data formatting | bytes 6291456 | tf_op jit(solution)/shard_map/reshape | solution.py:49
  386.4 9.5 %copy.244 = bf16[32,64,12,64]{1,0,3,2:T(8,128)(2,1)} copy(bf16[32,64,12,64]{3,1,2,0:T(8,128)(2,1)} %bitcast.367) | data formatting | bytes 6291456 | tf_op jit(solution)/shard_map/transpose | solution.py:49
  395.8 10.1 %reshape.309 = bf16[2048,768]{0,1:T(8,128)(2,1)} reshape(bf16[32,64,12,64]{1,0,3,2:T(8,128)(2,1)} %copy.244) | data formatting | bytes 6291456 | tf_op jit(solution)/shard_map/reshape | solution.py:49
  446.2 6.8 fusion.116
  453.0 7.7 gather_fusion.13
  460.7 5.9 fusion.115
  466.6 7.5 gather_fusion.12
  474.1 6.1 select_select_fusion
  492.0 6.6 fusion.114
  498.6 7.7 gather_fusion.11
  511.9 7.4 gather_fusion.10
  519.3 6.2 select_select_fusion.2
  536.3 6.7 fusion.112
  549.7 7.5 gather_fusion.9
  557.2 7.5 gather_fusion.8
  564.7 6.3 select_select_fusion.4
  593.9 19.3 %copy.284 = f32[2,3,128,4096]{3,0,1,2:T(2,128)} copy(f32[2,3,128,4096]{2,3,0,1:T(8,128)} %pad_maximum_fusion) | data formatting | bytes 25165824 | tf_op jit(solution)/shard_map/stack | solution.py:179
  616.3 7.9 all-to-all-start.1
  635.2 17.3 %all-to-all-done.1 = bf16[2,32,8,2048]{3,2,0,1:T(8,128)(2,1)S(1)} async-done(((bf16[2,32,8,2048]{3,2,0,1:T(8,128)(2,1)}), bf16[2,32,8,2048]{3,2,0,1:T(8,128)(2,1)S(1)}, u32[]{:S(2)}, u32[]{:S(2)}) %all-to-all-start.1) | async-done | bytes 2097184 | tf_op jit(solution)/shard_map/all_to_all | solution.py:155
  662.7 8.6 %scatter_custom_fusion = f32[256,2048]{1,0:T(8,128)S(1)} fusion(s32[512]{0:T(512)S(1)} %bitcast.405, bf16[512,2048]{1,0:T(8,128)(2,1)} %bitcast.385, f32[]{:T(128)} %constant.5.clone.1), kind=kCustom, calls=%fused_computation.28 | custom fusion | flops 2097152 | bytes 4194308 | tf_op jit(solution)/shard_map/scatter-add | solution.py:187
  672.5 13.9 %all-to-all-done.3 = bf16[2,32,8,2048]{3,2,0,1:T(8,128)(2,1)} async-done(((bf16[2,32,8,2048]{3,2,0,1:T(8,128)(2,1)}), bf16[2,32,8,2048]{3,2,0,1:T(8,128)(2,1)}, u32[]{:S(2)}, u32[]{:S(2)}) %all-to-all-start.3) | async-done | bytes 2097184 | tf_op jit(solution)/shard_map/all_to_all | solution.py:183
  688.0 8.7 %scatter_custom_fusion.1 = f32[256,2048]{1,0:T(8,128)} fusion(s32[512]{0:T(512)S(1)} %bitcast.406, bf16[512,2048]{1,0:T(8,128)(2,1)S(1)} %bitcast.384, f32[]{:T(128)} %constant.5.clone.1), kind=kCustom, calls=%fused_computation.26 | custom fusion | flops 2097152 | bytes 4194308 | tf_op jit(solution)/shard_map/scatter-add | solution.py:187
  699.5 142.5 %all-reduce.9.cloned.1.call-done = f32[2,3,128,4096]{3,0,1,2:T(2,128)} async-done(((f32[2,3,128,4096]{3,0,1,2:T(2,128)}), f32[2,3,128,4096]{3,0,1,2:T(2,128)}) %all-reduce.9.cloned.1.call-update) | async-done | bytes 12582928
  842.0 8.8 %multiply_reduce_fusion = (f32[2,3,32]{0,1,2:T(4,128)S(1)}, f32[2,3,32,4096]{3,0,1,2:T(2,128)S(1)}) fusion(f32[2,3,128,4096]{3,0,1,2:T(2,128)} %all-reduce.9.cloned.1.call-done, u32[]{:T(128)S(6)} %multiply.1, f32[2,3,32,4096]{3,2,1,0:T(8,128)} %param.18), kind=kLoop, calls=%fused_computation.36 | loop fusion | flops 3145536 | bytes 9437956 | tf_op jit(solution)/shard_map/reduce_sum | solution.py:191
  (283 shorter events, 248.5 us)
Async XLA Ops:
  7.2 6.3 copy-start
  7.2 5.6 copy-start.49
  7.2 74.6 %all-gather.2.cloned.1.call-start = ((), (), s32[]{:S(2)}) async-start(), calls=%async_computation.5 | async-start | bytes 7864320 | tf_op jit(solution)/shard_map/all_gather | solution.py:120
  25.7 9.7 %copy-start.51 = (s32[2,3,128]{2,0,1:T(2,128)S(1)}, s32[2,3,128]{2,0,1:T(2,128)}, u32[]{:S(2)}) copy-start(s32[2,3,128]{2,0,1:T(2,128)} %param.17) | copy-start | bytes 9220
  25.7 38.0 %all-to-all-start = ((bf16[2,32,8,2048]{3,2,0,1:T(8,128)(2,1)}), bf16[2,32,8,2048]{3,2,0,1:T(8,128)(2,1)S(1)}, u32[]{:S(2)}, u32[]{:S(2)}) async-start(bf16[2,32,8,2048]{3,2,0,1:T(8,128)(2,1)} %copy.239), calls=%async_computation | async-start | bytes 4194304 | tf_op jit(solution)/shard_map/all_to_all | solution.py:145
  36.1 74.2 %copy-start.45 = (pred[128]{0:T(512)(128)(4,1)}, pred[128]{0:T(512)(128)(4,1)S(1)}, u32[]{:S(2)}) copy-start(pred[128]{0:T(512)(128)(4,1)S(1)} %get-tuple-element.102) | copy-start | bytes 388
  36.1 83.7 %copy-start.41 = (pred[128]{0:T(512)(128)(4,1)}, pred[128]{0:T(512)(128)(4,1)S(1)}, u32[]{:S(2)}) copy-start(pred[128]{0:T(512)(128)(4,1)S(1)} %get-tuple-element.103) | copy-start | bytes 388
  36.1 96.8 %copy-start.35 = (pred[128]{0:T(512)(128)(4,1)}, pred[128]{0:T(512)(128)(4,1)S(1)}, u32[]{:S(2)}) copy-start(pred[128]{0:T(512)(128)(4,1)S(1)} %get-tuple-element.98) | copy-start | bytes 388
  36.1 109.7 %copy-start.43 = (pred[128]{0:T(512)(128)(4,1)}, pred[128]{0:T(512)(128)(4,1)S(1)}, u32[]{:S(2)}) copy-start(pred[128]{0:T(512)(128)(4,1)S(1)} %get-tuple-element.99) | copy-start | bytes 388
  36.1 122.3 %copy-start.39 = (pred[128]{0:T(512)(128)(4,1)}, pred[128]{0:T(512)(128)(4,1)S(1)}, u32[]{:S(2)}) copy-start(pred[128]{0:T(512)(128)(4,1)S(1)} %get-tuple-element.100) | copy-start | bytes 388
  36.1 134.8 %copy-start.37 = (pred[128]{0:T(512)(128)(4,1)}, pred[128]{0:T(512)(128)(4,1)S(1)}, u32[]{:S(2)}) copy-start(pred[128]{0:T(512)(128)(4,1)S(1)} %get-tuple-element.101) | copy-start | bytes 388
  63.7 10.5 %copy-start.7 = (bf16[2,32,8,2048]{3,2,0,1:T(8,128)(2,1)}, bf16[2,32,8,2048]{3,2,0,1:T(8,128)(2,1)S(1)}, u32[]{:S(2)}) copy-start(bf16[2,32,8,2048]{3,2,0,1:T(8,128)(2,1)S(1)} %all-to-all-done) | copy-start | bytes 6291460
  63.8 354.2 %all-to-all-start.2 = ((bf16[2,32,8,2048]{3,2,0,1:T(8,128)(2,1)}), bf16[2,32,8,2048]{3,2,0,1:T(8,128)(2,1)}, u32[]{:S(2)}, u32[]{:S(2)}) async-start(bf16[2,32,8,2048]{3,2,0,1:T(8,128)(2,1)} %copy.264), calls=%async_computation.2 | async-start | bytes 4194304 | tf_op jit(solution)/shard_map/all_to_all | solution.py:156
  69.0 590.6 %reduce-scatter.4.cloned.1.call-start = ((), (), s32[]{:S(2)}) async-start(), calls=%async_computation.6 | async-start | bytes 1310720
  116.0 5.6 copy-start.16
  200.2 7.4 copy-start.3
  220.6 7.2 copy-start.4
  240.8 7.2 copy-start.5
  261.2 7.2 copy-start.6
  395.8 10.1 %copy-start.8 = (bf16[2,32,8,2048]{3,2,0,1:T(8,128)(2,1)S(1)}, bf16[2,32,8,2048]{3,2,0,1:T(8,128)(2,1)}, u32[]{:S(2)}) copy-start(bf16[2,32,8,2048]{3,2,0,1:T(8,128)(2,1)} %copy-done.7) | copy-start | bytes 6291460
  409.0 5.7 copy-start.65
  425.0 5.1 copy-start.34
  453.0 7.7 copy-start.17
  453.0 7.7 copy-start.27
  466.6 7.5 copy-start.44
  466.6 7.5 copy-start.46
  466.6 7.5 copy-start.56
  466.6 7.5 copy-start.57
  485.0 4.9 copy-start.28
  485.0 7.0 copy-start.10
  498.6 7.7 copy-start.9
  511.8 7.5 copy-start.40
  511.8 7.5 copy-start.42
  511.8 7.5 copy-start.54
  511.9 7.5 copy-start.55
  557.2 7.5 copy-start.36
  557.2 7.5 copy-start.38
  557.2 7.5 copy-start.52
  557.2 7.5 copy-start.53
  575.8 4.9 copy-start.48
  575.8 5.4 copy-start.47
  583.1 258.8 %all-reduce.9.cloned.1.call-start = ((), (), s32[]{:S(2)}) async-start(), calls=%async_computation.7 | async-start | bytes 25165824
  616.3 7.9 copy-start.62
  616.3 36.2 %all-to-all-start.1 = ((bf16[2,32,8,2048]{3,2,0,1:T(8,128)(2,1)}), bf16[2,32,8,2048]{3,2,0,1:T(8,128)(2,1)S(1)}, u32[]{:S(2)}, u32[]{:S(2)}) async-start(bf16[2,32,8,2048]{3,2,0,1:T(8,128)(2,1)} %pad_maximum_fusion.1), calls=%async_computation.1 | async-start | bytes 4194304 | tf_op jit(solution)/shard_map/all_to_all | solution.py:155
  635.1 22.9 %copy-start.30 = (s32[2,32,8]{2,1,0:T(8,128)S(1)}, s32[2,32,8]{2,1,0:T(8,128)}, u32[]{:S(2)}) copy-start(s32[2,32,8]{2,1,0:T(8,128)} %copy-done.29) | copy-start | bytes 6148
  635.1 23.0 %copy-start.50 = (f32[2,3,32]{2,0,1:T(2,128)S(1)}, f32[2,3,32]{2,0,1:T(2,128)}, u32[]{:S(2)}) copy-start(f32[2,3,32]{2,0,1:T(2,128)} %param.19) | copy-start | bytes 2308
  635.1 23.2 %copy-start.58 = (u32[128]{0:T(128)S(1)}, u32[128]{0:T(128)}, u32[]{:S(2)}) copy-start(u32[128]{0:T(128)} %constant.77) | copy-start | bytes 1540
  652.5 33.8 %all-to-all-start.3 = ((bf16[2,32,8,2048]{3,2,0,1:T(8,128)(2,1)}), bf16[2,32,8,2048]{3,2,0,1:T(8,128)(2,1)}, u32[]{:S(2)}, u32[]{:S(2)}) async-start(bf16[2,32,8,2048]{3,2,0,1:T(8,128)(2,1)} %pad_maximum_fusion.2), calls=%async_computation.3 | async-start | bytes 4194304 | tf_op jit(solution)/shard_map/all_to_all | solution.py:183
  (27 other events, 65.4 us)
Sparse Core Ops, SparseCore 0:
  12.9 68.8 all-gather.1
  583.2 22.9 reduce-scatter.3
  613.4 228.5 all-reduce.8
where the time goes:
time: 873 us; the launch traced here: 862 us
  local copies, waits for them, and re-layouts  415 us (48%)
  waiting for transfers between devices  200 us (23%)
  other arithmetic  131 us (15%)
  matrix products  71.1 us (8%)
  starting transfers between devices  28.8 us (3%)
  between operations  15.7 us (2%)
    unnamed x5, waiting for transfers between devices  143 us
    gather x6, local copies, waits for them, and re-layouts, block_matrix(): jnp.take(padded, slot_of, axis=0)  70.8 us
    reshape x6, local copies, waits for them, and re-layouts, block_matrix(): placed.transpose(0, 2, 1, 3)  58.9 us
    transpose x6, local copies, waits for them, and re-layouts, block_matrix(): placed.transpose(0, 2, 1, 3)  58.3 us
    unnamed x150, local copies, waits for them, and re-layouts  51.5 us
    gather x6, local copies, waits for them, and re-layouts, weight_grad(): jnp.take(full_grad.reshape(-1, tile_width, tile_width), block_plan[3], ax...  45.3 us
    select_n x6, other arithmetic, block_matrix(): jnp.take(padded, slot_of, axis=0)  43.2 us
    dot_general x6, matrix products, weight_grad(): lax.dot_general(operand, cotangent, (((0,), (0,)), ((), ())), preferred_e...  37 us
  transfers between devices with their start and end apart: 7, of which 5 were waited for; matrix products, arithmetic and copies ran while one was open for 49% of the time, Pallas kernels for 0%

commit v1 on v0

v1 whole, which is shorter than its diff:
```python
import functools

import jax
import jax.numpy as jnp
from jax import lax
from jax.experimental import pallas as pl
from jax.experimental.pallas import tpu as pltpu
from jax.sharding import PartitionSpec as P

D = 2048
FF = 768
BS = 64
MAXB = 128
BLOCKS = (D // BS) * (FF // BS)
LEARN_RATE = 0.005
SCORE_RATE = 0.05
CHUNK = 256
F32 = jnp.float32
BF16 = jnp.bfloat16
NN = (((1,), (0,)), ((), ()))
NT = (((1,), (1,)), ((), ()))
TN = (((0,), (0,)), ((), ()))


def dot(left, right, dims=NN):
    return lax.dot_general(left, right, dims, preferred_element_type=F32)


def iota(shape, dim):
    return lax.broadcasted_iota(jnp.int32, shape, dim)


def one_hot(flag):
    return jnp.where(flag, 1.0, 0.0).astype(BF16)


def split_matrix(size):
    col = iota((size, size), 1)
    source = ((col >> 6) << 6) + 2 * (col & 31) + ((col >> 5) & 1)
    return one_hot(iota((size, size), 0) == source)


def pick_columns(picks_ref, member, locals_count):
    peers = picks_ref.shape[0] // locals_count
    rows = 16 * peers
    row = iota((rows, picks_ref.shape[0]), 0)
    expert = (row >> 4) * locals_count + member
    spread = one_hot(iota((rows, picks_ref.shape[0]), 1) == expert)
    table = picks_ref[...].astype(F32).astype(BF16)
    wide = dot(spread, table)
    keep = iota(wide.shape, 1) == (iota(wide.shape, 0) & 7)
    return jnp.sum(jnp.where(keep, wide, 0.0), axis=1, keepdims=True).astype(jnp.int32)


def pick_kernel(picks_ref, tokens_ref, grads_ref, *rest, locals_count):
    out_refs, hot_ref = rest[:locals_count], rest[locals_count]
    rows = hot_ref.shape[1]
    count = tokens_ref.shape[0]

    @pl.when(pl.program_id(0) == 0)
    def _():
        for member in range(locals_count):
            index = pick_columns(picks_ref, member, locals_count)
            row = iota((rows, 1), 0)
            index = index + jnp.where((row & 8) > 0, count, 0)
            hot_ref[member] = one_hot(iota((rows, 2 * count), 1) == index)

    split = split_matrix(CHUNK)
    both = jnp.concatenate([dot(tokens_ref[...], split).astype(BF16), grads_ref[...]], axis=0)
    for member in range(locals_count):
        picked = dot(hot_ref[member], both).astype(BF16)
        out_refs[member][...] = picked.reshape(out_refs[member].shape)


def pack_kernel(masters_ref, out_ref, lines_ref):
    for group in range(masters_ref.shape[0] // 8):
        for k in range(32):
            lines_ref[group, 8 * k : 8 * k + 8, :] = masters_ref[
                8 * group : 8 * group + 8, 128 * k : 128 * k + 128
            ]
        for s in range(8):
            out_ref[8 * group + s] = lines_ref[group, pl.ds(s, 32, stride=8), :].astype(BF16)


def expert_kernel(
    inverse_ref, row_ref, lane_ref, valid_ref,
    copies_ref, arrived_ref, router_ref,
    send_ref, packed_ref, router_out_ref,
    wide_ref, down_ref, rows_ref, grads_ref, pre_ref, part_ref, both_ref,
    grad_wide_ref, grad_down_ref,
    *, base,
):
    lane = iota((32, 128), 1)
    half = lane < 64

    def place(target_ref, matrix, block, row, col):
        first = inverse_ref[base + matrix * BLOCKS + block]
        second = inverse_ref[base + matrix * BLOCKS + block + 1]
        one = copies_ref[jnp.maximum(first, 0)]
        two = copies_ref[jnp.maximum(second, 0)]
        one = jnp.where(lane < jnp.where(first >= 0, 128, 0), one, jnp.zeros_like(one))
        two = jnp.where(lane < jnp.where(second >= 0, 128, 0), two, jnp.zeros_like(two))
        target_ref[pl.ds(row, 32), col : col + 128] = jnp.where(half, one, pltpu.roll(two, 64, 1))
        target_ref[pl.ds(row + 32, 32), col : col + 128] = jnp.where(half, pltpu.roll(one, 64, 1), two)

    @pl.loop(0, D // BS)
    def _(r):
        row = pl.multiple_of(r * BS, BS)
        for matrix in range(2):
            for pair in range(FF // BS // 2):
                place(wide_ref, matrix, r * (FF // BS) + 2 * pair, row, matrix * FF + 128 * pair)

    @pl.loop(0, FF // BS)
    def _(r):
        row = pl.multiple_of(r * BS, BS)
        for pair in range(D // BS // 2):
            place(down_ref, 2, r * (D // BS) + 2 * pair, row, 128 * pair)

    count = rows_ref.shape[0]
    wanted = iota((count, 2 * count), 0)
    wanted = ((wanted >> 3) << 4) + (wanted & 7)
    first_rows = one_hot(iota((count, 2 * count), 1) == wanted)
    second_rows = one_hot(iota((count, 2 * count), 1) == wanted + 8)
    chunks = D // CHUNK

    def take(n, logit):
        cols = pl.ds(pl.multiple_of(n * CHUNK, CHUNK), CHUNK)
        block = arrived_ref[:, :, cols].reshape(2 * count, CHUNK)
        rows = dot(first_rows, block)
        rows_ref[:, cols] = rows.astype(BF16)
        grads_ref[:, cols] = dot(second_rows, block).astype(BF16)
        return logit + jnp.sum(rows * router_ref[:, cols], axis=1, keepdims=True)

    logit = lax.fori_loop(0, chunks, take, jnp.zeros((count, 1), F32))
    gating = 1.0 / (1.0 + jnp.exp(-logit))

    @pl.loop(0, 2 * FF // 512)
    def _(n):
        cols = pl.ds(pl.multiple_of(n * 512, 512), 512)
        pre_ref[:, cols] = dot(rows_ref[...], wide_ref[:, cols])

    split = split_matrix(CHUNK)
    hidden_list = []
    for n in range(FF // CHUNK):
        gate_pre = pre_ref[:, n * CHUNK : (n + 1) * CHUNK]
        up_pre = pre_ref[:, FF + n * CHUNK : FF + (n + 1) * CHUNK]
        hidden = (gate_pre / (1.0 + jnp.exp(-gate_pre)) * up_pre).astype(BF16)
        hidden_list.append(dot(hidden, split).astype(BF16))
    hidden_split = jnp.concatenate(hidden_list, axis=1)

    @pl.loop(0, D // 512)
    def _(n):
        cols = pl.ds(pl.multiple_of(n * 512, 512), 512)
        part_ref[:, cols] = (gating * dot(hidden_split, down_ref[:, cols])).astype(BF16)
        grads_ref[:, cols] = (gating * grads_ref[:, cols].astype(F32)).astype(BF16)

    logit_sum = jnp.zeros((count, 1), F32)
    for n in range(FF // CHUNK):
        spread = dot(grads_ref[...], down_ref[n * CHUNK : (n + 1) * CHUNK, :], NT)
        high = spread.astype(BF16)
        low = (spread - high.astype(F32)).astype(BF16)
        hidden_grad = dot(high, split, NT) + dot(low, split, NT)
        logit_sum = logit_sum + jnp.sum(
            hidden_list[n].astype(F32) * spread, axis=1, keepdims=True
        )
        gate_pre = pre_ref[:, n * CHUNK : (n + 1) * CHUNK]
        up_pre = pre_ref[:, FF + n * CHUNK : FF + (n + 1) * CHUNK]
        sigma = 1.0 / (1.0 + jnp.exp(-gate_pre))
        gate_grad = hidden_grad * up_pre * sigma * (1.0 + gate_pre * (1.0 - sigma))
        both_ref[:, n * CHUNK : (n + 1) * CHUNK] = gate_grad.astype(BF16)
        both_ref[:, FF + n * CHUNK : FF + (n + 1) * CHUNK] = (hidden_grad * gate_pre * sigma).astype(BF16)
        grad_down_ref[n * CHUNK : (n + 1) * CHUNK, :] = dot(hidden_list[n], grads_ref[...], TN).astype(BF16)
    logit_grad = logit_sum * (1.0 - gating)

    @pl.loop(0, chunks)
    def _(n):
        cols = pl.ds(pl.multiple_of(n * CHUNK, CHUNK), CHUNK)
        part = dot(both_ref[...], wide_ref[cols, :], NT) + logit_grad * router_ref[:, cols]
        pair = jnp.concatenate(
            [part_ref[:, cols].astype(F32).reshape(-1, 8, CHUNK), part.reshape(-1, 8, CHUNK)], axis=1
        )
        send_ref[:, :, cols] = pair.astype(BF16)
        rows = rows_ref[:, cols]
        router_out_ref[:, cols] = jnp.sum(logit_grad * rows.astype(F32), axis=0, keepdims=True)
        grad_wide_ref[cols, :] = dot(rows, both_ref[...], TN).astype(BF16)

    def cut(source_ref, matrix, slot, place_in):
        at = matrix * MAXB + slot
        row = pl.multiple_of(row_ref[at], 32)
        other = pl.multiple_of(row ^ 32, 32)
        cols = pl.ds(pl.multiple_of(lane_ref[at], 128), 128)
        odd = row & 32
        stay = source_ref[pl.ds(row, 32), cols]
        move = pltpu.roll(source_ref[pl.ds(other, 32), cols], 64, 1)
        tile = jnp.where((lane & 64) == 2 * odd, stay, move)
        limit = jnp.where(valid_ref[at] > 0, 128, 0)
        packed_ref[place_in] = jnp.where(lane < limit, tile, jnp.zeros_like(tile))

    slots = MAXB // (packed_ref.shape[0] // (3 * (MAXB // 4)))
    per = MAXB // 4

    for owner in range(4):
        for matrix in range(3):
            source_ref = grad_down_ref if matrix == 2 else grad_wide_ref

            @pl.loop(0, per // 4)
            def _(group, owner=owner, matrix=matrix, source_ref=source_ref):
                for step in range(4):
                    s = group * 4 + step
                    cut(source_ref, matrix, owner * per + s, (owner * 3 + matrix) * per + s)


def update_kernel(summed_ref, masters_ref, out_ref, total_ref, lines_ref):
    for group in range(masters_ref.shape[0] // 8):
        for s in range(8):
            lines_ref[group, pl.ds(s, 32, stride=8), :] = summed_ref[8 * group + s].astype(F32)
        total = jnp.zeros((8, 128), F32)
        rows = slice(8 * group, 8 * group + 8)
        for k in range(32):
            cols = slice(128 * k, 128 * k + 128)
            gradient = lines_ref[group, 8 * k : 8 * k + 8, :]
            held = masters_ref[rows, cols]
            out_ref[rows, cols] = held - LEARN_RATE * gradient
            total = total + held * gradient
        total_ref[rows, :] = jnp.sum(total, axis=1, keepdims=True)


def combine_kernel(picks_ref, *rest, locals_count):
    back_refs = rest[:locals_count]
    out_ref, in_ref, hot_ref = rest[locals_count:]
    rows, count = hot_ref.shape[2], hot_ref.shape[3]

    @pl.when(pl.program_id(0) == 0)
    def _():
        for member in range(locals_count):
            index = pick_columns(picks_ref, member, locals_count)
            late = (iota((rows, 1), 0) & 8) > 0
            for side in range(2):
                mine = jnp.where(late == (side == 1), index, -1)
                hot_ref[side, member] = one_hot(iota((rows, count), 1) == mine)

    sums = [jnp.zeros((count, CHUNK), F32), jnp.zeros((count, CHUNK), F32)]
    for member in range(locals_count):
        block = back_refs[member][...].reshape(rows, CHUNK)
        for side in range(2):
            sums[side] = sums[side] + dot(hot_ref[side, member], block, TN)
    out_ref[...] = sums[0].astype(BF16)
    in_ref[...] = dot(sums[1].astype(BF16), split_matrix(CHUNK), NT).astype(BF16)


def params(mib):
    return pltpu.CompilerParams(vmem_limit_bytes=mib * 1024 * 1024)


def cost(flops, moved):
    return pl.CostEstimate(flops=flops, bytes_accessed=moved, transcendentals=0)


def pick(picks, tokens, grads, locals_count, peers):
    count, width = tokens.shape
    rows = 16 * peers
    column = pl.BlockSpec((count, CHUNK), lambda n: (0, n))
    return pl.pallas_call(
        functools.partial(pick_kernel, locals_count=locals_count),
        grid=(width // CHUNK,),
        in_specs=[pl.BlockSpec(picks.shape, lambda n: (0, 0)), column, column],
        out_specs=[pl.BlockSpec((peers, 16, CHUNK), lambda n: (0, 0, n))] * locals_count,
        out_shape=[jax.ShapeDtypeStruct((peers, 16, width), BF16)] * locals_count,
        scratch_shapes=[pltpu.VMEM((locals_count, rows, 2 * count), BF16)],
        compiler_params=params(32),
        cost_estimate=cost(2 * rows * 2 * count * width * locals_count, 12 << 20),
        name="pick",
    )(picks, tokens, grads)


def pack(masters):
    slots = masters.shape[0]
    return pl.pallas_call(
        pack_kernel,
        grid=(slots // 32,),
        in_specs=[pl.BlockSpec((32, BS * BS), lambda n: (n, 0))],
        out_specs=pl.BlockSpec((32, 32, 128), lambda n: (n, 0, 0)),
        out_shape=jax.ShapeDtypeStruct((slots, 32, 128), BF16),
        scratch_shapes=[pltpu.VMEM((4, 256, 128), F32)],
        compiler_params=params(32),
        cost_estimate=cost(0, slots * BS * BS * 6),
        name="pack",
    )(masters)


def run_expert(member, tables, copies, arrived, router_row):
    inverse, rows, lanes, valid = tables
    peers = arrived.shape[0]
    count = 8 * peers
    whole = pl.BlockSpec(memory_space=pltpu.VMEM)
    scalar = pl.BlockSpec(memory_space=pltpu.SMEM)
    return pl.pallas_call(
        functools.partial(expert_kernel, base=0),
        in_specs=[scalar] * 4 + [whole] * 3,
        out_specs=[whole] * 3,
        out_shape=[
            jax.ShapeDtypeStruct((peers, 16, D), BF16),
            jax.ShapeDtypeStruct((3 * MAXB, 32, 128), BF16),
            jax.ShapeDtypeStruct((1, D), F32),
        ],
        scratch_shapes=[
            pltpu.VMEM((D, 2 * FF), BF16),
            pltpu.VMEM((FF, D), BF16),
            pltpu.VMEM((count, D), BF16),
            pltpu.VMEM((count, D), BF16),
            pltpu.VMEM((count, 2 * FF), F32),
            pltpu.VMEM((count, D), BF16),
            pltpu.VMEM((count, 2 * FF), BF16),
            pltpu.VMEM((D, 2 * FF), BF16),
            pltpu.VMEM((FF, D), BF16),
        ],
        compiler_params=params(56),
        cost_estimate=cost(9 * 2 * count * D * FF * 2, 60 << 20),
        name="expert_%d" % member,
    )(inverse[member], rows[member], lanes[member], valid[member], copies, arrived, router_row)


def update(summed, masters):
    slots = masters.shape[0]
    return pl.pallas_call(
        update_kernel,
        grid=(slots // 32,),
        in_specs=[
            pl.BlockSpec((32, 32, 128), lambda n: (n, 0, 0)),
            pl.BlockSpec((32, BS * BS), lambda n: (n, 0)),
        ],
        out_specs=[
            pl.BlockSpec((32, BS * BS), lambda n: (n, 0)),
            pl.BlockSpec((32, 1), lambda n: (n, 0)),
        ],
        out_shape=[
            jax.ShapeDtypeStruct((slots, BS * BS), F32),
            jax.ShapeDtypeStruct((slots, 1), F32),
        ],
        scratch_shapes=[pltpu.VMEM((4, 256, 128), F32)],
        compiler_params=params(32),
        cost_estimate=cost(4 * slots * BS * BS, slots * BS * BS * 10),
        name="update",
    )(summed, masters)


def combine(picks, back, count):
    locals_count = len(back)
    peers, _, width = back[0].shape
    rows = 16 * peers
    column = pl.BlockSpec((count, CHUNK), lambda n: (0, n))
    return pl.pallas_call(
        functools.partial(combine_kernel, locals_count=locals_count),
        grid=(width // CHUNK,),
        in_specs=[pl.BlockSpec(picks.shape, lambda n: (0, 0))]
        + [pl.BlockSpec((peers, 16, CHUNK), lambda n: (0, 0, n))] * locals_count,
        out_specs=[column, column],
        out_shape=[jax.ShapeDtypeStruct((count, width), BF16)] * 2,
        scratch_shapes=[pltpu.VMEM((2, locals_count, rows, count), BF16)],
        compiler_params=params(32),
        cost_estimate=cost(4 * rows * count * width * locals_count, 6 << 20),
        name="combine",
    )(picks, *back)


def slot_tables(kept, owners):
    numbers = jnp.arange(BLOCKS, dtype=jnp.int32)
    slots = jnp.arange(MAXB, dtype=jnp.int32)
    per = MAXB // owners
    matrix = jnp.arange(3, dtype=jnp.int32)[None, :, None]
    place = (slots // per) * (3 * per) + slots % per + matrix * per
    hits = kept[:, :, None, :] == numbers[None, None, :, None]
    inverse = jnp.sum(jnp.where(hits, place[:, :, None, :] + 1, 0), axis=-1) - 1
    valid = kept < BLOCKS
    block = jnp.where(valid, kept, 0)
    width = jnp.array([FF // BS, FF // BS, D // BS], jnp.int32)[None, :, None]
    block_row, block_col = block // width, block % width
    rows = block_row * BS + 32 * (block_col & 1)
    lanes = (block_col >> 1) * 128 + jnp.where(matrix == 1, FF, 0)
    flat = lambda table: table.reshape(table.shape[0], -1).astype(jnp.int32)
    return flat(inverse), flat(rows), flat(lanes), flat(valid)


def body(tokens, out_grad, token_picks, router, kept_blocks, masters, scores):
    locals_count = kept_blocks.shape[0]
    owners = lax.axis_size("dp")
    peers = lax.axis_size("expert")
    count, width = tokens.shape
    per = masters.shape[2]
    picks = token_picks[0]
    flat_masters = masters.reshape(locals_count * 3 * per, BS * BS)

    packed = pack(flat_masters)
    sent = pick(picks, tokens, out_grad, locals_count, peers)
    tables = slot_tables(kept_blocks, owners)
    router_rows = router.T.reshape(locals_count, width // BS, 32, 2).transpose(0, 1, 3, 2)
    router_rows = router_rows.reshape(locals_count, 1, width).astype(F32)

    copies, arrived = [], []
    for member in range(locals_count):
        mine = packed[member * 3 * per : (member + 1) * 3 * per]
        copies.append(lax.all_gather(mine, "dp", axis=0, tiled=True))
        arrived.append(lax.all_to_all(sent[member], "expert", split_axis=0, concat_axis=0, tiled=True))
    summed, back, router_parts = [], [], []
    for member in range(locals_count):
        send, gradient, router_part = run_expert(
            member, tables, copies[member], arrived[member], router_rows[member]
        )
        summed.append(lax.psum_scatter(gradient, "dp", scatter_dimension=0, tiled=True))
        back.append(lax.all_to_all(send, "expert", split_axis=0, concat_axis=0, tiled=True))
        router_parts.append(router_part)
    router_sum = jnp.stack(router_parts, axis=1).reshape(locals_count, owners, width // owners)
    router_sum = lax.psum_scatter(router_sum.transpose(1, 0, 2), "dp", scatter_dimension=0, tiled=True)
    router_new = router_sum.reshape(locals_count, width // owners // BS, 2, 32)
    router_new = router_new.transpose(1, 3, 2, 0).reshape(width // owners, locals_count)

    new_list, total_list = [], []
    for member in range(locals_count):
        mine = flat_masters[member * 3 * per : (member + 1) * 3 * per]
        new, total = update(summed[member], mine)
        new_list.append(new)
        total_list.append(total)
    layer_out, input_grad = combine(picks, back, count)
    master_new = jnp.stack(new_list).reshape(masters.shape)
    score_new = scores - SCORE_RATE * jnp.stack(total_list).reshape(scores.shape)
    return layer_out, input_grad, master_new, score_new, router_new


def solution(mesh):
    return jax.shard_map(
        body,
        mesh=mesh,
        in_specs=(
            P(("dp", "expert"), None),
            P(("dp", "expert"), None),
            P(("dp", "expert"), None, None),
            P(None, "expert"),
            P("expert", None, None),
            P("expert", None, "dp", None),
            P("expert", None, "dp"),
        ),
        out_specs=(
            P(("dp", "expert"), None),
            P(("dp", "expert"), None),
            P("expert", None, "dp", None),
            P("expert", None, "dp"),
            P("dp", "expert"),
        ),
        check_vma=False,
    )
```

time: 873 us -> 257 us (0.29); the launches traced: 862 us -> 256 us
  local copies, waits for them, and re-layouts: 415 us -> 26.7 us
  waiting for transfers between devices: 200 us -> 58.1 us
  other arithmetic: 131 us -> 4.27 us
  Pallas kernels: 0 us -> 86.4 us
  matrix products: 71.1 us -> 0 us
  blocking collectives: 0 us -> 47.2 us
  starting transfers between devices: 28.8 us -> 19.6 us
    unnamed x5 -> x4, waiting for transfers between devices: 143 us -> 0.74 us
    gather x14 -> x0, local copies, waits for them, and re-layouts: 123 us -> none  [the longest x6 70.8 us: block_matrix(): jnp.take(padded, slot_of, axis=0)]
    pallas_call x0 -> x7, Pallas kernels: none -> 86.4 us  [the longest x2 68.9 us: run_expert(): pl.pallas_call(functools.partial(expert_kernel, base=0), in_specs=[scalar...]
    select_n x24 -> x1, other arithmetic: 78 us -> 0.01 us  [slot_tables(): lanes = (block_col >> 1) * 128 + jnp.where(matrix == 1, FF, 0)]
    dot_general x22 -> x0, matrix products: 71.1 us -> none  [the longest x6 37 us: weight_grad(): lax.dot_general(operand, cotangent, (((0,), (0,)), ((), ())), preferred_e...]
    reshape x10 -> x2, local copies, waits for them, and re-layouts: 63.9 us -> 0.86 us  [the longest x1 0.77 us: body(): router_new.transpose(1, 3, 2, 0).reshape(width // owners, locals_count)]
    transpose x7 -> x1, local copies, waits for them, and re-layouts: 58.3 us -> 0.18 us  [body(): router_new.transpose(1, 3, 2, 0).reshape(width // owners, locals_count)]
    unnamed x150 -> x53, local copies, waits for them, and re-layouts: 51.5 us -> 14.7 us
  transfers between devices with their start and end apart: 7 -> 7, of which waited for: 5 -> 3; matrix products, arithmetic and copies ran while one was open for 49% -> 5% of each run, Pallas kernels for 0% -> 33%
where the time goes in v1:
time: 257 us; the launch traced here: 256 us
  Pallas kernels  86.4 us (34%)
  waiting for transfers between devices  58.1 us (23%)
  blocking collectives  47.2 us (18%)
  local copies, waits for them, and re-layouts  26.7 us (10%)
  starting transfers between devices  19.6 us (8%)
  between operations  14 us (5%)
  other arithmetic  4.27 us (2%)
    pallas_call x2, Pallas kernels, run_expert(): pl.pallas_call(functools.partial(expert_kernel, base=0), in_specs=[scalar...  68.9 us
    all_to_all x2, waiting for transfers between devices, body(): lax.all_to_all(sent[member], 'expert', split_axis=0, concat_axis=0, tiled...  48.1 us
    all_to_all x1, blocking collectives, body(): lax.all_to_all(send, 'expert', split_axis=0, concat_axis=0, tiled=True)  32.4 us
    unnamed x1, blocking collectives  14.8 us
    unnamed x53, local copies, waits for them, and re-layouts  14.7 us
    all_to_all x2, starting transfers between devices, body(): lax.all_to_all(sent[member], 'expert', split_axis=0, concat_axis=0, tiled...  14.4 us
    all_to_all x1, waiting for transfers between devices, body(): lax.all_to_all(send, 'expert', split_axis=0, concat_axis=0, tiled=True)  9.28 us
    pallas_call x1, Pallas kernels, combine(): pl.pallas_call(functools.partial(combine_kernel, locals_count=locals_coun...  8.18 us
  transfers between devices with their start and end apart: 7, of which 3 were waited for; matrix products, arithmetic and copies ran while one was open for 5% of the time, Pallas kernels for 33%

profile of v1, /device:TPU:1, one launch (start us, length us, event | category | flops | bytes accessed | tf_op | source)
XLA Modules:
  0.0 256.4 jit_solution(17411764777085480045)
XLA Ops:
  7.2 1.9 copy-done
  9.1 0.8 pack.1
  10.0 1.4 fusion.4
  11.4 0.7 all-gather.3.cloned.1.call-update
  12.3 7.2 %pick.1 = (bf16[32,16,2048]{2,1,0:T(8,128)(2,1)}, bf16[32,16,2048]{2,1,0:T(8,128)(2,1)}) custom-call(s32[64,8]{1,0:T(8,128)S(1)} %bitcast.30, bf16[256,2048]{1,0:T(8,128)(2,1)S(1)} %copy-done.10, bf16[256,2048]{1,0:T(8,128)(2,1)S(1)} %copy-done.11), custom_call_target="tpu_custom_call" | custom-call | flops 2147483648 | bytes 12582912 | tf_op jit(solution)/shard_map/pick/pallas_call | solution.py:263
  19.4 9.7 %all-to-all-start.2 = ((bf16[32,16,2048]{2,1,0:T(8,128)(2,1)}), bf16[32,16,2048]{2,1,0:T(8,128)(2,1)S(1)}, u32[]{:S(2)}, u32[]{:S(2)}) async-start(bf16[32,16,2048]{2,1,0:T(8,128)(2,1)} %get-tuple-element.21), calls=%async_computation.2 | async-start | bytes 4194304 | tf_op jit(solution)/shard_map/all_to_all | solution.py:403
  29.3 1.0 reshape.162
  30.4 0.4 select_reduce_fusion
  30.8 0.6 squeeze.39.inverse_ref
  31.4 1.1 fusion.5
  32.5 1.3 copy.46
  33.8 0.7 squeeze.43.router_ref
  34.5 0.6 slice_reduce_fusion
  35.1 0.2 multiply_add_fusion
  35.3 0.6 slice_reduce_fusion.1
  35.9 21.5 %all-to-all-done.2.arrived_ref = bf16[32,16,2048]{2,1,0:T(8,128)(2,1)S(1)} async-done(((bf16[32,16,2048]{2,1,0:T(8,128)(2,1)}), bf16[32,16,2048]{2,1,0:T(8,128)(2,1)S(1)}, u32[]{:S(2)}, u32[]{:S(2)}) %all-to-all-start.2) | async-done | bytes 2097184 | tf_op jit(solution)/shard_map/all_to_all | solution.py:403
  57.5 1.4 copy-done.12
  58.9 34.5 %expert_1.1 = (bf16[32,16,2048]{2,1,0:T(8,128)(2,1)}, bf16[384,32,128]{2,1,0:T(8,128)(2,1)}, f32[1,2048]{1,0:T(1,128)}) custom-call(s32[1152]{0:T(1024)} %squeeze.39.inverse_ref, s32[384]{0:T(512)} %bitcast.41, s32[384]{0:T(512)} %bitcast.40, s32[384]{0:T(512)} %bitcast.39, bf16[384,32,128]{2,1,0:T(8,128)(2,1)} %all-gather.5.cloned.1.call-done.copies_ref, ...), custom_call_target="tpu_custom_call" | custom-call | flops 14495514624 | bytes 62914560 | tf_op jit(solution)/shard_map/expert_1/pallas_call | solution.py:297
  93.4 4.7 %all-to-all-start = ((bf16[32,16,2048]{2,1,0:T(8,128)(2,1)}), bf16[32,16,2048]{2,1,0:T(8,128)(2,1)S(1)}, u32[]{:S(2)}, u32[]{:S(2)}) async-start(bf16[32,16,2048]{2,1,0:T(8,128)(2,1)} %get-tuple-element.19), calls=%async_computation | async-start | bytes 4194304 | tf_op jit(solution)/shard_map/all_to_all | solution.py:403
  98.1 0.2 reduce-scatter.3.cloned.1.call-start
  98.3 0.6 squeeze.34.inverse_ref
  98.9 0.3 copy.45
  99.2 0.7 squeeze.38.router_ref
  99.9 26.6 %all-to-all-done.arrived_ref = bf16[32,16,2048]{2,1,0:T(8,128)(2,1)S(1)} async-done(((bf16[32,16,2048]{2,1,0:T(8,128)(2,1)}), bf16[32,16,2048]{2,1,0:T(8,128)(2,1)S(1)}, u32[]{:S(2)}, u32[]{:S(2)}) %all-to-all-start) | async-done | bytes 2097184 | tf_op jit(solution)/shard_map/all_to_all | solution.py:403
  126.5 1.4 copy-done.13
  127.9 34.5 %expert_0.1 = (bf16[32,16,2048]{2,1,0:T(8,128)(2,1)}, bf16[384,32,128]{2,1,0:T(8,128)(2,1)}, f32[1,2048]{1,0:T(1,128)}) custom-call(s32[1152]{0:T(1024)} %squeeze.34.inverse_ref, s32[384]{0:T(512)} %bitcast.38, s32[384]{0:T(512)} %bitcast.37, s32[384]{0:T(512)} %bitcast.36, bf16[384,32,128]{2,1,0:T(8,128)(2,1)} %all-gather.3.cloned.1.call-done.copies_ref, ...), custom_call_target="tpu_custom_call" | custom-call | flops 14495514624 | bytes 62914560 | tf_op jit(solution)/shard_map/expert_0/pallas_call | solution.py:297
  162.4 1.6 copy-done.14
  164.0 32.4 %all_to_all.20.rest_0_ = bf16[32,16,2048]{2,1,0:T(8,128)(2,1)} all-to-all(bf16[32,16,2048]{2,1,0:T(8,128)(2,1)S(1)} %copy-done.14), channel_id=1, replica_groups=mesh['dp'=4,'expert'=32] {'expert'}, dimensions={0} | all-to-all | bytes 4194304 | tf_op jit(solution)/shard_map/all_to_all | solution.py:410
  196.4 4.8 %all-to-all-start.3 = ((bf16[32,16,2048]{2,1,0:T(8,128)(2,1)}), bf16[32,16,2048]{2,1,0:T(8,128)(2,1)}, u32[]{:S(2)}, u32[]{:S(2)}) async-start(bf16[32,16,2048]{2,1,0:T(8,128)(2,1)} %get-tuple-element.22), calls=%async_computation.3 | async-start | bytes 4194304 | tf_op jit(solution)/shard_map/all_to_all | solution.py:410
  201.2 0.6 dynamic-slice
  201.8 1.9 fusion.3
  203.8 14.8 %all-reduce = f32[4,2,512]{2,1,0:T(2,128)S(1)} all-reduce(f32[4,2,512]{2,1,0:T(2,128)S(1)} %maximum_bitcast_fusion), channel_id=4, replica_groups=mesh['dp'=4,'expert'=32] {'dp'}, use_global_device_ids=true, to_apply=%region_3.4.clone | all-reduce | flops 4096 | bytes 32768
  218.6 0.6 constant_dynamic-slice_fusion
  219.4 0.2 copy.50
  219.5 0.8 reshape.161
  220.3 9.3 %all-to-all-done.3.rest_1_ = bf16[32,16,2048]{2,1,0:T(8,128)(2,1)} async-done(((bf16[32,16,2048]{2,1,0:T(8,128)(2,1)}), bf16[32,16,2048]{2,1,0:T(8,128)(2,1)}, u32[]{:S(2)}, u32[]{:S(2)}) %all-to-all-start.3) | async-done | bytes 2097184 | tf_op jit(solution)/shard_map/all_to_all | solution.py:410
  229.6 1.6 copy-done.4
  231.2 8.2 %combine.1 = (bf16[256,2048]{1,0:T(8,128)(2,1)}, bf16[256,2048]{1,0:T(8,128)(2,1)}) custom-call(s32[64,8]{1,0:T(8,128)S(1)} %bitcast.31, bf16[32,16,2048]{2,1,0:T(8,128)(2,1)S(1)} %copy-done.4, bf16[32,16,2048]{2,1,0:T(8,128)(2,1)} %all-to-all-done.3.rest_1_), custom_call_target="tpu_custom_call" | custom-call | flops 2147483648 | bytes 6291456 | tf_op jit(solution)/shard_map/combine/pallas_call | solution.py:352
  239.4 1.2 copy-done.8
  240.6 0.7 update.3
  241.3 1.2 copy-done.5
  242.5 0.1 reduce.7
  242.7 1.2 copy-done.9
  243.9 0.7 update.2
  244.6 1.1 copy-done.7
  245.7 0.1 reduce.6
  246.0 0.6 copy.51
  246.5 3.3 %pad_maximum_fusion = f32[2,3,32,4096]{3,2,1,0:T(8,128)} fusion(f32[1,3,32,4096]{3,2,1,0:T(8,128)S(1)} %bitcast.28, f32[1,3,32,4096]{3,2,1,0:T(8,128)} %bitcast.29), kind=kLoop, calls=%fused_computation | loop fusion | flops 786432 | bytes 6291456 | tf_op jit(solution)/shard_map/stack | solution.py:424
  (64 shorter events, 0.7 us)
Async XLA Ops:
  7.2 50.3 %all-gather.5.cloned.1.call-start = ((), (), s32[]{:S(2)}) async-start(), calls=%async_computation.7 | async-start | bytes 3932160 | tf_op jit(solution)/shard_map/all_gather | solution.py:402
  7.2 1.9 copy-start
  9.9 2.2 copy-start.20
  9.9 2.3 copy-start.10
  10.0 2.3 copy-start.11
  11.4 115.1 %all-gather.3.cloned.1.call-start = ((), (), s32[]{:S(2)}) async-start(), calls=%async_computation.6 | async-start | bytes 3932160 | tf_op jit(solution)/shard_map/all_gather | solution.py:402
  19.4 9.8 %copy-start.17 = (bf16[2048,2]{0,1:T(2,128)(2,1)S(1)}, bf16[2048,2]{0,1:T(2,128)(2,1)}, u32[]{:S(2)}) copy-start(bf16[2048,2]{0,1:T(2,128)(2,1)} %param.11) | copy-start | bytes 24580
  19.4 9.8 %copy-start.16 = (s32[2,3,128]{2,0,1:T(2,128)S(1)}, s32[2,3,128]{2,0,1:T(2,128)}, u32[]{:S(2)}) copy-start(s32[2,3,128]{2,0,1:T(2,128)} %param.12) | copy-start | bytes 9220
  19.4 38.0 %all-to-all-start.2 = ((bf16[32,16,2048]{2,1,0:T(8,128)(2,1)}), bf16[32,16,2048]{2,1,0:T(8,128)(2,1)S(1)}, u32[]{:S(2)}, u32[]{:S(2)}) async-start(bf16[32,16,2048]{2,1,0:T(8,128)(2,1)} %get-tuple-element.21), calls=%async_computation.2 | async-start | bytes 4194304 | tf_op jit(solution)/shard_map/all_to_all | solution.py:403
  29.2 5.9 %copy-start.22 = (s32[3]{0:T(128)S(1)}, s32[3]{0:T(128)}, u32[]{:S(2)}) copy-start(s32[3]{0:T(128)} %constant.64.clone) | copy-start | bytes 40
  29.2 210.2 %reduce-scatter.5.cloned.1.call-start = ((), (), s32[]{:S(2)}) async-start(), calls=%async_computation.9 | async-start | bytes 3932160 | tf_op jit(solution)/shard_map/reduce_scatter | solution.py:409
  57.5 1.4 copy-start.12
  93.4 5.5 %copy-start.15 = (f32[1,32,2,32]{2,3,1,0:T(8,128)S(1)}, f32[1,32,2,32]{2,3,1,0:T(8,128)}, u32[]{:S(2)}) copy-start(f32[1,32,2,32]{2,3,1,0:T(8,128)} %get-tuple-element.69) | copy-start | bytes 24580
  93.4 33.1 %all-to-all-start = ((bf16[32,16,2048]{2,1,0:T(8,128)(2,1)}), bf16[32,16,2048]{2,1,0:T(8,128)(2,1)S(1)}, u32[]{:S(2)}, u32[]{:S(2)}) async-start(bf16[32,16,2048]{2,1,0:T(8,128)(2,1)} %get-tuple-element.19), calls=%async_computation | async-start | bytes 4194304 | tf_op jit(solution)/shard_map/all_to_all | solution.py:403
  98.1 144.6 %reduce-scatter.3.cloned.1.call-start = ((), (), s32[]{:S(2)}) async-start(), calls=%async_computation.8 | async-start | bytes 3932160 | tf_op jit(solution)/shard_map/reduce_scatter | solution.py:409
  126.5 1.4 copy-start.13
  162.4 1.6 copy-start.14
  196.4 4.8 %copy-start.23 = (u32[128]{0:T(128)S(1)}, u32[128]{0:T(128)}, u32[]{:S(2)}) copy-start(u32[128]{0:T(128)} %constant.78) | copy-start | bytes 1540
  196.4 5.4 %copy-start.1 = (f32[2,3,32,4096]{3,2,1,0:T(8,128)S(1)}, f32[2,3,32,4096]{3,2,1,0:T(8,128)}, u32[]{:S(2)}) copy-start(f32[2,3,32,4096]{3,2,1,0:T(8,128)} %param.13) | copy-start | bytes 9437188
  196.4 33.2 %all-to-all-start.3 = ((bf16[32,16,2048]{2,1,0:T(8,128)(2,1)}), bf16[32,16,2048]{2,1,0:T(8,128)(2,1)}, u32[]{:S(2)}, u32[]{:S(2)}) async-start(bf16[32,16,2048]{2,1,0:T(8,128)(2,1)} %get-tuple-element.22), calls=%async_computation.3 | async-start | bytes 4194304 | tf_op jit(solution)/shard_map/all_to_all | solution.py:410
  201.8 1.9 copy-start.18
  201.8 1.9 copy-start.19
  220.3 19.1 %copy-start.3 = (f32[1,3,32,4096]{3,2,1,0:T(8,128)S(1)}, f32[1,3,32,4096]{3,2,1,0:T(8,128)}, u32[]{:S(2)}) copy-start(f32[1,3,32,4096]{3,2,1,0:T(8,128)} %get-tuple-element.65) | copy-start | bytes 4718596
  229.6 1.6 copy-start.4
  239.4 3.3 %copy-start.2 = (f32[1,3,32,4096]{3,2,1,0:T(8,128)S(1)}, f32[1,3,32,4096]{3,2,1,0:T(8,128)}, u32[]{:S(2)}) copy-start(f32[1,3,32,4096]{3,2,1,0:T(8,128)} %get-tuple-element.64) | copy-start | bytes 4718596
  239.4 1.3 copy-start.8
  240.6 5.3 %copy-start.21 = (f32[2,3,32]{2,0,1:T(2,128)S(1)}, f32[2,3,32]{2,0,1:T(2,128)}, u32[]{:S(2)}) copy-start(f32[2,3,32]{2,0,1:T(2,128)} %param.14) | copy-start | bytes 2308
  241.3 1.2 copy-start.5
  242.5 4.1 %copy-start.6 = (f32[96,4096]{1,0:T(8,128)S(1)}, f32[96,4096]{1,0:T(8,128)}, u32[]{:S(2)}) copy-start(f32[96,4096]{1,0:T(8,128)} %copy-done.5) | copy-start | bytes 4718596
  242.7 1.3 copy-start.9
  244.6 1.1 copy-start.7
Sparse Core Ops, SparseCore 0:
  11.5 42.7 all-gather.4
  56.5 39.7 all-gather.2
  98.7 38.4 reduce-scatter.4
  162.5 35.7 reduce-scatter.2

commit v2 on v1

v2 whole, which is shorter than its diff:
```python
import functools

import jax
import jax.numpy as jnp
from jax import lax
from jax.experimental import pallas as pl
from jax.experimental.pallas import tpu as pltpu
from jax.sharding import PartitionSpec as P

D = 2048
FF = 768
BS = 64
MAXB = 128
OWNERS = 4
BLOCKS = (D // BS) * (FF // BS)
LEARN_RATE = 0.005
SCORE_RATE = 0.05
CHUNK = 256
F32 = jnp.float32
BF16 = jnp.bfloat16
NN = (((1,), (0,)), ((), ()))
NT = (((1,), (1,)), ((), ()))
TN = (((0,), (0,)), ((), ()))


def dot(left, right, dims=NN):
    return lax.dot_general(left, right, dims, preferred_element_type=F32)


def iota(shape, dim):
    return lax.broadcasted_iota(jnp.int32, shape, dim)


def one_hot(flag):
    return jnp.where(flag, 1.0, 0.0).astype(BF16)


def split_matrix(size):
    col = iota((size, size), 1)
    source = ((col >> 6) << 6) + 2 * (col & 31) + ((col >> 5) & 1)
    return one_hot(iota((size, size), 0) == source)


def pick_columns(picks_ref, member, locals_count):
    experts = picks_ref.shape[0]
    rows = 8 * experts // locals_count
    expert = (iota((rows, experts), 0) >> 3) * locals_count + member
    spread = one_hot(iota((rows, experts), 1) == expert)
    wide = dot(spread, picks_ref[...].astype(F32).astype(BF16))
    keep = iota(wide.shape, 1) == (iota(wide.shape, 0) & 7)
    return jnp.sum(jnp.where(keep, wide, 0.0), axis=1, keepdims=True).astype(jnp.int32)


def interleave(first, second):
    width = first.shape[1]
    pair = [first.reshape(-1, 8, width), second.reshape(-1, 8, width)]
    return jnp.concatenate(pair, axis=1).astype(BF16)


def apart(block):
    wide = block.astype(F32)
    width = wide.shape[2]
    return wide[:, :8, :].reshape(-1, width), wide[:, 8:, :].reshape(-1, width)


def pick_kernel(picks_ref, tokens_ref, grads_ref, *rest, locals_count):
    out_refs, hot_ref = rest[:locals_count], rest[locals_count]

    @pl.when(pl.program_id(0) == 0)
    def _():
        for member in range(locals_count):
            index = pick_columns(picks_ref, member, locals_count)
            hot_ref[member] = one_hot(iota(hot_ref.shape[1:], 1) == index)

    tokens = dot(tokens_ref[...], split_matrix(CHUNK)).astype(BF16)
    for member in range(locals_count):
        hot = hot_ref[member]
        out_refs[member][...] = interleave(dot(hot, tokens), dot(hot, grads_ref[...]))


def pack_kernel(masters_ref, first_ref, second_ref, lines_ref):
    def fill(out_ref):
        for group in range(masters_ref.shape[0] // 8):
            for k in range(32):
                lines_ref[group, 8 * k : 8 * k + 8, :] = masters_ref[
                    8 * group : 8 * group + 8, 128 * k : 128 * k + 128
                ]
            for s in range(8):
                out_ref[8 * group + s] = lines_ref[group, pl.ds(s, 32, stride=8), :].astype(BF16)

    step, steps = pl.program_id(0), pl.num_programs(0)

    @pl.when(step < steps // 2)
    def _():
        fill(first_ref)

    @pl.when(step >= steps // 2)
    def _():
        fill(second_ref)


def expert_kernel(
    inverse_ref, row_ref, lane_ref, valid_ref,
    copies_ref, arrived_ref, router_ref,
    send_ref, packed_ref,
    wide_ref, down_ref, rows_ref, grads_ref, pre_ref, part_ref, both_ref,
    grad_wide_ref, grad_down_ref, router_out_ref,
    *, member,
):
    base, slot_base = member * 3 * BLOCKS, member * 3 * MAXB
    lane = iota((32, 128), 1)
    half = lane < 64

    def place(target_ref, matrix, block, row, col):
        first = inverse_ref[base + matrix * BLOCKS + block]
        second = inverse_ref[base + matrix * BLOCKS + block + 1]
        one = copies_ref[jnp.maximum(first, 0)]
        two = copies_ref[jnp.maximum(second, 0)]
        one = jnp.where(lane < jnp.where(first >= 0, 128, 0), one, jnp.zeros_like(one))
        two = jnp.where(lane < jnp.where(second >= 0, 128, 0), two, jnp.zeros_like(two))
        target_ref[pl.ds(row, 32), col : col + 128] = jnp.where(half, one, pltpu.roll(two, 64, 1))
        target_ref[pl.ds(row + 32, 32), col : col + 128] = jnp.where(half, pltpu.roll(one, 64, 1), two)

    @pl.loop(0, D // BS)
    def _(r):
        row = pl.multiple_of(r * BS, BS)
        for matrix in range(2):
            for pair in range(FF // BS // 2):
                place(wide_ref, matrix, r * (FF // BS) + 2 * pair, row, matrix * FF + 128 * pair)

    @pl.loop(0, FF // BS)
    def _(r):
        row = pl.multiple_of(r * BS, BS)
        for pair in range(D // BS // 2):
            place(down_ref, 2, r * (D // BS) + 2 * pair, row, 128 * pair)

    count = rows_ref.shape[0]
    chunks = D // CHUNK
    mine = slice(member, member + 1)

    def take(n, logit):
        cols = pl.ds(pl.multiple_of(n * CHUNK, CHUNK), CHUNK)
        rows, grads = apart(arrived_ref[:, :, cols])
        rows_ref[:, cols] = rows.astype(BF16)
        grads_ref[:, cols] = grads.astype(BF16)
        return logit + jnp.sum(rows * router_ref[mine, cols], axis=1, keepdims=True)

    logit = lax.fori_loop(0, chunks, take, jnp.zeros((count, 1), F32))
    gating = 1.0 / (1.0 + jnp.exp(-logit))

    @pl.loop(0, 2 * FF // 512)
    def _(n):
        cols = pl.ds(pl.multiple_of(n * 512, 512), 512)
        pre_ref[:, cols] = dot(rows_ref[...], wide_ref[:, cols])

    split = split_matrix(CHUNK)
    hidden_list = []
    for n in range(FF // CHUNK):
        gate_pre = pre_ref[:, n * CHUNK : (n + 1) * CHUNK]
        up_pre = pre_ref[:, FF + n * CHUNK : FF + (n + 1) * CHUNK]
        hidden = (gate_pre / (1.0 + jnp.exp(-gate_pre)) * up_pre).astype(BF16)
        hidden_list.append(dot(hidden, split).astype(BF16))
    hidden_split = jnp.concatenate(hidden_list, axis=1)

    @pl.loop(0, D // 512)
    def _(n):
        cols = pl.ds(pl.multiple_of(n * 512, 512), 512)
        part_ref[:, cols] = (gating * dot(hidden_split, down_ref[:, cols])).astype(BF16)
        grads_ref[:, cols] = (gating * grads_ref[:, cols].astype(F32)).astype(BF16)

    logit_sum = jnp.zeros((count, 1), F32)
    for n in range(FF // CHUNK):
        spread = dot(grads_ref[...], down_ref[n * CHUNK : (n + 1) * CHUNK, :], NT)
        high = spread.astype(BF16)
        low = (spread - high.astype(F32)).astype(BF16)
        hidden_grad = dot(high, split, NT) + dot(low, split, NT)
        logit_sum = logit_sum + jnp.sum(
            hidden_list[n].astype(F32) * spread, axis=1, keepdims=True
        )
        gate_pre = pre_ref[:, n * CHUNK : (n + 1) * CHUNK]
        up_pre = pre_ref[:, FF + n * CHUNK : FF + (n + 1) * CHUNK]
        sigma = 1.0 / (1.0 + jnp.exp(-gate_pre))
        gate_grad = hidden_grad * up_pre * sigma * (1.0 + gate_pre * (1.0 - sigma))
        both_ref[:, n * CHUNK : (n + 1) * CHUNK] = gate_grad.astype(BF16)
        both_ref[:, FF + n * CHUNK : FF + (n + 1) * CHUNK] = (hidden_grad * gate_pre * sigma).astype(BF16)
        grad_down_ref[n * CHUNK : (n + 1) * CHUNK, :] = dot(hidden_list[n], grads_ref[...], TN).astype(BF16)
    logit_grad = logit_sum * (1.0 - gating)

    @pl.loop(0, chunks)
    def _(n):
        cols = pl.ds(pl.multiple_of(n * CHUNK, CHUNK), CHUNK)
        part = dot(both_ref[...], wide_ref[cols, :], NT) + logit_grad * router_ref[mine, cols]
        send_ref[:, :, cols] = interleave(part_ref[:, cols].astype(F32), part)
        rows = rows_ref[:, cols]
        router_out_ref[:, cols] = jnp.sum(logit_grad * rows.astype(F32), axis=0, keepdims=True)
        grad_wide_ref[cols, :] = dot(rows, both_ref[...], TN).astype(BF16)

    def cut(source_ref, matrix, slot, place_in):
        at = slot_base + matrix * MAXB + slot
        row = pl.multiple_of(row_ref[at], 32)
        other = pl.multiple_of(row ^ 32, 32)
        cols = pl.ds(pl.multiple_of(lane_ref[at], 128), 128)
        odd = row & 32
        stay = source_ref[pl.ds(row, 32), cols]
        move = pltpu.roll(source_ref[pl.ds(other, 32), cols], 64, 1)
        tile = jnp.where((lane & 64) == 2 * odd, stay, move)
        limit = jnp.where(valid_ref[at] > 0, 128, 0)
        packed_ref[place_in] = jnp.where(lane < limit, tile, jnp.zeros_like(tile))

    per = MAXB // OWNERS
    part = packed_ref.shape[0] // OWNERS
    for owner in range(OWNERS):
        for matrix in range(3):
            source_ref = grad_down_ref if matrix == 2 else grad_wide_ref

            @pl.loop(0, per // 4)
            def _(group, owner=owner, matrix=matrix, source_ref=source_ref):
                for step in range(4):
                    s = group * 4 + step
                    cut(source_ref, matrix, owner * per + s, owner * part + matrix * per + s)

        start = owner * (D // OWNERS)
        lines = [router_out_ref[:, start + at : start + at + 128] for at in range(0, D // OWNERS, 128)]
        lines.append(jnp.zeros((32 - len(lines), 128), F32))
        packed_ref[owner * part + 3 * per] = jnp.concatenate(lines, axis=0).astype(BF16)


def update_kernel(summed_ref, masters_ref, *rest):
    out_ref, total_ref, lines_ref = rest[-3:]
    for group in range(masters_ref.shape[0] // 8):
        for s in range(8):
            lines_ref[group, pl.ds(s, 32, stride=8), :] = summed_ref[8 * group + s].astype(F32)
        total = jnp.zeros((8, 128), F32)
        rows = slice(8 * group, 8 * group + 8)
        for k in range(32):
            cols = slice(128 * k, 128 * k + 128)
            gradient = lines_ref[group, 8 * k : 8 * k + 8, :]
            held = masters_ref[rows, cols]
            out_ref[rows, cols] = held - LEARN_RATE * gradient
            total = total + held * gradient
        total_ref[rows, :] = jnp.sum(total, axis=1, keepdims=True)


def combine_kernel(picks_ref, *rest, locals_count):
    back_refs = rest[:locals_count]
    out_ref, in_ref, hot_ref = rest[locals_count:]
    count = out_ref.shape[0]

    @pl.when(pl.program_id(0) == 0)
    def _():
        same = one_hot(iota((count, count), 0) == iota((count, count), 1))
        for member in range(locals_count):
            index = pick_columns(picks_ref, member, locals_count)
            hot = one_hot(iota((index.shape[0], count), 1) == index)
            hot_ref[member] = dot(hot, same, TN).astype(BF16)

    out_sum = jnp.zeros(out_ref.shape, F32)
    in_sum = jnp.zeros(in_ref.shape, F32)
    for member in range(locals_count):
        out_rows, in_rows = apart(back_refs[member][...])
        out_sum = out_sum + dot(hot_ref[member], out_rows.astype(BF16))
        in_sum = in_sum + dot(hot_ref[member], in_rows.astype(BF16))
    out_ref[...] = out_sum.astype(BF16)
    in_ref[...] = dot(in_sum.astype(BF16), split_matrix(CHUNK), NT).astype(BF16)


def params(mib):
    return pltpu.CompilerParams(vmem_limit_bytes=mib * 1024 * 1024)


def cost(flops, moved):
    return pl.CostEstimate(flops=flops, bytes_accessed=moved, transcendentals=0)


def pick(picks, tokens, grads, locals_count, peers):
    count, width = tokens.shape
    column = pl.BlockSpec((count, CHUNK), lambda n: (0, n))
    return pl.pallas_call(
        functools.partial(pick_kernel, locals_count=locals_count),
        grid=(width // CHUNK,),
        in_specs=[pl.BlockSpec(picks.shape, lambda n: (0, 0)), column, column],
        out_specs=[pl.BlockSpec((peers, 16, CHUNK), lambda n: (0, 0, n))] * locals_count,
        out_shape=[jax.ShapeDtypeStruct((peers, 16, width), BF16)] * locals_count,
        scratch_shapes=[pltpu.VMEM((locals_count, 8 * peers, count), BF16)],
        compiler_params=params(56),
        cost_estimate=cost(0, 1 << 20),
        name="pick",
    )(picks, tokens, grads)


def pack(masters):
    half = masters.shape[0] // 2
    steps = 4
    rows = 2 * half // steps
    return pl.pallas_call(
        pack_kernel,
        grid=(steps,),
        in_specs=[pl.BlockSpec((rows, BS * BS), lambda n: (n, 0))],
        out_specs=[
            pl.BlockSpec((rows, 32, 128), lambda n: (jnp.minimum(n, steps // 2 - 1), 0, 0)),
            pl.BlockSpec((rows, 32, 128), lambda n: (jnp.maximum(n - steps // 2, 0), 0, 0)),
        ],
        out_shape=[jax.ShapeDtypeStruct((half, 32, 128), BF16)] * 2,
        scratch_shapes=[pltpu.VMEM((rows // 8, 256, 128), F32)],
        compiler_params=params(56),
        cost_estimate=cost(0, 1 << 20),
        name="pack",
    )(masters)


def run_expert(member, tables, copies, arrived, router_rows):
    peers = arrived.shape[0]
    count = 8 * peers
    whole = pl.BlockSpec(memory_space=pltpu.VMEM)
    scalar = pl.BlockSpec(memory_space=pltpu.SMEM)
    return pl.pallas_call(
        functools.partial(expert_kernel, member=member),
        in_specs=[scalar] * 4 + [whole] * 3,
        out_specs=[whole] * 2,
        out_shape=[
            jax.ShapeDtypeStruct((peers, 16, D), BF16),
            jax.ShapeDtypeStruct((3 * MAXB + OWNERS, 32, 128), BF16),
        ],
        scratch_shapes=[
            pltpu.VMEM((D, 2 * FF), BF16),
            pltpu.VMEM((FF, D), BF16),
            pltpu.VMEM((count, D), BF16),
            pltpu.VMEM((count, D), BF16),
            pltpu.VMEM((count, 2 * FF), F32),
            pltpu.VMEM((count, D), BF16),
            pltpu.VMEM((count, 2 * FF), BF16),
            pltpu.VMEM((D, 2 * FF), BF16),
            pltpu.VMEM((FF, D), BF16),
            pltpu.VMEM((1, D), F32),
        ],
        compiler_params=params(56),
        cost_estimate=cost(150 * 10**9, 1 << 20),
        name="expert_%d" % member,
    )(*tables, copies, arrived, router_rows)


def update(member, summed, masters, held):
    slots = masters.shape[0]
    mine = summed.shape[0] - 1
    steps = 3
    rows = mine // steps
    return pl.pallas_call(
        update_kernel,
        grid=(steps,),
        in_specs=[
            pl.BlockSpec((rows, 32, 128), lambda n: (n, 0, 0)),
            pl.BlockSpec((rows, BS * BS), lambda n: (member * steps + n, 0)),
        ]
        + [pl.BlockSpec(memory_space=pl.ANY)] * len(held),
        out_specs=[
            pl.BlockSpec((rows, BS * BS), lambda n: (member * steps + n, 0)),
            pl.BlockSpec((rows, 1), lambda n: (member * steps + n, 0)),
        ],
        out_shape=[
            jax.ShapeDtypeStruct((slots, BS * BS), F32),
            jax.ShapeDtypeStruct((slots, 1), F32),
        ],
        input_output_aliases={2 + at: at for at in range(len(held))},
        scratch_shapes=[pltpu.VMEM((rows // 8, 256, 128), F32)],
        compiler_params=params(56),
        cost_estimate=cost(0, 1 << 20),
        name="update_%d" % member,
    )(summed, masters, *held)


def combine(picks, back, count):
    locals_count = len(back)
    peers, _, width = back[0].shape
    column = pl.BlockSpec((count, CHUNK), lambda n: (0, n))
    return pl.pallas_call(
        functools.partial(combine_kernel, locals_count=locals_count),
        grid=(width // CHUNK,),
        in_specs=[pl.BlockSpec(picks.shape, lambda n: (0, 0))]
        + [pl.BlockSpec((peers, 16, CHUNK), lambda n: (0, 0, n))] * locals_count,
        out_specs=[column, column],
        out_shape=[jax.ShapeDtypeStruct((count, width), BF16)] * 2,
        scratch_shapes=[pltpu.VMEM((locals_count, count, 8 * peers), BF16)],
        compiler_params=params(56),
        cost_estimate=cost(150 * 10**9, 1 << 20),
        name="combine",
    )(picks, *back)


def slot_tables(kept, owners):
    numbers = jnp.arange(BLOCKS, dtype=jnp.int32)
    slots = jnp.arange(MAXB, dtype=jnp.int32)
    per = MAXB // owners
    matrix = jnp.arange(3, dtype=jnp.int32)[None, :, None]
    place = (slots // per) * (3 * per) + slots % per + matrix * per
    hits = kept[:, :, None, :] == numbers[None, None, :, None]
    inverse = jnp.sum(jnp.where(hits, place[:, :, None, :] + 1, 0), axis=-1) - 1
    valid = kept < BLOCKS
    block = jnp.where(valid, kept, 0)
    width = jnp.array([FF // BS, FF // BS, D // BS], jnp.int32)[None, :, None]
    block_row, block_col = block // width, block % width
    rows = block_row * BS + 32 * (block_col & 1)
    lanes = (block_col >> 1) * 128 + jnp.where(matrix == 1, FF, 0)
    flat = lambda table: table.reshape(-1).astype(jnp.int32)
    return flat(inverse), flat(rows), flat(lanes), flat(valid)


def body(tokens, out_grad, token_picks, router, kept_blocks, masters, scores):
    locals_count = kept_blocks.shape[0]
    owners = lax.axis_size("dp")
    peers = lax.axis_size("expert")
    count, width = tokens.shape
    per = masters.shape[2]
    picks = token_picks[0]
    flat_masters = masters.reshape(locals_count * 3 * per, BS * BS)

    packed = pack(flat_masters)
    sent = pick(picks, tokens, out_grad, locals_count, peers)
    tables = slot_tables(kept_blocks, owners)
    router_rows = router.T.reshape(locals_count, width // BS, 32, 2).transpose(0, 1, 3, 2)
    router_rows = router_rows.reshape(locals_count, width).astype(F32)
    tables, router_rows, sent = lax.optimization_barrier((tables, router_rows, sent))

    copies, arrived = [], []
    for member in range(locals_count):
        copies.append(lax.all_gather(packed[member], "dp", axis=0, tiled=True))
        arrived.append(lax.all_to_all(sent[member], "expert", split_axis=0, concat_axis=0, tiled=True))
    summed, back = [], []
    for member in range(locals_count):
        send, gradient = run_expert(member, tables, copies[member], arrived[member], router_rows)
        summed.append(lax.psum_scatter(gradient, "dp", scatter_dimension=0, tiled=True))
        back.append(lax.all_to_all(send, "expert", split_axis=0, concat_axis=0, tiled=True))
    held = ()
    for member in range(locals_count):
        held = update(member, summed[member], flat_masters, held)
    layer_out, input_grad = combine(picks, back, count)
    master_new = held[0].reshape(masters.shape)
    score_new = scores - SCORE_RATE * held[1].reshape(scores.shape)
    router_new = jnp.stack([part[-1, : width // owners // 128] for part in summed])
    router_new = router_new.reshape(locals_count, width // owners // BS, 2, 32).astype(F32)
    router_new = router_new.transpose(1, 3, 2, 0).reshape(width // owners, locals_count)
    return layer_out, input_grad, master_new, score_new, router_new


def solution(mesh):
    return jax.shard_map(
        body,
        mesh=mesh,
        in_specs=(
            P(("dp", "expert"), None),
            P(("dp", "expert"), None),
            P(("dp", "expert"), None, None),
            P(None, "expert"),
            P("expert", None, None),
            P("expert", None, "dp", None),
            P("expert", None, "dp"),
        ),
        out_specs=(
            P(("dp", "expert"), None),
            P(("dp", "expert"), None),
            P("expert", None, "dp", None),
            P("expert", None, "dp"),
            P("dp", "expert"),
        ),
        check_vma=False,
    )
```

time: 257 us -> 211 us (0.82)
  blocking collectives: 47.2 us -> 0 us
  local copies, waits for them, and re-layouts: 26.7 us -> 11 us
  starting transfers between devices: 19.6 us -> 29.9 us
  Pallas kernels: 86.4 us -> 92.7 us
  waiting for transfers between devices: 58.1 us -> 60.7 us
    all_to_all x1 -> x0, blocking collectives: 32.4 us -> none  [body(): lax.all_to_all(send, 'expert', split_axis=0, concat_axis=0, tiled=True)]
    all_to_all x2, waiting for transfers between devices: 48.1 us -> 27.5 us  [body(): lax.all_to_all(sent[member], 'expert', split_axis=0, concat_axis=0, tiled...]
    all_to_all x1 -> x2, waiting for transfers between devices: 9.28 us -> 27.7 us  [body(): lax.all_to_all(send, 'expert', split_axis=0, concat_axis=0, tiled=True)]
    unnamed x1 -> x0, blocking collectives: 14.8 us -> none
    unnamed x53 -> x17, local copies, waits for them, and re-layouts: 14.7 us -> 3.97 us
    all_to_all x1 -> x2, starting transfers between devices: 4.81 us -> 14.9 us  [body(): lax.all_to_all(send, 'expert', split_axis=0, concat_axis=0, tiled=True)]
    slice x8 -> x2, local copies, waits for them, and re-layouts: 7.21 us -> 1.35 us  [body(): part[-1, :width // owners // 128]]
    pallas_call x5, Pallas kernels: 71.1 us -> 76.6 us  [the longest x2 64.5 us: run_expert(): pl.pallas_call(functools.partial(expert_kernel, member=member), in_specs=...]
  transfers between devices with their start and end apart: 7 -> 8, of which waited for: 3 -> 3; matrix products, arithmetic and copies ran while one was open for 5% -> 3% of each run, Pallas kernels for 33% -> 38%
where the time goes in v2:
time: 211 us; the launch traced here: 210 us
  Pallas kernels  92.7 us (44%)
  waiting for transfers between devices  60.7 us (29%)
  starting transfers between devices  29.9 us (14%)
  between operations  13.9 us (7%)
  local copies, waits for them, and re-layouts  11 us (5%)
    pallas_call x2, Pallas kernels, run_expert(): pl.pallas_call(functools.partial(expert_kernel, member=member), in_specs=...  64.5 us
    all_to_all x2, waiting for transfers between devices, body(): lax.all_to_all(send, 'expert', split_axis=0, concat_axis=0, tiled=True)  27.7 us
    all_to_all x2, waiting for transfers between devices, body(): lax.all_to_all(sent[member], 'expert', split_axis=0, concat_axis=0, tiled...  27.5 us
    all_to_all x2, starting transfers between devices, body(): lax.all_to_all(send, 'expert', split_axis=0, concat_axis=0, tiled=True)  14.9 us
    all_to_all x2, starting transfers between devices, body(): lax.all_to_all(sent[member], 'expert', split_axis=0, concat_axis=0, tiled...  14.8 us
    pallas_call x1, Pallas kernels, combine(): pl.pallas_call(functools.partial(combine_kernel, locals_count=locals_coun...  8.13 us
    pallas_call x1, Pallas kernels, pick(): pl.pallas_call(functools.partial(pick_kernel, locals_count=locals_count),...  7.98 us
    pallas_call x2, Pallas kernels, update(): pl.pallas_call(update_kernel, grid=(steps,), in_specs=[pl.BlockSpec((rows...  7.72 us
  transfers between devices with their start and end apart: 8, of which 3 were waited for; matrix products, arithmetic and copies ran while one was open for 3% of the time, Pallas kernels for 38%

profile of v2, /device:TPU:1, one launch (start us, length us, event | category | flops | bytes accessed | tf_op | source)
XLA Modules:
  0.0 210.0 jit_solution(13993958873440898346)
XLA Ops:
  7.2 0.0 copy-start.6
  7.2 0.0 all-gather.5.cloned.1.call-start
  7.3 4.4 %pack.1 = (bf16[96,32,128]{2,1,0:T(8,128)(2,1)}, bf16[96,32,128]{2,1,0:T(8,128)(2,1)}) custom-call(f32[192,4096]{1,0:T(8,128)} %bitcast.11), custom_call_target="tpu_custom_call" | custom-call | bytes 1048576 | tf_op jit(solution)/shard_map/pack/pallas_call | solution.py:295
  11.6 0.0 all-gather.5.cloned.1.call-update
  11.6 0.7 copy.38
  12.4 0.2 multiply_add_fusion
  12.6 0.6 reshape.128.row_ref
  13.2 0.6 reshape.129.lane_ref
  13.8 1.0 reshape.139
  14.8 0.5 copy.43
  15.3 0.7 reshape.135.router_ref
  16.0 0.1 add_add_fusion
  16.1 0.4 select_reduce_fusion
  16.5 0.6 sub.25.inverse_ref
  17.1 0.6 reshape.134.valid_ref
  17.7 8.0 %pick.1 = (bf16[32,16,2048]{2,1,0:T(8,128)(2,1)}, bf16[32,16,2048]{2,1,0:T(8,128)(2,1)}) custom-call(s32[64,8]{1,0:T(8,128)} %bitcast.17, bf16[256,2048]{1,0:T(8,128)(2,1)} %tokens_ref.1, bf16[256,2048]{1,0:T(8,128)(2,1)} %grads_ref.1), custom_call_target="tpu_custom_call" | custom-call | bytes 1048576 | tf_op jit(solution)/shard_map/pick/pallas_call | solution.py:278
  25.7 9.6 %all-to-all-start.2 = ((bf16[32,16,2048]{2,1,0:T(8,128)(2,1)}), bf16[32,16,2048]{2,1,0:T(8,128)(2,1)S(1)}, u32[]{:S(2)}, u32[]{:S(2)}) async-start(bf16[32,16,2048]{2,1,0:T(8,128)(2,1)} %get-tuple-element.37), calls=%async_computation.2 | async-start | bytes 4194304 | tf_op jit(solution)/shard_map/all_to_all | solution.py:426
  35.3 0.0 all-gather.3.cloned.1.call-start
  35.4 0.7 all-gather.3.cloned.1.call-update
  36.1 27.5 %all-to-all-done.2.arrived_ref = bf16[32,16,2048]{2,1,0:T(8,128)(2,1)S(1)} async-done(((bf16[32,16,2048]{2,1,0:T(8,128)(2,1)}), bf16[32,16,2048]{2,1,0:T(8,128)(2,1)S(1)}, u32[]{:S(2)}, u32[]{:S(2)}) %all-to-all-start.2) | async-done | bytes 2097184 | tf_op jit(solution)/shard_map/all_to_all | solution.py:426
  63.6 1.3 copy-done
  65.0 5.2 %all-to-all-start = ((bf16[32,16,2048]{2,1,0:T(8,128)(2,1)}), bf16[32,16,2048]{2,1,0:T(8,128)(2,1)}, u32[]{:S(2)}, u32[]{:S(2)}) async-start(bf16[32,16,2048]{2,1,0:T(8,128)(2,1)} %get-tuple-element.33), calls=%async_computation | async-start | bytes 4194304 | tf_op jit(solution)/shard_map/all_to_all | solution.py:426
  70.2 0.0 reduce-scatter.3.cloned.1.call-start
  70.2 0.0 all-gather.5.cloned.1.call-done.copies_ref
  70.3 32.3 %expert_1.1 = (bf16[32,16,2048]{2,1,0:T(8,128)(2,1)}, bf16[388,32,128]{2,1,0:T(8,128)(2,1)}) custom-call(s32[2304]{0:T(1024)} %sub.25.inverse_ref, s32[768]{0:T(1024)} %reshape.128.row_ref, s32[768]{0:T(1024)} %reshape.129.lane_ref, s32[768]{0:T(1024)} %reshape.134.valid_ref, bf16[384,32,128]{2,1,0:T(8,128)(2,1)} %all-gather.5.cloned.1.call-done.copies_ref, ...), custom_call_target="tpu_custom_call" | custom-call | flops 149999992832 | bytes 1048576 | tf_op jit(solution)/shard_map/expert_1/pallas_call | solution.py:316
  102.6 0.0 reduce-scatter.3.cloned.1.call-update
  102.6 0.0 all-to-all-done.arrived_ref
  102.6 7.6 %all-to-all-start.3 = ((bf16[32,16,2048]{2,1,0:T(8,128)(2,1)}), bf16[32,16,2048]{2,1,0:T(8,128)(2,1)}, u32[]{:S(2)}, u32[]{:S(2)}) async-start(bf16[32,16,2048]{2,1,0:T(8,128)(2,1)} %get-tuple-element.38), calls=%async_computation.3 | async-start | bytes 4194304 | tf_op jit(solution)/shard_map/all_to_all | solution.py:431
  110.2 0.0 all-gather.3.cloned.1.call-done.copies_ref
  110.2 32.2 %expert_0.1 = (bf16[32,16,2048]{2,1,0:T(8,128)(2,1)}, bf16[388,32,128]{2,1,0:T(8,128)(2,1)}) custom-call(s32[2304]{0:T(1024)} %sub.25.inverse_ref, s32[768]{0:T(1024)} %reshape.128.row_ref, s32[768]{0:T(1024)} %reshape.129.lane_ref, s32[768]{0:T(1024)} %reshape.134.valid_ref, bf16[384,32,128]{2,1,0:T(8,128)(2,1)} %all-gather.3.cloned.1.call-done.copies_ref, ...), custom_call_target="tpu_custom_call" | custom-call | flops 149999992832 | bytes 1048576 | tf_op jit(solution)/shard_map/expert_0/pallas_call | solution.py:316
  142.4 0.0 all-to-all-done.3.rest_1_
  142.5 7.4 %all-to-all-start.1 = ((bf16[32,16,2048]{2,1,0:T(8,128)(2,1)}), bf16[32,16,2048]{2,1,0:T(8,128)(2,1)S(1)}, u32[]{:S(2)}, u32[]{:S(2)}) async-start(bf16[32,16,2048]{2,1,0:T(8,128)(2,1)} %get-tuple-element.35), calls=%async_computation.1 | async-start | bytes 4194304 | tf_op jit(solution)/shard_map/all_to_all | solution.py:431
  149.8 0.0 reduce-scatter.5.cloned.1.call-start
  149.9 0.5 reduce-scatter.5.cloned.1.call-update
  150.4 27.7 %all-to-all-done.1.rest_0_ = bf16[32,16,2048]{2,1,0:T(8,128)(2,1)S(1)} async-done(((bf16[32,16,2048]{2,1,0:T(8,128)(2,1)}), bf16[32,16,2048]{2,1,0:T(8,128)(2,1)S(1)}, u32[]{:S(2)}, u32[]{:S(2)}) %all-to-all-start.1) | async-done | bytes 2097184 | tf_op jit(solution)/shard_map/all_to_all | solution.py:431
  178.1 1.3 copy-done.1
  179.4 8.1 %combine.1 = (bf16[256,2048]{1,0:T(8,128)(2,1)}, bf16[256,2048]{1,0:T(8,128)(2,1)}) custom-call(s32[64,8]{1,0:T(8,128)} %bitcast.18, bf16[32,16,2048]{2,1,0:T(8,128)(2,1)} %copy-done.1, bf16[32,16,2048]{2,1,0:T(8,128)(2,1)} %all-to-all-done.3.rest_1_), custom_call_target="tpu_custom_call" | custom-call | flops 149999992832 | bytes 1048576 | tf_op jit(solution)/shard_map/combine/pallas_call | solution.py:375
  187.6 0.7 slice.9
  188.2 4.1 %reduce-scatter.5.cloned.1.call-done.summed_ref = bf16[97,32,128]{2,1,0:T(8,128)(2,1)} async-done(((bf16[388,32,128]{2,1,0:T(8,128)(2,1)}), bf16[97,32,128]{2,1,0:T(8,128)(2,1)}) %reduce-scatter.5.cloned.1.call-update) | async-done | bytes 794640 | tf_op jit(solution)/shard_map/reduce_scatter | solution.py:430
  192.3 0.7 slice.8
  193.0 0.1 reshape.141
  193.1 0.2 copy.45
  193.3 0.8 reshape.137
  194.1 3.9 %update_0.1 = (f32[192,4096]{1,0:T(8,128)}, f32[192,1]{1,0:T(8,128)}) custom-call(bf16[97,32,128]{2,1,0:T(8,128)(2,1)} %reduce-scatter.5.cloned.1.call-done.summed_ref, f32[192,4096]{1,0:T(8,128)} %bitcast.12), custom_call_target="tpu_custom_call" | custom-call | bytes 1048576 | tf_op jit(solution)/shard_map/update_0/pallas_call | solution.py:347
  197.9 3.9 %update_1.1 = (f32[192,4096]{1,0:T(8,128)}, f32[192,1]{1,0:T(8,128)}) custom-call(bf16[97,32,128]{2,1,0:T(8,128)(2,1)} %reduce-scatter.3.cloned.1.call-done.summed_ref, f32[192,4096]{1,0:T(8,128)} %bitcast.13, f32[192,4096]{1,0:T(8,128)} %get-tuple-element.43.rest_0_, f32[192,1]{1,0:T(8,128)} %get-tuple-element.44.rest_1_), custom_call_target="tpu_custom_call", output_to_operand_aliasing={{0}: (2, {}), {1}: (3, {})} | custom-call | bytes 1048576 | tf_op jit(solution)/shard_map/update_1/pallas_call | solution.py:347
  201.8 1.0 multiply_reduce_fusion
  202.8 0.1 mul.56
  202.9 0.6 copy.46
  (24 shorter events, 0.1 us)
Async XLA Ops:
  7.2 5.2 %copy-start.6 = (s32[3]{0:T(128)S(1)}, s32[3]{0:T(128)}, u32[]{:S(2)}) copy-start(s32[3]{0:T(128)} %constant.64.clone) | copy-start | bytes 40
  7.2 4.5 %copy-start.4 = (s32[1,64,8]{1,2,0:T(8,128)S(1)}, s32[1,64,8]{1,2,0:T(8,128)}, u32[]{:S(2)}) copy-start(s32[1,64,8]{1,2,0:T(8,128)} %param.10) | copy-start | bytes 6148
  7.2 5.2 %copy-start.2 = (s32[2,3,128]{2,0,1:T(2,128)S(1)}, s32[2,3,128]{2,0,1:T(2,128)}, u32[]{:S(2)}) copy-start(s32[2,3,128]{2,0,1:T(2,128)} %param.12) | copy-start | bytes 9220
  7.2 6.6 %copy-start.3 = (bf16[2048,2]{0,1:T(2,128)(2,1)S(1)}, bf16[2048,2]{0,1:T(2,128)(2,1)}, u32[]{:S(2)}) copy-start(bf16[2048,2]{0,1:T(2,128)(2,1)} %param.11) | copy-start | bytes 24580
  7.2 63.0 %all-gather.5.cloned.1.call-start = ((), (), s32[]{:S(2)}) async-start(), calls=%async_computation.7 | async-start | bytes 3932160 | tf_op jit(solution)/shard_map/all_gather | solution.py:425
  25.7 37.9 %all-to-all-start.2 = ((bf16[32,16,2048]{2,1,0:T(8,128)(2,1)}), bf16[32,16,2048]{2,1,0:T(8,128)(2,1)S(1)}, u32[]{:S(2)}, u32[]{:S(2)}) async-start(bf16[32,16,2048]{2,1,0:T(8,128)(2,1)} %get-tuple-element.37), calls=%async_computation.2 | async-start | bytes 4194304 | tf_op jit(solution)/shard_map/all_to_all | solution.py:426
  35.3 74.9 %all-gather.3.cloned.1.call-start = ((), (), s32[]{:S(2)}) async-start(), calls=%async_computation.6 | async-start | bytes 3932160 | tf_op jit(solution)/shard_map/all_gather | solution.py:425
  63.6 1.3 copy-start
  65.0 37.6 %all-to-all-start = ((bf16[32,16,2048]{2,1,0:T(8,128)(2,1)}), bf16[32,16,2048]{2,1,0:T(8,128)(2,1)}, u32[]{:S(2)}, u32[]{:S(2)}) async-start(bf16[32,16,2048]{2,1,0:T(8,128)(2,1)} %get-tuple-element.33), calls=%async_computation | async-start | bytes 4194304 | tf_op jit(solution)/shard_map/all_to_all | solution.py:426
  70.2 117.4 %reduce-scatter.3.cloned.1.call-start = ((), (), s32[]{:S(2)}) async-start(), calls=%async_computation.8 | async-start | bytes 3973120 | tf_op jit(solution)/shard_map/reduce_scatter | solution.py:430
  102.6 39.9 %all-to-all-start.3 = ((bf16[32,16,2048]{2,1,0:T(8,128)(2,1)}), bf16[32,16,2048]{2,1,0:T(8,128)(2,1)}, u32[]{:S(2)}, u32[]{:S(2)}) async-start(bf16[32,16,2048]{2,1,0:T(8,128)(2,1)} %get-tuple-element.38), calls=%async_computation.3 | async-start | bytes 4194304 | tf_op jit(solution)/shard_map/all_to_all | solution.py:431
  142.5 35.7 %all-to-all-start.1 = ((bf16[32,16,2048]{2,1,0:T(8,128)(2,1)}), bf16[32,16,2048]{2,1,0:T(8,128)(2,1)S(1)}, u32[]{:S(2)}, u32[]{:S(2)}) async-start(bf16[32,16,2048]{2,1,0:T(8,128)(2,1)} %get-tuple-element.35), calls=%async_computation.1 | async-start | bytes 4194304 | tf_op jit(solution)/shard_map/all_to_all | solution.py:431
  149.8 42.5 %reduce-scatter.5.cloned.1.call-start = ((), (), s32[]{:S(2)}) async-start(), calls=%async_computation.9 | async-start | bytes 3973120 | tf_op jit(solution)/shard_map/reduce_scatter | solution.py:430
  178.1 1.3 copy-start.1
  197.9 5.0 %copy-start.5 = (f32[2,3,32]{2,0,1:T(2,128)S(1)}, f32[2,3,32]{2,0,1:T(2,128)}, u32[]{:S(2)}) copy-start(f32[2,3,32]{2,0,1:T(2,128)} %param.14) | copy-start | bytes 2308
Sparse Core Ops, SparseCore 0:
  11.8 42.7 all-gather.4
  56.7 39.7 all-gather.2
  102.7 39.6 reduce-scatter.2
  152.8 39.5 reduce-scatter.4

commit v3 on v2

--- a/solution.py
+++ b/solution.py
@@ -16,6 +16,7 @@
 LEARN_RATE = 0.005
 SCORE_RATE = 0.05
 CHUNK = 256
+STEP = 512
 F32 = jnp.float32
 BF16 = jnp.bfloat16
 NN = (((1,), (0,)), ((), ()))
@@ -65,38 +66,34 @@
 
 def pick_kernel(picks_ref, tokens_ref, grads_ref, *rest, locals_count):
     out_refs, hot_ref = rest[:locals_count], rest[locals_count]
+    rows = hot_ref.shape[0] // locals_count
 
     @pl.when(pl.program_id(0) == 0)
     def _():
         for member in range(locals_count):
             index = pick_columns(picks_ref, member, locals_count)
-            hot_ref[member] = one_hot(iota(hot_ref.shape[1:], 1) == index)
-
-    tokens = dot(tokens_ref[...], split_matrix(CHUNK)).astype(BF16)
-    for member in range(locals_count):
-        hot = hot_ref[member]
-        out_refs[member][...] = interleave(dot(hot, tokens), dot(hot, grads_ref[...]))
-
-
-def pack_kernel(masters_ref, first_ref, second_ref, lines_ref):
-    def fill(out_ref):
-        for group in range(masters_ref.shape[0] // 8):
-            for k in range(32):
-                lines_ref[group, 8 * k : 8 * k + 8, :] = masters_ref[
-                    8 * group : 8 * group + 8, 128 * k : 128 * k + 128
-                ]
-            for s in range(8):
-                out_ref[8 * group + s] = lines_ref[group, pl.ds(s, 32, stride=8), :].astype(BF16)
-
-    step, steps = pl.program_id(0), pl.num_programs(0)
-
-    @pl.when(step < steps // 2)
-    def _():
-        fill(first_ref)
-
-    @pl.when(step >= steps // 2)
-    def _():
-        fill(second_ref)
+            hot_ref[member * rows : (member + 1) * rows, :] = one_hot(
+                iota((rows, hot_ref.shape[1]), 1) == index
+            )
+
+    split = split_matrix(CHUNK)
+    for start in range(0, tokens_ref.shape[1], CHUNK):
+        cols = slice(start, start + CHUNK)
+        tokens = dot(hot_ref[...], dot(tokens_ref[:, cols], split).astype(BF16))
+        grads = dot(hot_ref[...], grads_ref[:, cols])
+        for member in range(locals_count):
+            mine = slice(member * rows, (member + 1) * rows)
+            out_refs[member][:, :, cols] = interleave(tokens[mine], grads[mine])
+
+
+def pack_kernel(masters_ref, out_ref, lines_ref):
+    for group in range(masters_ref.shape[0] // 8):
+        for k in range(32):
+            lines_ref[group, 8 * k : 8 * k + 8, :] = masters_ref[
+                8 * group : 8 * group + 8, 128 * k : 128 * k + 128
+            ]
+        for s in range(8):
+            out_ref[8 * group + s] = lines_ref[group, pl.ds(s, 32, stride=8), :].astype(BF16)
 
 
 def expert_kernel(
@@ -252,16 +249,17 @@
         for member in range(locals_count):
             index = pick_columns(picks_ref, member, locals_count)
             hot = one_hot(iota((index.shape[0], count), 1) == index)
-            hot_ref[member] = dot(hot, same, TN).astype(BF16)
-
-    out_sum = jnp.zeros(out_ref.shape, F32)
-    in_sum = jnp.zeros(in_ref.shape, F32)
-    for member in range(locals_count):
-        out_rows, in_rows = apart(back_refs[member][...])
-        out_sum = out_sum + dot(hot_ref[member], out_rows.astype(BF16))
-        in_sum = in_sum + dot(hot_ref[member], in_rows.astype(BF16))
-    out_ref[...] = out_sum.astype(BF16)
-    in_ref[...] = dot(in_sum.astype(BF16), split_matrix(CHUNK), NT).astype(BF16)
+            rows = index.shape[0]
+            hot_ref[:, member * rows : (member + 1) * rows] = dot(hot, same, TN).astype(BF16)
+
+    split = split_matrix(CHUNK)
+    for start in range(0, out_ref.shape[1], CHUNK):
+        cols = slice(start, start + CHUNK)
+        pairs = [apart(back_ref[:, :, cols]) for back_ref in back_refs]
+        out_rows = jnp.concatenate([pair[0].astype(BF16) for pair in pairs], axis=0)
+        in_rows = jnp.concatenate([pair[1].astype(BF16) for pair in pairs], axis=0)
+        out_ref[:, cols] = dot(hot_ref[...], out_rows).astype(BF16)
+        in_ref[:, cols] = dot(dot(hot_ref[...], in_rows).astype(BF16), split, NT).astype(BF16)
 
 
 def params(mib):
@@ -274,37 +272,34 @@
 
 def pick(picks, tokens, grads, locals_count, peers):
     count, width = tokens.shape
-    column = pl.BlockSpec((count, CHUNK), lambda n: (0, n))
+    column = pl.BlockSpec((count, STEP), lambda n: (0, n))
     return pl.pallas_call(
         functools.partial(pick_kernel, locals_count=locals_count),
-        grid=(width // CHUNK,),
+        grid=(width // STEP,),
         in_specs=[pl.BlockSpec(picks.shape, lambda n: (0, 0)), column, column],
-        out_specs=[pl.BlockSpec((peers, 16, CHUNK), lambda n: (0, 0, n))] * locals_count,
+        out_specs=[pl.BlockSpec((peers, 16, STEP), lambda n: (0, 0, n))] * locals_count,
         out_shape=[jax.ShapeDtypeStruct((peers, 16, width), BF16)] * locals_count,
-        scratch_shapes=[pltpu.VMEM((locals_count, 8 * peers, count), BF16)],
+        scratch_shapes=[pltpu.VMEM((locals_count * 8 * peers, count), BF16)],
         compiler_params=params(56),
         cost_estimate=cost(0, 1 << 20),
         name="pick",
     )(picks, tokens, grads)
 
 
-def pack(masters):
-    half = masters.shape[0] // 2
-    steps = 4
-    rows = 2 * half // steps
+def pack(masters, member, locals_count):
+    mine = masters.shape[0] // locals_count
+    steps = 3
+    rows = mine // steps
     return pl.pallas_call(
         pack_kernel,
         grid=(steps,),
-        in_specs=[pl.BlockSpec((rows, BS * BS), lambda n: (n, 0))],
-        out_specs=[
-            pl.BlockSpec((rows, 32, 128), lambda n: (jnp.minimum(n, steps // 2 - 1), 0, 0)),
-            pl.BlockSpec((rows, 32, 128), lambda n: (jnp.maximum(n - steps // 2, 0), 0, 0)),
-        ],
-        out_shape=[jax.ShapeDtypeStruct((half, 32, 128), BF16)] * 2,
+        in_specs=[pl.BlockSpec((rows, BS * BS), lambda n: (member * steps + n, 0))],
+        out_specs=pl.BlockSpec((rows, 32, 128), lambda n: (n, 0, 0)),
+        out_shape=jax.ShapeDtypeStruct((mine, 32, 128), BF16),
         scratch_shapes=[pltpu.VMEM((rows // 8, 256, 128), F32)],
         compiler_params=params(56),
         cost_estimate=cost(0, 1 << 20),
-        name="pack",
+        name="pack_%d" % member,
     )(masters)
 
 
@@ -371,15 +366,15 @@
 def combine(picks, back, count):
     locals_count = len(back)
     peers, _, width = back[0].shape
-    column = pl.BlockSpec((count, CHUNK), lambda n: (0, n))
+    column = pl.BlockSpec((count, STEP), lambda n: (0, n))
     return pl.pallas_call(
         functools.partial(combine_kernel, locals_count=locals_count),
-        grid=(width // CHUNK,),
+        grid=(width // STEP,),
         in_specs=[pl.BlockSpec(picks.shape, lambda n: (0, 0))]
-        + [pl.BlockSpec((peers, 16, CHUNK), lambda n: (0, 0, n))] * locals_count,
+        + [pl.BlockSpec((peers, 16, STEP), lambda n: (0, 0, n))] * locals_count,
         out_specs=[column, column],
         out_shape=[jax.ShapeDtypeStruct((count, width), BF16)] * 2,
-        scratch_shapes=[pltpu.VMEM((locals_count, count, 8 * peers), BF16)],
+        scratch_shapes=[pltpu.VMEM((count, locals_count * 8 * peers), BF16)],
         compiler_params=params(56),
         cost_estimate=cost(150 * 10**9, 1 << 20),
         name="combine",
@@ -413,26 +408,40 @@
     picks = token_picks[0]
     flat_masters = masters.reshape(locals_count * 3 * per, BS * BS)
 
-    packed = pack(flat_masters)
-    sent = pick(picks, tokens, out_grad, locals_count, peers)
+    after = lax.optimization_barrier
+    packed = [pack(flat_masters, 0, locals_count)]
+    tokens, packed[0] = after((tokens, packed[0]))
+    sent = list(pick(picks, tokens, out_grad, locals_count, peers))
+    sent[0], rest_masters, kept_blocks, router = after((sent[0], flat_masters, kept_blocks, router))
+    packed += [pack(rest_masters, member, locals_count) for member in range(1, locals_count)]
     tables = slot_tables(kept_blocks, owners)
     router_rows = router.T.reshape(locals_count, width // BS, 32, 2).transpose(0, 1, 3, 2)
     router_rows = router_rows.reshape(locals_count, width).astype(F32)
-    tables, router_rows, sent = lax.optimization_barrier((tables, router_rows, sent))
 
     copies, arrived = [], []
     for member in range(locals_count):
         copies.append(lax.all_gather(packed[member], "dp", axis=0, tiled=True))
-        arrived.append(lax.all_to_all(sent[member], "expert", split_axis=0, concat_axis=0, tiled=True))
+        rows = sent[member]
+        if member:
+            rows, arrived[-1] = after((rows, arrived[-1]))
+        arrived.append(lax.all_to_all(rows, "expert", split_axis=0, concat_axis=0, tiled=True))
     summed, back = [], []
     for member in range(locals_count):
-        send, gradient = run_expert(member, tables, copies[member], arrived[member], router_rows)
+        rows = arrived[member]
+        if member:
+            rows, send = after((rows, send))
+            back.append(lax.all_to_all(send, "expert", split_axis=0, concat_axis=0, tiled=True))
+        send, gradient = run_expert(member, tables, copies[member], rows, router_rows)
         summed.append(lax.psum_scatter(gradient, "dp", scatter_dimension=0, tiled=True))
-        back.append(lax.all_to_all(send, "expert", split_axis=0, concat_axis=0, tiled=True))
+    send, back = after((send, back))
+    back.append(lax.all_to_all(send, "expert", split_axis=0, concat_axis=0, tiled=True))
     held = ()
-    for member in range(locals_count):
+    for member in range(locals_count - 1):
         held = update(member, summed[member], flat_masters, held)
+    held, picks = after((held, picks))
     layer_out, input_grad = combine(picks, back, count)
+    summed[-1], layer_out = after((summed[-1], layer_out))
+    held = update(locals_count - 1, summed[-1], flat_masters, held)
     master_new = held[0].reshape(masters.shape)
     score_new = scores - SCORE_RATE * held[1].reshape(scores.shape)
     router_new = jnp.stack([part[-1, : width // owners // 128] for part in summed])

time: 211 us -> 200 us (0.948)
  waiting for transfers between devices: 60.7 us -> 51.7 us
    all_to_all x2, waiting for transfers between devices: 27.5 us -> 19.5 us  [body(): lax.all_to_all(rows, 'expert', split_axis=0, concat_axis=0, tiled=True)]
    all_to_all x2, waiting for transfers between devices: 27.7 us -> 22 us  [body(): lax.all_to_all(send, 'expert', split_axis=0, concat_axis=0, tiled=True)]
    reduce_scatter x2, waiting for transfers between devices: 4.11 us -> 9.12 us  [body(): lax.psum_scatter(gradient, 'dp', scatter_dimension=0, tiled=True)]
    pallas_call x1 -> x2, Pallas kernels: 4.36 us -> 6.52 us  [pack(): pl.pallas_call(pack_kernel, grid=(steps,), in_specs=[pl.BlockSpec((rows,...]
  transfers between devices with their start and end apart: 8 -> 8, of which waited for: 3 -> 4; matrix products, arithmetic and copies ran while one was open for 3% -> 3% of each run, Pallas kernels for 38% -> 42%
where the time goes in v3:
time: 200 us; the launch traced here: 199 us
  Pallas kernels  90.8 us (45%)
  waiting for transfers between devices  51.7 us (26%)
  starting transfers between devices  30.1 us (15%)
  between operations  13.9 us (7%)
  local copies, waits for them, and re-layouts  11.1 us (6%)
    pallas_call x2, Pallas kernels, run_expert(): pl.pallas_call(functools.partial(expert_kernel, member=member), in_specs=...  64.4 us
    all_to_all x2, waiting for transfers between devices, body(): lax.all_to_all(send, 'expert', split_axis=0, concat_axis=0, tiled=True)  22 us
    all_to_all x2, waiting for transfers between devices, body(): lax.all_to_all(rows, 'expert', split_axis=0, concat_axis=0, tiled=True)  19.5 us
    all_to_all x2, starting transfers between devices, body(): lax.all_to_all(send, 'expert', split_axis=0, concat_axis=0, tiled=True)  14.9 us
    all_to_all x2, starting transfers between devices, body(): lax.all_to_all(rows, 'expert', split_axis=0, concat_axis=0, tiled=True)  14.8 us
    reduce_scatter x2, waiting for transfers between devices, body(): lax.psum_scatter(gradient, 'dp', scatter_dimension=0, tiled=True)  9.12 us
    pallas_call x2, Pallas kernels, update(): pl.pallas_call(update_kernel, grid=(steps,), in_specs=[pl.BlockSpec((rows...  7.72 us
    pallas_call x2, Pallas kernels, pack(): pl.pallas_call(pack_kernel, grid=(steps,), in_specs=[pl.BlockSpec((rows,...  6.52 us
  transfers between devices with their start and end apart: 8, of which 4 were waited for; matrix products, arithmetic and copies ran while one was open for 3% of the time, Pallas kernels for 42%

profile of v3, /device:TPU:1, one launch (start us, length us, event | category | flops | bytes accessed | tf_op | source)
XLA Modules:
  0.0 199.3 jit_solution(12092587630645271065)
XLA Ops:
  7.2 0.0 all-gather.5.cloned.1.call-start
  7.2 3.3 %pack_0.1 = bf16[96,32,128]{2,1,0:T(8,128)(2,1)} custom-call(f32[192,4096]{1,0:T(8,128)} %bitcast.11), custom_call_target="tpu_custom_call" | custom-call | bytes 1048576 | tf_op jit(solution)/shard_map/pack_0/pallas_call | solution.py:293
  10.5 0.0 all-gather.5.cloned.1.call-update
  10.5 0.7 copy.38
  11.2 6.1 %pick.1 = (bf16[32,16,2048]{2,1,0:T(8,128)(2,1)}, bf16[32,16,2048]{2,1,0:T(8,128)(2,1)}) custom-call(s32[64,8]{1,0:T(8,128)} %bitcast.18, bf16[256,2048]{1,0:T(8,128)(2,1)} %tokens_ref, bf16[256,2048]{1,0:T(8,128)(2,1)} %grads_ref.1), custom_call_target="tpu_custom_call" | custom-call | bytes 1048576 | tf_op jit(solution)/shard_map/pick/pallas_call | solution.py:276
  17.3 9.6 %all-to-all-start = ((bf16[32,16,2048]{2,1,0:T(8,128)(2,1)}), bf16[32,16,2048]{2,1,0:T(8,128)(2,1)S(1)}, u32[]{:S(2)}, u32[]{:S(2)}) async-start(bf16[32,16,2048]{2,1,0:T(8,128)(2,1)} %get-tuple-element.39), calls=%async_computation | async-start | bytes 4194304 | tf_op jit(solution)/shard_map/all_to_all | solution.py:427
  26.9 0.0 copy-start.6
  26.9 0.0 all-gather.3.cloned.1.call-start
  27.0 3.3 %pack_1.1 = bf16[96,32,128]{2,1,0:T(8,128)(2,1)} custom-call(f32[192,4096]{1,0:T(8,128)} %bitcast.12), custom_call_target="tpu_custom_call" | custom-call | bytes 1048576 | tf_op jit(solution)/shard_map/pack_1/pallas_call | solution.py:293
  30.2 0.0 all-gather.3.cloned.1.call-update
  30.3 0.6 reshape.134.valid_ref
  30.9 0.2 multiply_add_fusion
  31.2 0.6 reshape.130.lane_ref
  31.8 0.6 reshape.129.row_ref
  32.4 0.1 add_add_fusion
  32.4 0.4 select_reduce_fusion
  32.8 0.6 sub.25.inverse_ref
  33.5 1.0 reshape.139
  34.5 0.5 copy.43
  34.9 0.7 reshape.135.router_ref
  35.7 19.5 %all-to-all-done.arrived_ref = bf16[32,16,2048]{2,1,0:T(8,128)(2,1)S(1)} async-done(((bf16[32,16,2048]{2,1,0:T(8,128)(2,1)}), bf16[32,16,2048]{2,1,0:T(8,128)(2,1)S(1)}, u32[]{:S(2)}, u32[]{:S(2)}) %all-to-all-start) | async-done | bytes 2097184 | tf_op jit(solution)/shard_map/all_to_all | solution.py:427
  55.2 1.3 copy-done
  56.5 5.2 %all-to-all-start.1 = ((bf16[32,16,2048]{2,1,0:T(8,128)(2,1)}), bf16[32,16,2048]{2,1,0:T(8,128)(2,1)}, u32[]{:S(2)}, u32[]{:S(2)}) async-start(bf16[32,16,2048]{2,1,0:T(8,128)(2,1)} %get-tuple-element.40), calls=%async_computation.1 | async-start | bytes 4194304 | tf_op jit(solution)/shard_map/all_to_all | solution.py:427
  61.7 0.0 all-gather.5.cloned.1.call-done.copies_ref
  61.8 32.2 %expert_0.1 = (bf16[32,16,2048]{2,1,0:T(8,128)(2,1)}, bf16[388,32,128]{2,1,0:T(8,128)(2,1)}) custom-call(s32[2304]{0:T(1024)} %sub.25.inverse_ref, s32[768]{0:T(1024)} %reshape.129.row_ref, s32[768]{0:T(1024)} %reshape.130.lane_ref, s32[768]{0:T(1024)} %reshape.134.valid_ref, bf16[384,32,128]{2,1,0:T(8,128)(2,1)} %all-gather.5.cloned.1.call-done.copies_ref, ...), custom_call_target="tpu_custom_call" | custom-call | flops 149999992832 | bytes 1048576 | tf_op jit(solution)/shard_map/expert_0/pallas_call | solution.py:311
  93.9 7.6 %all-to-all-start.2 = ((bf16[32,16,2048]{2,1,0:T(8,128)(2,1)}), bf16[32,16,2048]{2,1,0:T(8,128)(2,1)}, u32[]{:S(2)}, u32[]{:S(2)}) async-start(bf16[32,16,2048]{2,1,0:T(8,128)(2,1)} %get-tuple-element.52), calls=%async_computation.4 | async-start | bytes 4194304 | tf_op jit(solution)/shard_map/all_to_all | solution.py:433
  101.5 0.2 reduce-scatter.5.cloned.1.call-start
  101.7 0.5 reduce-scatter.5.cloned.1.call-update
  102.2 0.0 all-gather.3.cloned.1.call-done.copies_ref
  102.3 32.2 %expert_1.1 = (bf16[32,16,2048]{2,1,0:T(8,128)(2,1)}, bf16[388,32,128]{2,1,0:T(8,128)(2,1)}) custom-call(s32[2304]{0:T(1024)} %sub.25.inverse_ref, s32[768]{0:T(1024)} %reshape.129.row_ref, s32[768]{0:T(1024)} %reshape.130.lane_ref, s32[768]{0:T(1024)} %reshape.134.valid_ref, bf16[384,32,128]{2,1,0:T(8,128)(2,1)} %all-gather.3.cloned.1.call-done.copies_ref, ...), custom_call_target="tpu_custom_call" | custom-call | flops 149999992832 | bytes 1048576 | tf_op jit(solution)/shard_map/expert_1/pallas_call | solution.py:311
  134.5 7.4 %all-to-all-start.3 = ((bf16[32,16,2048]{2,1,0:T(8,128)(2,1)}), bf16[32,16,2048]{2,1,0:T(8,128)(2,1)S(1)}, u32[]{:S(2)}, u32[]{:S(2)}) async-start(bf16[32,16,2048]{2,1,0:T(8,128)(2,1)} %get-tuple-element.54), calls=%async_computation.5 | async-start | bytes 4194304 | tf_op jit(solution)/shard_map/all_to_all | solution.py:437
  141.9 0.0 reduce-scatter.3.cloned.1.call-start
  141.9 0.5 reduce-scatter.3.cloned.1.call-update
  142.4 1.9 reduce-scatter.5.cloned.1.call-done.summed_ref
  144.3 3.9 %update_0.1 = (f32[192,4096]{1,0:T(8,128)}, f32[192,1]{1,0:T(8,128)}) custom-call(bf16[97,32,128]{2,1,0:T(8,128)(2,1)} %reduce-scatter.5.cloned.1.call-done.summed_ref, f32[192,4096]{1,0:T(8,128)} %bitcast.13), custom_call_target="tpu_custom_call" | custom-call | bytes 1048576 | tf_op jit(solution)/shard_map/update_0/pallas_call | solution.py:342
  148.2 22.0 %all-to-all-done.3.rest_1_ = bf16[32,16,2048]{2,1,0:T(8,128)(2,1)S(1)} async-done(((bf16[32,16,2048]{2,1,0:T(8,128)(2,1)}), bf16[32,16,2048]{2,1,0:T(8,128)(2,1)S(1)}, u32[]{:S(2)}, u32[]{:S(2)}) %all-to-all-start.3) | async-done | bytes 2097184 | tf_op jit(solution)/shard_map/all_to_all | solution.py:437
  170.2 1.4 copy-done.1
  171.6 6.0 %combine.1 = (bf16[256,2048]{1,0:T(8,128)(2,1)}, bf16[256,2048]{1,0:T(8,128)(2,1)}) custom-call(s32[64,8]{1,0:T(8,128)} %bitcast.19, bf16[32,16,2048]{2,1,0:T(8,128)(2,1)} %all-to-all-done.2.rest_0_, bf16[32,16,2048]{2,1,0:T(8,128)(2,1)} %copy-done.1), custom_call_target="tpu_custom_call" | custom-call | flops 149999992832 | bytes 1048576 | tf_op jit(solution)/shard_map/combine/pallas_call | solution.py:370
  177.6 7.2 %reduce-scatter.3.cloned.1.call-done.summed_ref = bf16[97,32,128]{2,1,0:T(8,128)(2,1)} async-done(((bf16[388,32,128]{2,1,0:T(8,128)(2,1)}), bf16[97,32,128]{2,1,0:T(8,128)(2,1)}) %reduce-scatter.3.cloned.1.call-update) | async-done | bytes 794640 | tf_op jit(solution)/shard_map/reduce_scatter | solution.py:435
  184.8 0.7 slice.7
  185.5 3.9 %update_1.1 = (f32[192,4096]{1,0:T(8,128)}, f32[192,1]{1,0:T(8,128)}) custom-call(bf16[97,32,128]{2,1,0:T(8,128)(2,1)} %reduce-scatter.3.cloned.1.call-done.summed_ref, f32[192,4096]{1,0:T(8,128)} %bitcast.14, f32[192,4096]{1,0:T(8,128)} %get-tuple-element.59.rest_0_, f32[192,1]{1,0:T(8,128)} %get-tuple-element.60.rest_1_), custom_call_target="tpu_custom_call", output_to_operand_aliasing={{0}: (2, {}), {1}: (3, {})} | custom-call | bytes 1048576 | tf_op jit(solution)/shard_map/update_1/pallas_call | solution.py:342
  189.4 1.0 multiply_reduce_fusion
  190.4 0.1 mul.56
  190.5 0.6 copy.46
  191.1 0.7 slice.8
  191.8 0.1 reshape.141
  191.8 0.2 copy.45
  192.0 0.8 reshape.137
  (25 shorter events, 0.1 us)
Async XLA Ops:
  7.2 54.6 %all-gather.5.cloned.1.call-start = ((), (), s32[]{:S(2)}) async-start(), calls=%async_computation.7 | async-start | bytes 3932160 | tf_op jit(solution)/shard_map/all_gather | solution.py:423
  7.2 3.3 %copy-start.4 = (s32[1,64,8]{1,2,0:T(8,128)S(1)}, s32[1,64,8]{1,2,0:T(8,128)}, u32[]{:S(2)}) copy-start(s32[1,64,8]{1,2,0:T(8,128)} %param.10) | copy-start | bytes 6148
  17.3 37.9 %all-to-all-start = ((bf16[32,16,2048]{2,1,0:T(8,128)(2,1)}), bf16[32,16,2048]{2,1,0:T(8,128)(2,1)S(1)}, u32[]{:S(2)}, u32[]{:S(2)}) async-start(bf16[32,16,2048]{2,1,0:T(8,128)(2,1)} %get-tuple-element.39), calls=%async_computation | async-start | bytes 4194304 | tf_op jit(solution)/shard_map/all_to_all | solution.py:427
  26.9 3.4 %copy-start.2 = (s32[2,3,128]{2,0,1:T(2,128)S(1)}, s32[2,3,128]{2,0,1:T(2,128)}, u32[]{:S(2)}) copy-start(s32[2,3,128]{2,0,1:T(2,128)} %param.12) | copy-start | bytes 9220
  26.9 4.0 %copy-start.6 = (s32[3]{0:T(128)S(1)}, s32[3]{0:T(128)}, u32[]{:S(2)}) copy-start(s32[3]{0:T(128)} %constant.64.clone) | copy-start | bytes 40
  26.9 6.5 %copy-start.3 = (bf16[2048,2]{0,1:T(2,128)(2,1)S(1)}, bf16[2048,2]{0,1:T(2,128)(2,1)}, u32[]{:S(2)}) copy-start(bf16[2048,2]{0,1:T(2,128)(2,1)} %param.11) | copy-start | bytes 24580
  26.9 75.3 %all-gather.3.cloned.1.call-start = ((), (), s32[]{:S(2)}) async-start(), calls=%async_computation.6 | async-start | bytes 3932160 | tf_op jit(solution)/shard_map/all_gather | solution.py:423
  55.2 1.3 copy-start
  56.5 37.4 %all-to-all-start.1 = ((bf16[32,16,2048]{2,1,0:T(8,128)(2,1)}), bf16[32,16,2048]{2,1,0:T(8,128)(2,1)}, u32[]{:S(2)}, u32[]{:S(2)}) async-start(bf16[32,16,2048]{2,1,0:T(8,128)(2,1)} %get-tuple-element.40), calls=%async_computation.1 | async-start | bytes 4194304 | tf_op jit(solution)/shard_map/all_to_all | solution.py:427
  93.9 40.5 %all-to-all-start.2 = ((bf16[32,16,2048]{2,1,0:T(8,128)(2,1)}), bf16[32,16,2048]{2,1,0:T(8,128)(2,1)}, u32[]{:S(2)}, u32[]{:S(2)}) async-start(bf16[32,16,2048]{2,1,0:T(8,128)(2,1)} %get-tuple-element.52), calls=%async_computation.4 | async-start | bytes 4194304 | tf_op jit(solution)/shard_map/all_to_all | solution.py:433
  101.5 42.8 %reduce-scatter.5.cloned.1.call-start = ((), (), s32[]{:S(2)}) async-start(), calls=%async_computation.9 | async-start | bytes 3973120 | tf_op jit(solution)/shard_map/reduce_scatter | solution.py:435
  134.5 35.7 %all-to-all-start.3 = ((bf16[32,16,2048]{2,1,0:T(8,128)(2,1)}), bf16[32,16,2048]{2,1,0:T(8,128)(2,1)S(1)}, u32[]{:S(2)}, u32[]{:S(2)}) async-start(bf16[32,16,2048]{2,1,0:T(8,128)(2,1)} %get-tuple-element.54), calls=%async_computation.5 | async-start | bytes 4194304 | tf_op jit(solution)/shard_map/all_to_all | solution.py:437
  141.9 43.0 %reduce-scatter.3.cloned.1.call-start = ((), (), s32[]{:S(2)}) async-start(), calls=%async_computation.8 | async-start | bytes 3973120 | tf_op jit(solution)/shard_map/reduce_scatter | solution.py:435
  170.2 1.4 copy-start.1
  185.5 4.9 %copy-start.5 = (f32[2,3,32]{2,0,1:T(2,128)S(1)}, f32[2,3,32]{2,0,1:T(2,128)}, u32[]{:S(2)}) copy-start(f32[2,3,32]{2,0,1:T(2,128)} %param.14) | copy-start | bytes 2308
Sparse Core Ops, SparseCore 0:
  10.6 42.7 all-gather.4
  55.6 39.7 all-gather.2
  104.7 39.5 reduce-scatter.4
  146.6 38.1 reduce-scatter.2

commit v4 on v3

--- a/solution.py
+++ b/solution.py
@@ -86,24 +86,42 @@
             out_refs[member][:, :, cols] = interleave(tokens[mine], grads[mine])
 
 
-def pack_kernel(masters_ref, out_ref, lines_ref):
-    for group in range(masters_ref.shape[0] // 8):
-        for k in range(32):
-            lines_ref[group, 8 * k : 8 * k + 8, :] = masters_ref[
-                8 * group : 8 * group + 8, 128 * k : 128 * k + 128
-            ]
-        for s in range(8):
-            out_ref[8 * group + s] = lines_ref[group, pl.ds(s, 32, stride=8), :].astype(BF16)
+def pack_kernel(masters_ref, *rest):
+    out_refs, lines_ref = rest[:-1], rest[-1]
+    for at, out_ref in enumerate(out_refs):
+
+        @pl.when(pl.program_id(0) == at)
+        def _(out_ref=out_ref):
+            for group in range(masters_ref.shape[0] // 8):
+                for k in range(32):
+                    lines_ref[group, 8 * k : 8 * k + 8, :] = masters_ref[
+                        8 * group : 8 * group + 8, 128 * k : 128 * k + 128
+                    ]
+                for s in range(8):
+                    line = lines_ref[group, pl.ds(s, 32, stride=8), :]
+                    out_ref[8 * group + s] = line.astype(BF16)
 
 
 def expert_kernel(
-    inverse_ref, row_ref, lane_ref, valid_ref,
-    copies_ref, arrived_ref, router_ref,
-    send_ref, packed_ref,
+    inverse_ref, row_ref, lane_ref, valid_ref, me_ref,
+    arrived_ref, router_ref, *rest,
+    member,
+):
+    piece_refs, send_ref, grad_refs = rest[:8], rest[8], rest[9:16]
+    (
+    copies_ref, packed_ref, in_sems, out_sems,
     wide_ref, down_ref, rows_ref, grads_ref, pre_ref, part_ref, both_ref,
     grad_wide_ref, grad_down_ref, router_out_ref,
-    *, member,
-):
+    ) = rest[16:]
+    length = piece_refs[0].shape[0]
+    loads = [
+        pltpu.make_async_copy(piece, copies_ref.at[pl.ds(at * length, length)], in_sems.at[at])
+        for at, piece in enumerate(piece_refs)
+    ]
+    for load in loads:
+        load.start()
+    for load in loads:
+        load.wait()
     base, slot_base = member * 3 * BLOCKS, member * 3 * MAXB
     lane = iota((32, 128), 1)
     half = lane < 64
@@ -206,36 +224,90 @@
 
     per = MAXB // OWNERS
     part = packed_ref.shape[0] // OWNERS
-    for owner in range(OWNERS):
+    half = 3 * per // 2
+    stores = []
+    for ahead in (2, 1, 3, 0):
+        owner = (me_ref[0] + ahead) & (OWNERS - 1)
+        first = ahead * part
         for matrix in range(3):
             source_ref = grad_down_ref if matrix == 2 else grad_wide_ref
 
             @pl.loop(0, per // 4)
-            def _(group, owner=owner, matrix=matrix, source_ref=source_ref):
+            def _(group, first=first, matrix=matrix, source_ref=source_ref, owner=owner):
                 for step in range(4):
                     s = group * 4 + step
-                    cut(source_ref, matrix, owner * per + s, owner * part + matrix * per + s)
+                    cut(source_ref, matrix, owner * per + s, first + matrix * per + s)
 
         start = owner * (D // OWNERS)
-        lines = [router_out_ref[:, start + at : start + at + 128] for at in range(0, D // OWNERS, 128)]
+        lines = [
+            router_out_ref[:, pl.ds(pl.multiple_of(start + at, 128), 128)]
+            for at in range(0, D // OWNERS, 128)
+        ]
         lines.append(jnp.zeros((32 - len(lines), 128), F32))
-        packed_ref[owner * part + 3 * per] = jnp.concatenate(lines, axis=0).astype(BF16)
-
-
-def update_kernel(summed_ref, masters_ref, *rest):
-    out_ref, total_ref, lines_ref = rest[-3:]
-    for group in range(masters_ref.shape[0] // 8):
-        for s in range(8):
-            lines_ref[group, pl.ds(s, 32, stride=8), :] = summed_ref[8 * group + s].astype(F32)
+        packed_ref[first + 3 * per] = jnp.concatenate(lines, axis=0).astype(BF16)
+        cuts = [(0, part)] if ahead == 0 else [(0, half), (half, part - half)]
+        for at, (begin, size) in enumerate(cuts):
+            number = 0 if ahead == 0 else 2 * ahead - 1 + at
+            store = pltpu.make_async_copy(
+                packed_ref.at[pl.ds(first + begin, size)], grad_refs[number], out_sems.at[number]
+            )
+            store.start()
+            stores.append(store)
+    for store in stores:
+        store.wait()
+
+
+def update_kernel(
+    own_ref, left_a_ref, right_a_ref, left_b_ref, right_b_ref,
+    own_last_ref, left_last_ref, right_last_ref,
+    masters_ref, scores_ref, router_ref, *rest,
+    member,
+):
+    out_ref, scores_out_ref, router_out_ref, lines_ref, total_ref = rest[-5:]
+    step, steps = pl.program_id(0), pl.num_programs(0)
+    rows = masters_ref.shape[0]
+
+    def gather(left_ref, right_ref):
+        for s in range(rows):
+            summed = own_ref[s].astype(F32) + left_ref[s].astype(F32) + right_ref[s].astype(F32)
+            lines_ref[s // 8, pl.ds(s % 8, 32, stride=8), :] = summed
+
+    @pl.when(step < steps // 2)
+    def _():
+        gather(left_a_ref, right_a_ref)
+
+    @pl.when(step >= steps // 2)
+    def _():
+        gather(left_b_ref, right_b_ref)
+
+    for group in range(rows // 8):
         total = jnp.zeros((8, 128), F32)
-        rows = slice(8 * group, 8 * group + 8)
+        here = slice(8 * group, 8 * group + 8)
         for k in range(32):
             cols = slice(128 * k, 128 * k + 128)
             gradient = lines_ref[group, 8 * k : 8 * k + 8, :]
-            held = masters_ref[rows, cols]
-            out_ref[rows, cols] = held - LEARN_RATE * gradient
+            held = masters_ref[here, cols]
+            out_ref[here, cols] = held - LEARN_RATE * gradient
             total = total + held * gradient
-        total_ref[rows, :] = jnp.sum(total, axis=1, keepdims=True)
+        total_ref[pl.ds(pl.multiple_of(step * rows + 8 * group, 8), 8), :] = total
+
+    @pl.when(step == steps - 1)
+    def _():
+        exact = functools.partial(
+            lax.dot_general, dimension_numbers=NT, precision=lax.Precision.HIGHEST, preferred_element_type=F32
+        )
+        count, experts, per = scores_ref.shape
+        mine = iota((experts, per), 0) == member
+        for matrix in range(count):
+            sums = exact(jnp.ones((8, 128), F32), total_ref[matrix * per : (matrix + 1) * per, :])
+            change = jnp.where(mine, jnp.broadcast_to(sums[:1], mine.shape), 0.0)
+            scores_out_ref[matrix] = scores_ref[matrix] - SCORE_RATE * change
+        last = own_last_ref[0].astype(F32) + left_last_ref[0].astype(F32) + right_last_ref[0].astype(F32)
+        last = exact(last, split_matrix(128).astype(F32))
+        width = router_ref.shape[1]
+        line = jnp.concatenate([last[at : at + 1] for at in range(width // 128)], axis=1)
+        held = iota(router_ref.shape, 0) == member
+        router_out_ref[...] = jnp.where(held, jnp.broadcast_to(line, router_ref.shape), router_ref[...])
 
 
 def combine_kernel(picks_ref, *rest, locals_count):
@@ -286,37 +358,41 @@
     )(picks, tokens, grads)
 
 
-def pack(masters, member, locals_count):
-    mine = masters.shape[0] // locals_count
-    steps = 3
-    rows = mine // steps
+def pack(masters, parts):
+    mine = masters.shape[0] // parts
     return pl.pallas_call(
         pack_kernel,
-        grid=(steps,),
-        in_specs=[pl.BlockSpec((rows, BS * BS), lambda n: (member * steps + n, 0))],
-        out_specs=pl.BlockSpec((rows, 32, 128), lambda n: (n, 0, 0)),
-        out_shape=jax.ShapeDtypeStruct((mine, 32, 128), BF16),
-        scratch_shapes=[pltpu.VMEM((rows // 8, 256, 128), F32)],
+        grid=(parts,),
+        in_specs=[pl.BlockSpec((mine, BS * BS), lambda n: (n, 0))],
+        out_specs=[pl.BlockSpec((mine, 32, 128), lambda n: (0, 0, 0))] * parts,
+        out_shape=[jax.ShapeDtypeStruct((mine, 32, 128), BF16)] * parts,
+        scratch_shapes=[pltpu.VMEM((mine // 8, 256, 128), F32)],
         compiler_params=params(56),
         cost_estimate=cost(0, 1 << 20),
-        name="pack_%d" % member,
+        name="pack",
     )(masters)
 
 
-def run_expert(member, tables, copies, arrived, router_rows):
+def run_expert(member, tables, place, pieces, arrived, router_rows):
     peers = arrived.shape[0]
     count = 8 * peers
     whole = pl.BlockSpec(memory_space=pltpu.VMEM)
     scalar = pl.BlockSpec(memory_space=pltpu.SMEM)
+    anywhere = pl.BlockSpec(memory_space=pl.ANY)
+    part = 3 * MAXB // OWNERS + 1
+    half = part // 2
+    lengths = [part] + [half, part - half] * 3
     return pl.pallas_call(
         functools.partial(expert_kernel, member=member),
-        in_specs=[scalar] * 4 + [whole] * 3,
-        out_specs=[whole] * 2,
-        out_shape=[
-            jax.ShapeDtypeStruct((peers, 16, D), BF16),
-            jax.ShapeDtypeStruct((3 * MAXB + OWNERS, 32, 128), BF16),
-        ],
+        in_specs=[scalar] * 5 + [whole] * 2 + [anywhere] * len(pieces),
+        out_specs=[whole] + [anywhere] * len(lengths),
+        out_shape=[jax.ShapeDtypeStruct((peers, 16, D), BF16)]
+        + [jax.ShapeDtypeStruct((length, 32, 128), BF16) for length in lengths],
         scratch_shapes=[
+            pltpu.VMEM((3 * MAXB, 32, 128), BF16),
+            pltpu.VMEM((OWNERS * part, 32, 128), BF16),
+            pltpu.SemaphoreType.DMA((len(pieces),)),
+            pltpu.SemaphoreType.DMA((len(lengths),)),
             pltpu.VMEM((D, 2 * FF), BF16),
             pltpu.VMEM((FF, D), BF16),
             pltpu.VMEM((count, D), BF16),
@@ -331,36 +407,38 @@
         compiler_params=params(56),
         cost_estimate=cost(150 * 10**9, 1 << 20),
         name="expert_%d" % member,
-    )(*tables, copies, arrived, router_rows)
-
-
-def update(member, summed, masters, held):
-    slots = masters.shape[0]
-    mine = summed.shape[0] - 1
-    steps = 3
+    )(*tables, place, arrived, router_rows, *pieces)
+
+
+def update(member, summed, masters, scores, router_sum, held):
+    own, left_a, right_a, left_b, right_b = summed
+    mine = own.shape[0] - 1
+    steps = 6
     rows = mine // steps
+    tile = lambda index: pl.BlockSpec((rows, 32, 128), index)
+    early = tile(lambda n: (jnp.minimum(n, steps // 2 - 1), 0, 0))
+    late = tile(lambda n: (jnp.maximum(n - steps // 2, 0), 0, 0))
+    last = lambda array: pl.BlockSpec((1, 32, 128), lambda n: (array.shape[0] - 1, 0, 0))
+    block = pl.BlockSpec((rows, BS * BS), lambda n: (member * steps + n, 0))
+    whole = lambda array: pl.BlockSpec(array.shape, lambda n: (0,) * array.ndim)
     return pl.pallas_call(
-        update_kernel,
+        functools.partial(update_kernel, member=member),
         grid=(steps,),
-        in_specs=[
-            pl.BlockSpec((rows, 32, 128), lambda n: (n, 0, 0)),
-            pl.BlockSpec((rows, BS * BS), lambda n: (member * steps + n, 0)),
-        ]
+        in_specs=[tile(lambda n: (n, 0, 0)), early, early, late, late]
+        + [last(own), last(left_b), last(right_b), block, whole(scores), whole(router_sum)]
         + [pl.BlockSpec(memory_space=pl.ANY)] * len(held),
-        out_specs=[
-            pl.BlockSpec((rows, BS * BS), lambda n: (member * steps + n, 0)),
-            pl.BlockSpec((rows, 1), lambda n: (member * steps + n, 0)),
+        out_specs=[block, whole(scores), whole(router_sum)],
+        out_shape=[
+            jax.ShapeDtypeStruct(masters.shape, F32),
+            jax.ShapeDtypeStruct(scores.shape, F32),
+            jax.ShapeDtypeStruct(router_sum.shape, F32),
         ],
-        out_shape=[
-            jax.ShapeDtypeStruct((slots, BS * BS), F32),
-            jax.ShapeDtypeStruct((slots, 1), F32),
-        ],
-        input_output_aliases={2 + at: at for at in range(len(held))},
-        scratch_shapes=[pltpu.VMEM((rows // 8, 256, 128), F32)],
+        input_output_aliases={11 + at: at for at in range(len(held))},
+        scratch_shapes=[pltpu.VMEM((rows // 8, 256, 128), F32), pltpu.VMEM((mine, 128), F32)],
         compiler_params=params(56),
         cost_estimate=cost(0, 1 << 20),
         name="update_%d" % member,
-    )(summed, masters, *held)
+    )(own, left_a, right_a, left_b, right_b, own, left_b, right_b, masters, scores, router_sum, *held)
 
 
 def combine(picks, back, count):
@@ -381,12 +459,14 @@
     )(picks, *back)
 
 
-def slot_tables(kept, owners):
+def slot_tables(kept, owners, me):
     numbers = jnp.arange(BLOCKS, dtype=jnp.int32)
     slots = jnp.arange(MAXB, dtype=jnp.int32)
     per = MAXB // owners
     matrix = jnp.arange(3, dtype=jnp.int32)[None, :, None]
-    place = (slots // per) * (3 * per) + slots % per + matrix * per
+    ahead = (slots // per - me) % owners
+    order = jnp.where(ahead == 0, 0, jnp.where(ahead == owners - 1, 1, ahead + 1))
+    place = order * (3 * per) + slots % per + matrix * per
     hits = kept[:, :, None, :] == numbers[None, None, :, None]
     inverse = jnp.sum(jnp.where(hits, place[:, :, None, :] + 1, 0), axis=-1) - 1
     valid = kept < BLOCKS
@@ -399,55 +479,80 @@
     return flat(inverse), flat(rows), flat(lanes), flat(valid)
 
 
+def shift(array, step):
+    owners = lax.axis_size("dp")
+    return lax.ppermute(array, "dp", [(i, (i + step) % owners) for i in range(owners)])
+
+
+def gather_pieces(first, second):
+    left_a, right_b = shift(first, 1), shift(second, -1)
+    left_b, right_a = shift(second, 1), shift(first, -1)
+    return [first, second, left_a, left_b, right_a, right_b, shift(left_a, 1), shift(right_b, -1)]
+
+
+def scatter_first(own, right_a, right_b, far_a, far_b, left_a, left_b):
+    moving = [shift(far_a, 1), shift(far_b, -1), shift(right_b, 1), shift(left_a, -1)]
+    return own, right_a, left_b, moving
+
+
+def scatter_second(own, right_a, left_b, moving):
+    passing_a, passing_b, from_left_b, from_right_a = moving
+    from_left_a = shift(right_a + passing_a, 1)
+    from_right_b = shift(left_b + passing_b, -1)
+    return own, from_left_a, from_right_a, from_left_b, from_right_b
+
+
 def body(tokens, out_grad, token_picks, router, kept_blocks, masters, scores):
     locals_count = kept_blocks.shape[0]
     owners = lax.axis_size("dp")
     peers = lax.axis_size("expert")
+    me = lax.axis_index("dp").astype(jnp.int32)
     count, width = tokens.shape
     per = masters.shape[2]
     picks = token_picks[0]
     flat_masters = masters.reshape(locals_count * 3 * per, BS * BS)
-
     after = lax.optimization_barrier
-    packed = [pack(flat_masters, 0, locals_count)]
-    tokens, packed[0] = after((tokens, packed[0]))
+
+    def exchange(array):
+        return lax.all_to_all(array, "expert", split_axis=0, concat_axis=0, tiled=True)
+
     sent = list(pick(picks, tokens, out_grad, locals_count, peers))
     sent[0], rest_masters, kept_blocks, router = after((sent[0], flat_masters, kept_blocks, router))
-    packed += [pack(rest_masters, member, locals_count) for member in range(1, locals_count)]
-    tables = slot_tables(kept_blocks, owners)
+    halves = pack(rest_masters, 2 * locals_count)
+    tables = slot_tables(kept_blocks, owners, me)
     router_rows = router.T.reshape(locals_count, width // BS, 32, 2).transpose(0, 1, 3, 2)
     router_rows = router_rows.reshape(locals_count, width).astype(F32)
-
-    copies, arrived = [], []
+    place = me.reshape(1)
+
+    pieces, arrived = [], []
     for member in range(locals_count):
-        copies.append(lax.all_gather(packed[member], "dp", axis=0, tiled=True))
+        pieces.append(gather_pieces(halves[2 * member], halves[2 * member + 1]))
         rows = sent[member]
         if member:
             rows, arrived[-1] = after((rows, arrived[-1]))
-        arrived.append(lax.all_to_all(rows, "expert", split_axis=0, concat_axis=0, tiled=True))
+        arrived.append(exchange(rows))
     summed, back = [], []
     for member in range(locals_count):
         rows = arrived[member]
         if member:
             rows, send = after((rows, send))
-            back.append(lax.all_to_all(send, "expert", split_axis=0, concat_axis=0, tiled=True))
-        send, gradient = run_expert(member, tables, copies[member], rows, router_rows)
-        summed.append(lax.psum_scatter(gradient, "dp", scatter_dimension=0, tiled=True))
-    send, back = after((send, back))
-    back.append(lax.all_to_all(send, "expert", split_axis=0, concat_axis=0, tiled=True))
+            back.append(exchange(send))
+        send, *gradients = run_expert(member, tables, place, pieces[member], rows, router_rows)
+        summed.append(scatter_first(*gradients))
+    send, back, summed[:-1] = after((send, back, summed[:-1]))
+    back.append(exchange(send))
+    summed = [scatter_second(*terms) for terms in summed]
+    score_sum = scores.transpose(1, 0, 2)
+    router_sum = jnp.zeros((locals_count, width // owners), F32)
     held = ()
     for member in range(locals_count - 1):
-        held = update(member, summed[member], flat_masters, held)
+        new, score_sum, router_sum = update(member, summed[member], flat_masters, score_sum, router_sum, held)
+        held = (new,)
     held, picks = after((held, picks))
     layer_out, input_grad = combine(picks, back, count)
-    summed[-1], layer_out = after((summed[-1], layer_out))
-    held = update(locals_count - 1, summed[-1], flat_masters, held)
-    master_new = held[0].reshape(masters.shape)
-    score_new = scores - SCORE_RATE * held[1].reshape(scores.shape)
-    router_new = jnp.stack([part[-1, : width // owners // 128] for part in summed])
-    router_new = router_new.reshape(locals_count, width // owners // BS, 2, 32).astype(F32)
-    router_new = router_new.transpose(1, 3, 2, 0).reshape(width // owners, locals_count)
-    return layer_out, input_grad, master_new, score_new, router_new
+    last, layer_out = after((summed[-1], layer_out))
+    new, score_sum, router_sum = update(locals_count - 1, last, flat_masters, score_sum, router_sum, held)
+    return layer_out, input_grad, new.reshape(masters.shape), score_sum.transpose(1, 0, 2), router_sum.T
 
 
 def solution(mesh):

time: 200 us -> 201 us (level)
  starting transfers between devices: 30.1 us -> 59.8 us
  waiting for transfers between devices: 51.7 us -> 30.1 us
  between operations: 13.9 us -> 1.09 us
  Pallas kernels: 90.8 us -> 94.3 us
  other arithmetic: 1.73 us -> 4.75 us
    all_to_all x4, waiting for transfers between devices: 41.5 us -> 0.01 us  [exchange(): lax.all_to_all(array, 'expert', split_axis=0, concat_axis=0, tiled=True)]
    ppermute x0 -> x24, waiting for transfers between devices: none -> 30.1 us  [shift(): lax.ppermute(array, 'dp', [(i, (i + step) % owners) for i in range(owners)])]
    ppermute x0 -> x24, starting transfers between devices: none -> 22.9 us  [shift(): lax.ppermute(array, 'dp', [(i, (i + step) % owners) for i in range(owners)])]
    reduce_scatter x2 -> x0, waiting for transfers between devices: 9.12 us -> none  [body(): lax.psum_scatter(gradient, 'dp', scatter_dimension=0, tiled=True)]
    all_to_all x4, starting transfers between devices: 29.7 us -> 36.9 us  [exchange(): lax.all_to_all(array, 'expert', split_axis=0, concat_axis=0, tiled=True)]
    add x1 -> x5, other arithmetic: 0.01 us -> 4.04 us  [the longest x2 2.05 us: scatter_second(): from_right_b = shift(left_b + passing_b, -1)]
    pallas_call x2, Pallas kernels: 64.4 us -> 66.5 us  [run_expert(): pl.pallas_call(functools.partial(expert_kernel, member=member), in_specs=...]
    pallas_call x4 -> x3, Pallas kernels: 14.2 us -> 15.7 us  [the longest x2 11.5 us: update(): pl.pallas_call(functools.partial(update_kernel, member=member), grid=(ste...]
  transfers between devices with their start and end apart: 8 -> 28, of which waited for: 4 -> 4; matrix products, arithmetic and copies ran while one was open for 3% -> 5% of each run, Pallas kernels for 42% -> 41%
where the time goes in v4:
time: 201 us; the launch traced here: 200 us
  Pallas kernels  94.3 us (47%)
  starting transfers between devices  59.8 us (30%)
  waiting for transfers between devices  30.1 us (15%)
  local copies, waits for them, and re-layouts  9.44 us (5%)
  other arithmetic  4.75 us (2%)
    pallas_call x2, Pallas kernels, run_expert(): pl.pallas_call(functools.partial(expert_kernel, member=member), in_specs=...  66.5 us
    all_to_all x4, starting transfers between devices, exchange(): lax.all_to_all(array, 'expert', split_axis=0, concat_axis=0, tiled=True)  36.9 us
    ppermute x24, waiting for transfers between devices, shift(): lax.ppermute(array, 'dp', [(i, (i + step) % owners) for i in range(owners)])  30.1 us
    ppermute x24, starting transfers between devices, shift(): lax.ppermute(array, 'dp', [(i, (i + step) % owners) for i in range(owners)])  22.9 us
    pallas_call x2, Pallas kernels, update(): pl.pallas_call(functools.partial(update_kernel, member=member), grid=(ste...  11.5 us
    pallas_call x1, Pallas kernels, pick(): pl.pallas_call(functools.partial(pick_kernel, locals_count=locals_count),...  6.09 us
    pallas_call x1, Pallas kernels, combine(): pl.pallas_call(functools.partial(combine_kernel, locals_count=locals_coun...  6.01 us
    unnamed x27, local copies, waits for them, and re-layouts  4.2 us
  transfers between devices with their start and end apart: 28, of which 4 were waited for; matrix products, arithmetic and copies ran while one was open for 5% of the time, Pallas kernels for 41%

profile of v4, /device:TPU:1, one launch (start us, length us, event | category | flops | bytes accessed | tf_op | source)
XLA Modules:
  0.0 199.5 jit_solution(1242857205453218345)
XLA Ops:
  0.6 1.4 copy.23
  2.0 6.1 %pick.1 = (bf16[32,16,2048]{2,1,0:T(8,128)(2,1)}, bf16[32,16,2048]{2,1,0:T(8,128)(2,1)}) custom-call(s32[64,8]{1,0:T(8,128)} %bitcast.15, bf16[256,2048]{1,0:T(8,128)(2,1)} %tokens_ref.1, bf16[256,2048]{1,0:T(8,128)(2,1)} %grads_ref.1), custom_call_target="tpu_custom_call" | custom-call | bytes 1048576 | tf_op jit(solution)/shard_map/pick/pallas_call | solution.py:348
  8.1 9.6 %all-to-all-start = ((bf16[32,16,2048]{2,1,0:T(8,128)(2,1)}), bf16[32,16,2048]{2,1,0:T(8,128)(2,1)S(1)}, u32[]{:S(2)}, u32[]{:S(2)}) async-start(bf16[32,16,2048]{2,1,0:T(8,128)(2,1)} %get-tuple-element.63), calls=%async_computation | async-start | bytes 4194304 | tf_op jit(solution)/shard_map/all_to_all | solution.py:517
  17.7 4.2 %pack.1 = (bf16[48,32,128]{2,1,0:T(8,128)(2,1)}, bf16[48,32,128]{2,1,0:T(8,128)(2,1)}, bf16[48,32,128]{2,1,0:T(8,128)(2,1)}, bf16[48,32,128]{2,1,0:T(8,128)(2,1)}) custom-call(f32[192,4096]{1,0:T(8,128)} %bitcast.10), custom_call_target="tpu_custom_call" | custom-call | bytes 1048576 | tf_op jit(solution)/shard_map/pack/pallas_call | solution.py:363
  21.9 2.5 %collective-permute-start.3 = (bf16[48,32,128]{2,1,0:T(8,128)(2,1)}, bf16[48,32,128]{2,1,0:T(8,128)(2,1)}, u32[]{:S(2)}, u32[]{:S(2)}) collective-permute-start(bf16[48,32,128]{2,1,0:T(8,128)(2,1)} %get-tuple-element.69.rest_1_), channel_id=1, source_target_pairs={{0,96},{32,0},{64,32},{96,64},{1,97},{33,1},{65,33},{97,65},{2,98}... | collective-permute-start | bytes 1179656 | tf_op jit(solution)/shard_map/ppermute | solution.py:484
  24.4 0.2 collective-permute-start
  24.6 2.5 %collective-permute-start.2 = (bf16[48,32,128]{2,1,0:T(8,128)(2,1)}, bf16[48,32,128]{2,1,0:T(8,128)(2,1)}, u32[]{:S(2)}, u32[]{:S(2)}) collective-permute-start(bf16[48,32,128]{2,1,0:T(8,128)(2,1)} %get-tuple-element.68.rest_0_), channel_id=1, source_target_pairs={{0,96},{32,0},{64,32},{96,64},{1,97},{33,1},{65,33},{97,65},{2,98}... | collective-permute-start | bytes 1179656 | tf_op jit(solution)/shard_map/ppermute | solution.py:484
  27.2 0.4 select_reduce_fusion
  27.6 0.6 sub.34.inverse_ref
  28.2 0.2 multiply_add_fusion
  28.5 0.6 reshape.137.row_ref
  29.1 0.6 reshape.138.lane_ref
  29.7 0.6 reshape.141.valid_ref
  30.3 14.2 %collective-permute-done.rest_2_ = bf16[48,32,128]{2,1,0:T(8,128)(2,1)} collective-permute-done((bf16[48,32,128]{2,1,0:T(8,128)(2,1)}, bf16[48,32,128]{2,1,0:T(8,128)(2,1)}, u32[]{:S(2)}, u32[]{:S(2)}) %collective-permute-start) | collective-permute-done | bytes 393248 | tf_op jit(solution)/shard_map/ppermute | solution.py:484
  44.5 1.5 collective-permute-start.4
  46.0 1.2 collective-permute-start.5
  47.2 1.0 reshape.143
  48.3 0.5 copy.28
  48.7 0.7 reshape.142.router_ref
  49.4 1.3 copy-done
  50.8 10.1 %all-to-all-start.1 = ((bf16[32,16,2048]{2,1,0:T(8,128)(2,1)}), bf16[32,16,2048]{2,1,0:T(8,128)(2,1)}, u32[]{:S(2)}, u32[]{:S(2)}) async-start(bf16[32,16,2048]{2,1,0:T(8,128)(2,1)} %get-tuple-element.64), calls=%async_computation.1 | async-start | bytes 4194304 | tf_op jit(solution)/shard_map/all_to_all | solution.py:517
  60.9 0.6 collective-permute-start.7
  61.5 2.1 %collective-permute-start.8 = (bf16[48,32,128]{2,1,0:T(8,128)(2,1)}, bf16[48,32,128]{2,1,0:T(8,128)(2,1)}, u32[]{:S(2)}, u32[]{:S(2)}) collective-permute-start(bf16[48,32,128]{2,1,0:T(8,128)(2,1)} %get-tuple-element.72.rest_0_), channel_id=1, source_target_pairs={{0,96},{32,0},{64,32},{96,64},{1,97},{33,1},{65,33},{97,65},{2,98}... | collective-permute-start | bytes 1179656 | tf_op jit(solution)/shard_map/ppermute | solution.py:484
  63.6 2.7 %collective-permute-start.11 = (bf16[48,32,128]{2,1,0:T(8,128)(2,1)}, bf16[48,32,128]{2,1,0:T(8,128)(2,1)}, u32[]{:S(2)}, u32[]{:S(2)}) collective-permute-start(bf16[48,32,128]{2,1,0:T(8,128)(2,1)} %collective-permute-done.9.rest_5_), channel_id=1, source_target_pairs={{0,96},{32,0},{64,32},{96,64},{1,97},{33,1},{65,33},{97,65},{2,98}... | collective-permute-start | bytes 1179656 | tf_op jit(solution)/shard_map/ppermute | solution.py:484
  66.3 33.2 %expert_0.1 = (bf16[32,16,2048]{2,1,0:T(8,128)(2,1)}, bf16[97,32,128]{2,1,0:T(8,128)(2,1)}, bf16[48,32,128]{2,1,0:T(8,128)(2,1)}, bf16[49,32,128]{2,1,0:T(8,128)...) custom-call(s32[2304]{0:T(1024)} %sub.34.inverse_ref, ...), custom_call_target="tpu_custom_call" | custom-call | flops 149999992832 | bytes 1048576 | tf_op jit(solution)/shard_map/expert_0/pallas_call | solution.py:385
  99.7 8.6 %all-to-all-start.2 = ((bf16[32,16,2048]{2,1,0:T(8,128)(2,1)}), bf16[32,16,2048]{2,1,0:T(8,128)(2,1)}, u32[]{:S(2)}, u32[]{:S(2)}) async-start(bf16[32,16,2048]{2,1,0:T(8,128)(2,1)} %get-tuple-element.82), calls=%async_computation.2 | async-start | bytes 4194304 | tf_op jit(solution)/shard_map/all_to_all | solution.py:517
  108.2 1.8 collective-permute-start.20
  110.1 2.6 %collective-permute-start.21 = (bf16[48,32,128]{2,1,0:T(8,128)(2,1)}, bf16[48,32,128]{2,1,0:T(8,128)(2,1)}, u32[]{:S(2)}, u32[]{:S(2)}) collective-permute-start(bf16[48,32,128]{2,1,0:T(8,128)(2,1)} %get-tuple-element.89), channel_id=1, source_target_pairs={{0,96},{32,0},{64,32},{96,64},{1,97},{33,1},{65,33},{97,65},{2,98}... | collective-permute-start | bytes 1179656 | tf_op jit(solution)/shard_map/ppermute | solution.py:484
  112.7 33.3 %expert_1.1 = (bf16[32,16,2048]{2,1,0:T(8,128)(2,1)}, bf16[97,32,128]{2,1,0:T(8,128)(2,1)}, bf16[48,32,128]{2,1,0:T(8,128)(2,1)}, bf16[49,32,128]{2,1,0:T(8,128)...) custom-call(s32[2304]{0:T(1024)} %sub.34.inverse_ref, ...), custom_call_target="tpu_custom_call" | custom-call | flops 149999992832 | bytes 1048576 | tf_op jit(solution)/shard_map/expert_1/pallas_call | solution.py:385
  146.1 8.6 %all-to-all-start.3 = ((bf16[32,16,2048]{2,1,0:T(8,128)(2,1)}), bf16[32,16,2048]{2,1,0:T(8,128)(2,1)S(1)}, u32[]{:S(2)}, u32[]{:S(2)}) async-start(bf16[32,16,2048]{2,1,0:T(8,128)(2,1)} %get-tuple-element.100), calls=%async_computation.3 | async-start | bytes 4194304 | tf_op jit(solution)/shard_map/all_to_all | solution.py:517
  154.8 1.2 add.122
  156.1 1.5 collective-permute-start.12
  157.5 1.1 add.121
  158.7 1.4 collective-permute-start.22
  160.2 7.9 %collective-permute-done.12 = bf16[48,32,128]{2,1,0:T(8,128)(2,1)S(1)} collective-permute-done((bf16[48,32,128]{2,1,0:T(8,128)(2,1)}, bf16[48,32,128]{2,1,0:T(8,128)(2,1)S(1)}, u32[]{:S(2)}, u32[]{:S(2)}) %collective-permute-start.12) | collective-permute-done | bytes 393248 | tf_op jit(solution)/shard_map/ppermute | solution.py:484
  168.1 0.4 collective-permute-start.14
  168.4 0.9 add.119
  169.3 1.1 collective-permute-start.13
  170.4 0.9 add.120
  171.3 5.2 %collective-permute-done.22.left_a_ref = bf16[48,32,128]{2,1,0:T(8,128)(2,1)S(1)} collective-permute-done((bf16[48,32,128]{2,1,0:T(8,128)(2,1)S(1)}, bf16[48,32,128]{2,1,0:T(8,128)(2,1)S(1)}, u32[]{:S(2)}, u32[]{:S(2)}) %collective-permute-start.22) | collective-permute-done | bytes 393248 | tf_op jit(solution)/shard_map/ppermute | solution.py:484
  176.5 0.5 collective-permute-start.17
  177.0 0.6 broadcast_in_dim.38.router_ref
  177.6 0.1 copy-done.2
  177.7 5.7 %update_0.1 = (f32[192,4096]{1,0:T(8,128)}, f32[3,2,32]{2,1,0:T(2,128)}, f32[2,512]{1,0:T(2,128)}) custom-call(bf16[97,32,128]{2,1,0:T(8,128)(2,1)} %get-tuple-element.90.own_ref.own_last_ref, bf16[48,32,128]{2,1,0:T(8,128)(2,1)} %copy-done.7, bf16[48,32,128]{2,1,0:T(8,128)(2,1)} %collective-permute-done.21.right_a_ref, ...), custom_call_target="tpu_custom_call" | custom-call | bytes 1048576 | tf_op jit(solution)/shard_map/update_0/pallas_call | solution.py:424
  183.5 1.3 copy-done.1
  184.8 6.0 %combine.1 = (bf16[256,2048]{1,0:T(8,128)(2,1)}, bf16[256,2048]{1,0:T(8,128)(2,1)}) custom-call(s32[64,8]{1,0:T(8,128)} %bitcast.16, bf16[32,16,2048]{2,1,0:T(8,128)(2,1)} %all-to-all-done.2.rest_0_, bf16[32,16,2048]{2,1,0:T(8,128)(2,1)} %copy-done.1), custom_call_target="tpu_custom_call" | custom-call | flops 149999992832 | bytes 1048576 | tf_op jit(solution)/shard_map/combine/pallas_call | solution.py:448
  190.8 2.8 %collective-permute-done.13.left_a_ref = bf16[48,32,128]{2,1,0:T(8,128)(2,1)} collective-permute-done((bf16[48,32,128]{2,1,0:T(8,128)(2,1)}, bf16[48,32,128]{2,1,0:T(8,128)(2,1)}, u32[]{:S(2)}, u32[]{:S(2)}) %collective-permute-start.13) | collective-permute-done | bytes 393248 | tf_op jit(solution)/shard_map/ppermute | solution.py:484
  193.6 5.8 %update_1.1 = (f32[192,4096]{1,0:T(8,128)}, f32[3,2,32]{2,1,0:T(2,128)}, f32[2,512]{1,0:T(2,128)}) custom-call(bf16[97,32,128]{2,1,0:T(8,128)(2,1)} %get-tuple-element.104.own_ref.own_last_ref, bf16[48,32,128]{2,1,0:T(8,128)(2,1)} %collective-permute-done.13.left_a_ref, ...), custom_call_target="tpu_custom_call", output_to_operand_aliasing={{0}: (11, {})} | custom-call | bytes 1048576 | tf_op jit(solution)/shard_map/update_1/pallas_call | solution.py:424
  (67 shorter events, 0.7 us)
Async XLA Ops:
  8.1 41.3 %all-to-all-start = ((bf16[32,16,2048]{2,1,0:T(8,128)(2,1)}), bf16[32,16,2048]{2,1,0:T(8,128)(2,1)S(1)}, u32[]{:S(2)}, u32[]{:S(2)}) async-start(bf16[32,16,2048]{2,1,0:T(8,128)(2,1)} %get-tuple-element.63), calls=%async_computation | async-start | bytes 4194304 | tf_op jit(solution)/shard_map/all_to_all | solution.py:517
  17.7 9.4 %copy-start.8 = (s32[2,3,128]{2,0,1:T(2,128)S(1)}, s32[2,3,128]{2,0,1:T(2,128)}, u32[]{:S(2)}) copy-start(s32[2,3,128]{2,0,1:T(2,128)} %param.12) | copy-start | bytes 9220
  17.7 10.5 %copy-start.10 = (s32[3]{0:T(128)S(1)}, s32[3]{0:T(128)}, u32[]{:S(2)}) copy-start(s32[3]{0:T(128)} %constant.85.clone) | copy-start | bytes 40
  17.7 29.5 %copy-start.9 = (bf16[2048,2]{0,1:T(2,128)(2,1)S(1)}, bf16[2048,2]{0,1:T(2,128)(2,1)}, u32[]{:S(2)}) copy-start(bf16[2048,2]{0,1:T(2,128)(2,1)} %param.11) | copy-start | bytes 24580
  21.9 22.6 %collective-permute-start.3 = (bf16[48,32,128]{2,1,0:T(8,128)(2,1)}, bf16[48,32,128]{2,1,0:T(8,128)(2,1)}, u32[]{:S(2)}, u32[]{:S(2)}) collective-permute-start(bf16[48,32,128]{2,1,0:T(8,128)(2,1)} %get-tuple-element.69.rest_1_), channel_id=1, source_target_pairs={{0,96},{32,0},{64,32},{96,64},{1,97},{33,1},{65,33},{97,65},{2,98}... | collective-permute-start | bytes 1179656 | tf_op jit(solution)/shard_map/ppermute | solution.py:484
  24.4 21.6 %collective-permute-start.1 = (bf16[48,32,128]{2,1,0:T(8,128)(2,1)}, bf16[48,32,128]{2,1,0:T(8,128)(2,1)S(1)}, u32[]{:S(2)}, u32[]{:S(2)}) collective-permute-start(bf16[48,32,128]{2,1,0:T(8,128)(2,1)} %get-tuple-element.69.rest_1_), channel_id=1, source_target_pairs={{0,32},{32,64},{64,96},{96,0},{1,33},{33,65},{65,97},{97,1},{2,34}... | collective-permute-start | bytes 1179656 | tf_op jit(solution)/shard_map/ppermute | solution.py:484
  24.4 20.1 %collective-permute-start = (bf16[48,32,128]{2,1,0:T(8,128)(2,1)}, bf16[48,32,128]{2,1,0:T(8,128)(2,1)}, u32[]{:S(2)}, u32[]{:S(2)}) collective-permute-start(bf16[48,32,128]{2,1,0:T(8,128)(2,1)} %get-tuple-element.68.rest_0_), channel_id=1, source_target_pairs={{0,32},{32,64},{64,96},{96,0},{1,33},{33,65},{65,97},{97,1},{2,34}... | collective-permute-start | bytes 1179656 | tf_op jit(solution)/shard_map/ppermute | solution.py:484
  24.6 36.3 %collective-permute-start.2 = (bf16[48,32,128]{2,1,0:T(8,128)(2,1)}, bf16[48,32,128]{2,1,0:T(8,128)(2,1)}, u32[]{:S(2)}, u32[]{:S(2)}) collective-permute-start(bf16[48,32,128]{2,1,0:T(8,128)(2,1)} %get-tuple-element.68.rest_0_), channel_id=1, source_target_pairs={{0,96},{32,0},{64,32},{96,64},{1,97},{33,1},{65,33},{97,65},{2,98}... | collective-permute-start | bytes 1179656 | tf_op jit(solution)/shard_map/ppermute | solution.py:484
  27.1 34.4 %collective-permute-start.6 = (bf16[48,32,128]{2,1,0:T(8,128)(2,1)}, bf16[48,32,128]{2,1,0:T(8,128)(2,1)}, u32[]{:S(2)}, u32[]{:S(2)}) collective-permute-start(bf16[48,32,128]{2,1,0:T(8,128)(2,1)} %get-tuple-element.72.rest_0_), channel_id=1, source_target_pairs={{0,32},{32,64},{64,96},{96,0},{1,33},{33,65},{65,97},{97,1},{2,34}... | collective-permute-start | bytes 1179656 | tf_op jit(solution)/shard_map/ppermute | solution.py:484
  44.5 19.1 %collective-permute-start.9 = (bf16[48,32,128]{2,1,0:T(8,128)(2,1)}, bf16[48,32,128]{2,1,0:T(8,128)(2,1)}, u32[]{:S(2)}, u32[]{:S(2)}) collective-permute-start(bf16[48,32,128]{2,1,0:T(8,128)(2,1)} %get-tuple-element.73.rest_1_), channel_id=1, source_target_pairs={{0,96},{32,0},{64,32},{96,64},{1,97},{33,1},{65,33},{97,65},{2,98}... | collective-permute-start | bytes 1179656 | tf_op jit(solution)/shard_map/ppermute | solution.py:484
  44.5 19.1 %collective-permute-start.4 = (bf16[48,32,128]{2,1,0:T(8,128)(2,1)}, bf16[48,32,128]{2,1,0:T(8,128)(2,1)}, u32[]{:S(2)}, u32[]{:S(2)}) collective-permute-start(bf16[48,32,128]{2,1,0:T(8,128)(2,1)} %collective-permute-done.rest_2_), channel_id=1, source_target_pairs={{0,32},{32,64},{64,96},{96,0},{1,33},{33,65},{65,97},{97,1},{2,34}... | collective-permute-start | bytes 1179656 | tf_op jit(solution)/shard_map/ppermute | solution.py:484
  46.0 1.2 copy-start.12
  46.0 20.3 %collective-permute-start.5 = (bf16[48,32,128]{2,1,0:T(8,128)(2,1)}, bf16[48,32,128]{2,1,0:T(8,128)(2,1)}, u32[]{:S(2)}, u32[]{:S(2)}) collective-permute-start(bf16[48,32,128]{2,1,0:T(8,128)(2,1)} %collective-permute-done.3.rest_5_), channel_id=1, source_target_pairs={{0,96},{32,0},{64,32},{96,64},{1,97},{33,1},{65,33},{97,65},{2,98}... | collective-permute-start | bytes 1179656 | tf_op jit(solution)/shard_map/ppermute | solution.py:484
  49.4 1.3 copy-start
  50.8 48.9 %all-to-all-start.1 = ((bf16[32,16,2048]{2,1,0:T(8,128)(2,1)}), bf16[32,16,2048]{2,1,0:T(8,128)(2,1)}, u32[]{:S(2)}, u32[]{:S(2)}) async-start(bf16[32,16,2048]{2,1,0:T(8,128)(2,1)} %get-tuple-element.64), calls=%async_computation.1 | async-start | bytes 4194304 | tf_op jit(solution)/shard_map/all_to_all | solution.py:517
  60.9 47.4 %collective-permute-start.7 = (bf16[48,32,128]{2,1,0:T(8,128)(2,1)}, bf16[48,32,128]{2,1,0:T(8,128)(2,1)}, u32[]{:S(2)}, u32[]{:S(2)}) collective-permute-start(bf16[48,32,128]{2,1,0:T(8,128)(2,1)} %get-tuple-element.73.rest_1_), channel_id=1, source_target_pairs={{0,32},{32,64},{64,96},{96,0},{1,33},{33,65},{65,97},{97,1},{2,34}... | collective-permute-start | bytes 1179656 | tf_op jit(solution)/shard_map/ppermute | solution.py:484
  61.5 48.5 %collective-permute-start.8 = (bf16[48,32,128]{2,1,0:T(8,128)(2,1)}, bf16[48,32,128]{2,1,0:T(8,128)(2,1)}, u32[]{:S(2)}, u32[]{:S(2)}) collective-permute-start(bf16[48,32,128]{2,1,0:T(8,128)(2,1)} %get-tuple-element.72.rest_0_), channel_id=1, source_target_pairs={{0,96},{32,0},{64,32},{96,64},{1,97},{33,1},{65,33},{97,65},{2,98}... | collective-permute-start | bytes 1179656 | tf_op jit(solution)/shard_map/ppermute | solution.py:484
  63.6 46.5 %collective-permute-start.10 = (bf16[48,32,128]{2,1,0:T(8,128)(2,1)}, bf16[48,32,128]{2,1,0:T(8,128)(2,1)}, u32[]{:S(2)}, u32[]{:S(2)}) collective-permute-start(bf16[48,32,128]{2,1,0:T(8,128)(2,1)} %collective-permute-done.6.rest_2_), channel_id=1, source_target_pairs={{0,32},{32,64},{64,96},{96,0},{1,33},{33,65},{65,97},{97,1},{2,34}... | collective-permute-start | bytes 1179656 | tf_op jit(solution)/shard_map/ppermute | solution.py:484
  63.6 49.1 %collective-permute-start.11 = (bf16[48,32,128]{2,1,0:T(8,128)(2,1)}, bf16[48,32,128]{2,1,0:T(8,128)(2,1)}, u32[]{:S(2)}, u32[]{:S(2)}) collective-permute-start(bf16[48,32,128]{2,1,0:T(8,128)(2,1)} %collective-permute-done.9.rest_5_), channel_id=1, source_target_pairs={{0,96},{32,0},{64,32},{96,64},{1,97},{33,1},{65,33},{97,65},{2,98}... | collective-permute-start | bytes 1179656 | tf_op jit(solution)/shard_map/ppermute | solution.py:484
  99.6 46.5 %collective-permute-start.19 = (bf16[49,32,128]{2,1,0:T(8,128)(2,1)}, bf16[49,32,128]{2,1,0:T(8,128)(2,1)}, u32[]{:S(2)}, u32[]{:S(2)}) collective-permute-start(bf16[49,32,128]{2,1,0:T(8,128)(2,1)} %get-tuple-element.87), channel_id=1, source_target_pairs={{0,96},{32,0},{64,32},{96,64},{1,97},{33,1},{65,33},{97,65},{2,98}... | collective-permute-start | bytes 1204232 | tf_op jit(solution)/shard_map/ppermute | solution.py:484
  99.7 46.4 %all-to-all-start.2 = ((bf16[32,16,2048]{2,1,0:T(8,128)(2,1)}), bf16[32,16,2048]{2,1,0:T(8,128)(2,1)}, u32[]{:S(2)}, u32[]{:S(2)}) async-start(bf16[32,16,2048]{2,1,0:T(8,128)(2,1)} %get-tuple-element.82), calls=%async_computation.2 | async-start | bytes 4194304 | tf_op jit(solution)/shard_map/all_to_all | solution.py:517
  108.2 37.8 %collective-permute-start.20 = (bf16[49,32,128]{2,1,0:T(8,128)(2,1)}, bf16[49,32,128]{2,1,0:T(8,128)(2,1)}, u32[]{:S(2)}, u32[]{:S(2)}) collective-permute-start(bf16[49,32,128]{2,1,0:T(8,128)(2,1)} %get-tuple-element.88), channel_id=1, source_target_pairs={{0,32},{32,64},{64,96},{96,0},{1,33},{33,65},{65,97},{97,1},{2,34}... | collective-permute-start | bytes 1204232 | tf_op jit(solution)/shard_map/ppermute | solution.py:484
  110.0 36.0 %collective-permute-start.18 = (bf16[48,32,128]{2,1,0:T(8,128)(2,1)}, bf16[48,32,128]{2,1,0:T(8,128)(2,1)}, u32[]{:S(2)}, u32[]{:S(2)}) collective-permute-start(bf16[48,32,128]{2,1,0:T(8,128)(2,1)} %get-tuple-element.86), channel_id=1, source_target_pairs={{0,32},{32,64},{64,96},{96,0},{1,33},{33,65},{65,97},{97,1},{2,34}... | collective-permute-start | bytes 1179656 | tf_op jit(solution)/shard_map/ppermute | solution.py:484
  110.1 35.9 %collective-permute-start.21 = (bf16[48,32,128]{2,1,0:T(8,128)(2,1)}, bf16[48,32,128]{2,1,0:T(8,128)(2,1)}, u32[]{:S(2)}, u32[]{:S(2)}) collective-permute-start(bf16[48,32,128]{2,1,0:T(8,128)(2,1)} %get-tuple-element.89), channel_id=1, source_target_pairs={{0,96},{32,0},{64,32},{96,64},{1,97},{33,1},{65,33},{97,65},{2,98}... | collective-permute-start | bytes 1179656 | tf_op jit(solution)/shard_map/ppermute | solution.py:484
  146.1 8.7 %copy-start.11 = (bf16[49,32,128]{2,1,0:T(8,128)(2,1)S(1)}, bf16[49,32,128]{2,1,0:T(8,128)(2,1)}, u32[]{:S(2)}) copy-start(bf16[49,32,128]{2,1,0:T(8,128)(2,1)} %get-tuple-element.80) | copy-start | bytes 1204228
  146.1 8.7 %copy-start.3 = (bf16[49,32,128]{2,1,0:T(8,128)(2,1)S(1)}, bf16[49,32,128]{2,1,0:T(8,128)(2,1)}, u32[]{:S(2)}) copy-start(bf16[49,32,128]{2,1,0:T(8,128)(2,1)} %get-tuple-element.95) | copy-start | bytes 1204228
  146.1 11.4 %copy-start.5 = (bf16[48,32,128]{2,1,0:T(8,128)(2,1)S(1)}, bf16[48,32,128]{2,1,0:T(8,128)(2,1)}, u32[]{:S(2)}) copy-start(bf16[48,32,128]{2,1,0:T(8,128)(2,1)} %get-tuple-element.91) | copy-start | bytes 1179652
  146.1 37.4 %all-to-all-start.3 = ((bf16[32,16,2048]{2,1,0:T(8,128)(2,1)}), bf16[32,16,2048]{2,1,0:T(8,128)(2,1)S(1)}, u32[]{:S(2)}, u32[]{:S(2)}) async-start(bf16[32,16,2048]{2,1,0:T(8,128)(2,1)} %get-tuple-element.100), calls=%async_computation.3 | async-start | bytes 4194304 | tf_op jit(solution)/shard_map/all_to_all | solution.py:517
  154.7 13.7 %copy-start.6 = (bf16[48,32,128]{2,1,0:T(8,128)(2,1)S(1)}, bf16[48,32,128]{2,1,0:T(8,128)(2,1)}, u32[]{:S(2)}) copy-start(bf16[48,32,128]{2,1,0:T(8,128)(2,1)} %get-tuple-element.75) | copy-start | bytes 1179652
  154.7 15.7 %copy-start.4 = (bf16[49,32,128]{2,1,0:T(8,128)(2,1)S(1)}, bf16[49,32,128]{2,1,0:T(8,128)(2,1)}, u32[]{:S(2)}) copy-start(bf16[49,32,128]{2,1,0:T(8,128)(2,1)} %get-tuple-element.79) | copy-start | bytes 1204228
  154.7 14.6 %collective-permute-start.16 = (bf16[49,32,128]{2,1,0:T(8,128)(2,1)S(1)}, bf16[49,32,128]{2,1,0:T(8,128)(2,1)S(1)}, u32[]{:S(2)}, u32[]{:S(2)}) collective-permute-start(bf16[49,32,128]{2,1,0:T(8,128)(2,1)S(1)} %copy-done.11), channel_id=1, source_target_pairs={{0,96},{32,0},{64,32},{96,64},{1,97},{33,1},{65,33},{97,65},{2,98}... | collective-permute-start | bytes 1204232 | tf_op jit(solution)/shard_map/ppermute | solution.py:484
  156.0 21.0 %collective-permute-start.23 = (bf16[49,32,128]{2,1,0:T(8,128)(2,1)S(1)}, bf16[49,32,128]{2,1,0:T(8,128)(2,1)S(1)}, u32[]{:S(2)}, u32[]{:S(2)}) collective-permute-start(bf16[49,32,128]{2,1,0:T(8,128)(2,1)S(1)} %add.122), channel_id=1, source_target_pairs={{0,96},{32,0},{64,32},{96,64},{1,97},{33,1},{65,33},{97,65},{2,98}... | collective-permute-start | bytes 1204232 | tf_op jit(solution)/shard_map/ppermute | solution.py:484
  156.1 12.0 %collective-permute-start.12 = (bf16[48,32,128]{2,1,0:T(8,128)(2,1)}, bf16[48,32,128]{2,1,0:T(8,128)(2,1)S(1)}, u32[]{:S(2)}, u32[]{:S(2)}) collective-permute-start(bf16[48,32,128]{2,1,0:T(8,128)(2,1)} %get-tuple-element.76), channel_id=1, source_target_pairs={{0,32},{32,64},{64,96},{96,0},{1,33},{33,65},{65,97},{97,1},{2,34}... | collective-permute-start | bytes 1179656 | tf_op jit(solution)/shard_map/ppermute | solution.py:484
  158.7 17.8 %collective-permute-start.22 = (bf16[48,32,128]{2,1,0:T(8,128)(2,1)S(1)}, bf16[48,32,128]{2,1,0:T(8,128)(2,1)S(1)}, u32[]{:S(2)}, u32[]{:S(2)}) collective-permute-start(bf16[48,32,128]{2,1,0:T(8,128)(2,1)S(1)} %add.121), channel_id=1, source_target_pairs={{0,32},{32,64},{64,96},{96,0},{1,33},{33,65},{65,97},{97,1},{2,34}... | collective-permute-start | bytes 1179656 | tf_op jit(solution)/shard_map/ppermute | solution.py:484
  160.1 30.7 %collective-permute-start.15 = (bf16[49,32,128]{2,1,0:T(8,128)(2,1)}, bf16[49,32,128]{2,1,0:T(8,128)(2,1)}, u32[]{:S(2)}, u32[]{:S(2)}) collective-permute-start(bf16[49,32,128]{2,1,0:T(8,128)(2,1)} %get-tuple-element.78), channel_id=1, source_target_pairs={{0,32},{32,64},{64,96},{96,0},{1,33},{33,65},{65,97},{97,1},{2,34}... | collective-permute-start | bytes 1204232 | tf_op jit(solution)/shard_map/ppermute | solution.py:484
  168.1 22.8 %collective-permute-start.14 = (bf16[48,32,128]{2,1,0:T(8,128)(2,1)}, bf16[48,32,128]{2,1,0:T(8,128)(2,1)}, u32[]{:S(2)}, u32[]{:S(2)}) collective-permute-start(bf16[48,32,128]{2,1,0:T(8,128)(2,1)} %get-tuple-element.77), channel_id=1, source_target_pairs={{0,96},{32,0},{64,32},{96,64},{1,97},{33,1},{65,33},{97,65},{2,98}... | collective-permute-start | bytes 1179656 | tf_op jit(solution)/shard_map/ppermute | solution.py:484
  169.3 24.3 %collective-permute-start.13 = (bf16[48,32,128]{2,1,0:T(8,128)(2,1)}, bf16[48,32,128]{2,1,0:T(8,128)(2,1)}, u32[]{:S(2)}, u32[]{:S(2)}) collective-permute-start(bf16[48,32,128]{2,1,0:T(8,128)(2,1)} %add.119), channel_id=1, source_target_pairs={{0,32},{32,64},{64,96},{96,0},{1,33},{33,65},{65,97},{97,1},{2,34}... | collective-permute-start | bytes 1179656 | tf_op jit(solution)/shard_map/ppermute | solution.py:484
  176.5 1.1 copy-start.7
  176.5 17.1 %collective-permute-start.17 = (bf16[49,32,128]{2,1,0:T(8,128)(2,1)}, bf16[49,32,128]{2,1,0:T(8,128)(2,1)}, u32[]{:S(2)}, u32[]{:S(2)}) collective-permute-start(bf16[49,32,128]{2,1,0:T(8,128)(2,1)} %add.120), channel_id=1, source_target_pairs={{0,96},{32,0},{64,32},{96,64},{1,97},{33,1},{65,33},{97,65},{2,98}... | collective-permute-start | bytes 1204232 | tf_op jit(solution)/shard_map/ppermute | solution.py:484
  177.0 0.8 copy-start.2
  183.5 1.3 copy-start.1

commit v5 on v4

--- a/solution.py
+++ b/solution.py
@@ -16,7 +16,8 @@
 LEARN_RATE = 0.005
 SCORE_RATE = 0.05
 CHUNK = 256
-STEP = 512
+STEP = 1024
+UNROLL = 32
 F32 = jnp.float32
 BF16 = jnp.bfloat16
 NN = (((1,), (0,)), ((), ()))
@@ -43,11 +44,11 @@
 
 
 def pick_columns(picks_ref, member, locals_count):
-    experts = picks_ref.shape[0]
+    experts = picks_ref.shape[1]
     rows = 8 * experts // locals_count
     expert = (iota((rows, experts), 0) >> 3) * locals_count + member
     spread = one_hot(iota((rows, experts), 1) == expert)
-    wide = dot(spread, picks_ref[...].astype(F32).astype(BF16))
+    wide = dot(spread, picks_ref[...].astype(F32).astype(BF16), NT)
     keep = iota(wide.shape, 1) == (iota(wide.shape, 0) & 7)
     return jnp.sum(jnp.where(keep, wide, 0.0), axis=1, keepdims=True).astype(jnp.int32)
 
@@ -103,7 +104,7 @@
 
 
 def expert_kernel(
-    inverse_ref, row_ref, lane_ref, valid_ref, me_ref,
+    inverse_ref, row_ref, lane_ref, me_ref,
     arrived_ref, router_ref, *rest,
     member,
 ):
@@ -120,21 +121,36 @@
     ]
     for load in loads:
         load.start()
-    for load in loads:
-        load.wait()
+    copies_ref[3 * MAXB] = jnp.zeros((32, 128), BF16)
+    grad_wide_ref[D:, :] = jnp.zeros((BS, 2 * FF), BF16)
+    grad_down_ref[FF:, :] = jnp.zeros((BS, D), BF16)
     base, slot_base = member * 3 * BLOCKS, member * 3 * MAXB
     lane = iota((32, 128), 1)
     half = lane < 64
 
+    count = rows_ref.shape[0]
+    chunks = D // CHUNK
+    mine = slice(member, member + 1)
+
+    def take(n, logit):
+        cols = pl.ds(pl.multiple_of(n * CHUNK, CHUNK), CHUNK)
+        rows, grads = apart(arrived_ref[:, :, cols])
+        rows_ref[:, cols] = rows.astype(BF16)
+        grads_ref[:, cols] = grads.astype(BF16)
+        return logit + jnp.sum(rows * router_ref[mine, cols], axis=1, keepdims=True)
+
+    logit = lax.fori_loop(0, chunks, take, jnp.zeros((count, 1), F32))
+    gating = 1.0 / (1.0 + jnp.exp(-logit))
+
+    for load in loads:
+        load.wait()
+
     def place(target_ref, matrix, block, row, col):
-        first = inverse_ref[base + matrix * BLOCKS + block]
-        second = inverse_ref[base + matrix * BLOCKS + block + 1]
-        one = copies_ref[jnp.maximum(first, 0)]
-        two = copies_ref[jnp.maximum(second, 0)]
-        one = jnp.where(lane < jnp.where(first >= 0, 128, 0), one, jnp.zeros_like(one))
-        two = jnp.where(lane < jnp.where(second >= 0, 128, 0), two, jnp.zeros_like(two))
-        target_ref[pl.ds(row, 32), col : col + 128] = jnp.where(half, one, pltpu.roll(two, 64, 1))
-        target_ref[pl.ds(row + 32, 32), col : col + 128] = jnp.where(half, pltpu.roll(one, 64, 1), two)
+        one = copies_ref[inverse_ref[base + matrix * BLOCKS + block]]
+        two = copies_ref[inverse_ref[base + matrix * BLOCKS + block + 1]]
+        crossed = pltpu.roll(jnp.where(half, two, one), 64, 1)
+        target_ref[pl.ds(row, 32), col : col + 128] = jnp.where(half, one, crossed)
+        target_ref[pl.ds(row + 32, 32), col : col + 128] = jnp.where(half, crossed, two)
 
     @pl.loop(0, D // BS)
     def _(r):
@@ -148,20 +164,6 @@
         row = pl.multiple_of(r * BS, BS)
         for pair in range(D // BS // 2):
             place(down_ref, 2, r * (D // BS) + 2 * pair, row, 128 * pair)
-
-    count = rows_ref.shape[0]
-    chunks = D // CHUNK
-    mine = slice(member, member + 1)
-
-    def take(n, logit):
-        cols = pl.ds(pl.multiple_of(n * CHUNK, CHUNK), CHUNK)
-        rows, grads = apart(arrived_ref[:, :, cols])
-        rows_ref[:, cols] = rows.astype(BF16)
-        grads_ref[:, cols] = grads.astype(BF16)
-        return logit + jnp.sum(rows * router_ref[mine, cols], axis=1, keepdims=True)
-
-    logit = lax.fori_loop(0, chunks, take, jnp.zeros((count, 1), F32))
-    gating = 1.0 / (1.0 + jnp.exp(-logit))
 
     @pl.loop(0, 2 * FF // 512)
     def _(n):
@@ -215,12 +217,9 @@
         row = pl.multiple_of(row_ref[at], 32)
         other = pl.multiple_of(row ^ 32, 32)
         cols = pl.ds(pl.multiple_of(lane_ref[at], 128), 128)
-        odd = row & 32
         stay = source_ref[pl.ds(row, 32), cols]
         move = pltpu.roll(source_ref[pl.ds(other, 32), cols], 64, 1)
-        tile = jnp.where((lane & 64) == 2 * odd, stay, move)
-        limit = jnp.where(valid_ref[at] > 0, 128, 0)
-        packed_ref[place_in] = jnp.where(lane < limit, tile, jnp.zeros_like(tile))
+        packed_ref[place_in] = jnp.where((lane & 64) == 2 * (row & 32), stay, move)
 
     per = MAXB // OWNERS
     part = packed_ref.shape[0] // OWNERS
@@ -232,10 +231,10 @@
         for matrix in range(3):
             source_ref = grad_down_ref if matrix == 2 else grad_wide_ref
 
-            @pl.loop(0, per // 4)
+            @pl.loop(0, per // UNROLL)
             def _(group, first=first, matrix=matrix, source_ref=source_ref, owner=owner):
-                for step in range(4):
-                    s = group * 4 + step
+                for step in range(UNROLL):
+                    s = group * UNROLL + step
                     cut(source_ref, matrix, owner * per + s, first + matrix * per + s)
 
         start = owner * (D // OWNERS)
@@ -384,12 +383,12 @@
     lengths = [part] + [half, part - half] * 3
     return pl.pallas_call(
         functools.partial(expert_kernel, member=member),
-        in_specs=[scalar] * 5 + [whole] * 2 + [anywhere] * len(pieces),
+        in_specs=[scalar] * 4 + [whole] * 2 + [anywhere] * len(pieces),
         out_specs=[whole] + [anywhere] * len(lengths),
         out_shape=[jax.ShapeDtypeStruct((peers, 16, D), BF16)]
         + [jax.ShapeDtypeStruct((length, 32, 128), BF16) for length in lengths],
         scratch_shapes=[
-            pltpu.VMEM((3 * MAXB, 32, 128), BF16),
+            pltpu.VMEM((3 * MAXB + 1, 32, 128), BF16),
             pltpu.VMEM((OWNERS * part, 32, 128), BF16),
             pltpu.SemaphoreType.DMA((len(pieces),)),
             pltpu.SemaphoreType.DMA((len(lengths),)),
@@ -400,8 +399,8 @@
             pltpu.VMEM((count, 2 * FF), F32),
             pltpu.VMEM((count, D), BF16),
             pltpu.VMEM((count, 2 * FF), BF16),
-            pltpu.VMEM((D, 2 * FF), BF16),
-            pltpu.VMEM((FF, D), BF16),
+            pltpu.VMEM((D + BS, 2 * FF), BF16),
+            pltpu.VMEM((FF + BS, D), BF16),
             pltpu.VMEM((1, D), F32),
         ],
         compiler_params=params(56),
@@ -413,7 +412,7 @@
 def update(member, summed, masters, scores, router_sum, held):
     own, left_a, right_a, left_b, right_b = summed
     mine = own.shape[0] - 1
-    steps = 6
+    steps = 2
     rows = mine // steps
     tile = lambda index: pl.BlockSpec((rows, 32, 128), index)
     early = tile(lambda n: (jnp.minimum(n, steps // 2 - 1), 0, 0))
@@ -468,15 +467,16 @@
     order = jnp.where(ahead == 0, 0, jnp.where(ahead == owners - 1, 1, ahead + 1))
     place = order * (3 * per) + slots % per + matrix * per
     hits = kept[:, :, None, :] == numbers[None, None, :, None]
-    inverse = jnp.sum(jnp.where(hits, place[:, :, None, :] + 1, 0), axis=-1) - 1
+    inverse = 3 * MAXB + jnp.sum(jnp.where(hits, place[:, :, None, :] - 3 * MAXB, 0), axis=-1)
     valid = kept < BLOCKS
     block = jnp.where(valid, kept, 0)
     width = jnp.array([FF // BS, FF // BS, D // BS], jnp.int32)[None, :, None]
     block_row, block_col = block // width, block % width
-    rows = block_row * BS + 32 * (block_col & 1)
+    empty = jnp.where(matrix == 2, FF, D)
+    rows = jnp.where(valid, block_row * BS + 32 * (block_col & 1), empty)
     lanes = (block_col >> 1) * 128 + jnp.where(matrix == 1, FF, 0)
     flat = lambda table: table.reshape(-1).astype(jnp.int32)
-    return flat(inverse), flat(rows), flat(lanes), flat(valid)
+    return flat(inverse), flat(rows), flat(lanes)
 
 
 def shift(array, step):
@@ -509,7 +509,7 @@
     me = lax.axis_index("dp").astype(jnp.int32)
     count, width = tokens.shape
     per = masters.shape[2]
-    picks = token_picks[0]
+    picks = token_picks[0].T
     flat_masters = masters.reshape(locals_count * 3 * per, BS * BS)
     after = lax.optimization_barrier
 

time: 201 us -> 179 us (0.89)
  Pallas kernels: 94.3 us -> 71.8 us
  waiting for transfers between devices: 30.1 us -> 33.5 us
    pallas_call x2, Pallas kernels: 66.5 us -> 49.3 us  [run_expert(): pl.pallas_call(functools.partial(expert_kernel, member=member), in_specs=...]
    pallas_call x2, Pallas kernels: 11.5 us -> 7.28 us  [update(): pl.pallas_call(functools.partial(update_kernel, member=member), grid=(ste...]
    unnamed x27 -> x26, local copies, waits for them, and re-layouts: 4.2 us -> 2.84 us
  transfers between devices with their start and end apart: 28 -> 28, of which waited for: 4 -> 5; matrix products, arithmetic and copies ran while one was open for 5% -> 5% of each run, Pallas kernels for 41% -> 35%
where the time goes in v5:
time: 179 us; the launch traced here: 178 us
  Pallas kernels  71.8 us (40%)
  starting transfers between devices  59.6 us (33%)
  waiting for transfers between devices  33.5 us (19%)
  local copies, waits for them, and re-layouts  7.48 us (4%)
  other arithmetic  4.75 us (3%)
    pallas_call x2, Pallas kernels, run_expert(): pl.pallas_call(functools.partial(expert_kernel, member=member), in_specs=...  49.3 us
    all_to_all x4, starting transfers between devices, exchange(): lax.all_to_all(array, 'expert', split_axis=0, concat_axis=0, tiled=True)  36.6 us
    ppermute x24, waiting for transfers between devices, shift(): lax.ppermute(array, 'dp', [(i, (i + step) % owners) for i in range(owners)])  31.8 us
    ppermute x24, starting transfers between devices, shift(): lax.ppermute(array, 'dp', [(i, (i + step) % owners) for i in range(owners)])  23 us
    pallas_call x2, Pallas kernels, update(): pl.pallas_call(functools.partial(update_kernel, member=member), grid=(ste...  7.28 us
    pallas_call x1, Pallas kernels, pick(): pl.pallas_call(functools.partial(pick_kernel, locals_count=locals_count),...  5.69 us
    pallas_call x1, Pallas kernels, combine(): pl.pallas_call(functools.partial(combine_kernel, locals_count=locals_coun...  5.33 us
    pallas_call x1, Pallas kernels, pack(): pl.pallas_call(pack_kernel, grid=(parts,), in_specs=[pl.BlockSpec((mine,...  4.18 us
  transfers between devices with their start and end apart: 28, of which 5 were waited for; matrix products, arithmetic and copies ran while one was open for 5% of the time, Pallas kernels for 35%

profile of v5, /device:TPU:1, one launch (start us, length us, event | category | flops | bytes accessed | tf_op | source)
XLA Modules:
  0.0 178.2 jit_solution(11308033310021796035)
XLA Ops:
  0.6 5.7 %pick.1 = (bf16[32,16,2048]{2,1,0:T(8,128)(2,1)}, bf16[32,16,2048]{2,1,0:T(8,128)(2,1)}) custom-call(s32[8,64]{1,0:T(8,128)} %bitcast.17, bf16[256,2048]{1,0:T(8,128)(2,1)} %tokens_ref.1, bf16[256,2048]{1,0:T(8,128)(2,1)} %grads_ref.1), custom_call_target="tpu_custom_call" | custom-call | bytes 1048576 | tf_op jit(solution)/shard_map/pick/pallas_call | solution.py:347
  6.3 9.6 %all-to-all-start = ((bf16[32,16,2048]{2,1,0:T(8,128)(2,1)}), bf16[32,16,2048]{2,1,0:T(8,128)(2,1)S(1)}, u32[]{:S(2)}, u32[]{:S(2)}) async-start(bf16[32,16,2048]{2,1,0:T(8,128)(2,1)} %get-tuple-element.63), calls=%async_computation | async-start | bytes 4194304 | tf_op jit(solution)/shard_map/all_to_all | solution.py:517
  16.0 4.2 %pack.1 = (bf16[48,32,128]{2,1,0:T(8,128)(2,1)}, bf16[48,32,128]{2,1,0:T(8,128)(2,1)}, bf16[48,32,128]{2,1,0:T(8,128)(2,1)}, bf16[48,32,128]{2,1,0:T(8,128)(2,1)}) custom-call(f32[192,4096]{1,0:T(8,128)} %bitcast.12), custom_call_target="tpu_custom_call" | custom-call | bytes 1048576 | tf_op jit(solution)/shard_map/pack/pallas_call | solution.py:362
  20.1 2.5 %collective-permute-start.3 = (bf16[48,32,128]{2,1,0:T(8,128)(2,1)}, bf16[48,32,128]{2,1,0:T(8,128)(2,1)}, u32[]{:S(2)}, u32[]{:S(2)}) collective-permute-start(bf16[48,32,128]{2,1,0:T(8,128)(2,1)} %get-tuple-element.69.rest_1_), channel_id=1, source_target_pairs={{0,96},{32,0},{64,32},{96,64},{1,97},{33,1},{65,33},{97,65},{2,98}... | collective-permute-start | bytes 1179656 | tf_op jit(solution)/shard_map/ppermute | solution.py:484
  22.6 0.2 collective-permute-start
  22.8 2.5 %collective-permute-start.2 = (bf16[48,32,128]{2,1,0:T(8,128)(2,1)}, bf16[48,32,128]{2,1,0:T(8,128)(2,1)}, u32[]{:S(2)}, u32[]{:S(2)}) collective-permute-start(bf16[48,32,128]{2,1,0:T(8,128)(2,1)} %get-tuple-element.68.rest_0_), channel_id=1, source_target_pairs={{0,96},{32,0},{64,32},{96,64},{1,97},{33,1},{65,33},{97,65},{2,98}... | collective-permute-start | bytes 1179656 | tf_op jit(solution)/shard_map/ppermute | solution.py:484
  25.4 0.2 multiply_add_fusion
  25.7 0.6 reshape.141.row_ref
  26.3 0.6 reshape.142.lane_ref
  26.9 0.4 select_reduce_fusion
  27.3 0.6 add.117.inverse_ref
  27.9 14.8 %collective-permute-done.rest_2_ = bf16[48,32,128]{2,1,0:T(8,128)(2,1)} collective-permute-done((bf16[48,32,128]{2,1,0:T(8,128)(2,1)}, bf16[48,32,128]{2,1,0:T(8,128)(2,1)}, u32[]{:S(2)}, u32[]{:S(2)}) %collective-permute-start) | collective-permute-done | bytes 393248 | tf_op jit(solution)/shard_map/ppermute | solution.py:484
  42.7 1.5 collective-permute-start.4
  44.2 1.2 collective-permute-start.5
  45.5 1.0 reshape.146
  46.5 0.5 copy.23
  46.9 0.7 reshape.145.router_ref
  47.7 1.3 copy-done
  49.0 10.1 %all-to-all-start.1 = ((bf16[32,16,2048]{2,1,0:T(8,128)(2,1)}), bf16[32,16,2048]{2,1,0:T(8,128)(2,1)}, u32[]{:S(2)}, u32[]{:S(2)}) async-start(bf16[32,16,2048]{2,1,0:T(8,128)(2,1)} %get-tuple-element.64), calls=%async_computation.1 | async-start | bytes 4194304 | tf_op jit(solution)/shard_map/all_to_all | solution.py:517
  59.1 0.6 collective-permute-start.7
  59.7 2.1 %collective-permute-start.8 = (bf16[48,32,128]{2,1,0:T(8,128)(2,1)}, bf16[48,32,128]{2,1,0:T(8,128)(2,1)}, u32[]{:S(2)}, u32[]{:S(2)}) collective-permute-start(bf16[48,32,128]{2,1,0:T(8,128)(2,1)} %get-tuple-element.72.rest_0_), channel_id=1, source_target_pairs={{0,96},{32,0},{64,32},{96,64},{1,97},{33,1},{65,33},{97,65},{2,98}... | collective-permute-start | bytes 1179656 | tf_op jit(solution)/shard_map/ppermute | solution.py:484
  61.9 2.7 %collective-permute-start.11 = (bf16[48,32,128]{2,1,0:T(8,128)(2,1)}, bf16[48,32,128]{2,1,0:T(8,128)(2,1)}, u32[]{:S(2)}, u32[]{:S(2)}) collective-permute-start(bf16[48,32,128]{2,1,0:T(8,128)(2,1)} %collective-permute-done.9.rest_5_), channel_id=1, source_target_pairs={{0,96},{32,0},{64,32},{96,64},{1,97},{33,1},{65,33},{97,65},{2,98}... | collective-permute-start | bytes 1179656 | tf_op jit(solution)/shard_map/ppermute | solution.py:484
  64.6 24.6 %expert_0.1 = (bf16[32,16,2048]{2,1,0:T(8,128)(2,1)}, bf16[97,32,128]{2,1,0:T(8,128)(2,1)}, bf16[48,32,128]{2,1,0:T(8,128)(2,1)}, bf16[49,32,128]{2,1,0:T(8,128)...) custom-call(s32[2304]{0:T(1024)} %add.117.inverse_ref, ...), custom_call_target="tpu_custom_call" | custom-call | flops 149999992832 | bytes 1048576 | tf_op jit(solution)/shard_map/expert_0/pallas_call | solution.py:384
  89.3 8.6 %all-to-all-start.2 = ((bf16[32,16,2048]{2,1,0:T(8,128)(2,1)}), bf16[32,16,2048]{2,1,0:T(8,128)(2,1)}, u32[]{:S(2)}, u32[]{:S(2)}) async-start(bf16[32,16,2048]{2,1,0:T(8,128)(2,1)} %get-tuple-element.82), calls=%async_computation.2 | async-start | bytes 4194304 | tf_op jit(solution)/shard_map/all_to_all | solution.py:517
  97.9 1.8 %collective-permute-start.20 = (bf16[49,32,128]{2,1,0:T(8,128)(2,1)}, bf16[49,32,128]{2,1,0:T(8,128)(2,1)}, u32[]{:S(2)}, u32[]{:S(2)}) collective-permute-start(bf16[49,32,128]{2,1,0:T(8,128)(2,1)} %get-tuple-element.88), channel_id=1, source_target_pairs={{0,32},{32,64},{64,96},{96,0},{1,33},{33,65},{65,97},{97,1},{2,34}... | collective-permute-start | bytes 1204232 | tf_op jit(solution)/shard_map/ppermute | solution.py:484
  99.6 0.1 collective-permute-start.18
  99.7 2.6 %collective-permute-start.21 = (bf16[48,32,128]{2,1,0:T(8,128)(2,1)}, bf16[48,32,128]{2,1,0:T(8,128)(2,1)}, u32[]{:S(2)}, u32[]{:S(2)}) collective-permute-start(bf16[48,32,128]{2,1,0:T(8,128)(2,1)} %get-tuple-element.89), channel_id=1, source_target_pairs={{0,96},{32,0},{64,32},{96,64},{1,97},{33,1},{65,33},{97,65},{2,98}... | collective-permute-start | bytes 1179656 | tf_op jit(solution)/shard_map/ppermute | solution.py:484
  102.3 24.7 %expert_1.1 = (bf16[32,16,2048]{2,1,0:T(8,128)(2,1)}, bf16[97,32,128]{2,1,0:T(8,128)(2,1)}, bf16[48,32,128]{2,1,0:T(8,128)(2,1)}, bf16[49,32,128]{2,1,0:T(8,128)...) custom-call(s32[2304]{0:T(1024)} %add.117.inverse_ref, ...), custom_call_target="tpu_custom_call" | custom-call | flops 149999992832 | bytes 1048576 | tf_op jit(solution)/shard_map/expert_1/pallas_call | solution.py:384
  127.1 8.4 %all-to-all-start.3 = ((bf16[32,16,2048]{2,1,0:T(8,128)(2,1)}), bf16[32,16,2048]{2,1,0:T(8,128)(2,1)S(1)}, u32[]{:S(2)}, u32[]{:S(2)}) async-start(bf16[32,16,2048]{2,1,0:T(8,128)(2,1)} %get-tuple-element.100), calls=%async_computation.3 | async-start | bytes 4194304 | tf_op jit(solution)/shard_map/all_to_all | solution.py:517
  135.6 1.2 add.125
  136.9 1.5 collective-permute-start.12
  138.3 1.1 add.124
  139.4 1.4 collective-permute-start.22
  141.0 7.8 %collective-permute-done.12 = bf16[48,32,128]{2,1,0:T(8,128)(2,1)S(1)} collective-permute-done((bf16[48,32,128]{2,1,0:T(8,128)(2,1)}, bf16[48,32,128]{2,1,0:T(8,128)(2,1)S(1)}, u32[]{:S(2)}, u32[]{:S(2)}) %collective-permute-start.12) | collective-permute-done | bytes 393248 | tf_op jit(solution)/shard_map/ppermute | solution.py:484
  148.8 0.4 collective-permute-start.14
  149.2 0.9 add.122
  150.1 1.1 collective-permute-start.13
  151.2 0.9 add.123
  152.0 5.2 %collective-permute-done.22.left_a_ref = bf16[48,32,128]{2,1,0:T(8,128)(2,1)S(1)} collective-permute-done((bf16[48,32,128]{2,1,0:T(8,128)(2,1)S(1)}, bf16[48,32,128]{2,1,0:T(8,128)(2,1)S(1)}, u32[]{:S(2)}, u32[]{:S(2)}) %collective-permute-start.22) | collective-permute-done | bytes 393248 | tf_op jit(solution)/shard_map/ppermute | solution.py:484
  157.2 0.5 collective-permute-start.17
  157.8 0.6 broadcast_in_dim.52.router_ref
  158.4 0.1 copy-done.2
  158.5 3.6 %update_0.1 = (f32[192,4096]{1,0:T(8,128)}, f32[3,2,32]{2,1,0:T(2,128)}, f32[2,512]{1,0:T(2,128)}) custom-call(bf16[97,32,128]{2,1,0:T(8,128)(2,1)} %get-tuple-element.90.own_ref.own_last_ref, bf16[48,32,128]{2,1,0:T(8,128)(2,1)} %copy-done.7, bf16[48,32,128]{2,1,0:T(8,128)(2,1)} %collective-permute-done.21.right_a_ref, ...), custom_call_target="tpu_custom_call" | custom-call | bytes 1048576 | tf_op jit(solution)/shard_map/update_0/pallas_call | solution.py:423
  162.1 1.6 all-to-all-done.3.rest_1_
  163.8 1.3 copy-done.1
  165.1 5.3 %combine.1 = (bf16[256,2048]{1,0:T(8,128)(2,1)}, bf16[256,2048]{1,0:T(8,128)(2,1)}) custom-call(s32[8,64]{1,0:T(8,128)} %bitcast.18, bf16[32,16,2048]{2,1,0:T(8,128)(2,1)} %all-to-all-done.2.rest_0_, bf16[32,16,2048]{2,1,0:T(8,128)(2,1)} %copy-done.1), custom_call_target="tpu_custom_call" | custom-call | flops 149999992832 | bytes 1048576 | tf_op jit(solution)/shard_map/combine/pallas_call | solution.py:447
  170.5 3.9 %collective-permute-done.13.left_a_ref = bf16[48,32,128]{2,1,0:T(8,128)(2,1)} collective-permute-done((bf16[48,32,128]{2,1,0:T(8,128)(2,1)}, bf16[48,32,128]{2,1,0:T(8,128)(2,1)}, u32[]{:S(2)}, u32[]{:S(2)}) %collective-permute-start.13) | collective-permute-done | bytes 393248 | tf_op jit(solution)/shard_map/ppermute | solution.py:484
  174.4 3.6 %update_1.1 = (f32[192,4096]{1,0:T(8,128)}, f32[3,2,32]{2,1,0:T(2,128)}, f32[2,512]{1,0:T(2,128)}) custom-call(bf16[97,32,128]{2,1,0:T(8,128)(2,1)} %get-tuple-element.104.own_ref.own_last_ref, bf16[48,32,128]{2,1,0:T(8,128)(2,1)} %collective-permute-done.13.left_a_ref, ...), custom_call_target="tpu_custom_call", output_to_operand_aliasing={{0}: (11, {})} | custom-call | bytes 1048576 | tf_op jit(solution)/shard_map/update_1/pallas_call | solution.py:423
  (63 shorter events, 0.6 us)
Async XLA Ops:
  6.3 41.3 %all-to-all-start = ((bf16[32,16,2048]{2,1,0:T(8,128)(2,1)}), bf16[32,16,2048]{2,1,0:T(8,128)(2,1)S(1)}, u32[]{:S(2)}, u32[]{:S(2)}) async-start(bf16[32,16,2048]{2,1,0:T(8,128)(2,1)} %get-tuple-element.63), calls=%async_computation | async-start | bytes 4194304 | tf_op jit(solution)/shard_map/all_to_all | solution.py:517
  15.9 9.4 %copy-start.8 = (s32[2,3,128]{2,0,1:T(2,128)S(1)}, s32[2,3,128]{2,0,1:T(2,128)}, u32[]{:S(2)}) copy-start(s32[2,3,128]{2,0,1:T(2,128)} %param.12) | copy-start | bytes 9220
  15.9 9.4 %copy-start.10 = (s32[3]{0:T(128)S(1)}, s32[3]{0:T(128)}, u32[]{:S(2)}) copy-start(s32[3]{0:T(128)} %constant.90.clone) | copy-start | bytes 40
  16.0 29.5 %copy-start.9 = (bf16[2048,2]{0,1:T(2,128)(2,1)S(1)}, bf16[2048,2]{0,1:T(2,128)(2,1)}, u32[]{:S(2)}) copy-start(bf16[2048,2]{0,1:T(2,128)(2,1)} %param.11) | copy-start | bytes 24580
  20.1 22.6 %collective-permute-start.3 = (bf16[48,32,128]{2,1,0:T(8,128)(2,1)}, bf16[48,32,128]{2,1,0:T(8,128)(2,1)}, u32[]{:S(2)}, u32[]{:S(2)}) collective-permute-start(bf16[48,32,128]{2,1,0:T(8,128)(2,1)} %get-tuple-element.69.rest_1_), channel_id=1, source_target_pairs={{0,96},{32,0},{64,32},{96,64},{1,97},{33,1},{65,33},{97,65},{2,98}... | collective-permute-start | bytes 1179656 | tf_op jit(solution)/shard_map/ppermute | solution.py:484
  22.6 21.6 %collective-permute-start.1 = (bf16[48,32,128]{2,1,0:T(8,128)(2,1)}, bf16[48,32,128]{2,1,0:T(8,128)(2,1)S(1)}, u32[]{:S(2)}, u32[]{:S(2)}) collective-permute-start(bf16[48,32,128]{2,1,0:T(8,128)(2,1)} %get-tuple-element.69.rest_1_), channel_id=1, source_target_pairs={{0,32},{32,64},{64,96},{96,0},{1,33},{33,65},{65,97},{97,1},{2,34}... | collective-permute-start | bytes 1179656 | tf_op jit(solution)/shard_map/ppermute | solution.py:484
  22.6 20.1 %collective-permute-start = (bf16[48,32,128]{2,1,0:T(8,128)(2,1)}, bf16[48,32,128]{2,1,0:T(8,128)(2,1)}, u32[]{:S(2)}, u32[]{:S(2)}) collective-permute-start(bf16[48,32,128]{2,1,0:T(8,128)(2,1)} %get-tuple-element.68.rest_0_), channel_id=1, source_target_pairs={{0,32},{32,64},{64,96},{96,0},{1,33},{33,65},{65,97},{97,1},{2,34}... | collective-permute-start | bytes 1179656 | tf_op jit(solution)/shard_map/ppermute | solution.py:484
  22.8 36.3 %collective-permute-start.2 = (bf16[48,32,128]{2,1,0:T(8,128)(2,1)}, bf16[48,32,128]{2,1,0:T(8,128)(2,1)}, u32[]{:S(2)}, u32[]{:S(2)}) collective-permute-start(bf16[48,32,128]{2,1,0:T(8,128)(2,1)} %get-tuple-element.68.rest_0_), channel_id=1, source_target_pairs={{0,96},{32,0},{64,32},{96,64},{1,97},{33,1},{65,33},{97,65},{2,98}... | collective-permute-start | bytes 1179656 | tf_op jit(solution)/shard_map/ppermute | solution.py:484
  25.3 34.4 %collective-permute-start.6 = (bf16[48,32,128]{2,1,0:T(8,128)(2,1)}, bf16[48,32,128]{2,1,0:T(8,128)(2,1)}, u32[]{:S(2)}, u32[]{:S(2)}) collective-permute-start(bf16[48,32,128]{2,1,0:T(8,128)(2,1)} %get-tuple-element.72.rest_0_), channel_id=1, source_target_pairs={{0,32},{32,64},{64,96},{96,0},{1,33},{33,65},{65,97},{97,1},{2,34}... | collective-permute-start | bytes 1179656 | tf_op jit(solution)/shard_map/ppermute | solution.py:484
  42.7 19.1 %collective-permute-start.9 = (bf16[48,32,128]{2,1,0:T(8,128)(2,1)}, bf16[48,32,128]{2,1,0:T(8,128)(2,1)}, u32[]{:S(2)}, u32[]{:S(2)}) collective-permute-start(bf16[48,32,128]{2,1,0:T(8,128)(2,1)} %get-tuple-element.73.rest_1_), channel_id=1, source_target_pairs={{0,96},{32,0},{64,32},{96,64},{1,97},{33,1},{65,33},{97,65},{2,98}... | collective-permute-start | bytes 1179656 | tf_op jit(solution)/shard_map/ppermute | solution.py:484
  42.7 19.1 %collective-permute-start.4 = (bf16[48,32,128]{2,1,0:T(8,128)(2,1)}, bf16[48,32,128]{2,1,0:T(8,128)(2,1)}, u32[]{:S(2)}, u32[]{:S(2)}) collective-permute-start(bf16[48,32,128]{2,1,0:T(8,128)(2,1)} %collective-permute-done.rest_2_), channel_id=1, source_target_pairs={{0,32},{32,64},{64,96},{96,0},{1,33},{33,65},{65,97},{97,1},{2,34}... | collective-permute-start | bytes 1179656 | tf_op jit(solution)/shard_map/ppermute | solution.py:484
  44.2 1.2 copy-start.12
  44.2 20.3 %collective-permute-start.5 = (bf16[48,32,128]{2,1,0:T(8,128)(2,1)}, bf16[48,32,128]{2,1,0:T(8,128)(2,1)}, u32[]{:S(2)}, u32[]{:S(2)}) collective-permute-start(bf16[48,32,128]{2,1,0:T(8,128)(2,1)} %collective-permute-done.3.rest_5_), channel_id=1, source_target_pairs={{0,96},{32,0},{64,32},{96,64},{1,97},{33,1},{65,33},{97,65},{2,98}... | collective-permute-start | bytes 1179656 | tf_op jit(solution)/shard_map/ppermute | solution.py:484
  47.7 1.3 copy-start
  49.0 40.3 %all-to-all-start.1 = ((bf16[32,16,2048]{2,1,0:T(8,128)(2,1)}), bf16[32,16,2048]{2,1,0:T(8,128)(2,1)}, u32[]{:S(2)}, u32[]{:S(2)}) async-start(bf16[32,16,2048]{2,1,0:T(8,128)(2,1)} %get-tuple-element.64), calls=%async_computation.1 | async-start | bytes 4194304 | tf_op jit(solution)/shard_map/all_to_all | solution.py:517
  59.1 38.7 %collective-permute-start.7 = (bf16[48,32,128]{2,1,0:T(8,128)(2,1)}, bf16[48,32,128]{2,1,0:T(8,128)(2,1)}, u32[]{:S(2)}, u32[]{:S(2)}) collective-permute-start(bf16[48,32,128]{2,1,0:T(8,128)(2,1)} %get-tuple-element.73.rest_1_), channel_id=1, source_target_pairs={{0,32},{32,64},{64,96},{96,0},{1,33},{33,65},{65,97},{97,1},{2,34}... | collective-permute-start | bytes 1179656 | tf_op jit(solution)/shard_map/ppermute | solution.py:484
  59.7 39.9 %collective-permute-start.8 = (bf16[48,32,128]{2,1,0:T(8,128)(2,1)}, bf16[48,32,128]{2,1,0:T(8,128)(2,1)}, u32[]{:S(2)}, u32[]{:S(2)}) collective-permute-start(bf16[48,32,128]{2,1,0:T(8,128)(2,1)} %get-tuple-element.72.rest_0_), channel_id=1, source_target_pairs={{0,96},{32,0},{64,32},{96,64},{1,97},{33,1},{65,33},{97,65},{2,98}... | collective-permute-start | bytes 1179656 | tf_op jit(solution)/shard_map/ppermute | solution.py:484
  61.9 37.9 %collective-permute-start.10 = (bf16[48,32,128]{2,1,0:T(8,128)(2,1)}, bf16[48,32,128]{2,1,0:T(8,128)(2,1)}, u32[]{:S(2)}, u32[]{:S(2)}) collective-permute-start(bf16[48,32,128]{2,1,0:T(8,128)(2,1)} %collective-permute-done.6.rest_2_), channel_id=1, source_target_pairs={{0,32},{32,64},{64,96},{96,0},{1,33},{33,65},{65,97},{97,1},{2,34}... | collective-permute-start | bytes 1179656 | tf_op jit(solution)/shard_map/ppermute | solution.py:484
  61.9 40.5 %collective-permute-start.11 = (bf16[48,32,128]{2,1,0:T(8,128)(2,1)}, bf16[48,32,128]{2,1,0:T(8,128)(2,1)}, u32[]{:S(2)}, u32[]{:S(2)}) collective-permute-start(bf16[48,32,128]{2,1,0:T(8,128)(2,1)} %collective-permute-done.9.rest_5_), channel_id=1, source_target_pairs={{0,96},{32,0},{64,32},{96,64},{1,97},{33,1},{65,33},{97,65},{2,98}... | collective-permute-start | bytes 1179656 | tf_op jit(solution)/shard_map/ppermute | solution.py:484
  89.2 37.9 %collective-permute-start.19 = (bf16[49,32,128]{2,1,0:T(8,128)(2,1)}, bf16[49,32,128]{2,1,0:T(8,128)(2,1)}, u32[]{:S(2)}, u32[]{:S(2)}) collective-permute-start(bf16[49,32,128]{2,1,0:T(8,128)(2,1)} %get-tuple-element.87), channel_id=1, source_target_pairs={{0,96},{32,0},{64,32},{96,64},{1,97},{33,1},{65,33},{97,65},{2,98}... | collective-permute-start | bytes 1204232 | tf_op jit(solution)/shard_map/ppermute | solution.py:484
  89.3 37.8 %all-to-all-start.2 = ((bf16[32,16,2048]{2,1,0:T(8,128)(2,1)}), bf16[32,16,2048]{2,1,0:T(8,128)(2,1)}, u32[]{:S(2)}, u32[]{:S(2)}) async-start(bf16[32,16,2048]{2,1,0:T(8,128)(2,1)} %get-tuple-element.82), calls=%async_computation.2 | async-start | bytes 4194304 | tf_op jit(solution)/shard_map/all_to_all | solution.py:517
  97.9 29.2 %collective-permute-start.20 = (bf16[49,32,128]{2,1,0:T(8,128)(2,1)}, bf16[49,32,128]{2,1,0:T(8,128)(2,1)}, u32[]{:S(2)}, u32[]{:S(2)}) collective-permute-start(bf16[49,32,128]{2,1,0:T(8,128)(2,1)} %get-tuple-element.88), channel_id=1, source_target_pairs={{0,32},{32,64},{64,96},{96,0},{1,33},{33,65},{65,97},{97,1},{2,34}... | collective-permute-start | bytes 1204232 | tf_op jit(solution)/shard_map/ppermute | solution.py:484
  99.6 27.4 %collective-permute-start.18 = (bf16[48,32,128]{2,1,0:T(8,128)(2,1)}, bf16[48,32,128]{2,1,0:T(8,128)(2,1)}, u32[]{:S(2)}, u32[]{:S(2)}) collective-permute-start(bf16[48,32,128]{2,1,0:T(8,128)(2,1)} %get-tuple-element.86), channel_id=1, source_target_pairs={{0,32},{32,64},{64,96},{96,0},{1,33},{33,65},{65,97},{97,1},{2,34}... | collective-permute-start | bytes 1179656 | tf_op jit(solution)/shard_map/ppermute | solution.py:484
  99.7 27.3 %collective-permute-start.21 = (bf16[48,32,128]{2,1,0:T(8,128)(2,1)}, bf16[48,32,128]{2,1,0:T(8,128)(2,1)}, u32[]{:S(2)}, u32[]{:S(2)}) collective-permute-start(bf16[48,32,128]{2,1,0:T(8,128)(2,1)} %get-tuple-element.89), channel_id=1, source_target_pairs={{0,96},{32,0},{64,32},{96,64},{1,97},{33,1},{65,33},{97,65},{2,98}... | collective-permute-start | bytes 1179656 | tf_op jit(solution)/shard_map/ppermute | solution.py:484
  127.1 8.4 %copy-start.11 = (bf16[49,32,128]{2,1,0:T(8,128)(2,1)S(1)}, bf16[49,32,128]{2,1,0:T(8,128)(2,1)}, u32[]{:S(2)}) copy-start(bf16[49,32,128]{2,1,0:T(8,128)(2,1)} %get-tuple-element.80) | copy-start | bytes 1204228
  127.1 8.5 %copy-start.3 = (bf16[49,32,128]{2,1,0:T(8,128)(2,1)S(1)}, bf16[49,32,128]{2,1,0:T(8,128)(2,1)}, u32[]{:S(2)}) copy-start(bf16[49,32,128]{2,1,0:T(8,128)(2,1)} %get-tuple-element.95) | copy-start | bytes 1204228
  127.1 11.2 %copy-start.5 = (bf16[48,32,128]{2,1,0:T(8,128)(2,1)S(1)}, bf16[48,32,128]{2,1,0:T(8,128)(2,1)}, u32[]{:S(2)}) copy-start(bf16[48,32,128]{2,1,0:T(8,128)(2,1)} %get-tuple-element.91) | copy-start | bytes 1179652
  127.1 36.7 %all-to-all-start.3 = ((bf16[32,16,2048]{2,1,0:T(8,128)(2,1)}), bf16[32,16,2048]{2,1,0:T(8,128)(2,1)S(1)}, u32[]{:S(2)}, u32[]{:S(2)}) async-start(bf16[32,16,2048]{2,1,0:T(8,128)(2,1)} %get-tuple-element.100), calls=%async_computation.3 | async-start | bytes 4194304 | tf_op jit(solution)/shard_map/all_to_all | solution.py:517
  135.5 13.7 %copy-start.6 = (bf16[48,32,128]{2,1,0:T(8,128)(2,1)S(1)}, bf16[48,32,128]{2,1,0:T(8,128)(2,1)}, u32[]{:S(2)}) copy-start(bf16[48,32,128]{2,1,0:T(8,128)(2,1)} %get-tuple-element.75) | copy-start | bytes 1179652
  135.5 15.7 %copy-start.4 = (bf16[49,32,128]{2,1,0:T(8,128)(2,1)S(1)}, bf16[49,32,128]{2,1,0:T(8,128)(2,1)}, u32[]{:S(2)}) copy-start(bf16[49,32,128]{2,1,0:T(8,128)(2,1)} %get-tuple-element.79) | copy-start | bytes 1204228
  135.5 14.6 %collective-permute-start.16 = (bf16[49,32,128]{2,1,0:T(8,128)(2,1)S(1)}, bf16[49,32,128]{2,1,0:T(8,128)(2,1)S(1)}, u32[]{:S(2)}, u32[]{:S(2)}) collective-permute-start(bf16[49,32,128]{2,1,0:T(8,128)(2,1)S(1)} %copy-done.11), channel_id=1, source_target_pairs={{0,96},{32,0},{64,32},{96,64},{1,97},{33,1},{65,33},{97,65},{2,98}... | collective-permute-start | bytes 1204232 | tf_op jit(solution)/shard_map/ppermute | solution.py:484
  136.8 21.0 %collective-permute-start.23 = (bf16[49,32,128]{2,1,0:T(8,128)(2,1)S(1)}, bf16[49,32,128]{2,1,0:T(8,128)(2,1)S(1)}, u32[]{:S(2)}, u32[]{:S(2)}) collective-permute-start(bf16[49,32,128]{2,1,0:T(8,128)(2,1)S(1)} %add.125), channel_id=1, source_target_pairs={{0,96},{32,0},{64,32},{96,64},{1,97},{33,1},{65,33},{97,65},{2,98}... | collective-permute-start | bytes 1204232 | tf_op jit(solution)/shard_map/ppermute | solution.py:484
  136.9 11.9 %collective-permute-start.12 = (bf16[48,32,128]{2,1,0:T(8,128)(2,1)}, bf16[48,32,128]{2,1,0:T(8,128)(2,1)S(1)}, u32[]{:S(2)}, u32[]{:S(2)}) collective-permute-start(bf16[48,32,128]{2,1,0:T(8,128)(2,1)} %get-tuple-element.76), channel_id=1, source_target_pairs={{0,32},{32,64},{64,96},{96,0},{1,33},{33,65},{65,97},{97,1},{2,34}... | collective-permute-start | bytes 1179656 | tf_op jit(solution)/shard_map/ppermute | solution.py:484
  139.4 17.8 %collective-permute-start.22 = (bf16[48,32,128]{2,1,0:T(8,128)(2,1)S(1)}, bf16[48,32,128]{2,1,0:T(8,128)(2,1)S(1)}, u32[]{:S(2)}, u32[]{:S(2)}) collective-permute-start(bf16[48,32,128]{2,1,0:T(8,128)(2,1)S(1)} %add.124), channel_id=1, source_target_pairs={{0,32},{32,64},{64,96},{96,0},{1,33},{33,65},{65,97},{97,1},{2,34}... | collective-permute-start | bytes 1179656 | tf_op jit(solution)/shard_map/ppermute | solution.py:484
  140.9 29.6 %collective-permute-start.15 = (bf16[49,32,128]{2,1,0:T(8,128)(2,1)}, bf16[49,32,128]{2,1,0:T(8,128)(2,1)}, u32[]{:S(2)}, u32[]{:S(2)}) collective-permute-start(bf16[49,32,128]{2,1,0:T(8,128)(2,1)} %get-tuple-element.78), channel_id=1, source_target_pairs={{0,32},{32,64},{64,96},{96,0},{1,33},{33,65},{65,97},{97,1},{2,34}... | collective-permute-start | bytes 1204232 | tf_op jit(solution)/shard_map/ppermute | solution.py:484
  148.8 21.7 %collective-permute-start.14 = (bf16[48,32,128]{2,1,0:T(8,128)(2,1)}, bf16[48,32,128]{2,1,0:T(8,128)(2,1)}, u32[]{:S(2)}, u32[]{:S(2)}) collective-permute-start(bf16[48,32,128]{2,1,0:T(8,128)(2,1)} %get-tuple-element.77), channel_id=1, source_target_pairs={{0,96},{32,0},{64,32},{96,64},{1,97},{33,1},{65,33},{97,65},{2,98}... | collective-permute-start | bytes 1179656 | tf_op jit(solution)/shard_map/ppermute | solution.py:484
  150.1 24.3 %collective-permute-start.13 = (bf16[48,32,128]{2,1,0:T(8,128)(2,1)}, bf16[48,32,128]{2,1,0:T(8,128)(2,1)}, u32[]{:S(2)}, u32[]{:S(2)}) collective-permute-start(bf16[48,32,128]{2,1,0:T(8,128)(2,1)} %add.122), channel_id=1, source_target_pairs={{0,32},{32,64},{64,96},{96,0},{1,33},{33,65},{65,97},{97,1},{2,34}... | collective-permute-start | bytes 1179656 | tf_op jit(solution)/shard_map/ppermute | solution.py:484
  157.2 1.1 copy-start.7
  157.2 17.1 %collective-permute-start.17 = (bf16[49,32,128]{2,1,0:T(8,128)(2,1)}, bf16[49,32,128]{2,1,0:T(8,128)(2,1)}, u32[]{:S(2)}, u32[]{:S(2)}) collective-permute-start(bf16[49,32,128]{2,1,0:T(8,128)(2,1)} %add.123), channel_id=1, source_target_pairs={{0,96},{32,0},{64,32},{96,64},{1,97},{33,1},{65,33},{97,65},{2,98}... | collective-permute-start | bytes 1204232 | tf_op jit(solution)/shard_map/ppermute | solution.py:484
  157.8 0.8 copy-start.2
  163.8 1.3 copy-start.1

commit v6 on v5

--- a/solution.py
+++ b/solution.py
@@ -357,18 +357,18 @@
     )(picks, tokens, grads)
 
 
-def pack(masters, parts):
-    mine = masters.shape[0] // parts
+def pack(masters, member, experts):
+    mine = masters.shape[0] // experts // 2
     return pl.pallas_call(
         pack_kernel,
-        grid=(parts,),
-        in_specs=[pl.BlockSpec((mine, BS * BS), lambda n: (n, 0))],
-        out_specs=[pl.BlockSpec((mine, 32, 128), lambda n: (0, 0, 0))] * parts,
-        out_shape=[jax.ShapeDtypeStruct((mine, 32, 128), BF16)] * parts,
+        grid=(2,),
+        in_specs=[pl.BlockSpec((mine, BS * BS), lambda n: (2 * member + n, 0))],
+        out_specs=[pl.BlockSpec((mine, 32, 128), lambda n: (0, 0, 0))] * 2,
+        out_shape=[jax.ShapeDtypeStruct((mine, 32, 128), BF16)] * 2,
         scratch_shapes=[pltpu.VMEM((mine // 8, 256, 128), F32)],
         compiler_params=params(56),
         cost_estimate=cost(0, 1 << 20),
-        name="pack",
+        name="pack_%d" % member,
     )(masters)
 
 
@@ -452,7 +452,7 @@
         out_specs=[column, column],
         out_shape=[jax.ShapeDtypeStruct((count, width), BF16)] * 2,
         scratch_shapes=[pltpu.VMEM((count, locals_count * 8 * peers), BF16)],
-        compiler_params=params(56),
+        compiler_params=params(24),
         cost_estimate=cost(150 * 10**9, 1 << 20),
         name="combine",
     )(picks, *back)
@@ -484,10 +484,13 @@
     return lax.ppermute(array, "dp", [(i, (i + step) % owners) for i in range(owners)])
 
 
-def gather_pieces(first, second):
+def gather_first(first, second):
     left_a, right_b = shift(first, 1), shift(second, -1)
-    left_b, right_a = shift(second, 1), shift(first, -1)
-    return [first, second, left_a, left_b, right_a, right_b, shift(left_a, 1), shift(right_b, -1)]
+    return [first, second, left_a, shift(second, 1), shift(first, -1), right_b]
+
+
+def gather_second(pieces):
+    return list(pieces) + [shift(pieces[2], 1), shift(pieces[5], -1)]
 
 
 def scatter_first(own, right_a, right_b, far_a, far_b, left_a, left_b):
@@ -518,24 +521,28 @@
 
     sent = list(pick(picks, tokens, out_grad, locals_count, peers))
     sent[0], rest_masters, kept_blocks, router = after((sent[0], flat_masters, kept_blocks, router))
-    halves = pack(rest_masters, 2 * locals_count)
+    halves = [pack(rest_masters, member, locals_count) for member in range(locals_count)]
     tables = slot_tables(kept_blocks, owners, me)
     router_rows = router.T.reshape(locals_count, width // BS, 32, 2).transpose(0, 1, 3, 2)
     router_rows = router_rows.reshape(locals_count, width).astype(F32)
     place = me.reshape(1)
 
-    pieces, arrived = [], []
-    for member in range(locals_count):
-        pieces.append(gather_pieces(halves[2 * member], halves[2 * member + 1]))
-        rows = sent[member]
-        if member:
-            rows, arrived[-1] = after((rows, arrived[-1]))
+    pieces = [gather_first(*halves[0])]
+    through, tables, router_rows, halves[1:] = after(((pieces[0][2], pieces[0][5]), tables, router_rows, halves[1:]))
+    pieces[0][2], pieces[0][5] = through
+    pieces[0] = gather_second(pieces[0])
+    arrived = [exchange(sent[0])]
+    for member in range(1, locals_count):
+        pieces.append(gather_first(*halves[member]))
+        rows, arrived[-1] = after((sent[member], arrived[-1]))
         arrived.append(exchange(rows))
     summed, back = [], []
     for member in range(locals_count):
         rows = arrived[member]
         if member:
-            rows, send = after((rows, send))
+            rows, send, through = after((rows, send, (pieces[member][2], pieces[member][5])))
+            pieces[member][2], pieces[member][5] = through
+            pieces[member] = gather_second(pieces[member])
             back.append(exchange(send))
         send, *gradients = run_expert(member, tables, place, pieces[member], rows, router_rows)
         summed.append(scatter_first(*gradients))

time: 179 us -> 178 us (level)
  waiting for transfers between devices: 33.5 us -> 31.2 us
    ppermute x24, waiting for transfers between devices: 31.8 us -> 29 us  [shift(): lax.ppermute(array, 'dp', [(i, (i + step) % owners) for i in range(owners)])]
    pallas_call x1 -> x2, Pallas kernels: 4.18 us -> 4.92 us  [pack(): pl.pallas_call(pack_kernel, grid=(2,), in_specs=[pl.BlockSpec((mine, BS *...]
  transfers between devices with their start and end apart: 28 -> 28, of which waited for: 5 -> 6; matrix products, arithmetic and copies ran while one was open for 5% -> 5% of each run, Pallas kernels for 35% -> 36%
where the time goes in v6:
time: 178 us; the launch traced here: 177 us
  Pallas kernels  72.2 us (41%)
  starting transfers between devices  60 us (34%)
  waiting for transfers between devices  31.2 us (18%)
  local copies, waits for them, and re-layouts  7.69 us (4%)
  other arithmetic  4.69 us (3%)
    pallas_call x2, Pallas kernels, run_expert(): pl.pallas_call(functools.partial(expert_kernel, member=member), in_specs=...  49.3 us
    all_to_all x4, starting transfers between devices, exchange(): lax.all_to_all(array, 'expert', split_axis=0, concat_axis=0, tiled=True)  35.4 us
    ppermute x24, waiting for transfers between devices, shift(): lax.ppermute(array, 'dp', [(i, (i + step) % owners) for i in range(owners)])  29 us
    ppermute x24, starting transfers between devices, shift(): lax.ppermute(array, 'dp', [(i, (i + step) % owners) for i in range(owners)])  24.7 us
    pallas_call x2, Pallas kernels, update(): pl.pallas_call(functools.partial(update_kernel, member=member), grid=(ste...  7.28 us
    pallas_call x1, Pallas kernels, pick(): pl.pallas_call(functools.partial(pick_kernel, locals_count=locals_count),...  5.69 us
    pallas_call x1, Pallas kernels, combine(): pl.pallas_call(functools.partial(combine_kernel, locals_count=locals_coun...  5 us
    pallas_call x2, Pallas kernels, pack(): pl.pallas_call(pack_kernel, grid=(2,), in_specs=[pl.BlockSpec((mine, BS *...  4.92 us
  transfers between devices with their start and end apart: 28, of which 6 were waited for; matrix products, arithmetic and copies ran while one was open for 5% of the time, Pallas kernels for 36%

profile of v6, /device:TPU:1, one launch (start us, length us, event | category | flops | bytes accessed | tf_op | source)
XLA Modules:
  0.0 176.9 jit_solution(15669958985315982241)
XLA Ops:
  0.6 5.7 %pick.1 = (bf16[32,16,2048]{2,1,0:T(8,128)(2,1)}, bf16[32,16,2048]{2,1,0:T(8,128)(2,1)}) custom-call(s32[8,64]{1,0:T(8,128)} %bitcast.12, bf16[256,2048]{1,0:T(8,128)(2,1)} %tokens_ref.1, bf16[256,2048]{1,0:T(8,128)(2,1)} %grads_ref.1), custom_call_target="tpu_custom_call" | custom-call | bytes 1048576 | tf_op jit(solution)/shard_map/pick/pallas_call | solution.py:347
  6.3 9.6 %all-to-all-start = ((bf16[32,16,2048]{2,1,0:T(8,128)(2,1)}), bf16[32,16,2048]{2,1,0:T(8,128)(2,1)S(1)}, u32[]{:S(2)}, u32[]{:S(2)}) async-start(bf16[32,16,2048]{2,1,0:T(8,128)(2,1)} %get-tuple-element.82), calls=%async_computation | async-start | bytes 4194304 | tf_op jit(solution)/shard_map/all_to_all | solution.py:520
  15.9 2.5 %pack_0.1 = (bf16[48,32,128]{2,1,0:T(8,128)(2,1)}, bf16[48,32,128]{2,1,0:T(8,128)(2,1)}) custom-call(f32[192,4096]{1,0:T(8,128)} %bitcast.14), custom_call_target="tpu_custom_call" | custom-call | bytes 1048576 | tf_op jit(solution)/shard_map/pack_0/pallas_call | solution.py:362
  18.4 2.5 %collective-permute-start.1 = (bf16[48,32,128]{2,1,0:T(8,128)(2,1)}, bf16[48,32,128]{2,1,0:T(8,128)(2,1)}, u32[]{:S(2)}, u32[]{:S(2)}) collective-permute-start(bf16[48,32,128]{2,1,0:T(8,128)(2,1)} %get-tuple-element.73.rest_1_), channel_id=1, source_target_pairs={{0,96},{32,0},{64,32},{96,64},{1,97},{33,1},{65,33},{97,65},{2,98}... | collective-permute-start | bytes 1179656 | tf_op jit(solution)/shard_map/ppermute | solution.py:484
  21.2 2.5 %collective-permute-start.3 = (bf16[48,32,128]{2,1,0:T(8,128)(2,1)}, bf16[48,32,128]{2,1,0:T(8,128)(2,1)}, u32[]{:S(2)}, u32[]{:S(2)}) collective-permute-start(bf16[48,32,128]{2,1,0:T(8,128)(2,1)} %get-tuple-element.72.rest_0_), channel_id=1, source_target_pairs={{0,96},{32,0},{64,32},{96,64},{1,97},{33,1},{65,33},{97,65},{2,98}... | collective-permute-start | bytes 1179656 | tf_op jit(solution)/shard_map/ppermute | solution.py:484
  23.7 2.4 %pack_1.1 = (bf16[48,32,128]{2,1,0:T(8,128)(2,1)}, bf16[48,32,128]{2,1,0:T(8,128)(2,1)}) custom-call(f32[192,4096]{1,0:T(8,128)} %bitcast.15), custom_call_target="tpu_custom_call" | custom-call | bytes 1048576 | tf_op jit(solution)/shard_map/pack_1/pallas_call | solution.py:362
  26.1 0.2 multiply_add_fusion
  26.4 0.6 reshape.141.row_ref
  27.0 0.6 reshape.142.lane_ref
  27.7 0.4 select_reduce_fusion
  28.1 0.6 add.117.inverse_ref
  28.7 1.0 reshape.146
  29.7 0.5 copy.23
  30.2 0.7 reshape.145.router_ref
  30.9 10.2 %collective-permute-done.rest_2_ = bf16[48,32,128]{2,1,0:T(8,128)(2,1)} collective-permute-done((bf16[48,32,128]{2,1,0:T(8,128)(2,1)}, bf16[48,32,128]{2,1,0:T(8,128)(2,1)}, u32[]{:S(2)}, u32[]{:S(2)}) %collective-permute-start) | collective-permute-done | bytes 393248 | tf_op jit(solution)/shard_map/ppermute | solution.py:484
  41.1 2.7 %collective-permute-start.5 = (bf16[48,32,128]{2,1,0:T(8,128)(2,1)}, bf16[48,32,128]{2,1,0:T(8,128)(2,1)S(1)}, u32[]{:S(2)}, u32[]{:S(2)}) collective-permute-start(bf16[48,32,128]{2,1,0:T(8,128)(2,1)} %collective-permute-done.1.rest_5_), channel_id=1, source_target_pairs={{0,96},{32,0},{64,32},{96,64},{1,97},{33,1},{65,33},{97,65},{2,98}... | collective-permute-start | bytes 1179656 | tf_op jit(solution)/shard_map/ppermute | solution.py:484
  43.8 0.4 all-to-all-done.arrived_ref
  44.2 1.3 copy-done.1
  45.5 8.6 %all-to-all-start.1 = ((bf16[32,16,2048]{2,1,0:T(8,128)(2,1)}), bf16[32,16,2048]{2,1,0:T(8,128)(2,1)}, u32[]{:S(2)}, u32[]{:S(2)}) async-start(bf16[32,16,2048]{2,1,0:T(8,128)(2,1)} %get-tuple-element.83), calls=%async_computation.1 | async-start | bytes 4194304 | tf_op jit(solution)/shard_map/all_to_all | solution.py:520
  54.1 1.8 %collective-permute-start.8 = (bf16[48,32,128]{2,1,0:T(8,128)(2,1)}, bf16[48,32,128]{2,1,0:T(8,128)(2,1)}, u32[]{:S(2)}, u32[]{:S(2)}) collective-permute-start(bf16[48,32,128]{2,1,0:T(8,128)(2,1)} %get-tuple-element.90.rest_1_), channel_id=1, source_target_pairs={{0,32},{32,64},{64,96},{96,0},{1,33},{33,65},{65,97},{97,1},{2,34}... | collective-permute-start | bytes 1179656 | tf_op jit(solution)/shard_map/ppermute | solution.py:484
  56.0 2.6 %collective-permute-start.9 = (bf16[48,32,128]{2,1,0:T(8,128)(2,1)}, bf16[48,32,128]{2,1,0:T(8,128)(2,1)}, u32[]{:S(2)}, u32[]{:S(2)}) collective-permute-start(bf16[48,32,128]{2,1,0:T(8,128)(2,1)} %get-tuple-element.89.rest_0_), channel_id=1, source_target_pairs={{0,96},{32,0},{64,32},{96,64},{1,97},{33,1},{65,33},{97,65},{2,98}... | collective-permute-start | bytes 1179656 | tf_op jit(solution)/shard_map/ppermute | solution.py:484
  58.6 0.8 copy-done.14
  59.4 24.6 %expert_0.1 = (bf16[32,16,2048]{2,1,0:T(8,128)(2,1)}, bf16[97,32,128]{2,1,0:T(8,128)(2,1)}, bf16[48,32,128]{2,1,0:T(8,128)(2,1)}, bf16[49,32,128]{2,1,0:T(8,128)...) custom-call(s32[2304]{0:T(1024)} %add.117.inverse_ref, ...), custom_call_target="tpu_custom_call" | custom-call | flops 149999992832 | bytes 1048576 | tf_op jit(solution)/shard_map/expert_0/pallas_call | solution.py:384
  84.2 2.6 %collective-permute-start.11 = (bf16[48,32,128]{2,1,0:T(8,128)(2,1)}, bf16[48,32,128]{2,1,0:T(8,128)(2,1)S(1)}, u32[]{:S(2)}, u32[]{:S(2)}) collective-permute-start(bf16[48,32,128]{2,1,0:T(8,128)(2,1)} %collective-permute-done.7.rest_5_), channel_id=1, source_target_pairs={{0,96},{32,0},{64,32},{96,64},{1,97},{33,1},{65,33},{97,65},{2,98}... | collective-permute-start | bytes 1179656 | tf_op jit(solution)/shard_map/ppermute | solution.py:484
  86.8 8.8 %all-to-all-start.2 = ((bf16[32,16,2048]{2,1,0:T(8,128)(2,1)}), bf16[32,16,2048]{2,1,0:T(8,128)(2,1)}, u32[]{:S(2)}, u32[]{:S(2)}) async-start(bf16[32,16,2048]{2,1,0:T(8,128)(2,1)} %get-tuple-element.102), calls=%async_computation.2 | async-start | bytes 4194304 | tf_op jit(solution)/shard_map/all_to_all | solution.py:520
  95.7 1.8 %collective-permute-start.20 = (bf16[49,32,128]{2,1,0:T(8,128)(2,1)}, bf16[49,32,128]{2,1,0:T(8,128)(2,1)}, u32[]{:S(2)}, u32[]{:S(2)}) collective-permute-start(bf16[49,32,128]{2,1,0:T(8,128)(2,1)} %get-tuple-element.108), channel_id=1, source_target_pairs={{0,32},{32,64},{64,96},{96,0},{1,33},{33,65},{65,97},{97,1},{2,34}... | collective-permute-start | bytes 1204232 | tf_op jit(solution)/shard_map/ppermute | solution.py:484
  97.6 2.6 %collective-permute-start.21 = (bf16[48,32,128]{2,1,0:T(8,128)(2,1)}, bf16[48,32,128]{2,1,0:T(8,128)(2,1)}, u32[]{:S(2)}, u32[]{:S(2)}) collective-permute-start(bf16[48,32,128]{2,1,0:T(8,128)(2,1)} %get-tuple-element.109), channel_id=1, source_target_pairs={{0,96},{32,0},{64,32},{96,64},{1,97},{33,1},{65,33},{97,65},{2,98}... | collective-permute-start | bytes 1179656 | tf_op jit(solution)/shard_map/ppermute | solution.py:484
  100.2 0.8 copy-done.15
  100.9 24.7 %expert_1.1 = (bf16[32,16,2048]{2,1,0:T(8,128)(2,1)}, bf16[97,32,128]{2,1,0:T(8,128)(2,1)}, bf16[48,32,128]{2,1,0:T(8,128)(2,1)}, bf16[49,32,128]{2,1,0:T(8,128)...) custom-call(s32[2304]{0:T(1024)} %add.117.inverse_ref, ...), custom_call_target="tpu_custom_call" | custom-call | flops 149999992832 | bytes 1048576 | tf_op jit(solution)/shard_map/expert_1/pallas_call | solution.py:384
  125.7 8.4 %all-to-all-start.3 = ((bf16[32,16,2048]{2,1,0:T(8,128)(2,1)}), bf16[32,16,2048]{2,1,0:T(8,128)(2,1)S(1)}, u32[]{:S(2)}, u32[]{:S(2)}) async-start(bf16[32,16,2048]{2,1,0:T(8,128)(2,1)} %get-tuple-element.120), calls=%async_computation.3 | async-start | bytes 4194304 | tf_op jit(solution)/shard_map/all_to_all | solution.py:520
  134.1 0.5 collective-permute-start.16
  134.6 1.1 add.125
  135.9 1.4 collective-permute-start.12
  137.3 1.1 add.124
  138.4 1.1 collective-permute-start.22
  139.5 7.9 %collective-permute-done.12 = bf16[48,32,128]{2,1,0:T(8,128)(2,1)S(1)} collective-permute-done((bf16[48,32,128]{2,1,0:T(8,128)(2,1)}, bf16[48,32,128]{2,1,0:T(8,128)(2,1)S(1)}, u32[]{:S(2)}, u32[]{:S(2)}) %collective-permute-start.12) | collective-permute-done | bytes 393248 | tf_op jit(solution)/shard_map/ppermute | solution.py:484
  147.5 0.3 collective-permute-start.14
  147.8 0.9 add.122
  148.7 1.1 collective-permute-start.13
  149.8 0.9 add.123
  150.7 5.2 %collective-permute-done.22.left_a_ref = bf16[48,32,128]{2,1,0:T(8,128)(2,1)S(1)} collective-permute-done((bf16[48,32,128]{2,1,0:T(8,128)(2,1)S(1)}, bf16[48,32,128]{2,1,0:T(8,128)(2,1)S(1)}, u32[]{:S(2)}, u32[]{:S(2)}) %collective-permute-start.22) | collective-permute-done | bytes 393248 | tf_op jit(solution)/shard_map/ppermute | solution.py:484
  155.9 0.3 collective-permute-start.17
  156.2 0.6 broadcast_in_dim.52.router_ref
  157.0 3.6 %update_0.1 = (f32[192,4096]{1,0:T(8,128)}, f32[3,2,32]{2,1,0:T(2,128)}, f32[2,512]{1,0:T(2,128)}) custom-call(bf16[97,32,128]{2,1,0:T(8,128)(2,1)} %get-tuple-element.110.own_ref.own_last_ref, bf16[48,32,128]{2,1,0:T(8,128)(2,1)} %copy-done.7, bf16[48,32,128]{2,1,0:T(8,128)(2,1)} %collective-permute-done.21.right_a_ref, ...), custom_call_target="tpu_custom_call" | custom-call | bytes 1048576 | tf_op jit(solution)/shard_map/update_0/pallas_call | solution.py:423
  160.6 1.7 all-to-all-done.3.rest_1_
  162.4 5.0 %combine.1 = (bf16[256,2048]{1,0:T(8,128)(2,1)}, bf16[256,2048]{1,0:T(8,128)(2,1)}) custom-call(s32[8,64]{1,0:T(8,128)S(1)} %bitcast.13, bf16[32,16,2048]{2,1,0:T(8,128)(2,1)} %all-to-all-done.2.rest_0_, bf16[32,16,2048]{2,1,0:T(8,128)(2,1)S(1)} %all-to-all-done.3.rest_1_), custom_call_target="tpu_custom_call" | custom-call | flops 149999992832 | bytes 1048576 | tf_op jit(solution)/shard_map/combine/pallas_call | solution.py:447
  167.4 5.7 %collective-permute-done.13.left_a_ref = bf16[48,32,128]{2,1,0:T(8,128)(2,1)} collective-permute-done((bf16[48,32,128]{2,1,0:T(8,128)(2,1)}, bf16[48,32,128]{2,1,0:T(8,128)(2,1)}, u32[]{:S(2)}, u32[]{:S(2)}) %collective-permute-start.13) | collective-permute-done | bytes 393248 | tf_op jit(solution)/shard_map/ppermute | solution.py:484
  173.0 3.6 %update_1.1 = (f32[192,4096]{1,0:T(8,128)}, f32[3,2,32]{2,1,0:T(2,128)}, f32[2,512]{1,0:T(2,128)}) custom-call(bf16[97,32,128]{2,1,0:T(8,128)(2,1)} %get-tuple-element.124.own_ref.own_last_ref, bf16[48,32,128]{2,1,0:T(8,128)(2,1)} %collective-permute-done.13.left_a_ref, ...), custom_call_target="tpu_custom_call", output_to_operand_aliasing={{0}: (11, {})} | custom-call | bytes 1048576 | tf_op jit(solution)/shard_map/update_1/pallas_call | solution.py:423
  (70 shorter events, 1.2 us)
Async XLA Ops:
  6.3 37.9 %all-to-all-start = ((bf16[32,16,2048]{2,1,0:T(8,128)(2,1)}), bf16[32,16,2048]{2,1,0:T(8,128)(2,1)S(1)}, u32[]{:S(2)}, u32[]{:S(2)}) async-start(bf16[32,16,2048]{2,1,0:T(8,128)(2,1)} %get-tuple-element.82), calls=%async_computation | async-start | bytes 4194304 | tf_op jit(solution)/shard_map/all_to_all | solution.py:520
  18.4 7.7 %copy-start.8 = (s32[2,3,128]{2,0,1:T(2,128)S(1)}, s32[2,3,128]{2,0,1:T(2,128)}, u32[]{:S(2)}) copy-start(s32[2,3,128]{2,0,1:T(2,128)} %param.12) | copy-start | bytes 9220
  18.4 7.7 %copy-start.10 = (s32[3]{0:T(128)S(1)}, s32[3]{0:T(128)}, u32[]{:S(2)}) copy-start(s32[3]{0:T(128)} %constant.90.clone) | copy-start | bytes 40
  18.4 10.3 %copy-start.9 = (bf16[2048,2]{0,1:T(2,128)(2,1)S(1)}, bf16[2048,2]{0,1:T(2,128)(2,1)}, u32[]{:S(2)}) copy-start(bf16[2048,2]{0,1:T(2,128)(2,1)} %param.11) | copy-start | bytes 24580
  18.4 22.7 %collective-permute-start.1 = (bf16[48,32,128]{2,1,0:T(8,128)(2,1)}, bf16[48,32,128]{2,1,0:T(8,128)(2,1)}, u32[]{:S(2)}, u32[]{:S(2)}) collective-permute-start(bf16[48,32,128]{2,1,0:T(8,128)(2,1)} %get-tuple-element.73.rest_1_), channel_id=1, source_target_pairs={{0,96},{32,0},{64,32},{96,64},{1,97},{33,1},{65,33},{97,65},{2,98}... | collective-permute-start | bytes 1179656 | tf_op jit(solution)/shard_map/ppermute | solution.py:484
  21.0 33.2 %collective-permute-start.2 = (bf16[48,32,128]{2,1,0:T(8,128)(2,1)}, bf16[48,32,128]{2,1,0:T(8,128)(2,1)}, u32[]{:S(2)}, u32[]{:S(2)}) collective-permute-start(bf16[48,32,128]{2,1,0:T(8,128)(2,1)} %get-tuple-element.73.rest_1_), channel_id=1, source_target_pairs={{0,32},{32,64},{64,96},{96,0},{1,33},{33,65},{65,97},{97,1},{2,34}... | collective-permute-start | bytes 1179656 | tf_op jit(solution)/shard_map/ppermute | solution.py:484
  21.0 20.1 %collective-permute-start = (bf16[48,32,128]{2,1,0:T(8,128)(2,1)}, bf16[48,32,128]{2,1,0:T(8,128)(2,1)}, u32[]{:S(2)}, u32[]{:S(2)}) collective-permute-start(bf16[48,32,128]{2,1,0:T(8,128)(2,1)} %get-tuple-element.72.rest_0_), channel_id=1, source_target_pairs={{0,32},{32,64},{64,96},{96,0},{1,33},{33,65},{65,97},{97,1},{2,34}... | collective-permute-start | bytes 1179656 | tf_op jit(solution)/shard_map/ppermute | solution.py:484
  21.2 34.8 %collective-permute-start.3 = (bf16[48,32,128]{2,1,0:T(8,128)(2,1)}, bf16[48,32,128]{2,1,0:T(8,128)(2,1)}, u32[]{:S(2)}, u32[]{:S(2)}) collective-permute-start(bf16[48,32,128]{2,1,0:T(8,128)(2,1)} %get-tuple-element.72.rest_0_), channel_id=1, source_target_pairs={{0,96},{32,0},{64,32},{96,64},{1,97},{33,1},{65,33},{97,65},{2,98}... | collective-permute-start | bytes 1179656 | tf_op jit(solution)/shard_map/ppermute | solution.py:484
  41.1 14.9 %collective-permute-start.4 = (bf16[48,32,128]{2,1,0:T(8,128)(2,1)}, bf16[48,32,128]{2,1,0:T(8,128)(2,1)S(1)}, u32[]{:S(2)}, u32[]{:S(2)}) collective-permute-start(bf16[48,32,128]{2,1,0:T(8,128)(2,1)} %collective-permute-done.rest_2_), channel_id=1, source_target_pairs={{0,32},{32,64},{64,96},{96,0},{1,33},{33,65},{65,97},{97,1},{2,34}... | collective-permute-start | bytes 1179656 | tf_op jit(solution)/shard_map/ppermute | solution.py:484
  41.1 17.5 %collective-permute-start.5 = (bf16[48,32,128]{2,1,0:T(8,128)(2,1)}, bf16[48,32,128]{2,1,0:T(8,128)(2,1)S(1)}, u32[]{:S(2)}, u32[]{:S(2)}) collective-permute-start(bf16[48,32,128]{2,1,0:T(8,128)(2,1)} %collective-permute-done.1.rest_5_), channel_id=1, source_target_pairs={{0,96},{32,0},{64,32},{96,64},{1,97},{33,1},{65,33},{97,65},{2,98}... | collective-permute-start | bytes 1179656 | tf_op jit(solution)/shard_map/ppermute | solution.py:484
  43.8 40.3 %collective-permute-start.7 = (bf16[48,32,128]{2,1,0:T(8,128)(2,1)}, bf16[48,32,128]{2,1,0:T(8,128)(2,1)}, u32[]{:S(2)}, u32[]{:S(2)}) collective-permute-start(bf16[48,32,128]{2,1,0:T(8,128)(2,1)} %get-tuple-element.90.rest_1_), channel_id=1, source_target_pairs={{0,96},{32,0},{64,32},{96,64},{1,97},{33,1},{65,33},{97,65},{2,98}... | collective-permute-start | bytes 1179656 | tf_op jit(solution)/shard_map/ppermute | solution.py:484
  44.2 1.3 copy-start.1
  45.5 38.5 %all-to-all-start.1 = ((bf16[32,16,2048]{2,1,0:T(8,128)(2,1)}), bf16[32,16,2048]{2,1,0:T(8,128)(2,1)}, u32[]{:S(2)}, u32[]{:S(2)}) async-start(bf16[32,16,2048]{2,1,0:T(8,128)(2,1)} %get-tuple-element.83), calls=%async_computation.1 | async-start | bytes 4194304 | tf_op jit(solution)/shard_map/all_to_all | solution.py:520
  54.1 41.5 %collective-permute-start.8 = (bf16[48,32,128]{2,1,0:T(8,128)(2,1)}, bf16[48,32,128]{2,1,0:T(8,128)(2,1)}, u32[]{:S(2)}, u32[]{:S(2)}) collective-permute-start(bf16[48,32,128]{2,1,0:T(8,128)(2,1)} %get-tuple-element.90.rest_1_), channel_id=1, source_target_pairs={{0,32},{32,64},{64,96},{96,0},{1,33},{33,65},{65,97},{97,1},{2,34}... | collective-permute-start | bytes 1179656 | tf_op jit(solution)/shard_map/ppermute | solution.py:484
  55.9 28.1 %collective-permute-start.6 = (bf16[48,32,128]{2,1,0:T(8,128)(2,1)}, bf16[48,32,128]{2,1,0:T(8,128)(2,1)}, u32[]{:S(2)}, u32[]{:S(2)}) collective-permute-start(bf16[48,32,128]{2,1,0:T(8,128)(2,1)} %get-tuple-element.89.rest_0_), channel_id=1, source_target_pairs={{0,32},{32,64},{64,96},{96,0},{1,33},{33,65},{65,97},{97,1},{2,34}... | collective-permute-start | bytes 1179656 | tf_op jit(solution)/shard_map/ppermute | solution.py:484
  56.0 2.6 %copy-start.12 = (bf16[48,32,128]{2,1,0:T(8,128)(2,1)}, bf16[48,32,128]{2,1,0:T(8,128)(2,1)S(1)}, u32[]{:S(2)}) copy-start(bf16[48,32,128]{2,1,0:T(8,128)(2,1)S(1)} %collective-permute-done.4.rest_6_) | copy-start | bytes 1179652
  56.0 41.5 %collective-permute-start.9 = (bf16[48,32,128]{2,1,0:T(8,128)(2,1)}, bf16[48,32,128]{2,1,0:T(8,128)(2,1)}, u32[]{:S(2)}, u32[]{:S(2)}) collective-permute-start(bf16[48,32,128]{2,1,0:T(8,128)(2,1)} %get-tuple-element.89.rest_0_), channel_id=1, source_target_pairs={{0,96},{32,0},{64,32},{96,64},{1,97},{33,1},{65,33},{97,65},{2,98}... | collective-permute-start | bytes 1179656 | tf_op jit(solution)/shard_map/ppermute | solution.py:484
  58.6 0.8 copy-start.14
  84.1 13.5 %collective-permute-start.10 = (bf16[48,32,128]{2,1,0:T(8,128)(2,1)}, bf16[48,32,128]{2,1,0:T(8,128)(2,1)S(1)}, u32[]{:S(2)}, u32[]{:S(2)}) collective-permute-start(bf16[48,32,128]{2,1,0:T(8,128)(2,1)} %collective-permute-done.6.rest_2_), channel_id=1, source_target_pairs={{0,32},{32,64},{64,96},{96,0},{1,33},{33,65},{65,97},{97,1},{2,34}... | collective-permute-start | bytes 1179656 | tf_op jit(solution)/shard_map/ppermute | solution.py:484
  84.2 16.0 %collective-permute-start.11 = (bf16[48,32,128]{2,1,0:T(8,128)(2,1)}, bf16[48,32,128]{2,1,0:T(8,128)(2,1)S(1)}, u32[]{:S(2)}, u32[]{:S(2)}) collective-permute-start(bf16[48,32,128]{2,1,0:T(8,128)(2,1)} %collective-permute-done.7.rest_5_), channel_id=1, source_target_pairs={{0,96},{32,0},{64,32},{96,64},{1,97},{33,1},{65,33},{97,65},{2,98}... | collective-permute-start | bytes 1179656 | tf_op jit(solution)/shard_map/ppermute | solution.py:484
  86.8 38.8 %collective-permute-start.19 = (bf16[49,32,128]{2,1,0:T(8,128)(2,1)}, bf16[49,32,128]{2,1,0:T(8,128)(2,1)}, u32[]{:S(2)}, u32[]{:S(2)}) collective-permute-start(bf16[49,32,128]{2,1,0:T(8,128)(2,1)} %get-tuple-element.107), channel_id=1, source_target_pairs={{0,96},{32,0},{64,32},{96,64},{1,97},{33,1},{65,33},{97,65},{2,98}... | collective-permute-start | bytes 1204232 | tf_op jit(solution)/shard_map/ppermute | solution.py:484
  86.8 38.8 %all-to-all-start.2 = ((bf16[32,16,2048]{2,1,0:T(8,128)(2,1)}), bf16[32,16,2048]{2,1,0:T(8,128)(2,1)}, u32[]{:S(2)}, u32[]{:S(2)}) async-start(bf16[32,16,2048]{2,1,0:T(8,128)(2,1)} %get-tuple-element.102), calls=%async_computation.2 | async-start | bytes 4194304 | tf_op jit(solution)/shard_map/all_to_all | solution.py:520
  95.7 30.0 %collective-permute-start.20 = (bf16[49,32,128]{2,1,0:T(8,128)(2,1)}, bf16[49,32,128]{2,1,0:T(8,128)(2,1)}, u32[]{:S(2)}, u32[]{:S(2)}) collective-permute-start(bf16[49,32,128]{2,1,0:T(8,128)(2,1)} %get-tuple-element.108), channel_id=1, source_target_pairs={{0,32},{32,64},{64,96},{96,0},{1,33},{33,65},{65,97},{97,1},{2,34}... | collective-permute-start | bytes 1204232 | tf_op jit(solution)/shard_map/ppermute | solution.py:484
  97.5 28.1 %collective-permute-start.18 = (bf16[48,32,128]{2,1,0:T(8,128)(2,1)}, bf16[48,32,128]{2,1,0:T(8,128)(2,1)}, u32[]{:S(2)}, u32[]{:S(2)}) collective-permute-start(bf16[48,32,128]{2,1,0:T(8,128)(2,1)} %get-tuple-element.106), channel_id=1, source_target_pairs={{0,32},{32,64},{64,96},{96,0},{1,33},{33,65},{65,97},{97,1},{2,34}... | collective-permute-start | bytes 1179656 | tf_op jit(solution)/shard_map/ppermute | solution.py:484
  97.6 2.6 %copy-start.13 = (bf16[48,32,128]{2,1,0:T(8,128)(2,1)}, bf16[48,32,128]{2,1,0:T(8,128)(2,1)S(1)}, u32[]{:S(2)}) copy-start(bf16[48,32,128]{2,1,0:T(8,128)(2,1)S(1)} %collective-permute-done.10.rest_6_) | copy-start | bytes 1179652
  97.6 28.1 %collective-permute-start.21 = (bf16[48,32,128]{2,1,0:T(8,128)(2,1)}, bf16[48,32,128]{2,1,0:T(8,128)(2,1)}, u32[]{:S(2)}, u32[]{:S(2)}) collective-permute-start(bf16[48,32,128]{2,1,0:T(8,128)(2,1)} %get-tuple-element.109), channel_id=1, source_target_pairs={{0,96},{32,0},{64,32},{96,64},{1,97},{33,1},{65,33},{97,65},{2,98}... | collective-permute-start | bytes 1179656 | tf_op jit(solution)/shard_map/ppermute | solution.py:484
  100.2 0.8 copy-start.15
  125.7 8.4 %copy-start.11 = (bf16[49,32,128]{2,1,0:T(8,128)(2,1)S(1)}, bf16[49,32,128]{2,1,0:T(8,128)(2,1)}, u32[]{:S(2)}) copy-start(bf16[49,32,128]{2,1,0:T(8,128)(2,1)} %get-tuple-element.100) | copy-start | bytes 1204228
  125.7 9.0 %copy-start.3 = (bf16[49,32,128]{2,1,0:T(8,128)(2,1)S(1)}, bf16[49,32,128]{2,1,0:T(8,128)(2,1)}, u32[]{:S(2)}) copy-start(bf16[49,32,128]{2,1,0:T(8,128)(2,1)} %get-tuple-element.115) | copy-start | bytes 1204228
  125.7 11.6 %copy-start.5 = (bf16[48,32,128]{2,1,0:T(8,128)(2,1)S(1)}, bf16[48,32,128]{2,1,0:T(8,128)(2,1)}, u32[]{:S(2)}) copy-start(bf16[48,32,128]{2,1,0:T(8,128)(2,1)} %get-tuple-element.111) | copy-start | bytes 1179652
  125.7 36.7 %all-to-all-start.3 = ((bf16[32,16,2048]{2,1,0:T(8,128)(2,1)}), bf16[32,16,2048]{2,1,0:T(8,128)(2,1)S(1)}, u32[]{:S(2)}, u32[]{:S(2)}) async-start(bf16[32,16,2048]{2,1,0:T(8,128)(2,1)} %get-tuple-element.120), calls=%async_computation.3 | async-start | bytes 4194304 | tf_op jit(solution)/shard_map/all_to_all | solution.py:520
  134.1 13.7 %copy-start.6 = (bf16[48,32,128]{2,1,0:T(8,128)(2,1)S(1)}, bf16[48,32,128]{2,1,0:T(8,128)(2,1)}, u32[]{:S(2)}) copy-start(bf16[48,32,128]{2,1,0:T(8,128)(2,1)} %get-tuple-element.95) | copy-start | bytes 1179652
  134.1 15.7 %copy-start.4 = (bf16[49,32,128]{2,1,0:T(8,128)(2,1)S(1)}, bf16[49,32,128]{2,1,0:T(8,128)(2,1)}, u32[]{:S(2)}) copy-start(bf16[49,32,128]{2,1,0:T(8,128)(2,1)} %get-tuple-element.99) | copy-start | bytes 1204228
  134.1 14.6 %collective-permute-start.16 = (bf16[49,32,128]{2,1,0:T(8,128)(2,1)S(1)}, bf16[49,32,128]{2,1,0:T(8,128)(2,1)S(1)}, u32[]{:S(2)}, u32[]{:S(2)}) collective-permute-start(bf16[49,32,128]{2,1,0:T(8,128)(2,1)S(1)} %copy-done.11), channel_id=1, source_target_pairs={{0,96},{32,0},{64,32},{96,64},{1,97},{33,1},{65,33},{97,65},{2,98}... | collective-permute-start | bytes 1204232 | tf_op jit(solution)/shard_map/ppermute | solution.py:484
  135.7 20.5 %collective-permute-start.23 = (bf16[49,32,128]{2,1,0:T(8,128)(2,1)S(1)}, bf16[49,32,128]{2,1,0:T(8,128)(2,1)S(1)}, u32[]{:S(2)}, u32[]{:S(2)}) collective-permute-start(bf16[49,32,128]{2,1,0:T(8,128)(2,1)S(1)} %add.125), channel_id=1, source_target_pairs={{0,96},{32,0},{64,32},{96,64},{1,97},{33,1},{65,33},{97,65},{2,98}... | collective-permute-start | bytes 1204232 | tf_op jit(solution)/shard_map/ppermute | solution.py:484
  135.9 11.6 %collective-permute-start.12 = (bf16[48,32,128]{2,1,0:T(8,128)(2,1)}, bf16[48,32,128]{2,1,0:T(8,128)(2,1)S(1)}, u32[]{:S(2)}, u32[]{:S(2)}) collective-permute-start(bf16[48,32,128]{2,1,0:T(8,128)(2,1)} %get-tuple-element.96), channel_id=1, source_target_pairs={{0,32},{32,64},{64,96},{96,0},{1,33},{33,65},{65,97},{97,1},{2,34}... | collective-permute-start | bytes 1179656 | tf_op jit(solution)/shard_map/ppermute | solution.py:484
  138.4 17.5 %collective-permute-start.22 = (bf16[48,32,128]{2,1,0:T(8,128)(2,1)S(1)}, bf16[48,32,128]{2,1,0:T(8,128)(2,1)S(1)}, u32[]{:S(2)}, u32[]{:S(2)}) collective-permute-start(bf16[48,32,128]{2,1,0:T(8,128)(2,1)S(1)} %add.124), channel_id=1, source_target_pairs={{0,32},{32,64},{64,96},{96,0},{1,33},{33,65},{65,97},{97,1},{2,34}... | collective-permute-start | bytes 1179656 | tf_op jit(solution)/shard_map/ppermute | solution.py:484
  139.5 27.9 %collective-permute-start.15 = (bf16[49,32,128]{2,1,0:T(8,128)(2,1)}, bf16[49,32,128]{2,1,0:T(8,128)(2,1)}, u32[]{:S(2)}, u32[]{:S(2)}) collective-permute-start(bf16[49,32,128]{2,1,0:T(8,128)(2,1)} %get-tuple-element.98), channel_id=1, source_target_pairs={{0,32},{32,64},{64,96},{96,0},{1,33},{33,65},{65,97},{97,1},{2,34}... | collective-permute-start | bytes 1204232 | tf_op jit(solution)/shard_map/ppermute | solution.py:484
  147.5 19.9 %collective-permute-start.14 = (bf16[48,32,128]{2,1,0:T(8,128)(2,1)}, bf16[48,32,128]{2,1,0:T(8,128)(2,1)}, u32[]{:S(2)}, u32[]{:S(2)}) collective-permute-start(bf16[48,32,128]{2,1,0:T(8,128)(2,1)} %get-tuple-element.97), channel_id=1, source_target_pairs={{0,96},{32,0},{64,32},{96,64},{1,97},{33,1},{65,33},{97,65},{2,98}... | collective-permute-start | bytes 1179656 | tf_op jit(solution)/shard_map/ppermute | solution.py:484
  148.7 24.4 %collective-permute-start.13 = (bf16[48,32,128]{2,1,0:T(8,128)(2,1)}, bf16[48,32,128]{2,1,0:T(8,128)(2,1)}, u32[]{:S(2)}, u32[]{:S(2)}) collective-permute-start(bf16[48,32,128]{2,1,0:T(8,128)(2,1)} %add.122), channel_id=1, source_target_pairs={{0,32},{32,64},{64,96},{96,0},{1,33},{33,65},{65,97},{97,1},{2,34}... | collective-permute-start | bytes 1179656 | tf_op jit(solution)/shard_map/ppermute | solution.py:484
  155.9 0.9 copy-start.7
  155.9 17.1 %collective-permute-start.17 = (bf16[49,32,128]{2,1,0:T(8,128)(2,1)}, bf16[49,32,128]{2,1,0:T(8,128)(2,1)}, u32[]{:S(2)}, u32[]{:S(2)}) collective-permute-start(bf16[49,32,128]{2,1,0:T(8,128)(2,1)} %add.123), channel_id=1, source_target_pairs={{0,96},{32,0},{64,32},{96,64},{1,97},{33,1},{65,33},{97,65},{2,98}... | collective-permute-start | bytes 1204232 | tf_op jit(solution)/shard_map/ppermute | solution.py:484
  156.2 0.8 copy-start.2
  157.0 5.4 %copy-start = (s32[1,64,8]{1,2,0:T(8,128)S(1)}, s32[1,64,8]{1,2,0:T(8,128)}, u32[]{:S(2)}) copy-start(s32[1,64,8]{1,2,0:T(8,128)} %param.10) | copy-start | bytes 6148

commit v7 on v6

--- a/solution.py
+++ b/solution.py
@@ -105,20 +105,22 @@
 
 def expert_kernel(
     inverse_ref, row_ref, lane_ref, me_ref,
-    arrived_ref, router_ref, *rest,
+    arriving_ref, router_ref, *rest,
     member,
 ):
-    piece_refs, send_ref, grad_refs = rest[:8], rest[8], rest[9:16]
+    piece_refs, sending_ref, grad_refs = rest[:8], rest[8], rest[9:13]
     (
-    copies_ref, packed_ref, in_sems, out_sems,
+    copies_ref, packed_ref, arrived_ref, send_ref, sigma_ref, in_sems, out_sems,
     wide_ref, down_ref, rows_ref, grads_ref, pre_ref, part_ref, both_ref,
     grad_wide_ref, grad_down_ref, router_out_ref,
-    ) = rest[16:]
+    ) = rest[13:]
     length = piece_refs[0].shape[0]
     loads = [
         pltpu.make_async_copy(piece, copies_ref.at[pl.ds(at * length, length)], in_sems.at[at])
         for at, piece in enumerate(piece_refs)
     ]
+    rows_in = pltpu.make_async_copy(arriving_ref, arrived_ref, in_sems.at[len(loads)])
+    rows_in.start()
     for load in loads:
         load.start()
     copies_ref[3 * MAXB] = jnp.zeros((32, 128), BF16)
@@ -139,6 +141,7 @@
         grads_ref[:, cols] = grads.astype(BF16)
         return logit + jnp.sum(rows * router_ref[mine, cols], axis=1, keepdims=True)
 
+    rows_in.wait()
     logit = lax.fori_loop(0, chunks, take, jnp.zeros((count, 1), F32))
     gating = 1.0 / (1.0 + jnp.exp(-logit))
 
@@ -175,7 +178,9 @@
     for n in range(FF // CHUNK):
         gate_pre = pre_ref[:, n * CHUNK : (n + 1) * CHUNK]
         up_pre = pre_ref[:, FF + n * CHUNK : FF + (n + 1) * CHUNK]
-        hidden = (gate_pre / (1.0 + jnp.exp(-gate_pre)) * up_pre).astype(BF16)
+        sigma = 1.0 / (1.0 + jnp.exp(-gate_pre))
+        sigma_ref[:, n * CHUNK : (n + 1) * CHUNK] = sigma
+        hidden = (gate_pre * sigma * up_pre).astype(BF16)
         hidden_list.append(dot(hidden, split).astype(BF16))
     hidden_split = jnp.concatenate(hidden_list, axis=1)
 
@@ -196,7 +201,7 @@
         )
         gate_pre = pre_ref[:, n * CHUNK : (n + 1) * CHUNK]
         up_pre = pre_ref[:, FF + n * CHUNK : FF + (n + 1) * CHUNK]
-        sigma = 1.0 / (1.0 + jnp.exp(-gate_pre))
+        sigma = sigma_ref[:, n * CHUNK : (n + 1) * CHUNK]
         gate_grad = hidden_grad * up_pre * sigma * (1.0 + gate_pre * (1.0 - sigma))
         both_ref[:, n * CHUNK : (n + 1) * CHUNK] = gate_grad.astype(BF16)
         both_ref[:, FF + n * CHUNK : FF + (n + 1) * CHUNK] = (hidden_grad * gate_pre * sigma).astype(BF16)
@@ -212,6 +217,9 @@
         router_out_ref[:, cols] = jnp.sum(logit_grad * rows.astype(F32), axis=0, keepdims=True)
         grad_wide_ref[cols, :] = dot(rows, both_ref[...], TN).astype(BF16)
 
+    rows_out = pltpu.make_async_copy(send_ref, sending_ref, out_sems.at[len(grad_refs)])
+    rows_out.start()
+
     def cut(source_ref, matrix, slot, place_in):
         at = slot_base + matrix * MAXB + slot
         row = pl.multiple_of(row_ref[at], 32)
@@ -223,8 +231,7 @@
 
     per = MAXB // OWNERS
     part = packed_ref.shape[0] // OWNERS
-    half = 3 * per // 2
-    stores = []
+    stores = [rows_out]
     for ahead in (2, 1, 3, 0):
         owner = (me_ref[0] + ahead) & (OWNERS - 1)
         first = ahead * part
@@ -244,40 +251,26 @@
         ]
         lines.append(jnp.zeros((32 - len(lines), 128), F32))
         packed_ref[first + 3 * per] = jnp.concatenate(lines, axis=0).astype(BF16)
-        cuts = [(0, part)] if ahead == 0 else [(0, half), (half, part - half)]
-        for at, (begin, size) in enumerate(cuts):
-            number = 0 if ahead == 0 else 2 * ahead - 1 + at
-            store = pltpu.make_async_copy(
-                packed_ref.at[pl.ds(first + begin, size)], grad_refs[number], out_sems.at[number]
-            )
-            store.start()
-            stores.append(store)
+        store = pltpu.make_async_copy(
+            packed_ref.at[pl.ds(first, part)], grad_refs[ahead], out_sems.at[ahead]
+        )
+        store.start()
+        stores.append(store)
     for store in stores:
         store.wait()
 
 
 def update_kernel(
-    own_ref, left_a_ref, right_a_ref, left_b_ref, right_b_ref,
-    own_last_ref, left_last_ref, right_last_ref,
+    own_ref, first_ref, second_ref, own_last_ref, first_last_ref, second_last_ref,
     masters_ref, scores_ref, router_ref, *rest,
     member,
 ):
     out_ref, scores_out_ref, router_out_ref, lines_ref, total_ref = rest[-5:]
     step, steps = pl.program_id(0), pl.num_programs(0)
     rows = masters_ref.shape[0]
-
-    def gather(left_ref, right_ref):
-        for s in range(rows):
-            summed = own_ref[s].astype(F32) + left_ref[s].astype(F32) + right_ref[s].astype(F32)
-            lines_ref[s // 8, pl.ds(s % 8, 32, stride=8), :] = summed
-
-    @pl.when(step < steps // 2)
-    def _():
-        gather(left_a_ref, right_a_ref)
-
-    @pl.when(step >= steps // 2)
-    def _():
-        gather(left_b_ref, right_b_ref)
+    for s in range(rows):
+        summed = own_ref[s].astype(F32) + first_ref[s].astype(F32) + second_ref[s].astype(F32)
+        lines_ref[s // 8, pl.ds(s % 8, 32, stride=8), :] = summed
 
     for group in range(rows // 8):
         total = jnp.zeros((8, 128), F32)
@@ -301,7 +294,7 @@
             sums = exact(jnp.ones((8, 128), F32), total_ref[matrix * per : (matrix + 1) * per, :])
             change = jnp.where(mine, jnp.broadcast_to(sums[:1], mine.shape), 0.0)
             scores_out_ref[matrix] = scores_ref[matrix] - SCORE_RATE * change
-        last = own_last_ref[0].astype(F32) + left_last_ref[0].astype(F32) + right_last_ref[0].astype(F32)
+        last = own_last_ref[0].astype(F32) + first_last_ref[0].astype(F32) + second_last_ref[0].astype(F32)
         last = exact(last, split_matrix(128).astype(F32))
         width = router_ref.shape[1]
         line = jnp.concatenate([last[at : at + 1] for at in range(width // 128)], axis=1)
@@ -379,19 +372,21 @@
     scalar = pl.BlockSpec(memory_space=pltpu.SMEM)
     anywhere = pl.BlockSpec(memory_space=pl.ANY)
     part = 3 * MAXB // OWNERS + 1
-    half = part // 2
-    lengths = [part] + [half, part - half] * 3
+    lengths = [part] * OWNERS
     return pl.pallas_call(
         functools.partial(expert_kernel, member=member),
-        in_specs=[scalar] * 4 + [whole] * 2 + [anywhere] * len(pieces),
-        out_specs=[whole] + [anywhere] * len(lengths),
+        in_specs=[scalar] * 4 + [anywhere, whole] + [anywhere] * len(pieces),
+        out_specs=[anywhere] * (1 + len(lengths)),
         out_shape=[jax.ShapeDtypeStruct((peers, 16, D), BF16)]
         + [jax.ShapeDtypeStruct((length, 32, 128), BF16) for length in lengths],
         scratch_shapes=[
             pltpu.VMEM((3 * MAXB + 1, 32, 128), BF16),
             pltpu.VMEM((OWNERS * part, 32, 128), BF16),
-            pltpu.SemaphoreType.DMA((len(pieces),)),
-            pltpu.SemaphoreType.DMA((len(lengths),)),
+            pltpu.VMEM((peers, 16, D), BF16),
+            pltpu.VMEM((peers, 16, D), BF16),
+            pltpu.VMEM((count, FF), F32),
+            pltpu.SemaphoreType.DMA((len(pieces) + 1,)),
+            pltpu.SemaphoreType.DMA((len(lengths) + 1,)),
             pltpu.VMEM((D, 2 * FF), BF16),
             pltpu.VMEM((FF, D), BF16),
             pltpu.VMEM((count, D), BF16),
@@ -410,21 +405,20 @@
 
 
 def update(member, summed, masters, scores, router_sum, held):
-    own, left_a, right_a, left_b, right_b = summed
+    own, first, second = summed
     mine = own.shape[0] - 1
     steps = 2
     rows = mine // steps
-    tile = lambda index: pl.BlockSpec((rows, 32, 128), index)
-    early = tile(lambda n: (jnp.minimum(n, steps // 2 - 1), 0, 0))
-    late = tile(lambda n: (jnp.maximum(n - steps // 2, 0), 0, 0))
-    last = lambda array: pl.BlockSpec((1, 32, 128), lambda n: (array.shape[0] - 1, 0, 0))
+    tile = pl.BlockSpec((rows, 32, 128), lambda n: (n, 0, 0))
+    last = pl.BlockSpec((1, 32, 128), lambda n: (mine, 0, 0))
     block = pl.BlockSpec((rows, BS * BS), lambda n: (member * steps + n, 0))
     whole = lambda array: pl.BlockSpec(array.shape, lambda n: (0,) * array.ndim)
     return pl.pallas_call(
         functools.partial(update_kernel, member=member),
         grid=(steps,),
-        in_specs=[tile(lambda n: (n, 0, 0)), early, early, late, late]
-        + [last(own), last(left_b), last(right_b), block, whole(scores), whole(router_sum)]
+        in_specs=[tile] * 3
+        + [last] * 3
+        + [block, whole(scores), whole(router_sum)]
         + [pl.BlockSpec(memory_space=pl.ANY)] * len(held),
         out_specs=[block, whole(scores), whole(router_sum)],
         out_shape=[
@@ -432,12 +426,12 @@
             jax.ShapeDtypeStruct(scores.shape, F32),
             jax.ShapeDtypeStruct(router_sum.shape, F32),
         ],
-        input_output_aliases={11 + at: at for at in range(len(held))},
+        input_output_aliases={9 + at: at for at in range(len(held))},
         scratch_shapes=[pltpu.VMEM((rows // 8, 256, 128), F32), pltpu.VMEM((mine, 128), F32)],
         compiler_params=params(56),
         cost_estimate=cost(0, 1 << 20),
         name="update_%d" % member,
-    )(own, left_a, right_a, left_b, right_b, own, left_b, right_b, masters, scores, router_sum, *held)
+    )(own, first, second, own, first, second, masters, scores, router_sum, *held)
 
 
 def combine(picks, back, count):
@@ -493,16 +487,14 @@
     return list(pieces) + [shift(pieces[2], 1), shift(pieces[5], -1)]
 
 
-def scatter_first(own, right_a, right_b, far_a, far_b, left_a, left_b):
-    moving = [shift(far_a, 1), shift(far_b, -1), shift(right_b, 1), shift(left_a, -1)]
-    return own, right_a, left_b, moving
-
-
-def scatter_second(own, right_a, left_b, moving):
-    passing_a, passing_b, from_left_b, from_right_a = moving
-    from_left_a = shift(right_a + passing_a, 1)
-    from_right_b = shift(left_b + passing_b, -1)
-    return own, from_left_a, from_right_a, from_left_b, from_right_b
+def scatter_first(step, own, right, far, left):
+    ahead, behind = (right, left) if step == 1 else (left, right)
+    return own, ahead, [shift(far, step), shift(behind, -step)]
+
+
+def scatter_second(step, own, ahead, moving):
+    passing, direct = moving
+    return own, direct, shift(ahead + passing, step)
 
 
 def body(tokens, out_grad, token_picks, router, kept_blocks, masters, scores):
@@ -545,10 +537,10 @@
             pieces[member] = gather_second(pieces[member])
             back.append(exchange(send))
         send, *gradients = run_expert(member, tables, place, pieces[member], rows, router_rows)
-        summed.append(scatter_first(*gradients))
+        summed.append(scatter_first(1 - 2 * (member % 2), *gradients))
     send, back, summed[:-1] = after((send, back, summed[:-1]))
     back.append(exchange(send))
-    summed = [scatter_second(*terms) for terms in summed]
+    summed = [scatter_second(1 - 2 * (member % 2), *terms) for member, terms in enumerate(summed)]
     score_sum = scores.transpose(1, 0, 2)
     router_sum = jnp.zeros((locals_count, width // owners), F32)
     held = ()

time: 178 us -> 176 us (0.989)
  starting transfers between devices: 60 us -> 56.3 us
  waiting for transfers between devices: 31.2 us -> 34.4 us
    ppermute x24 -> x18, waiting for transfers between devices: 29 us -> 32.2 us  [shift(): lax.ppermute(array, 'dp', [(i, (i + step) % owners) for i in range(owners)])]
    ppermute x24 -> x18, starting transfers between devices: 24.7 us -> 21.5 us  [shift(): lax.ppermute(array, 'dp', [(i, (i + step) % owners) for i in range(owners)])]
    add x4 -> x2, other arithmetic: 3.96 us -> 2.49 us  [scatter_second(): return (own, direct, shift(ahead + passing, step))]
    unnamed x32 -> x24, local copies, waits for them, and re-layouts: 3.05 us -> 3.84 us
  transfers between devices with their start and end apart: 28 -> 22, of which waited for: 6 -> 5; matrix products, arithmetic and copies ran while one was open for 5% -> 5% of each run, Pallas kernels for 36% -> 35%
where the time goes in v7:
time: 176 us; the launch traced here: 174 us
  Pallas kernels  70.7 us (40%)
  starting transfers between devices  56.3 us (32%)
  waiting for transfers between devices  34.4 us (20%)
  local copies, waits for them, and re-layouts  8.49 us (5%)
  other arithmetic  3.21 us (2%)
    pallas_call x2, Pallas kernels, run_expert(): pl.pallas_call(functools.partial(expert_kernel, member=member), in_specs=...  47.8 us
    all_to_all x4, starting transfers between devices, exchange(): lax.all_to_all(array, 'expert', split_axis=0, concat_axis=0, tiled=True)  34.8 us
    ppermute x18, waiting for transfers between devices, shift(): lax.ppermute(array, 'dp', [(i, (i + step) % owners) for i in range(owners)])  32.2 us
    ppermute x18, starting transfers between devices, shift(): lax.ppermute(array, 'dp', [(i, (i + step) % owners) for i in range(owners)])  21.5 us
    pallas_call x2, Pallas kernels, update(): pl.pallas_call(functools.partial(update_kernel, member=member), grid=(ste...  7.29 us
    pallas_call x1, Pallas kernels, pick(): pl.pallas_call(functools.partial(pick_kernel, locals_count=locals_count),...  5.74 us
    pallas_call x1, Pallas kernels, combine(): pl.pallas_call(functools.partial(combine_kernel, locals_count=locals_coun...  5 us
    pallas_call x2, Pallas kernels, pack(): pl.pallas_call(pack_kernel, grid=(2,), in_specs=[pl.BlockSpec((mine, BS *...  4.91 us
  transfers between devices with their start and end apart: 22, of which 5 were waited for; matrix products, arithmetic and copies ran while one was open for 5% of the time, Pallas kernels for 35%

profile of v7, /device:TPU:1, one launch (start us, length us, event | category | flops | bytes accessed | tf_op | source)
XLA Modules:
  0.0 174.2 jit_solution(13794223196686574549)
XLA Ops:
  0.6 5.7 %pick.1 = (bf16[32,16,2048]{2,1,0:T(8,128)(2,1)}, bf16[32,16,2048]{2,1,0:T(8,128)(2,1)}) custom-call(s32[8,64]{1,0:T(8,128)} %bitcast.12, bf16[256,2048]{1,0:T(8,128)(2,1)} %tokens_ref.1, bf16[256,2048]{1,0:T(8,128)(2,1)} %grads_ref.1), custom_call_target="tpu_custom_call" | custom-call | bytes 1048576 | tf_op jit(solution)/shard_map/pick/pallas_call | solution.py:340
  6.4 9.6 %all-to-all-start = ((bf16[32,16,2048]{2,1,0:T(8,128)(2,1)}), bf16[32,16,2048]{2,1,0:T(8,128)(2,1)S(1)}, u32[]{:S(2)}, u32[]{:S(2)}) async-start(bf16[32,16,2048]{2,1,0:T(8,128)(2,1)} %get-tuple-element.71), calls=%async_computation | async-start | bytes 4194304 | tf_op jit(solution)/shard_map/all_to_all | solution.py:512
  16.0 2.5 %pack_0.1 = (bf16[48,32,128]{2,1,0:T(8,128)(2,1)}, bf16[48,32,128]{2,1,0:T(8,128)(2,1)}) custom-call(f32[192,4096]{1,0:T(8,128)} %bitcast.14), custom_call_target="tpu_custom_call" | custom-call | bytes 1048576 | tf_op jit(solution)/shard_map/pack_0/pallas_call | solution.py:355
  18.4 2.5 %collective-permute-start.1 = (bf16[48,32,128]{2,1,0:T(8,128)(2,1)}, bf16[48,32,128]{2,1,0:T(8,128)(2,1)}, u32[]{:S(2)}, u32[]{:S(2)}) collective-permute-start(bf16[48,32,128]{2,1,0:T(8,128)(2,1)} %get-tuple-element.62.rest_1_), channel_id=1, source_target_pairs={{0,96},{32,0},{64,32},{96,64},{1,97},{33,1},{65,33},{97,65},{2,98}... | collective-permute-start | bytes 1179656 | tf_op jit(solution)/shard_map/ppermute | solution.py:478
  21.0 0.2 collective-permute-start
  21.2 2.5 %collective-permute-start.3 = (bf16[48,32,128]{2,1,0:T(8,128)(2,1)}, bf16[48,32,128]{2,1,0:T(8,128)(2,1)}, u32[]{:S(2)}, u32[]{:S(2)}) collective-permute-start(bf16[48,32,128]{2,1,0:T(8,128)(2,1)} %get-tuple-element.61.rest_0_), channel_id=1, source_target_pairs={{0,96},{32,0},{64,32},{96,64},{1,97},{33,1},{65,33},{97,65},{2,98}... | collective-permute-start | bytes 1179656 | tf_op jit(solution)/shard_map/ppermute | solution.py:478
  23.7 2.5 %pack_1.1 = (bf16[48,32,128]{2,1,0:T(8,128)(2,1)}, bf16[48,32,128]{2,1,0:T(8,128)(2,1)}) custom-call(f32[192,4096]{1,0:T(8,128)} %bitcast.15), custom_call_target="tpu_custom_call" | custom-call | bytes 1048576 | tf_op jit(solution)/shard_map/pack_1/pallas_call | solution.py:355
  26.2 0.2 multiply_add_fusion
  26.4 0.6 reshape.141.row_ref
  27.0 0.6 reshape.142.lane_ref
  27.6 0.1 add_add_fusion
  27.7 0.4 select_reduce_fusion
  28.1 0.6 add.111.inverse_ref
  28.7 1.0 reshape.146
  29.7 0.5 copy.23
  30.2 0.7 reshape.145.router_ref
  30.9 10.2 %collective-permute-done.rest_2_ = bf16[48,32,128]{2,1,0:T(8,128)(2,1)} collective-permute-done((bf16[48,32,128]{2,1,0:T(8,128)(2,1)}, bf16[48,32,128]{2,1,0:T(8,128)(2,1)}, u32[]{:S(2)}, u32[]{:S(2)}) %collective-permute-start) | collective-permute-done | bytes 393248 | tf_op jit(solution)/shard_map/ppermute | solution.py:478
  41.1 2.7 %collective-permute-start.5 = (bf16[48,32,128]{2,1,0:T(8,128)(2,1)}, bf16[48,32,128]{2,1,0:T(8,128)(2,1)S(1)}, u32[]{:S(2)}, u32[]{:S(2)}) collective-permute-start(bf16[48,32,128]{2,1,0:T(8,128)(2,1)} %collective-permute-done.1.rest_5_), channel_id=1, source_target_pairs={{0,96},{32,0},{64,32},{96,64},{1,97},{33,1},{65,33},{97,65},{2,98}... | collective-permute-start | bytes 1179656 | tf_op jit(solution)/shard_map/ppermute | solution.py:478
  43.8 0.5 all-to-all-done.arriving_ref
  44.3 1.3 copy-done.2
  45.6 8.5 %all-to-all-start.1 = ((bf16[32,16,2048]{2,1,0:T(8,128)(2,1)}), bf16[32,16,2048]{2,1,0:T(8,128)(2,1)}, u32[]{:S(2)}, u32[]{:S(2)}) async-start(bf16[32,16,2048]{2,1,0:T(8,128)(2,1)} %get-tuple-element.72), calls=%async_computation.1 | async-start | bytes 4194304 | tf_op jit(solution)/shard_map/all_to_all | solution.py:512
  54.2 1.8 %collective-permute-start.8 = (bf16[48,32,128]{2,1,0:T(8,128)(2,1)}, bf16[48,32,128]{2,1,0:T(8,128)(2,1)}, u32[]{:S(2)}, u32[]{:S(2)}) collective-permute-start(bf16[48,32,128]{2,1,0:T(8,128)(2,1)} %get-tuple-element.79.rest_1_), channel_id=1, source_target_pairs={{0,32},{32,64},{64,96},{96,0},{1,33},{33,65},{65,97},{97,1},{2,34}... | collective-permute-start | bytes 1179656 | tf_op jit(solution)/shard_map/ppermute | solution.py:478
  55.9 0.1 collective-permute-start.6
  56.0 2.6 %collective-permute-start.9 = (bf16[48,32,128]{2,1,0:T(8,128)(2,1)}, bf16[48,32,128]{2,1,0:T(8,128)(2,1)}, u32[]{:S(2)}, u32[]{:S(2)}) collective-permute-start(bf16[48,32,128]{2,1,0:T(8,128)(2,1)} %get-tuple-element.78.rest_0_), channel_id=1, source_target_pairs={{0,96},{32,0},{64,32},{96,64},{1,97},{33,1},{65,33},{97,65},{2,98}... | collective-permute-start | bytes 1179656 | tf_op jit(solution)/shard_map/ppermute | solution.py:478
  58.6 0.8 copy-done.9
  59.4 23.9 %expert_0.1 = (bf16[32,16,2048]{2,1,0:T(8,128)(2,1)}, bf16[97,32,128]{2,1,0:T(8,128)(2,1)}, bf16[97,32,128]{2,1,0:T(8,128)(2,1)}, bf16[97,32,128]{2,1,0:T(8,128)(2,1)}, bf16[97,32,128]{2,1,0:T(8,128)(2,1)}) custom-call(s32[2304]{0:T(1024)} %add.111.inverse_ref, s32[768]{0:T(1024)} %reshape.141.row_ref, s32[768]{0:T(1024)} %reshape.142.lane_ref, ...), custom_call_target="tpu_custom_call" | custom-call | flops 149999992832 | bytes 1048576 | tf_op jit(solution)/shard_map/expert_0/pallas_call | solution.py:376
  83.3 0.9 collective-permute-start.10
  84.2 1.8 %collective-permute-start.11 = (bf16[48,32,128]{2,1,0:T(8,128)(2,1)}, bf16[48,32,128]{2,1,0:T(8,128)(2,1)S(1)}, u32[]{:S(2)}, u32[]{:S(2)}) collective-permute-start(bf16[48,32,128]{2,1,0:T(8,128)(2,1)} %collective-permute-done.7.rest_5_), channel_id=1, source_target_pairs={{0,96},{32,0},{64,32},{96,64},{1,97},{33,1},{65,33},{97,65},{2,98}... | collective-permute-start | bytes 1179656 | tf_op jit(solution)/shard_map/ppermute | solution.py:478
  86.0 8.8 %all-to-all-start.2 = ((bf16[32,16,2048]{2,1,0:T(8,128)(2,1)}), bf16[32,16,2048]{2,1,0:T(8,128)(2,1)}, u32[]{:S(2)}, u32[]{:S(2)}) async-start(bf16[32,16,2048]{2,1,0:T(8,128)(2,1)} %get-tuple-element.88), calls=%async_computation.2 | async-start | bytes 4194304 | tf_op jit(solution)/shard_map/all_to_all | solution.py:512
  94.9 3.2 %collective-permute-start.16 = (bf16[97,32,128]{2,1,0:T(8,128)(2,1)}, bf16[97,32,128]{2,1,0:T(8,128)(2,1)}, u32[]{:S(2)}, u32[]{:S(2)}) collective-permute-start(bf16[97,32,128]{2,1,0:T(8,128)(2,1)} %get-tuple-element.92), channel_id=1, source_target_pairs={{0,96},{32,0},{64,32},{96,64},{1,97},{33,1},{65,33},{97,65},{2,98}... | collective-permute-start | bytes 2383880 | tf_op jit(solution)/shard_map/ppermute | solution.py:478
  98.1 0.7 copy-done.10
  98.9 0.7 copy-done.11
  99.6 23.9 %expert_1.1 = (bf16[32,16,2048]{2,1,0:T(8,128)(2,1)}, bf16[97,32,128]{2,1,0:T(8,128)(2,1)}, bf16[97,32,128]{2,1,0:T(8,128)(2,1)}, bf16[97,32,128]{2,1,0:T(8,128)(2,1)}, bf16[97,32,128]{2,1,0:T(8,128)(2,1)}) custom-call(s32[2304]{0:T(1024)} %add.111.inverse_ref, s32[768]{0:T(1024)} %reshape.141.row_ref, s32[768]{0:T(1024)} %reshape.142.lane_ref, ...), custom_call_target="tpu_custom_call" | custom-call | flops 149999992832 | bytes 1048576 | tf_op jit(solution)/shard_map/expert_1/pallas_call | solution.py:376
  123.6 7.8 %all-to-all-start.3 = ((bf16[32,16,2048]{2,1,0:T(8,128)(2,1)}), bf16[32,16,2048]{2,1,0:T(8,128)(2,1)S(1)}, u32[]{:S(2)}, u32[]{:S(2)}) async-start(bf16[32,16,2048]{2,1,0:T(8,128)(2,1)} %get-tuple-element.100), calls=%async_computation.3 | async-start | bytes 4194304 | tf_op jit(solution)/shard_map/all_to_all | solution.py:512
  131.4 0.1 collective-permute-start.13
  131.5 1.4 add.117
  132.9 1.5 collective-permute-start.17
  134.4 0.1 collective-permute-start.12
  134.4 16.3 %collective-permute-done.13 = bf16[97,32,128]{2,1,0:T(8,128)(2,1)S(1)} collective-permute-done((bf16[97,32,128]{2,1,0:T(8,128)(2,1)}, bf16[97,32,128]{2,1,0:T(8,128)(2,1)S(1)}, u32[]{:S(2)}, u32[]{:S(2)}) %collective-permute-start.13) | collective-permute-done | bytes 794656 | tf_op jit(solution)/shard_map/ppermute | solution.py:478
  150.8 1.1 add.116
  151.9 1.5 collective-permute-start.14
  153.3 0.6 broadcast_in_dim.52.router_ref
  154.0 0.3 copy-done.1
  154.2 3.6 %update_0.1 = (f32[192,4096]{1,0:T(8,128)}, f32[3,2,32]{2,1,0:T(2,128)}, f32[2,512]{1,0:T(2,128)}) custom-call(bf16[97,32,128]{2,1,0:T(8,128)(2,1)} %get-tuple-element.93.own_ref.own_last_ref, bf16[97,32,128]{2,1,0:T(8,128)(2,1)} %collective-permute-done.16.first_ref.first_last_ref, bf16[97,32,128]{2,1,0:T(8,128)(2,1)} %copy-done.1, ...), custom_call_target="tpu_custom_call" | custom-call | bytes 1048576 | tf_op jit(solution)/shard_map/update_0/pallas_call | solution.py:416
  157.9 1.8 %all-to-all-done.3.rest_1_ = bf16[32,16,2048]{2,1,0:T(8,128)(2,1)S(1)} async-done(((bf16[32,16,2048]{2,1,0:T(8,128)(2,1)}), bf16[32,16,2048]{2,1,0:T(8,128)(2,1)S(1)}, u32[]{:S(2)}, u32[]{:S(2)}) %all-to-all-start.3) | async-done | bytes 2097184 | tf_op jit(solution)/shard_map/all_to_all | solution.py:512
  159.7 5.0 %combine.1 = (bf16[256,2048]{1,0:T(8,128)(2,1)}, bf16[256,2048]{1,0:T(8,128)(2,1)}) custom-call(s32[8,64]{1,0:T(8,128)S(1)} %bitcast.13, bf16[32,16,2048]{2,1,0:T(8,128)(2,1)} %all-to-all-done.2.rest_0_, bf16[32,16,2048]{2,1,0:T(8,128)(2,1)S(1)} %all-to-all-done.3.rest_1_), custom_call_target="tpu_custom_call" | custom-call | flops 149999992832 | bytes 1048576 | tf_op jit(solution)/shard_map/combine/pallas_call | solution.py:441
  164.7 5.7 %collective-permute-done.12.first_ref.first_last_ref = bf16[97,32,128]{2,1,0:T(8,128)(2,1)} collective-permute-done((bf16[97,32,128]{2,1,0:T(8,128)(2,1)}, bf16[97,32,128]{2,1,0:T(8,128)(2,1)}, u32[]{:S(2)}, u32[]{:S(2)}) %collective-permute-start.12) | collective-permute-done | bytes 794656 | tf_op jit(solution)/shard_map/ppermute | solution.py:478
  170.4 3.6 %update_1.1 = (f32[192,4096]{1,0:T(8,128)}, f32[3,2,32]{2,1,0:T(2,128)}, f32[2,512]{1,0:T(2,128)}) custom-call(bf16[97,32,128]{2,1,0:T(8,128)(2,1)} %get-tuple-element.104.own_ref.own_last_ref, bf16[97,32,128]{2,1,0:T(8,128)(2,1)} %collective-permute-done.12.first_ref.first_last_ref, ...), custom_call_target="tpu_custom_call", output_to_operand_aliasing={{0}: (9, {})} | custom-call | bytes 1048576 | tf_op jit(solution)/shard_map/update_1/pallas_call | solution.py:416
  (48 shorter events, 0.2 us)
Async XLA Ops:
  6.4 37.9 %all-to-all-start = ((bf16[32,16,2048]{2,1,0:T(8,128)(2,1)}), bf16[32,16,2048]{2,1,0:T(8,128)(2,1)S(1)}, u32[]{:S(2)}, u32[]{:S(2)}) async-start(bf16[32,16,2048]{2,1,0:T(8,128)(2,1)} %get-tuple-element.71), calls=%async_computation | async-start | bytes 4194304 | tf_op jit(solution)/shard_map/all_to_all | solution.py:512
  18.4 7.7 %copy-start.5 = (s32[2,3,128]{2,0,1:T(2,128)S(1)}, s32[2,3,128]{2,0,1:T(2,128)}, u32[]{:S(2)}) copy-start(s32[2,3,128]{2,0,1:T(2,128)} %param.12) | copy-start | bytes 9220
  18.4 7.7 %copy-start.7 = (s32[3]{0:T(128)S(1)}, s32[3]{0:T(128)}, u32[]{:S(2)}) copy-start(s32[3]{0:T(128)} %constant.90.clone) | copy-start | bytes 40
  18.4 10.3 %copy-start.6 = (bf16[2048,2]{0,1:T(2,128)(2,1)S(1)}, bf16[2048,2]{0,1:T(2,128)(2,1)}, u32[]{:S(2)}) copy-start(bf16[2048,2]{0,1:T(2,128)(2,1)} %param.11) | copy-start | bytes 24580
  18.4 22.7 %collective-permute-start.1 = (bf16[48,32,128]{2,1,0:T(8,128)(2,1)}, bf16[48,32,128]{2,1,0:T(8,128)(2,1)}, u32[]{:S(2)}, u32[]{:S(2)}) collective-permute-start(bf16[48,32,128]{2,1,0:T(8,128)(2,1)} %get-tuple-element.62.rest_1_), channel_id=1, source_target_pairs={{0,96},{32,0},{64,32},{96,64},{1,97},{33,1},{65,33},{97,65},{2,98}... | collective-permute-start | bytes 1179656 | tf_op jit(solution)/shard_map/ppermute | solution.py:478
  21.0 33.2 %collective-permute-start.2 = (bf16[48,32,128]{2,1,0:T(8,128)(2,1)}, bf16[48,32,128]{2,1,0:T(8,128)(2,1)}, u32[]{:S(2)}, u32[]{:S(2)}) collective-permute-start(bf16[48,32,128]{2,1,0:T(8,128)(2,1)} %get-tuple-element.62.rest_1_), channel_id=1, source_target_pairs={{0,32},{32,64},{64,96},{96,0},{1,33},{33,65},{65,97},{97,1},{2,34}... | collective-permute-start | bytes 1179656 | tf_op jit(solution)/shard_map/ppermute | solution.py:478
  21.0 20.1 %collective-permute-start = (bf16[48,32,128]{2,1,0:T(8,128)(2,1)}, bf16[48,32,128]{2,1,0:T(8,128)(2,1)}, u32[]{:S(2)}, u32[]{:S(2)}) collective-permute-start(bf16[48,32,128]{2,1,0:T(8,128)(2,1)} %get-tuple-element.61.rest_0_), channel_id=1, source_target_pairs={{0,32},{32,64},{64,96},{96,0},{1,33},{33,65},{65,97},{97,1},{2,34}... | collective-permute-start | bytes 1179656 | tf_op jit(solution)/shard_map/ppermute | solution.py:478
  21.2 34.8 %collective-permute-start.3 = (bf16[48,32,128]{2,1,0:T(8,128)(2,1)}, bf16[48,32,128]{2,1,0:T(8,128)(2,1)}, u32[]{:S(2)}, u32[]{:S(2)}) collective-permute-start(bf16[48,32,128]{2,1,0:T(8,128)(2,1)} %get-tuple-element.61.rest_0_), channel_id=1, source_target_pairs={{0,96},{32,0},{64,32},{96,64},{1,97},{33,1},{65,33},{97,65},{2,98}... | collective-permute-start | bytes 1179656 | tf_op jit(solution)/shard_map/ppermute | solution.py:478
  41.1 14.9 %collective-permute-start.4 = (bf16[48,32,128]{2,1,0:T(8,128)(2,1)}, bf16[48,32,128]{2,1,0:T(8,128)(2,1)S(1)}, u32[]{:S(2)}, u32[]{:S(2)}) collective-permute-start(bf16[48,32,128]{2,1,0:T(8,128)(2,1)} %collective-permute-done.rest_2_), channel_id=1, source_target_pairs={{0,32},{32,64},{64,96},{96,0},{1,33},{33,65},{65,97},{97,1},{2,34}... | collective-permute-start | bytes 1179656 | tf_op jit(solution)/shard_map/ppermute | solution.py:478
  41.1 17.5 %collective-permute-start.5 = (bf16[48,32,128]{2,1,0:T(8,128)(2,1)}, bf16[48,32,128]{2,1,0:T(8,128)(2,1)S(1)}, u32[]{:S(2)}, u32[]{:S(2)}) collective-permute-start(bf16[48,32,128]{2,1,0:T(8,128)(2,1)} %collective-permute-done.1.rest_5_), channel_id=1, source_target_pairs={{0,96},{32,0},{64,32},{96,64},{1,97},{33,1},{65,33},{97,65},{2,98}... | collective-permute-start | bytes 1179656 | tf_op jit(solution)/shard_map/ppermute | solution.py:478
  43.8 39.5 %collective-permute-start.7 = (bf16[48,32,128]{2,1,0:T(8,128)(2,1)}, bf16[48,32,128]{2,1,0:T(8,128)(2,1)}, u32[]{:S(2)}, u32[]{:S(2)}) collective-permute-start(bf16[48,32,128]{2,1,0:T(8,128)(2,1)} %get-tuple-element.79.rest_1_), channel_id=1, source_target_pairs={{0,96},{32,0},{64,32},{96,64},{1,97},{33,1},{65,33},{97,65},{2,98}... | collective-permute-start | bytes 1179656 | tf_op jit(solution)/shard_map/ppermute | solution.py:478
  44.3 1.3 copy-start.2
  45.6 37.7 %all-to-all-start.1 = ((bf16[32,16,2048]{2,1,0:T(8,128)(2,1)}), bf16[32,16,2048]{2,1,0:T(8,128)(2,1)}, u32[]{:S(2)}, u32[]{:S(2)}) async-start(bf16[32,16,2048]{2,1,0:T(8,128)(2,1)} %get-tuple-element.72), calls=%async_computation.1 | async-start | bytes 4194304 | tf_op jit(solution)/shard_map/all_to_all | solution.py:512
  54.2 40.7 %collective-permute-start.8 = (bf16[48,32,128]{2,1,0:T(8,128)(2,1)}, bf16[48,32,128]{2,1,0:T(8,128)(2,1)}, u32[]{:S(2)}, u32[]{:S(2)}) collective-permute-start(bf16[48,32,128]{2,1,0:T(8,128)(2,1)} %get-tuple-element.79.rest_1_), channel_id=1, source_target_pairs={{0,32},{32,64},{64,96},{96,0},{1,33},{33,65},{65,97},{97,1},{2,34}... | collective-permute-start | bytes 1179656 | tf_op jit(solution)/shard_map/ppermute | solution.py:478
  55.9 27.3 %collective-permute-start.6 = (bf16[48,32,128]{2,1,0:T(8,128)(2,1)}, bf16[48,32,128]{2,1,0:T(8,128)(2,1)}, u32[]{:S(2)}, u32[]{:S(2)}) collective-permute-start(bf16[48,32,128]{2,1,0:T(8,128)(2,1)} %get-tuple-element.78.rest_0_), channel_id=1, source_target_pairs={{0,32},{32,64},{64,96},{96,0},{1,33},{33,65},{65,97},{97,1},{2,34}... | collective-permute-start | bytes 1179656 | tf_op jit(solution)/shard_map/ppermute | solution.py:478
  56.0 2.6 %copy-start.8 = (bf16[48,32,128]{2,1,0:T(8,128)(2,1)}, bf16[48,32,128]{2,1,0:T(8,128)(2,1)S(1)}, u32[]{:S(2)}) copy-start(bf16[48,32,128]{2,1,0:T(8,128)(2,1)S(1)} %collective-permute-done.4.rest_6_) | copy-start | bytes 1179652
  56.0 42.1 %collective-permute-start.9 = (bf16[48,32,128]{2,1,0:T(8,128)(2,1)}, bf16[48,32,128]{2,1,0:T(8,128)(2,1)}, u32[]{:S(2)}, u32[]{:S(2)}) collective-permute-start(bf16[48,32,128]{2,1,0:T(8,128)(2,1)} %get-tuple-element.78.rest_0_), channel_id=1, source_target_pairs={{0,96},{32,0},{64,32},{96,64},{1,97},{33,1},{65,33},{97,65},{2,98}... | collective-permute-start | bytes 1179656 | tf_op jit(solution)/shard_map/ppermute | solution.py:478
  58.6 0.8 copy-start.9
  83.3 14.8 %collective-permute-start.10 = (bf16[48,32,128]{2,1,0:T(8,128)(2,1)}, bf16[48,32,128]{2,1,0:T(8,128)(2,1)S(1)}, u32[]{:S(2)}, u32[]{:S(2)}) collective-permute-start(bf16[48,32,128]{2,1,0:T(8,128)(2,1)} %collective-permute-done.6.rest_2_), channel_id=1, source_target_pairs={{0,32},{32,64},{64,96},{96,0},{1,33},{33,65},{65,97},{97,1},{2,34}... | collective-permute-start | bytes 1179656 | tf_op jit(solution)/shard_map/ppermute | solution.py:478
  84.2 13.9 %collective-permute-start.11 = (bf16[48,32,128]{2,1,0:T(8,128)(2,1)}, bf16[48,32,128]{2,1,0:T(8,128)(2,1)S(1)}, u32[]{:S(2)}, u32[]{:S(2)}) collective-permute-start(bf16[48,32,128]{2,1,0:T(8,128)(2,1)} %collective-permute-done.7.rest_5_), channel_id=1, source_target_pairs={{0,96},{32,0},{64,32},{96,64},{1,97},{33,1},{65,33},{97,65},{2,98}... | collective-permute-start | bytes 1179656 | tf_op jit(solution)/shard_map/ppermute | solution.py:478
  86.0 37.5 %collective-permute-start.15 = (bf16[97,32,128]{2,1,0:T(8,128)(2,1)}, bf16[97,32,128]{2,1,0:T(8,128)(2,1)}, u32[]{:S(2)}, u32[]{:S(2)}) collective-permute-start(bf16[97,32,128]{2,1,0:T(8,128)(2,1)} %get-tuple-element.91), channel_id=1, source_target_pairs={{0,32},{32,64},{64,96},{96,0},{1,33},{33,65},{65,97},{97,1},{2,34}... | collective-permute-start | bytes 2383880 | tf_op jit(solution)/shard_map/ppermute | solution.py:478
  86.0 37.5 %all-to-all-start.2 = ((bf16[32,16,2048]{2,1,0:T(8,128)(2,1)}), bf16[32,16,2048]{2,1,0:T(8,128)(2,1)}, u32[]{:S(2)}, u32[]{:S(2)}) async-start(bf16[32,16,2048]{2,1,0:T(8,128)(2,1)} %get-tuple-element.88), calls=%async_computation.2 | async-start | bytes 4194304 | tf_op jit(solution)/shard_map/all_to_all | solution.py:512
  94.9 28.7 %collective-permute-start.16 = (bf16[97,32,128]{2,1,0:T(8,128)(2,1)}, bf16[97,32,128]{2,1,0:T(8,128)(2,1)}, u32[]{:S(2)}, u32[]{:S(2)}) collective-permute-start(bf16[97,32,128]{2,1,0:T(8,128)(2,1)} %get-tuple-element.92), channel_id=1, source_target_pairs={{0,96},{32,0},{64,32},{96,64},{1,97},{33,1},{65,33},{97,65},{2,98}... | collective-permute-start | bytes 2383880 | tf_op jit(solution)/shard_map/ppermute | solution.py:478
  98.1 0.8 copy-start.10
  98.9 0.7 copy-start.11
  123.6 7.9 %copy-start.3 = (bf16[97,32,128]{2,1,0:T(8,128)(2,1)S(1)}, bf16[97,32,128]{2,1,0:T(8,128)(2,1)}, u32[]{:S(2)}) copy-start(bf16[97,32,128]{2,1,0:T(8,128)(2,1)} %get-tuple-element.95) | copy-start | bytes 2383876
  123.6 36.1 %all-to-all-start.3 = ((bf16[32,16,2048]{2,1,0:T(8,128)(2,1)}), bf16[32,16,2048]{2,1,0:T(8,128)(2,1)S(1)}, u32[]{:S(2)}, u32[]{:S(2)}) async-start(bf16[32,16,2048]{2,1,0:T(8,128)(2,1)} %get-tuple-element.100), calls=%async_computation.3 | async-start | bytes 4194304 | tf_op jit(solution)/shard_map/all_to_all | solution.py:512
  131.4 19.4 %copy-start.4 = (bf16[97,32,128]{2,1,0:T(8,128)(2,1)S(1)}, bf16[97,32,128]{2,1,0:T(8,128)(2,1)}, u32[]{:S(2)}) copy-start(bf16[97,32,128]{2,1,0:T(8,128)(2,1)} %get-tuple-element.85) | copy-start | bytes 2383876
  131.4 19.4 %collective-permute-start.13 = (bf16[97,32,128]{2,1,0:T(8,128)(2,1)}, bf16[97,32,128]{2,1,0:T(8,128)(2,1)S(1)}, u32[]{:S(2)}, u32[]{:S(2)}) collective-permute-start(bf16[97,32,128]{2,1,0:T(8,128)(2,1)} %get-tuple-element.86), channel_id=1, source_target_pairs={{0,96},{32,0},{64,32},{96,64},{1,97},{33,1},{65,33},{97,65},{2,98}... | collective-permute-start | bytes 2383880 | tf_op jit(solution)/shard_map/ppermute | solution.py:478
  132.9 20.4 %collective-permute-start.17 = (bf16[97,32,128]{2,1,0:T(8,128)(2,1)S(1)}, bf16[97,32,128]{2,1,0:T(8,128)(2,1)S(1)}, u32[]{:S(2)}, u32[]{:S(2)}) collective-permute-start(bf16[97,32,128]{2,1,0:T(8,128)(2,1)S(1)} %add.117), channel_id=1, source_target_pairs={{0,32},{32,64},{64,96},{96,0},{1,33},{33,65},{65,97},{97,1},{2,34}... | collective-permute-start | bytes 2383880 | tf_op jit(solution)/shard_map/ppermute | solution.py:478
  134.4 36.0 %collective-permute-start.12 = (bf16[97,32,128]{2,1,0:T(8,128)(2,1)}, bf16[97,32,128]{2,1,0:T(8,128)(2,1)}, u32[]{:S(2)}, u32[]{:S(2)}) collective-permute-start(bf16[97,32,128]{2,1,0:T(8,128)(2,1)} %get-tuple-element.84), channel_id=1, source_target_pairs={{0,32},{32,64},{64,96},{96,0},{1,33},{33,65},{65,97},{97,1},{2,34}... | collective-permute-start | bytes 2383880 | tf_op jit(solution)/shard_map/ppermute | solution.py:478
  151.9 18.5 %collective-permute-start.14 = (bf16[97,32,128]{2,1,0:T(8,128)(2,1)}, bf16[97,32,128]{2,1,0:T(8,128)(2,1)}, u32[]{:S(2)}, u32[]{:S(2)}) collective-permute-start(bf16[97,32,128]{2,1,0:T(8,128)(2,1)} %add.116), channel_id=1, source_target_pairs={{0,96},{32,0},{64,32},{96,64},{1,97},{33,1},{65,33},{97,65},{2,98}... | collective-permute-start | bytes 2383880 | tf_op jit(solution)/shard_map/ppermute | solution.py:478
  153.3 0.9 copy-start.1
  154.2 5.5 %copy-start = (s32[1,64,8]{1,2,0:T(8,128)S(1)}, s32[1,64,8]{1,2,0:T(8,128)}, u32[]{:S(2)}) copy-start(s32[1,64,8]{1,2,0:T(8,128)} %param.10) | copy-start | bytes 6148

commit v8 on v7

--- a/solution.py
+++ b/solution.py
@@ -398,7 +398,7 @@
             pltpu.VMEM((FF + BS, D), BF16),
             pltpu.VMEM((1, D), F32),
         ],
-        compiler_params=params(56),
+        compiler_params=params(46),
         cost_estimate=cost(150 * 10**9, 1 << 20),
         name="expert_%d" % member,
     )(*tables, place, arrived, router_rows, *pieces)

time: 176 us -> 177 us (level)
  waiting for transfers between devices: 34.4 us -> 36.9 us
    unnamed x24 -> x32, local copies, waits for them, and re-layouts: 3.84 us -> 7.33 us
    ppermute x18, waiting for transfers between devices: 32.2 us -> 34.4 us  [shift(): lax.ppermute(array, 'dp', [(i, (i + step) % owners) for i in range(owners)])]
  transfers between devices with their start and end apart: 22 -> 22, of which waited for: 5 -> 6; matrix products, arithmetic and copies ran while one was open for 5% -> 3% of each run, Pallas kernels for 35% -> 34%
where the time goes in v8:
time: 177 us; the launch traced here: 176 us
  Pallas kernels  69.1 us (39%)
  starting transfers between devices  56.2 us (32%)
  waiting for transfers between devices  36.9 us (21%)
  local copies, waits for them, and re-layouts  9.6 us (5%)
  other arithmetic  3.16 us (2%)
    pallas_call x2, Pallas kernels, run_expert(): pl.pallas_call(functools.partial(expert_kernel, member=member), in_specs=...  46.2 us
    all_to_all x4, starting transfers between devices, exchange(): lax.all_to_all(array, 'expert', split_axis=0, concat_axis=0, tiled=True)  34.7 us
    ppermute x18, waiting for transfers between devices, shift(): lax.ppermute(array, 'dp', [(i, (i + step) % owners) for i in range(owners)])  34.4 us
    ppermute x18, starting transfers between devices, shift(): lax.ppermute(array, 'dp', [(i, (i + step) % owners) for i in range(owners)])  21.5 us
    unnamed x32, local copies, waits for them, and re-layouts  7.33 us
    pallas_call x2, Pallas kernels, update(): pl.pallas_call(functools.partial(update_kernel, member=member), grid=(ste...  7.27 us
    pallas_call x1, Pallas kernels, pick(): pl.pallas_call(functools.partial(pick_kernel, locals_count=locals_count),...  5.69 us
    pallas_call x1, Pallas kernels, combine(): pl.pallas_call(functools.partial(combine_kernel, locals_count=locals_coun...  5 us
  transfers between devices with their start and end apart: 22, of which 6 were waited for; matrix products, arithmetic and copies ran while one was open for 3% of the time, Pallas kernels for 34%

profile of v8, /device:TPU:1, one launch (start us, length us, event | category | flops | bytes accessed | tf_op | source)
XLA Modules:
  0.0 176.0 jit_solution(15088960607572924115)
XLA Ops:
  0.6 5.7 %pick.1 = (bf16[32,16,2048]{2,1,0:T(8,128)(2,1)}, bf16[32,16,2048]{2,1,0:T(8,128)(2,1)}) custom-call(s32[8,64]{1,0:T(8,128)} %bitcast.12, bf16[256,2048]{1,0:T(8,128)(2,1)} %tokens_ref.1, bf16[256,2048]{1,0:T(8,128)(2,1)} %grads_ref.1), custom_call_target="tpu_custom_call" | custom-call | bytes 1048576 | tf_op jit(solution)/shard_map/pick/pallas_call | solution.py:340
  6.3 9.7 %all-to-all-start = ((bf16[32,16,2048]{2,1,0:T(8,128)(2,1)}), bf16[32,16,2048]{2,1,0:T(8,128)(2,1)}, u32[]{:S(2)}, u32[]{:S(2)}) async-start(bf16[32,16,2048]{2,1,0:T(8,128)(2,1)} %get-tuple-element.71), calls=%async_computation | async-start | bytes 4194304 | tf_op jit(solution)/shard_map/all_to_all | solution.py:512
  16.0 2.5 %pack_0.1 = (bf16[48,32,128]{2,1,0:T(8,128)(2,1)}, bf16[48,32,128]{2,1,0:T(8,128)(2,1)}) custom-call(f32[192,4096]{1,0:T(8,128)} %bitcast.14), custom_call_target="tpu_custom_call" | custom-call | bytes 1048576 | tf_op jit(solution)/shard_map/pack_0/pallas_call | solution.py:355
  18.4 2.5 %collective-permute-start.1 = (bf16[48,32,128]{2,1,0:T(8,128)(2,1)}, bf16[48,32,128]{2,1,0:T(8,128)(2,1)S(1)}, u32[]{:S(2)}, u32[]{:S(2)}) collective-permute-start(bf16[48,32,128]{2,1,0:T(8,128)(2,1)} %get-tuple-element.62.rest_1_), channel_id=1, source_target_pairs={{0,96},{32,0},{64,32},{96,64},{1,97},{33,1},{65,33},{97,65},{2,98}... | collective-permute-start | bytes 1179656 | tf_op jit(solution)/shard_map/ppermute | solution.py:478
  21.0 0.2 collective-permute-start
  21.2 2.5 %collective-permute-start.3 = (bf16[48,32,128]{2,1,0:T(8,128)(2,1)}, bf16[48,32,128]{2,1,0:T(8,128)(2,1)S(1)}, u32[]{:S(2)}, u32[]{:S(2)}) collective-permute-start(bf16[48,32,128]{2,1,0:T(8,128)(2,1)} %get-tuple-element.61.rest_0_), channel_id=1, source_target_pairs={{0,96},{32,0},{64,32},{96,64},{1,97},{33,1},{65,33},{97,65},{2,98}... | collective-permute-start | bytes 1179656 | tf_op jit(solution)/shard_map/ppermute | solution.py:478
  23.7 2.4 %pack_1.1 = (bf16[48,32,128]{2,1,0:T(8,128)(2,1)}, bf16[48,32,128]{2,1,0:T(8,128)(2,1)}) custom-call(f32[192,4096]{1,0:T(8,128)} %bitcast.15), custom_call_target="tpu_custom_call" | custom-call | bytes 1048576 | tf_op jit(solution)/shard_map/pack_1/pallas_call | solution.py:355
  26.2 0.2 multiply_add_fusion
  26.5 0.4 select_reduce_fusion
  27.0 1.0 reshape.146
  28.0 0.5 copy.23
  28.5 0.1 reshape.145.router_ref
  28.6 12.4 %collective-permute-done.rest_2_ = bf16[48,32,128]{2,1,0:T(8,128)(2,1)S(1)} collective-permute-done((bf16[48,32,128]{2,1,0:T(8,128)(2,1)}, bf16[48,32,128]{2,1,0:T(8,128)(2,1)S(1)}, u32[]{:S(2)}, u32[]{:S(2)}) %collective-permute-start) | collective-permute-done | bytes 393248 | tf_op jit(solution)/shard_map/ppermute | solution.py:478
  41.0 2.7 %collective-permute-start.5 = (bf16[48,32,128]{2,1,0:T(8,128)(2,1)S(1)}, bf16[48,32,128]{2,1,0:T(8,128)(2,1)S(1)}, u32[]{:S(2)}, u32[]{:S(2)}) collective-permute-start(bf16[48,32,128]{2,1,0:T(8,128)(2,1)S(1)} %collective-permute-done.1.rest_5_), channel_id=1, source_target_pairs={{0,96},{32,0},{64,32},{96,64},{1,97},{33,1},{65,33},{97,65},{2,98}... | collective-permute-start | bytes 1179656 | tf_op jit(solution)/shard_map/ppermute | solution.py:478
  43.7 0.6 all-to-all-done.arriving_ref
  44.3 8.5 %all-to-all-start.1 = ((bf16[32,16,2048]{2,1,0:T(8,128)(2,1)}), bf16[32,16,2048]{2,1,0:T(8,128)(2,1)}, u32[]{:S(2)}, u32[]{:S(2)}) async-start(bf16[32,16,2048]{2,1,0:T(8,128)(2,1)} %get-tuple-element.72), calls=%async_computation.1 | async-start | bytes 4194304 | tf_op jit(solution)/shard_map/all_to_all | solution.py:512
  52.9 1.8 %collective-permute-start.8 = (bf16[48,32,128]{2,1,0:T(8,128)(2,1)}, bf16[48,32,128]{2,1,0:T(8,128)(2,1)}, u32[]{:S(2)}, u32[]{:S(2)}) collective-permute-start(bf16[48,32,128]{2,1,0:T(8,128)(2,1)} %get-tuple-element.79.rest_1_), channel_id=1, source_target_pairs={{0,32},{32,64},{64,96},{96,0},{1,33},{33,65},{65,97},{97,1},{2,34}... | collective-permute-start | bytes 1179656 | tf_op jit(solution)/shard_map/ppermute | solution.py:478
  54.7 0.1 collective-permute-start.6
  54.8 0.7 copy-done.8
  55.5 2.6 %collective-permute-start.9 = (bf16[48,32,128]{2,1,0:T(8,128)(2,1)}, bf16[48,32,128]{2,1,0:T(8,128)(2,1)}, u32[]{:S(2)}, u32[]{:S(2)}) collective-permute-start(bf16[48,32,128]{2,1,0:T(8,128)(2,1)} %get-tuple-element.78.rest_0_), channel_id=1, source_target_pairs={{0,96},{32,0},{64,32},{96,64},{1,97},{33,1},{65,33},{97,65},{2,98}... | collective-permute-start | bytes 1179656 | tf_op jit(solution)/shard_map/ppermute | solution.py:478
  58.1 0.7 copy-done.10
  58.8 1.0 copy-done.9
  59.8 1.0 copy-done.11
  60.8 23.2 %expert_0.1 = (bf16[32,16,2048]{2,1,0:T(8,128)(2,1)}, bf16[97,32,128]{2,1,0:T(8,128)(2,1)S(1)}, bf16[97,32,128]{2,1,0:T(8,128)(2,1)S(1)}, bf16[97,32,128]{2,1,0:T(8,128)(2,1)}, bf16[97,32,128]{2,1,0:T(8,128)(2,1)}) custom-call(s32[2304]{0:T(1024)S(1)} %add.111.inverse_ref, s32[768]{0:T(1024)S(1)} %reshape.141.row_ref, s32[768]{0:T(1024)S(1)} %reshape.142.lane_ref, ...), custom_call_target="tpu_custom_call" | custom-call | flops 149999992832 | bytes 1048576 | tf_op jit(solution)/shard_map/expert_0/pallas_call | solution.py:376
  84.0 0.9 copy-done
  85.0 2.7 %collective-permute-start.11 = (bf16[48,32,128]{2,1,0:T(8,128)(2,1)}, bf16[48,32,128]{2,1,0:T(8,128)(2,1)S(1)}, u32[]{:S(2)}, u32[]{:S(2)}) collective-permute-start(bf16[48,32,128]{2,1,0:T(8,128)(2,1)} %collective-permute-done.7.rest_5_), channel_id=1, source_target_pairs={{0,96},{32,0},{64,32},{96,64},{1,97},{33,1},{65,33},{97,65},{2,98}... | collective-permute-start | bytes 1179656 | tf_op jit(solution)/shard_map/ppermute | solution.py:478
  87.7 8.9 %all-to-all-start.2 = ((bf16[32,16,2048]{2,1,0:T(8,128)(2,1)}), bf16[32,16,2048]{2,1,0:T(8,128)(2,1)}, u32[]{:S(2)}, u32[]{:S(2)}) async-start(bf16[32,16,2048]{2,1,0:T(8,128)(2,1)} %get-tuple-element.88), calls=%async_computation.2 | async-start | bytes 4194304 | tf_op jit(solution)/shard_map/all_to_all | solution.py:512
  96.6 3.2 %collective-permute-start.16 = (bf16[97,32,128]{2,1,0:T(8,128)(2,1)}, bf16[97,32,128]{2,1,0:T(8,128)(2,1)}, u32[]{:S(2)}, u32[]{:S(2)}) collective-permute-start(bf16[97,32,128]{2,1,0:T(8,128)(2,1)} %get-tuple-element.92), channel_id=1, source_target_pairs={{0,96},{32,0},{64,32},{96,64},{1,97},{33,1},{65,33},{97,65},{2,98}... | collective-permute-start | bytes 2383880 | tf_op jit(solution)/shard_map/ppermute | solution.py:478
  99.8 23.0 %expert_1.1 = (bf16[32,16,2048]{2,1,0:T(8,128)(2,1)}, bf16[97,32,128]{2,1,0:T(8,128)(2,1)S(1)}, bf16[97,32,128]{2,1,0:T(8,128)(2,1)}, bf16[97,32,128]{2,1,0:T(8,128)(2,1)S(1)}, bf16[97,32,128]{2,1,0:T(8,128)(2,1)S(1)}) custom-call(s32[2304]{0:T(1024)S(1)} %add.111.inverse_ref, s32[768]{0:T(1024)S(1)} %reshape.141.row_ref, s32[768]{0:T(1024)S(1)} %reshape.142.lane_ref, ...), custom_call_target="tpu_custom_call" | custom-call | flops 149999992832 | bytes 1048576 | tf_op jit(solution)/shard_map/expert_1/pallas_call | solution.py:376
  122.9 0.9 copy-done.1
  123.8 0.9 copy-done.2
  124.7 0.9 copy-done.5
  125.6 7.7 %all-to-all-start.3 = ((bf16[32,16,2048]{2,1,0:T(8,128)(2,1)}), bf16[32,16,2048]{2,1,0:T(8,128)(2,1)S(1)}, u32[]{:S(2)}, u32[]{:S(2)}) async-start(bf16[32,16,2048]{2,1,0:T(8,128)(2,1)} %get-tuple-element.100), calls=%async_computation.3 | async-start | bytes 4194304 | tf_op jit(solution)/shard_map/all_to_all | solution.py:512
  133.3 0.2 collective-permute-start.13
  133.5 1.3 add.117
  134.9 1.4 collective-permute-start.17
  136.2 0.1 collective-permute-start.12
  136.3 16.3 %collective-permute-done.13 = bf16[97,32,128]{2,1,0:T(8,128)(2,1)S(1)} collective-permute-done((bf16[97,32,128]{2,1,0:T(8,128)(2,1)}, bf16[97,32,128]{2,1,0:T(8,128)(2,1)S(1)}, u32[]{:S(2)}, u32[]{:S(2)}) %collective-permute-start.13) | collective-permute-done | bytes 794656 | tf_op jit(solution)/shard_map/ppermute | solution.py:478
  152.6 1.1 add.116
  153.7 1.4 collective-permute-start.14
  155.1 0.6 broadcast_in_dim.52.router_ref
  155.8 0.3 copy-done.12
  156.0 3.6 %update_0.1 = (f32[192,4096]{1,0:T(8,128)}, f32[3,2,32]{2,1,0:T(2,128)}, f32[2,512]{1,0:T(2,128)}) custom-call(bf16[97,32,128]{2,1,0:T(8,128)(2,1)} %copy-done, bf16[97,32,128]{2,1,0:T(8,128)(2,1)} %collective-permute-done.16.first_ref.first_last_ref, bf16[97,32,128]{2,1,0:T(8,128)(2,1)} %copy-done.12, bf16[97,32,128]{2,1,0:T(8,128)(2,1)} %copy-done, ...), custom_call_target="tpu_custom_call" | custom-call | bytes 1048576 | tf_op jit(solution)/shard_map/update_0/pallas_call | solution.py:416
  159.7 1.9 %all-to-all-done.3.rest_1_ = bf16[32,16,2048]{2,1,0:T(8,128)(2,1)S(1)} async-done(((bf16[32,16,2048]{2,1,0:T(8,128)(2,1)}), bf16[32,16,2048]{2,1,0:T(8,128)(2,1)S(1)}, u32[]{:S(2)}, u32[]{:S(2)}) %all-to-all-start.3) | async-done | bytes 2097184 | tf_op jit(solution)/shard_map/all_to_all | solution.py:512
  161.6 5.0 %combine.1 = (bf16[256,2048]{1,0:T(8,128)(2,1)}, bf16[256,2048]{1,0:T(8,128)(2,1)}) custom-call(s32[8,64]{1,0:T(8,128)S(1)} %bitcast.13, bf16[32,16,2048]{2,1,0:T(8,128)(2,1)} %all-to-all-done.2.rest_0_, bf16[32,16,2048]{2,1,0:T(8,128)(2,1)S(1)} %all-to-all-done.3.rest_1_), custom_call_target="tpu_custom_call" | custom-call | flops 149999992832 | bytes 1048576 | tf_op jit(solution)/shard_map/combine/pallas_call | solution.py:441
  166.6 5.5 %collective-permute-done.12.first_ref.first_last_ref = bf16[97,32,128]{2,1,0:T(8,128)(2,1)} collective-permute-done((bf16[97,32,128]{2,1,0:T(8,128)(2,1)}, bf16[97,32,128]{2,1,0:T(8,128)(2,1)}, u32[]{:S(2)}, u32[]{:S(2)}) %collective-permute-start.12) | collective-permute-done | bytes 794656 | tf_op jit(solution)/shard_map/ppermute | solution.py:478
  172.1 0.2 collective-permute-done.14.second_ref.second_last_ref
  172.2 3.6 %update_1.1 = (f32[192,4096]{1,0:T(8,128)}, f32[3,2,32]{2,1,0:T(2,128)}, f32[2,512]{1,0:T(2,128)}) custom-call(bf16[97,32,128]{2,1,0:T(8,128)(2,1)} %copy-done.1, bf16[97,32,128]{2,1,0:T(8,128)(2,1)} %collective-permute-done.12.first_ref.first_last_ref, ...), custom_call_target="tpu_custom_call", output_to_operand_aliasing={{0}: (9, {})} | custom-call | bytes 1048576 | tf_op jit(solution)/shard_map/update_1/pallas_call | solution.py:416
  (56 shorter events, 0.3 us)
Async XLA Ops:
  6.3 38.0 %all-to-all-start = ((bf16[32,16,2048]{2,1,0:T(8,128)(2,1)}), bf16[32,16,2048]{2,1,0:T(8,128)(2,1)}, u32[]{:S(2)}, u32[]{:S(2)}) async-start(bf16[32,16,2048]{2,1,0:T(8,128)(2,1)} %get-tuple-element.71), calls=%async_computation | async-start | bytes 4194304 | tf_op jit(solution)/shard_map/all_to_all | solution.py:512
  18.4 7.7 %copy-start.13 = (s32[2,3,128]{2,0,1:T(2,128)S(1)}, s32[2,3,128]{2,0,1:T(2,128)}, u32[]{:S(2)}) copy-start(s32[2,3,128]{2,0,1:T(2,128)} %param.12) | copy-start | bytes 9220
  18.4 7.7 %copy-start.15 = (s32[3]{0:T(128)S(1)}, s32[3]{0:T(128)}, u32[]{:S(2)}) copy-start(s32[3]{0:T(128)} %constant.90.clone) | copy-start | bytes 40
  18.4 8.5 %copy-start.14 = (bf16[2048,2]{0,1:T(2,128)(2,1)S(1)}, bf16[2048,2]{0,1:T(2,128)(2,1)}, u32[]{:S(2)}) copy-start(bf16[2048,2]{0,1:T(2,128)(2,1)} %param.11) | copy-start | bytes 24580
  18.4 22.6 %collective-permute-start.1 = (bf16[48,32,128]{2,1,0:T(8,128)(2,1)}, bf16[48,32,128]{2,1,0:T(8,128)(2,1)S(1)}, u32[]{:S(2)}, u32[]{:S(2)}) collective-permute-start(bf16[48,32,128]{2,1,0:T(8,128)(2,1)} %get-tuple-element.62.rest_1_), channel_id=1, source_target_pairs={{0,96},{32,0},{64,32},{96,64},{1,97},{33,1},{65,33},{97,65},{2,98}... | collective-permute-start | bytes 1179656 | tf_op jit(solution)/shard_map/ppermute | solution.py:478
  21.0 31.9 %collective-permute-start.2 = (bf16[48,32,128]{2,1,0:T(8,128)(2,1)}, bf16[48,32,128]{2,1,0:T(8,128)(2,1)S(1)}, u32[]{:S(2)}, u32[]{:S(2)}) collective-permute-start(bf16[48,32,128]{2,1,0:T(8,128)(2,1)} %get-tuple-element.62.rest_1_), channel_id=1, source_target_pairs={{0,32},{32,64},{64,96},{96,0},{1,33},{33,65},{65,97},{97,1},{2,34}... | collective-permute-start | bytes 1179656 | tf_op jit(solution)/shard_map/ppermute | solution.py:478
  21.0 20.0 %collective-permute-start = (bf16[48,32,128]{2,1,0:T(8,128)(2,1)}, bf16[48,32,128]{2,1,0:T(8,128)(2,1)S(1)}, u32[]{:S(2)}, u32[]{:S(2)}) collective-permute-start(bf16[48,32,128]{2,1,0:T(8,128)(2,1)} %get-tuple-element.61.rest_0_), channel_id=1, source_target_pairs={{0,32},{32,64},{64,96},{96,0},{1,33},{33,65},{65,97},{97,1},{2,34}... | collective-permute-start | bytes 1179656 | tf_op jit(solution)/shard_map/ppermute | solution.py:478
  21.2 33.5 %collective-permute-start.3 = (bf16[48,32,128]{2,1,0:T(8,128)(2,1)}, bf16[48,32,128]{2,1,0:T(8,128)(2,1)S(1)}, u32[]{:S(2)}, u32[]{:S(2)}) collective-permute-start(bf16[48,32,128]{2,1,0:T(8,128)(2,1)} %get-tuple-element.61.rest_0_), channel_id=1, source_target_pairs={{0,96},{32,0},{64,32},{96,64},{1,97},{33,1},{65,33},{97,65},{2,98}... | collective-permute-start | bytes 1179656 | tf_op jit(solution)/shard_map/ppermute | solution.py:478
  41.0 13.7 %collective-permute-start.4 = (bf16[48,32,128]{2,1,0:T(8,128)(2,1)S(1)}, bf16[48,32,128]{2,1,0:T(8,128)(2,1)S(1)}, u32[]{:S(2)}, u32[]{:S(2)}) collective-permute-start(bf16[48,32,128]{2,1,0:T(8,128)(2,1)S(1)} %collective-permute-done.rest_2_), channel_id=1, source_target_pairs={{0,32},{32,64},{64,96},{96,0},{1,33},{33,65},{65,97},{97,1},{2,34}... | collective-permute-start | bytes 1179656 | tf_op jit(solution)/shard_map/ppermute | solution.py:478
  41.0 17.1 %collective-permute-start.5 = (bf16[48,32,128]{2,1,0:T(8,128)(2,1)S(1)}, bf16[48,32,128]{2,1,0:T(8,128)(2,1)S(1)}, u32[]{:S(2)}, u32[]{:S(2)}) collective-permute-start(bf16[48,32,128]{2,1,0:T(8,128)(2,1)S(1)} %collective-permute-done.1.rest_5_), channel_id=1, source_target_pairs={{0,96},{32,0},{64,32},{96,64},{1,97},{33,1},{65,33},{97,65},{2,98}... | collective-permute-start | bytes 1179656 | tf_op jit(solution)/shard_map/ppermute | solution.py:478
  43.7 41.2 %collective-permute-start.7 = (bf16[48,32,128]{2,1,0:T(8,128)(2,1)}, bf16[48,32,128]{2,1,0:T(8,128)(2,1)}, u32[]{:S(2)}, u32[]{:S(2)}) collective-permute-start(bf16[48,32,128]{2,1,0:T(8,128)(2,1)} %get-tuple-element.79.rest_1_), channel_id=1, source_target_pairs={{0,96},{32,0},{64,32},{96,64},{1,97},{33,1},{65,33},{97,65},{2,98}... | collective-permute-start | bytes 1179656 | tf_op jit(solution)/shard_map/ppermute | solution.py:478
  44.3 14.5 %copy-start.6 = (bf16[48,32,128]{2,1,0:T(8,128)(2,1)S(1)}, bf16[48,32,128]{2,1,0:T(8,128)(2,1)}, u32[]{:S(2)}) copy-start(bf16[48,32,128]{2,1,0:T(8,128)(2,1)} %get-tuple-element.61.rest_0_) | copy-start | bytes 1179652
  44.3 14.5 %copy-start.7 = (bf16[48,32,128]{2,1,0:T(8,128)(2,1)S(1)}, bf16[48,32,128]{2,1,0:T(8,128)(2,1)}, u32[]{:S(2)}) copy-start(bf16[48,32,128]{2,1,0:T(8,128)(2,1)} %get-tuple-element.62.rest_1_) | copy-start | bytes 1179652
  44.3 40.6 %all-to-all-start.1 = ((bf16[32,16,2048]{2,1,0:T(8,128)(2,1)}), bf16[32,16,2048]{2,1,0:T(8,128)(2,1)}, u32[]{:S(2)}, u32[]{:S(2)}) async-start(bf16[32,16,2048]{2,1,0:T(8,128)(2,1)} %get-tuple-element.72), calls=%async_computation.1 | async-start | bytes 4194304 | tf_op jit(solution)/shard_map/all_to_all | solution.py:512
  52.9 43.7 %collective-permute-start.8 = (bf16[48,32,128]{2,1,0:T(8,128)(2,1)}, bf16[48,32,128]{2,1,0:T(8,128)(2,1)}, u32[]{:S(2)}, u32[]{:S(2)}) collective-permute-start(bf16[48,32,128]{2,1,0:T(8,128)(2,1)} %get-tuple-element.79.rest_1_), channel_id=1, source_target_pairs={{0,32},{32,64},{64,96},{96,0},{1,33},{33,65},{65,97},{97,1},{2,34}... | collective-permute-start | bytes 1179656 | tf_op jit(solution)/shard_map/ppermute | solution.py:478
  54.7 30.3 %collective-permute-start.6 = (bf16[48,32,128]{2,1,0:T(8,128)(2,1)}, bf16[48,32,128]{2,1,0:T(8,128)(2,1)}, u32[]{:S(2)}, u32[]{:S(2)}) collective-permute-start(bf16[48,32,128]{2,1,0:T(8,128)(2,1)} %get-tuple-element.78.rest_0_), channel_id=1, source_target_pairs={{0,32},{32,64},{64,96},{96,0},{1,33},{33,65},{65,97},{97,1},{2,34}... | collective-permute-start | bytes 1179656 | tf_op jit(solution)/shard_map/ppermute | solution.py:478
  54.8 0.7 copy-start.8
  55.5 44.3 %collective-permute-start.9 = (bf16[48,32,128]{2,1,0:T(8,128)(2,1)}, bf16[48,32,128]{2,1,0:T(8,128)(2,1)}, u32[]{:S(2)}, u32[]{:S(2)}) collective-permute-start(bf16[48,32,128]{2,1,0:T(8,128)(2,1)} %get-tuple-element.78.rest_0_), channel_id=1, source_target_pairs={{0,96},{32,0},{64,32},{96,64},{1,97},{33,1},{65,33},{97,65},{2,98}... | collective-permute-start | bytes 1179656 | tf_op jit(solution)/shard_map/ppermute | solution.py:478
  58.1 0.7 copy-start.10
  58.8 1.0 copy-start.9
  59.8 1.0 copy-start.11
  84.0 0.9 copy-start
  84.9 14.9 %collective-permute-start.10 = (bf16[48,32,128]{2,1,0:T(8,128)(2,1)}, bf16[48,32,128]{2,1,0:T(8,128)(2,1)S(1)}, u32[]{:S(2)}, u32[]{:S(2)}) collective-permute-start(bf16[48,32,128]{2,1,0:T(8,128)(2,1)} %collective-permute-done.6.rest_2_), channel_id=1, source_target_pairs={{0,32},{32,64},{64,96},{96,0},{1,33},{33,65},{65,97},{97,1},{2,34}... | collective-permute-start | bytes 1179656 | tf_op jit(solution)/shard_map/ppermute | solution.py:478
  85.0 14.8 %collective-permute-start.11 = (bf16[48,32,128]{2,1,0:T(8,128)(2,1)}, bf16[48,32,128]{2,1,0:T(8,128)(2,1)S(1)}, u32[]{:S(2)}, u32[]{:S(2)}) collective-permute-start(bf16[48,32,128]{2,1,0:T(8,128)(2,1)} %collective-permute-done.7.rest_5_), channel_id=1, source_target_pairs={{0,96},{32,0},{64,32},{96,64},{1,97},{33,1},{65,33},{97,65},{2,98}... | collective-permute-start | bytes 1179656 | tf_op jit(solution)/shard_map/ppermute | solution.py:478
  87.7 37.9 %collective-permute-start.15 = (bf16[97,32,128]{2,1,0:T(8,128)(2,1)}, bf16[97,32,128]{2,1,0:T(8,128)(2,1)}, u32[]{:S(2)}, u32[]{:S(2)}) collective-permute-start(bf16[97,32,128]{2,1,0:T(8,128)(2,1)} %get-tuple-element.91), channel_id=1, source_target_pairs={{0,32},{32,64},{64,96},{96,0},{1,33},{33,65},{65,97},{97,1},{2,34}... | collective-permute-start | bytes 2383880 | tf_op jit(solution)/shard_map/ppermute | solution.py:478
  87.7 37.9 %all-to-all-start.2 = ((bf16[32,16,2048]{2,1,0:T(8,128)(2,1)}), bf16[32,16,2048]{2,1,0:T(8,128)(2,1)}, u32[]{:S(2)}, u32[]{:S(2)}) async-start(bf16[32,16,2048]{2,1,0:T(8,128)(2,1)} %get-tuple-element.88), calls=%async_computation.2 | async-start | bytes 4194304 | tf_op jit(solution)/shard_map/all_to_all | solution.py:512
  96.6 29.0 %collective-permute-start.16 = (bf16[97,32,128]{2,1,0:T(8,128)(2,1)}, bf16[97,32,128]{2,1,0:T(8,128)(2,1)}, u32[]{:S(2)}, u32[]{:S(2)}) collective-permute-start(bf16[97,32,128]{2,1,0:T(8,128)(2,1)} %get-tuple-element.92), channel_id=1, source_target_pairs={{0,96},{32,0},{64,32},{96,64},{1,97},{33,1},{65,33},{97,65},{2,98}... | collective-permute-start | bytes 2383880 | tf_op jit(solution)/shard_map/ppermute | solution.py:478
  122.9 0.9 copy-start.1
  123.8 0.9 copy-start.2
  124.7 0.9 copy-start.5
  125.6 36.0 %all-to-all-start.3 = ((bf16[32,16,2048]{2,1,0:T(8,128)(2,1)}), bf16[32,16,2048]{2,1,0:T(8,128)(2,1)S(1)}, u32[]{:S(2)}, u32[]{:S(2)}) async-start(bf16[32,16,2048]{2,1,0:T(8,128)(2,1)} %get-tuple-element.100), calls=%async_computation.3 | async-start | bytes 4194304 | tf_op jit(solution)/shard_map/all_to_all | solution.py:512
  133.3 19.4 %copy-start.3 = (bf16[97,32,128]{2,1,0:T(8,128)(2,1)S(1)}, bf16[97,32,128]{2,1,0:T(8,128)(2,1)}, u32[]{:S(2)}) copy-start(bf16[97,32,128]{2,1,0:T(8,128)(2,1)} %copy-done.2) | copy-start | bytes 2383876
  133.3 19.4 %collective-permute-start.13 = (bf16[97,32,128]{2,1,0:T(8,128)(2,1)}, bf16[97,32,128]{2,1,0:T(8,128)(2,1)S(1)}, u32[]{:S(2)}, u32[]{:S(2)}) collective-permute-start(bf16[97,32,128]{2,1,0:T(8,128)(2,1)} %copy-done.5), channel_id=1, source_target_pairs={{0,96},{32,0},{64,32},{96,64},{1,97},{33,1},{65,33},{97,65},{2,98}... | collective-permute-start | bytes 2383880 | tf_op jit(solution)/shard_map/ppermute | solution.py:478
  134.9 20.3 %collective-permute-start.17 = (bf16[97,32,128]{2,1,0:T(8,128)(2,1)S(1)}, bf16[97,32,128]{2,1,0:T(8,128)(2,1)S(1)}, u32[]{:S(2)}, u32[]{:S(2)}) collective-permute-start(bf16[97,32,128]{2,1,0:T(8,128)(2,1)S(1)} %add.117), channel_id=1, source_target_pairs={{0,32},{32,64},{64,96},{96,0},{1,33},{33,65},{65,97},{97,1},{2,34}... | collective-permute-start | bytes 2383880 | tf_op jit(solution)/shard_map/ppermute | solution.py:478
  136.2 35.8 %collective-permute-start.12 = (bf16[97,32,128]{2,1,0:T(8,128)(2,1)}, bf16[97,32,128]{2,1,0:T(8,128)(2,1)}, u32[]{:S(2)}, u32[]{:S(2)}) collective-permute-start(bf16[97,32,128]{2,1,0:T(8,128)(2,1)} %get-tuple-element.84), channel_id=1, source_target_pairs={{0,32},{32,64},{64,96},{96,0},{1,33},{33,65},{65,97},{97,1},{2,34}... | collective-permute-start | bytes 2383880 | tf_op jit(solution)/shard_map/ppermute | solution.py:478
  153.7 18.5 %collective-permute-start.14 = (bf16[97,32,128]{2,1,0:T(8,128)(2,1)}, bf16[97,32,128]{2,1,0:T(8,128)(2,1)}, u32[]{:S(2)}, u32[]{:S(2)}) collective-permute-start(bf16[97,32,128]{2,1,0:T(8,128)(2,1)} %add.116), channel_id=1, source_target_pairs={{0,96},{32,0},{64,32},{96,64},{1,97},{33,1},{65,33},{97,65},{2,98}... | collective-permute-start | bytes 2383880 | tf_op jit(solution)/shard_map/ppermute | solution.py:478
  155.1 0.9 copy-start.12
  156.0 5.6 %copy-start.4 = (s32[1,64,8]{1,2,0:T(8,128)S(1)}, s32[1,64,8]{1,2,0:T(8,128)}, u32[]{:S(2)}) copy-start(s32[1,64,8]{1,2,0:T(8,128)} %param.10) | copy-start | bytes 6148

commit v9 on v8

--- a/solution.py
+++ b/solution.py
@@ -155,20 +155,20 @@
         target_ref[pl.ds(row, 32), col : col + 128] = jnp.where(half, one, crossed)
         target_ref[pl.ds(row + 32, 32), col : col + 128] = jnp.where(half, crossed, two)
 
-    @pl.loop(0, D // BS)
+    @pl.loop(0, D // BS, unroll=2)
     def _(r):
         row = pl.multiple_of(r * BS, BS)
         for matrix in range(2):
             for pair in range(FF // BS // 2):
                 place(wide_ref, matrix, r * (FF // BS) + 2 * pair, row, matrix * FF + 128 * pair)
 
-    @pl.loop(0, FF // BS)
+    @pl.loop(0, FF // BS, unroll=2)
     def _(r):
         row = pl.multiple_of(r * BS, BS)
         for pair in range(D // BS // 2):
             place(down_ref, 2, r * (D // BS) + 2 * pair, row, 128 * pair)
 
-    @pl.loop(0, 2 * FF // 512)
+    @pl.loop(0, 2 * FF // 512, unroll=3)
     def _(n):
         cols = pl.ds(pl.multiple_of(n * 512, 512), 512)
         pre_ref[:, cols] = dot(rows_ref[...], wide_ref[:, cols])
@@ -398,7 +398,7 @@
             pltpu.VMEM((FF + BS, D), BF16),
             pltpu.VMEM((1, D), F32),
         ],
-        compiler_params=params(46),
+        compiler_params=params(51),
         cost_estimate=cost(150 * 10**9, 1 << 20),
         name="expert_%d" % member,
     )(*tables, place, arrived, router_rows, *pieces)

time: 177 us -> 171 us (0.966)
  local copies, waits for them, and re-layouts: 9.6 us -> 4.06 us
  waiting for transfers between devices: 36.9 us -> 39.6 us
  Pallas kernels: 69.1 us -> 66.7 us
    unnamed x32 -> x22, local copies, waits for them, and re-layouts: 7.33 us -> 1.79 us
    all_to_all x4, starting transfers between devices: 34.7 us -> 30.8 us  [exchange(): lax.all_to_all(array, 'expert', split_axis=0, concat_axis=0, tiled=True)]
    ppermute x18, starting transfers between devices: 21.5 us -> 24.4 us  [shift(): lax.ppermute(array, 'dp', [(i, (i + step) % owners) for i in range(owners)])]
    pallas_call x2, Pallas kernels: 46.2 us -> 43.8 us  [run_expert(): pl.pallas_call(functools.partial(expert_kernel, member=member), in_specs=...]
where the time goes in v9:
time: 171 us; the launch traced here: 170 us
  Pallas kernels  66.7 us (39%)
  starting transfers between devices  55.3 us (32%)
  waiting for transfers between devices  39.6 us (23%)
  local copies, waits for them, and re-layouts  4.06 us (2%)
  other arithmetic  3.18 us (2%)
    pallas_call x2, Pallas kernels, run_expert(): pl.pallas_call(functools.partial(expert_kernel, member=member), in_specs=...  43.8 us
    ppermute x18, waiting for transfers between devices, shift(): lax.ppermute(array, 'dp', [(i, (i + step) % owners) for i in range(owners)])  35.4 us
    all_to_all x4, starting transfers between devices, exchange(): lax.all_to_all(array, 'expert', split_axis=0, concat_axis=0, tiled=True)  30.8 us
    ppermute x18, starting transfers between devices, shift(): lax.ppermute(array, 'dp', [(i, (i + step) % owners) for i in range(owners)])  24.4 us
    pallas_call x2, Pallas kernels, update(): pl.pallas_call(functools.partial(update_kernel, member=member), grid=(ste...  7.29 us
    pallas_call x1, Pallas kernels, pick(): pl.pallas_call(functools.partial(pick_kernel, locals_count=locals_count),...  5.71 us
    pallas_call x1, Pallas kernels, combine(): pl.pallas_call(functools.partial(combine_kernel, locals_count=locals_coun...  4.99 us
    pallas_call x2, Pallas kernels, pack(): pl.pallas_call(pack_kernel, grid=(2,), in_specs=[pl.BlockSpec((mine, BS *...  4.89 us
  transfers between devices with their start and end apart: 22, of which 6 were waited for; matrix products, arithmetic and copies ran while one was open for 3% of the time, Pallas kernels for 34%

profile of v9, /device:TPU:1, one launch (start us, length us, event | category | flops | bytes accessed | tf_op | source)
XLA Modules:
  0.0 169.9 jit_solution(336767162409134510)
XLA Ops:
  0.6 5.7 %pick.1 = (bf16[32,16,2048]{2,1,0:T(8,128)(2,1)}, bf16[32,16,2048]{2,1,0:T(8,128)(2,1)}) custom-call(s32[8,64]{1,0:T(8,128)} %bitcast.12, bf16[256,2048]{1,0:T(8,128)(2,1)} %tokens_ref.1, bf16[256,2048]{1,0:T(8,128)(2,1)} %grads_ref.1), custom_call_target="tpu_custom_call" | custom-call | bytes 1048576 | tf_op jit(solution)/shard_map/pick/pallas_call | solution.py:340
  6.3 9.7 %all-to-all-start = ((bf16[32,16,2048]{2,1,0:T(8,128)(2,1)}), bf16[32,16,2048]{2,1,0:T(8,128)(2,1)}, u32[]{:S(2)}, u32[]{:S(2)}) async-start(bf16[32,16,2048]{2,1,0:T(8,128)(2,1)} %get-tuple-element.71), calls=%async_computation | async-start | bytes 4194304 | tf_op jit(solution)/shard_map/all_to_all | solution.py:512
  16.0 2.5 %pack_0.1 = (bf16[48,32,128]{2,1,0:T(8,128)(2,1)}, bf16[48,32,128]{2,1,0:T(8,128)(2,1)}) custom-call(f32[192,4096]{1,0:T(8,128)} %bitcast.14), custom_call_target="tpu_custom_call" | custom-call | bytes 1048576 | tf_op jit(solution)/shard_map/pack_0/pallas_call | solution.py:355
  18.5 2.5 %collective-permute-start.1 = (bf16[48,32,128]{2,1,0:T(8,128)(2,1)}, bf16[48,32,128]{2,1,0:T(8,128)(2,1)S(1)}, u32[]{:S(2)}, u32[]{:S(2)}) collective-permute-start(bf16[48,32,128]{2,1,0:T(8,128)(2,1)} %get-tuple-element.62.rest_1_), channel_id=1, source_target_pairs={{0,96},{32,0},{64,32},{96,64},{1,97},{33,1},{65,33},{97,65},{2,98}... | collective-permute-start | bytes 1179656 | tf_op jit(solution)/shard_map/ppermute | solution.py:478
  21.0 0.0 collective-permute-start.2
  21.0 0.2 collective-permute-start
  21.2 2.5 %collective-permute-start.3 = (bf16[48,32,128]{2,1,0:T(8,128)(2,1)}, bf16[48,32,128]{2,1,0:T(8,128)(2,1)S(1)}, u32[]{:S(2)}, u32[]{:S(2)}) collective-permute-start(bf16[48,32,128]{2,1,0:T(8,128)(2,1)} %get-tuple-element.61.rest_0_), channel_id=1, source_target_pairs={{0,96},{32,0},{64,32},{96,64},{1,97},{33,1},{65,33},{97,65},{2,98}... | collective-permute-start | bytes 1179656 | tf_op jit(solution)/shard_map/ppermute | solution.py:478
  23.7 2.4 %pack_1.1 = (bf16[48,32,128]{2,1,0:T(8,128)(2,1)}, bf16[48,32,128]{2,1,0:T(8,128)(2,1)}) custom-call(f32[192,4096]{1,0:T(8,128)} %bitcast.15), custom_call_target="tpu_custom_call" | custom-call | bytes 1048576 | tf_op jit(solution)/shard_map/pack_1/pallas_call | solution.py:355
  26.2 0.2 multiply_add_fusion
  26.5 0.1 add_add_fusion
  26.6 0.4 select_reduce_fusion
  27.0 1.0 reshape.146
  28.0 0.5 copy.23
  28.5 0.1 reshape.145.router_ref
  28.6 12.4 %collective-permute-done.rest_2_ = bf16[48,32,128]{2,1,0:T(8,128)(2,1)S(1)} collective-permute-done((bf16[48,32,128]{2,1,0:T(8,128)(2,1)}, bf16[48,32,128]{2,1,0:T(8,128)(2,1)S(1)}, u32[]{:S(2)}, u32[]{:S(2)}) %collective-permute-start) | collective-permute-done | bytes 393248 | tf_op jit(solution)/shard_map/ppermute | solution.py:478
  41.0 2.7 %collective-permute-start.5 = (bf16[48,32,128]{2,1,0:T(8,128)(2,1)S(1)}, bf16[48,32,128]{2,1,0:T(8,128)(2,1)S(1)}, u32[]{:S(2)}, u32[]{:S(2)}) collective-permute-start(bf16[48,32,128]{2,1,0:T(8,128)(2,1)S(1)} %collective-permute-done.1.rest_5_), channel_id=1, source_target_pairs={{0,96},{32,0},{64,32},{96,64},{1,97},{33,1},{65,33},{97,65},{2,98}... | collective-permute-start | bytes 1179656 | tf_op jit(solution)/shard_map/ppermute | solution.py:478
  43.7 0.0 collective-permute-start.7
  43.7 0.6 all-to-all-done.arriving_ref
  44.4 8.5 %all-to-all-start.1 = ((bf16[32,16,2048]{2,1,0:T(8,128)(2,1)}), bf16[32,16,2048]{2,1,0:T(8,128)(2,1)}, u32[]{:S(2)}, u32[]{:S(2)}) async-start(bf16[32,16,2048]{2,1,0:T(8,128)(2,1)} %get-tuple-element.72), calls=%async_computation.1 | async-start | bytes 4194304 | tf_op jit(solution)/shard_map/all_to_all | solution.py:512
  52.9 1.8 %collective-permute-start.8 = (bf16[48,32,128]{2,1,0:T(8,128)(2,1)}, bf16[48,32,128]{2,1,0:T(8,128)(2,1)}, u32[]{:S(2)}, u32[]{:S(2)}) collective-permute-start(bf16[48,32,128]{2,1,0:T(8,128)(2,1)} %get-tuple-element.79.rest_1_), channel_id=1, source_target_pairs={{0,32},{32,64},{64,96},{96,0},{1,33},{33,65},{65,97},{97,1},{2,34}... | collective-permute-start | bytes 1179656 | tf_op jit(solution)/shard_map/ppermute | solution.py:478
  54.7 0.1 collective-permute-start.6
  54.8 2.6 %collective-permute-start.9 = (bf16[48,32,128]{2,1,0:T(8,128)(2,1)}, bf16[48,32,128]{2,1,0:T(8,128)(2,1)}, u32[]{:S(2)}, u32[]{:S(2)}) collective-permute-start(bf16[48,32,128]{2,1,0:T(8,128)(2,1)} %get-tuple-element.78.rest_0_), channel_id=1, source_target_pairs={{0,96},{32,0},{64,32},{96,64},{1,97},{33,1},{65,33},{97,65},{2,98}... | collective-permute-start | bytes 1179656 | tf_op jit(solution)/shard_map/ppermute | solution.py:478
  57.4 0.8 copy-done.9
  58.1 21.9 %expert_0.1 = (bf16[32,16,2048]{2,1,0:T(8,128)(2,1)}, bf16[97,32,128]{2,1,0:T(8,128)(2,1)}, bf16[97,32,128]{2,1,0:T(8,128)(2,1)}, bf16[97,32,128]{2,1,0:T(8,128)(2,1)}, bf16[97,32,128]{2,1,0:T(8,128)(2,1)}) custom-call(s32[2304]{0:T(1024)S(1)} %add.111.inverse_ref, s32[768]{0:T(1024)S(1)} %reshape.141.row_ref, s32[768]{0:T(1024)S(1)} %reshape.142.lane_ref, ...), custom_call_target="tpu_custom_call" | custom-call | flops 149999992832 | bytes 1048576 | tf_op jit(solution)/shard_map/expert_0/pallas_call | solution.py:376
  80.0 1.2 all-to-all-done.1.arriving_ref
  81.2 1.7 %collective-permute-start.10 = (bf16[48,32,128]{2,1,0:T(8,128)(2,1)}, bf16[48,32,128]{2,1,0:T(8,128)(2,1)S(1)}, u32[]{:S(2)}, u32[]{:S(2)}) collective-permute-start(bf16[48,32,128]{2,1,0:T(8,128)(2,1)} %collective-permute-done.6.rest_2_), channel_id=1, source_target_pairs={{0,32},{32,64},{64,96},{96,0},{1,33},{33,65},{65,97},{97,1},{2,34}... | collective-permute-start | bytes 1179656 | tf_op jit(solution)/shard_map/ppermute | solution.py:478
  82.9 1.0 collective-permute-start.11
  83.9 0.5 collective-permute-start.15
  84.4 7.2 %all-to-all-start.2 = ((bf16[32,16,2048]{2,1,0:T(8,128)(2,1)}), bf16[32,16,2048]{2,1,0:T(8,128)(2,1)}, u32[]{:S(2)}, u32[]{:S(2)}) async-start(bf16[32,16,2048]{2,1,0:T(8,128)(2,1)} %get-tuple-element.88), calls=%async_computation.2 | async-start | bytes 4194304 | tf_op jit(solution)/shard_map/all_to_all | solution.py:512
  91.6 3.2 %collective-permute-start.16 = (bf16[97,32,128]{2,1,0:T(8,128)(2,1)}, bf16[97,32,128]{2,1,0:T(8,128)(2,1)}, u32[]{:S(2)}, u32[]{:S(2)}) collective-permute-start(bf16[97,32,128]{2,1,0:T(8,128)(2,1)} %get-tuple-element.92), channel_id=1, source_target_pairs={{0,96},{32,0},{64,32},{96,64},{1,97},{33,1},{65,33},{97,65},{2,98}... | collective-permute-start | bytes 2383880 | tf_op jit(solution)/shard_map/ppermute | solution.py:478
  94.9 0.7 copy-done.10
  95.6 21.9 %expert_1.1 = (bf16[32,16,2048]{2,1,0:T(8,128)(2,1)}, bf16[97,32,128]{2,1,0:T(8,128)(2,1)}, bf16[97,32,128]{2,1,0:T(8,128)(2,1)}, bf16[97,32,128]{2,1,0:T(8,128)(2,1)}, bf16[97,32,128]{2,1,0:T(8,128)(2,1)}) custom-call(s32[2304]{0:T(1024)S(1)} %add.111.inverse_ref, s32[768]{0:T(1024)S(1)} %reshape.141.row_ref, s32[768]{0:T(1024)S(1)} %reshape.142.lane_ref, ...), custom_call_target="tpu_custom_call" | custom-call | flops 149999992832 | bytes 1048576 | tf_op jit(solution)/shard_map/expert_1/pallas_call | solution.py:376
  117.6 2.4 %all-to-all-done.2.rest_0_ = bf16[32,16,2048]{2,1,0:T(8,128)(2,1)} async-done(((bf16[32,16,2048]{2,1,0:T(8,128)(2,1)}), bf16[32,16,2048]{2,1,0:T(8,128)(2,1)}, u32[]{:S(2)}, u32[]{:S(2)}) %all-to-all-start.2) | async-done | bytes 2097184 | tf_op jit(solution)/shard_map/all_to_all | solution.py:512
  120.0 5.5 %all-to-all-start.3 = ((bf16[32,16,2048]{2,1,0:T(8,128)(2,1)}), bf16[32,16,2048]{2,1,0:T(8,128)(2,1)S(1)}, u32[]{:S(2)}, u32[]{:S(2)}) async-start(bf16[32,16,2048]{2,1,0:T(8,128)(2,1)} %get-tuple-element.100), calls=%async_computation.3 | async-start | bytes 4194304 | tf_op jit(solution)/shard_map/all_to_all | solution.py:512
  125.4 2.2 %collective-permute-start.13 = (bf16[97,32,128]{2,1,0:T(8,128)(2,1)}, bf16[97,32,128]{2,1,0:T(8,128)(2,1)S(1)}, u32[]{:S(2)}, u32[]{:S(2)}) collective-permute-start(bf16[97,32,128]{2,1,0:T(8,128)(2,1)} %get-tuple-element.86), channel_id=1, source_target_pairs={{0,96},{32,0},{64,32},{96,64},{1,97},{33,1},{65,33},{97,65},{2,98}... | collective-permute-start | bytes 2383880 | tf_op jit(solution)/shard_map/ppermute | solution.py:478
  127.7 1.3 add.117
  129.0 0.1 collective-permute-start.17
  129.1 0.1 collective-permute-start.12
  129.2 15.6 %collective-permute-done.13 = bf16[97,32,128]{2,1,0:T(8,128)(2,1)S(1)} collective-permute-done((bf16[97,32,128]{2,1,0:T(8,128)(2,1)}, bf16[97,32,128]{2,1,0:T(8,128)(2,1)S(1)}, u32[]{:S(2)}, u32[]{:S(2)}) %collective-permute-start.13) | collective-permute-done | bytes 794656 | tf_op jit(solution)/shard_map/ppermute | solution.py:478
  144.8 1.1 add.116
  145.9 3.2 %collective-permute-start.14 = (bf16[97,32,128]{2,1,0:T(8,128)(2,1)}, bf16[97,32,128]{2,1,0:T(8,128)(2,1)}, u32[]{:S(2)}, u32[]{:S(2)}) collective-permute-start(bf16[97,32,128]{2,1,0:T(8,128)(2,1)} %add.116), channel_id=1, source_target_pairs={{0,96},{32,0},{64,32},{96,64},{1,97},{33,1},{65,33},{97,65},{2,98}... | collective-permute-start | bytes 2383880 | tf_op jit(solution)/shard_map/ppermute | solution.py:478
  149.2 0.6 broadcast_in_dim.52.router_ref
  149.8 0.3 copy-done.3
  150.1 3.6 %update_0.1 = (f32[192,4096]{1,0:T(8,128)}, f32[3,2,32]{2,1,0:T(2,128)}, f32[2,512]{1,0:T(2,128)}) custom-call(bf16[97,32,128]{2,1,0:T(8,128)(2,1)} %get-tuple-element.93.own_ref.own_last_ref, bf16[97,32,128]{2,1,0:T(8,128)(2,1)} %collective-permute-done.16.first_ref.first_last_ref, bf16[97,32,128]{2,1,0:T(8,128)(2,1)} %copy-done.3, ...), custom_call_target="tpu_custom_call" | custom-call | bytes 1048576 | tf_op jit(solution)/shard_map/update_0/pallas_call | solution.py:416
  153.7 0.0 all-to-all-done.3.rest_1_
  153.7 5.0 %combine.1 = (bf16[256,2048]{1,0:T(8,128)(2,1)}, bf16[256,2048]{1,0:T(8,128)(2,1)}) custom-call(s32[8,64]{1,0:T(8,128)S(1)} %bitcast.13, bf16[32,16,2048]{2,1,0:T(8,128)(2,1)} %all-to-all-done.2.rest_0_, bf16[32,16,2048]{2,1,0:T(8,128)(2,1)S(1)} %all-to-all-done.3.rest_1_), custom_call_target="tpu_custom_call" | custom-call | flops 149999992832 | bytes 1048576 | tf_op jit(solution)/shard_map/combine/pallas_call | solution.py:441
  158.7 7.3 %collective-permute-done.12.first_ref.first_last_ref = bf16[97,32,128]{2,1,0:T(8,128)(2,1)} collective-permute-done((bf16[97,32,128]{2,1,0:T(8,128)(2,1)}, bf16[97,32,128]{2,1,0:T(8,128)(2,1)}, u32[]{:S(2)}, u32[]{:S(2)}) %collective-permute-start.12) | collective-permute-done | bytes 794656 | tf_op jit(solution)/shard_map/ppermute | solution.py:478
  166.1 3.6 %update_1.1 = (f32[192,4096]{1,0:T(8,128)}, f32[3,2,32]{2,1,0:T(2,128)}, f32[2,512]{1,0:T(2,128)}) custom-call(bf16[97,32,128]{2,1,0:T(8,128)(2,1)} %get-tuple-element.104.own_ref.own_last_ref, bf16[97,32,128]{2,1,0:T(8,128)(2,1)} %collective-permute-done.12.first_ref.first_last_ref, ...), custom_call_target="tpu_custom_call", output_to_operand_aliasing={{0}: (9, {})} | custom-call | bytes 1048576 | tf_op jit(solution)/shard_map/update_1/pallas_call | solution.py:416
  (46 shorter events, 0.2 us)
Async XLA Ops:
  6.3 38.0 %all-to-all-start = ((bf16[32,16,2048]{2,1,0:T(8,128)(2,1)}), bf16[32,16,2048]{2,1,0:T(8,128)(2,1)}, u32[]{:S(2)}, u32[]{:S(2)}) async-start(bf16[32,16,2048]{2,1,0:T(8,128)(2,1)} %get-tuple-element.71), calls=%async_computation | async-start | bytes 4194304 | tf_op jit(solution)/shard_map/all_to_all | solution.py:512
  18.5 7.7 %copy-start.6 = (s32[2,3,128]{2,0,1:T(2,128)S(1)}, s32[2,3,128]{2,0,1:T(2,128)}, u32[]{:S(2)}) copy-start(s32[2,3,128]{2,0,1:T(2,128)} %param.12) | copy-start | bytes 9220
  18.5 7.7 %copy-start.8 = (s32[3]{0:T(128)S(1)}, s32[3]{0:T(128)}, u32[]{:S(2)}) copy-start(s32[3]{0:T(128)} %constant.90.clone) | copy-start | bytes 40
  18.5 8.5 %copy-start.7 = (bf16[2048,2]{0,1:T(2,128)(2,1)S(1)}, bf16[2048,2]{0,1:T(2,128)(2,1)}, u32[]{:S(2)}) copy-start(bf16[2048,2]{0,1:T(2,128)(2,1)} %param.11) | copy-start | bytes 24580
  18.5 22.6 %collective-permute-start.1 = (bf16[48,32,128]{2,1,0:T(8,128)(2,1)}, bf16[48,32,128]{2,1,0:T(8,128)(2,1)S(1)}, u32[]{:S(2)}, u32[]{:S(2)}) collective-permute-start(bf16[48,32,128]{2,1,0:T(8,128)(2,1)} %get-tuple-element.62.rest_1_), channel_id=1, source_target_pairs={{0,96},{32,0},{64,32},{96,64},{1,97},{33,1},{65,33},{97,65},{2,98}... | collective-permute-start | bytes 1179656 | tf_op jit(solution)/shard_map/ppermute | solution.py:478
  21.0 31.9 %collective-permute-start.2 = (bf16[48,32,128]{2,1,0:T(8,128)(2,1)}, bf16[48,32,128]{2,1,0:T(8,128)(2,1)S(1)}, u32[]{:S(2)}, u32[]{:S(2)}) collective-permute-start(bf16[48,32,128]{2,1,0:T(8,128)(2,1)} %get-tuple-element.62.rest_1_), channel_id=1, source_target_pairs={{0,32},{32,64},{64,96},{96,0},{1,33},{33,65},{65,97},{97,1},{2,34}... | collective-permute-start | bytes 1179656 | tf_op jit(solution)/shard_map/ppermute | solution.py:478
  21.0 20.0 %collective-permute-start = (bf16[48,32,128]{2,1,0:T(8,128)(2,1)}, bf16[48,32,128]{2,1,0:T(8,128)(2,1)S(1)}, u32[]{:S(2)}, u32[]{:S(2)}) collective-permute-start(bf16[48,32,128]{2,1,0:T(8,128)(2,1)} %get-tuple-element.61.rest_0_), channel_id=1, source_target_pairs={{0,32},{32,64},{64,96},{96,0},{1,33},{33,65},{65,97},{97,1},{2,34}... | collective-permute-start | bytes 1179656 | tf_op jit(solution)/shard_map/ppermute | solution.py:478
  21.2 33.5 %collective-permute-start.3 = (bf16[48,32,128]{2,1,0:T(8,128)(2,1)}, bf16[48,32,128]{2,1,0:T(8,128)(2,1)S(1)}, u32[]{:S(2)}, u32[]{:S(2)}) collective-permute-start(bf16[48,32,128]{2,1,0:T(8,128)(2,1)} %get-tuple-element.61.rest_0_), channel_id=1, source_target_pairs={{0,96},{32,0},{64,32},{96,64},{1,97},{33,1},{65,33},{97,65},{2,98}... | collective-permute-start | bytes 1179656 | tf_op jit(solution)/shard_map/ppermute | solution.py:478
  41.0 13.7 %collective-permute-start.4 = (bf16[48,32,128]{2,1,0:T(8,128)(2,1)S(1)}, bf16[48,32,128]{2,1,0:T(8,128)(2,1)S(1)}, u32[]{:S(2)}, u32[]{:S(2)}) collective-permute-start(bf16[48,32,128]{2,1,0:T(8,128)(2,1)S(1)} %collective-permute-done.rest_2_), channel_id=1, source_target_pairs={{0,32},{32,64},{64,96},{96,0},{1,33},{33,65},{65,97},{97,1},{2,34}... | collective-permute-start | bytes 1179656 | tf_op jit(solution)/shard_map/ppermute | solution.py:478
  41.0 16.3 %collective-permute-start.5 = (bf16[48,32,128]{2,1,0:T(8,128)(2,1)S(1)}, bf16[48,32,128]{2,1,0:T(8,128)(2,1)S(1)}, u32[]{:S(2)}, u32[]{:S(2)}) collective-permute-start(bf16[48,32,128]{2,1,0:T(8,128)(2,1)S(1)} %collective-permute-done.1.rest_5_), channel_id=1, source_target_pairs={{0,96},{32,0},{64,32},{96,64},{1,97},{33,1},{65,33},{97,65},{2,98}... | collective-permute-start | bytes 1179656 | tf_op jit(solution)/shard_map/ppermute | solution.py:478
  43.7 36.3 %collective-permute-start.7 = (bf16[48,32,128]{2,1,0:T(8,128)(2,1)}, bf16[48,32,128]{2,1,0:T(8,128)(2,1)}, u32[]{:S(2)}, u32[]{:S(2)}) collective-permute-start(bf16[48,32,128]{2,1,0:T(8,128)(2,1)} %get-tuple-element.79.rest_1_), channel_id=1, source_target_pairs={{0,96},{32,0},{64,32},{96,64},{1,97},{33,1},{65,33},{97,65},{2,98}... | collective-permute-start | bytes 1179656 | tf_op jit(solution)/shard_map/ppermute | solution.py:478
  44.3 13.8 %copy-start.1 = (bf16[48,32,128]{2,1,0:T(8,128)(2,1)S(1)}, bf16[48,32,128]{2,1,0:T(8,128)(2,1)}, u32[]{:S(2)}) copy-start(bf16[48,32,128]{2,1,0:T(8,128)(2,1)} %get-tuple-element.61.rest_0_) | copy-start | bytes 1179652
  44.3 13.8 %copy-start.2 = (bf16[48,32,128]{2,1,0:T(8,128)(2,1)S(1)}, bf16[48,32,128]{2,1,0:T(8,128)(2,1)}, u32[]{:S(2)}) copy-start(bf16[48,32,128]{2,1,0:T(8,128)(2,1)} %get-tuple-element.62.rest_1_) | copy-start | bytes 1179652
  44.4 36.9 %all-to-all-start.1 = ((bf16[32,16,2048]{2,1,0:T(8,128)(2,1)}), bf16[32,16,2048]{2,1,0:T(8,128)(2,1)}, u32[]{:S(2)}, u32[]{:S(2)}) async-start(bf16[32,16,2048]{2,1,0:T(8,128)(2,1)} %get-tuple-element.72), calls=%async_computation.1 | async-start | bytes 4194304 | tf_op jit(solution)/shard_map/all_to_all | solution.py:512
  52.9 38.7 %collective-permute-start.8 = (bf16[48,32,128]{2,1,0:T(8,128)(2,1)}, bf16[48,32,128]{2,1,0:T(8,128)(2,1)}, u32[]{:S(2)}, u32[]{:S(2)}) collective-permute-start(bf16[48,32,128]{2,1,0:T(8,128)(2,1)} %get-tuple-element.79.rest_1_), channel_id=1, source_target_pairs={{0,32},{32,64},{64,96},{96,0},{1,33},{33,65},{65,97},{97,1},{2,34}... | collective-permute-start | bytes 1179656 | tf_op jit(solution)/shard_map/ppermute | solution.py:478
  54.7 25.3 %collective-permute-start.6 = (bf16[48,32,128]{2,1,0:T(8,128)(2,1)}, bf16[48,32,128]{2,1,0:T(8,128)(2,1)}, u32[]{:S(2)}, u32[]{:S(2)}) collective-permute-start(bf16[48,32,128]{2,1,0:T(8,128)(2,1)} %get-tuple-element.78.rest_0_), channel_id=1, source_target_pairs={{0,32},{32,64},{64,96},{96,0},{1,33},{33,65},{65,97},{97,1},{2,34}... | collective-permute-start | bytes 1179656 | tf_op jit(solution)/shard_map/ppermute | solution.py:478
  54.8 40.1 %collective-permute-start.9 = (bf16[48,32,128]{2,1,0:T(8,128)(2,1)}, bf16[48,32,128]{2,1,0:T(8,128)(2,1)}, u32[]{:S(2)}, u32[]{:S(2)}) collective-permute-start(bf16[48,32,128]{2,1,0:T(8,128)(2,1)} %get-tuple-element.78.rest_0_), channel_id=1, source_target_pairs={{0,96},{32,0},{64,32},{96,64},{1,97},{33,1},{65,33},{97,65},{2,98}... | collective-permute-start | bytes 1179656 | tf_op jit(solution)/shard_map/ppermute | solution.py:478
  57.4 0.8 copy-start.9
  81.2 13.7 %collective-permute-start.10 = (bf16[48,32,128]{2,1,0:T(8,128)(2,1)}, bf16[48,32,128]{2,1,0:T(8,128)(2,1)S(1)}, u32[]{:S(2)}, u32[]{:S(2)}) collective-permute-start(bf16[48,32,128]{2,1,0:T(8,128)(2,1)} %collective-permute-done.6.rest_2_), channel_id=1, source_target_pairs={{0,32},{32,64},{64,96},{96,0},{1,33},{33,65},{65,97},{97,1},{2,34}... | collective-permute-start | bytes 1179656 | tf_op jit(solution)/shard_map/ppermute | solution.py:478
  82.9 11.9 %collective-permute-start.11 = (bf16[48,32,128]{2,1,0:T(8,128)(2,1)}, bf16[48,32,128]{2,1,0:T(8,128)(2,1)S(1)}, u32[]{:S(2)}, u32[]{:S(2)}) collective-permute-start(bf16[48,32,128]{2,1,0:T(8,128)(2,1)} %collective-permute-done.7.rest_5_), channel_id=1, source_target_pairs={{0,96},{32,0},{64,32},{96,64},{1,97},{33,1},{65,33},{97,65},{2,98}... | collective-permute-start | bytes 1179656 | tf_op jit(solution)/shard_map/ppermute | solution.py:478
  83.9 33.7 %collective-permute-start.15 = (bf16[97,32,128]{2,1,0:T(8,128)(2,1)}, bf16[97,32,128]{2,1,0:T(8,128)(2,1)}, u32[]{:S(2)}, u32[]{:S(2)}) collective-permute-start(bf16[97,32,128]{2,1,0:T(8,128)(2,1)} %get-tuple-element.91), channel_id=1, source_target_pairs={{0,32},{32,64},{64,96},{96,0},{1,33},{33,65},{65,97},{97,1},{2,34}... | collective-permute-start | bytes 2383880 | tf_op jit(solution)/shard_map/ppermute | solution.py:478
  84.4 35.6 %all-to-all-start.2 = ((bf16[32,16,2048]{2,1,0:T(8,128)(2,1)}), bf16[32,16,2048]{2,1,0:T(8,128)(2,1)}, u32[]{:S(2)}, u32[]{:S(2)}) async-start(bf16[32,16,2048]{2,1,0:T(8,128)(2,1)} %get-tuple-element.88), calls=%async_computation.2 | async-start | bytes 4194304 | tf_op jit(solution)/shard_map/all_to_all | solution.py:512
  91.6 26.0 %collective-permute-start.16 = (bf16[97,32,128]{2,1,0:T(8,128)(2,1)}, bf16[97,32,128]{2,1,0:T(8,128)(2,1)}, u32[]{:S(2)}, u32[]{:S(2)}) collective-permute-start(bf16[97,32,128]{2,1,0:T(8,128)(2,1)} %get-tuple-element.92), channel_id=1, source_target_pairs={{0,96},{32,0},{64,32},{96,64},{1,97},{33,1},{65,33},{97,65},{2,98}... | collective-permute-start | bytes 2383880 | tf_op jit(solution)/shard_map/ppermute | solution.py:478
  94.9 0.7 copy-start.10
  120.0 7.7 %copy-start.4 = (bf16[97,32,128]{2,1,0:T(8,128)(2,1)S(1)}, bf16[97,32,128]{2,1,0:T(8,128)(2,1)}, u32[]{:S(2)}) copy-start(bf16[97,32,128]{2,1,0:T(8,128)(2,1)} %get-tuple-element.95) | copy-start | bytes 2383876
  120.0 33.8 %all-to-all-start.3 = ((bf16[32,16,2048]{2,1,0:T(8,128)(2,1)}), bf16[32,16,2048]{2,1,0:T(8,128)(2,1)S(1)}, u32[]{:S(2)}, u32[]{:S(2)}) async-start(bf16[32,16,2048]{2,1,0:T(8,128)(2,1)} %get-tuple-element.100), calls=%async_computation.3 | async-start | bytes 4194304 | tf_op jit(solution)/shard_map/all_to_all | solution.py:512
  125.4 19.4 %copy-start.5 = (bf16[97,32,128]{2,1,0:T(8,128)(2,1)S(1)}, bf16[97,32,128]{2,1,0:T(8,128)(2,1)}, u32[]{:S(2)}) copy-start(bf16[97,32,128]{2,1,0:T(8,128)(2,1)} %get-tuple-element.85) | copy-start | bytes 2383876
  125.4 19.4 %collective-permute-start.13 = (bf16[97,32,128]{2,1,0:T(8,128)(2,1)}, bf16[97,32,128]{2,1,0:T(8,128)(2,1)S(1)}, u32[]{:S(2)}, u32[]{:S(2)}) collective-permute-start(bf16[97,32,128]{2,1,0:T(8,128)(2,1)} %get-tuple-element.86), channel_id=1, source_target_pairs={{0,96},{32,0},{64,32},{96,64},{1,97},{33,1},{65,33},{97,65},{2,98}... | collective-permute-start | bytes 2383880 | tf_op jit(solution)/shard_map/ppermute | solution.py:478
  129.0 20.1 %collective-permute-start.17 = (bf16[97,32,128]{2,1,0:T(8,128)(2,1)S(1)}, bf16[97,32,128]{2,1,0:T(8,128)(2,1)S(1)}, u32[]{:S(2)}, u32[]{:S(2)}) collective-permute-start(bf16[97,32,128]{2,1,0:T(8,128)(2,1)S(1)} %add.117), channel_id=1, source_target_pairs={{0,32},{32,64},{64,96},{96,0},{1,33},{33,65},{65,97},{97,1},{2,34}... | collective-permute-start | bytes 2383880 | tf_op jit(solution)/shard_map/ppermute | solution.py:478
  129.1 37.0 %collective-permute-start.12 = (bf16[97,32,128]{2,1,0:T(8,128)(2,1)}, bf16[97,32,128]{2,1,0:T(8,128)(2,1)}, u32[]{:S(2)}, u32[]{:S(2)}) collective-permute-start(bf16[97,32,128]{2,1,0:T(8,128)(2,1)} %get-tuple-element.84), channel_id=1, source_target_pairs={{0,32},{32,64},{64,96},{96,0},{1,33},{33,65},{65,97},{97,1},{2,34}... | collective-permute-start | bytes 2383880 | tf_op jit(solution)/shard_map/ppermute | solution.py:478
  145.9 20.1 %collective-permute-start.14 = (bf16[97,32,128]{2,1,0:T(8,128)(2,1)}, bf16[97,32,128]{2,1,0:T(8,128)(2,1)}, u32[]{:S(2)}, u32[]{:S(2)}) collective-permute-start(bf16[97,32,128]{2,1,0:T(8,128)(2,1)} %add.116), channel_id=1, source_target_pairs={{0,96},{32,0},{64,32},{96,64},{1,97},{33,1},{65,33},{97,65},{2,98}... | collective-permute-start | bytes 2383880 | tf_op jit(solution)/shard_map/ppermute | solution.py:478
  149.2 0.9 copy-start.3
  150.0 3.7 %copy-start = (s32[1,64,8]{1,2,0:T(8,128)S(1)}, s32[1,64,8]{1,2,0:T(8,128)}, u32[]{:S(2)}) copy-start(s32[1,64,8]{1,2,0:T(8,128)} %param.10) | copy-start | bytes 6148

commit v10 on v9

--- a/solution.py
+++ b/solution.py
@@ -184,7 +184,7 @@
         hidden_list.append(dot(hidden, split).astype(BF16))
     hidden_split = jnp.concatenate(hidden_list, axis=1)
 
-    @pl.loop(0, D // 512)
+    @pl.loop(0, D // 512, unroll=2)
     def _(n):
         cols = pl.ds(pl.multiple_of(n * 512, 512), 512)
         part_ref[:, cols] = (gating * dot(hidden_split, down_ref[:, cols])).astype(BF16)
@@ -208,7 +208,7 @@
         grad_down_ref[n * CHUNK : (n + 1) * CHUNK, :] = dot(hidden_list[n], grads_ref[...], TN).astype(BF16)
     logit_grad = logit_sum * (1.0 - gating)
 
-    @pl.loop(0, chunks)
+    @pl.loop(0, chunks, unroll=2)
     def _(n):
         cols = pl.ds(pl.multiple_of(n * CHUNK, CHUNK), CHUNK)
         part = dot(both_ref[...], wide_ref[cols, :], NT) + logit_grad * router_ref[mine, cols]

time: 171 us -> 171 us (level)
  Pallas kernels: 66.7 us -> 64.9 us
    pallas_call x2, Pallas kernels: 43.8 us -> 42 us  [run_expert(): pl.pallas_call(functools.partial(expert_kernel, member=member), in_specs=...]
    all_to_all x4, waiting for transfers between devices: 4.21 us -> 5.94 us  [exchange(): lax.all_to_all(array, 'expert', split_axis=0, concat_axis=0, tiled=True)]
  transfers between devices with their start and end apart: 22 -> 22, of which waited for: 6 -> 6; matrix products, arithmetic and copies ran while one was open for 3% -> 3% of each run, Pallas kernels for 34% -> 33%
where the time goes in v10:
time: 171 us; the launch traced here: 169 us
  Pallas kernels  64.9 us (38%)
  starting transfers between devices  54.5 us (32%)
  waiting for transfers between devices  41.3 us (24%)
  local copies, waits for them, and re-layouts  4.06 us (2%)
  other arithmetic  3.18 us (2%)
    pallas_call x2, Pallas kernels, run_expert(): pl.pallas_call(functools.partial(expert_kernel, member=member), in_specs=...  42 us
    ppermute x18, waiting for transfers between devices, shift(): lax.ppermute(array, 'dp', [(i, (i + step) % owners) for i in range(owners)])  35.4 us
    all_to_all x4, starting transfers between devices, exchange(): lax.all_to_all(array, 'expert', split_axis=0, concat_axis=0, tiled=True)  29.2 us
    ppermute x18, starting transfers between devices, shift(): lax.ppermute(array, 'dp', [(i, (i + step) % owners) for i in range(owners)])  25.3 us
    pallas_call x2, Pallas kernels, update(): pl.pallas_call(functools.partial(update_kernel, member=member), grid=(ste...  7.29 us
    all_to_all x4, waiting for transfers between devices, exchange(): lax.all_to_all(array, 'expert', split_axis=0, concat_axis=0, tiled=True)  5.94 us
    pallas_call x1, Pallas kernels, pick(): pl.pallas_call(functools.partial(pick_kernel, locals_count=locals_count),...  5.71 us
    pallas_call x1, Pallas kernels, combine(): pl.pallas_call(functools.partial(combine_kernel, locals_count=locals_coun...  5 us
  transfers between devices with their start and end apart: 22, of which 6 were waited for; matrix products, arithmetic and copies ran while one was open for 3% of the time, Pallas kernels for 33%

profile of v10, /device:TPU:1, one launch (start us, length us, event | category | flops | bytes accessed | tf_op | source)
XLA Modules:
  0.0 169.0 jit_solution(6988905696727610768)
XLA Ops:
  0.6 5.7 %pick.1 = (bf16[32,16,2048]{2,1,0:T(8,128)(2,1)}, bf16[32,16,2048]{2,1,0:T(8,128)(2,1)}) custom-call(s32[8,64]{1,0:T(8,128)} %bitcast.12, bf16[256,2048]{1,0:T(8,128)(2,1)} %tokens_ref.1, bf16[256,2048]{1,0:T(8,128)(2,1)} %grads_ref.1), custom_call_target="tpu_custom_call" | custom-call | bytes 1048576 | tf_op jit(solution)/shard_map/pick/pallas_call | solution.py:340
  6.3 9.7 %all-to-all-start = ((bf16[32,16,2048]{2,1,0:T(8,128)(2,1)}), bf16[32,16,2048]{2,1,0:T(8,128)(2,1)}, u32[]{:S(2)}, u32[]{:S(2)}) async-start(bf16[32,16,2048]{2,1,0:T(8,128)(2,1)} %get-tuple-element.71), calls=%async_computation | async-start | bytes 4194304 | tf_op jit(solution)/shard_map/all_to_all | solution.py:512
  16.0 2.5 %pack_0.1 = (bf16[48,32,128]{2,1,0:T(8,128)(2,1)}, bf16[48,32,128]{2,1,0:T(8,128)(2,1)}) custom-call(f32[192,4096]{1,0:T(8,128)} %bitcast.14), custom_call_target="tpu_custom_call" | custom-call | bytes 1048576 | tf_op jit(solution)/shard_map/pack_0/pallas_call | solution.py:355
  18.5 2.5 %collective-permute-start.1 = (bf16[48,32,128]{2,1,0:T(8,128)(2,1)}, bf16[48,32,128]{2,1,0:T(8,128)(2,1)S(1)}, u32[]{:S(2)}, u32[]{:S(2)}) collective-permute-start(bf16[48,32,128]{2,1,0:T(8,128)(2,1)} %get-tuple-element.62.rest_1_), channel_id=1, source_target_pairs={{0,96},{32,0},{64,32},{96,64},{1,97},{33,1},{65,33},{97,65},{2,98}... | collective-permute-start | bytes 1179656 | tf_op jit(solution)/shard_map/ppermute | solution.py:478
  21.0 0.0 collective-permute-start.2
  21.0 0.2 collective-permute-start
  21.2 2.5 %collective-permute-start.3 = (bf16[48,32,128]{2,1,0:T(8,128)(2,1)}, bf16[48,32,128]{2,1,0:T(8,128)(2,1)S(1)}, u32[]{:S(2)}, u32[]{:S(2)}) collective-permute-start(bf16[48,32,128]{2,1,0:T(8,128)(2,1)} %get-tuple-element.61.rest_0_), channel_id=1, source_target_pairs={{0,96},{32,0},{64,32},{96,64},{1,97},{33,1},{65,33},{97,65},{2,98}... | collective-permute-start | bytes 1179656 | tf_op jit(solution)/shard_map/ppermute | solution.py:478
  23.7 2.4 %pack_1.1 = (bf16[48,32,128]{2,1,0:T(8,128)(2,1)}, bf16[48,32,128]{2,1,0:T(8,128)(2,1)}) custom-call(f32[192,4096]{1,0:T(8,128)} %bitcast.15), custom_call_target="tpu_custom_call" | custom-call | bytes 1048576 | tf_op jit(solution)/shard_map/pack_1/pallas_call | solution.py:355
  26.2 0.2 multiply_add_fusion
  26.5 0.1 add_add_fusion
  26.6 0.4 select_reduce_fusion
  27.0 1.0 reshape.146
  28.0 0.5 copy.23
  28.5 0.1 reshape.145.router_ref
  28.6 12.4 %collective-permute-done.rest_2_ = bf16[48,32,128]{2,1,0:T(8,128)(2,1)S(1)} collective-permute-done((bf16[48,32,128]{2,1,0:T(8,128)(2,1)}, bf16[48,32,128]{2,1,0:T(8,128)(2,1)S(1)}, u32[]{:S(2)}, u32[]{:S(2)}) %collective-permute-start) | collective-permute-done | bytes 393248 | tf_op jit(solution)/shard_map/ppermute | solution.py:478
  41.0 0.0 collective-permute-done.1.rest_5_
  41.0 2.7 %collective-permute-start.5 = (bf16[48,32,128]{2,1,0:T(8,128)(2,1)S(1)}, bf16[48,32,128]{2,1,0:T(8,128)(2,1)S(1)}, u32[]{:S(2)}, u32[]{:S(2)}) collective-permute-start(bf16[48,32,128]{2,1,0:T(8,128)(2,1)S(1)} %collective-permute-done.1.rest_5_), channel_id=1, source_target_pairs={{0,96},{32,0},{64,32},{96,64},{1,97},{33,1},{65,33},{97,65},{2,98}... | collective-permute-start | bytes 1179656 | tf_op jit(solution)/shard_map/ppermute | solution.py:478
  43.7 0.0 collective-permute-start.7
  43.7 0.6 all-to-all-done.arriving_ref
  44.4 8.5 %all-to-all-start.1 = ((bf16[32,16,2048]{2,1,0:T(8,128)(2,1)}), bf16[32,16,2048]{2,1,0:T(8,128)(2,1)}, u32[]{:S(2)}, u32[]{:S(2)}) async-start(bf16[32,16,2048]{2,1,0:T(8,128)(2,1)} %get-tuple-element.72), calls=%async_computation.1 | async-start | bytes 4194304 | tf_op jit(solution)/shard_map/all_to_all | solution.py:512
  52.9 1.8 %collective-permute-start.8 = (bf16[48,32,128]{2,1,0:T(8,128)(2,1)}, bf16[48,32,128]{2,1,0:T(8,128)(2,1)}, u32[]{:S(2)}, u32[]{:S(2)}) collective-permute-start(bf16[48,32,128]{2,1,0:T(8,128)(2,1)} %get-tuple-element.79.rest_1_), channel_id=1, source_target_pairs={{0,32},{32,64},{64,96},{96,0},{1,33},{33,65},{65,97},{97,1},{2,34}... | collective-permute-start | bytes 1179656 | tf_op jit(solution)/shard_map/ppermute | solution.py:478
  54.7 0.1 collective-permute-start.6
  54.8 2.6 %collective-permute-start.9 = (bf16[48,32,128]{2,1,0:T(8,128)(2,1)}, bf16[48,32,128]{2,1,0:T(8,128)(2,1)}, u32[]{:S(2)}, u32[]{:S(2)}) collective-permute-start(bf16[48,32,128]{2,1,0:T(8,128)(2,1)} %get-tuple-element.78.rest_0_), channel_id=1, source_target_pairs={{0,96},{32,0},{64,32},{96,64},{1,97},{33,1},{65,33},{97,65},{2,98}... | collective-permute-start | bytes 1179656 | tf_op jit(solution)/shard_map/ppermute | solution.py:478
  57.4 0.8 copy-done.9
  58.1 21.0 %expert_0.1 = (bf16[32,16,2048]{2,1,0:T(8,128)(2,1)}, bf16[97,32,128]{2,1,0:T(8,128)(2,1)}, bf16[97,32,128]{2,1,0:T(8,128)(2,1)}, bf16[97,32,128]{2,1,0:T(8,128)(2,1)}, bf16[97,32,128]{2,1,0:T(8,128)(2,1)}) custom-call(s32[2304]{0:T(1024)S(1)} %add.111.inverse_ref, s32[768]{0:T(1024)S(1)} %reshape.141.row_ref, s32[768]{0:T(1024)S(1)} %reshape.142.lane_ref, ...), custom_call_target="tpu_custom_call" | custom-call | flops 149999992832 | bytes 1048576 | tf_op jit(solution)/shard_map/expert_0/pallas_call | solution.py:376
  79.1 2.1 %all-to-all-done.1.arriving_ref = bf16[32,16,2048]{2,1,0:T(8,128)(2,1)} async-done(((bf16[32,16,2048]{2,1,0:T(8,128)(2,1)}), bf16[32,16,2048]{2,1,0:T(8,128)(2,1)}, u32[]{:S(2)}, u32[]{:S(2)}) %all-to-all-start.1) | async-done | bytes 2097184 | tf_op jit(solution)/shard_map/all_to_all | solution.py:512
  81.2 1.7 %collective-permute-start.10 = (bf16[48,32,128]{2,1,0:T(8,128)(2,1)}, bf16[48,32,128]{2,1,0:T(8,128)(2,1)S(1)}, u32[]{:S(2)}, u32[]{:S(2)}) collective-permute-start(bf16[48,32,128]{2,1,0:T(8,128)(2,1)} %collective-permute-done.6.rest_2_), channel_id=1, source_target_pairs={{0,32},{32,64},{64,96},{96,0},{1,33},{33,65},{65,97},{97,1},{2,34}... | collective-permute-start | bytes 1179656 | tf_op jit(solution)/shard_map/ppermute | solution.py:478
  82.9 1.0 collective-permute-start.11
  83.9 0.5 collective-permute-start.15
  84.4 6.3 %all-to-all-start.2 = ((bf16[32,16,2048]{2,1,0:T(8,128)(2,1)}), bf16[32,16,2048]{2,1,0:T(8,128)(2,1)}, u32[]{:S(2)}, u32[]{:S(2)}) async-start(bf16[32,16,2048]{2,1,0:T(8,128)(2,1)} %get-tuple-element.88), calls=%async_computation.2 | async-start | bytes 4194304 | tf_op jit(solution)/shard_map/all_to_all | solution.py:512
  90.8 3.2 %collective-permute-start.16 = (bf16[97,32,128]{2,1,0:T(8,128)(2,1)}, bf16[97,32,128]{2,1,0:T(8,128)(2,1)}, u32[]{:S(2)}, u32[]{:S(2)}) collective-permute-start(bf16[97,32,128]{2,1,0:T(8,128)(2,1)} %get-tuple-element.92), channel_id=1, source_target_pairs={{0,96},{32,0},{64,32},{96,64},{1,97},{33,1},{65,33},{97,65},{2,98}... | collective-permute-start | bytes 2383880 | tf_op jit(solution)/shard_map/ppermute | solution.py:478
  94.0 0.7 copy-done.10
  94.8 21.0 %expert_1.1 = (bf16[32,16,2048]{2,1,0:T(8,128)(2,1)}, bf16[97,32,128]{2,1,0:T(8,128)(2,1)}, bf16[97,32,128]{2,1,0:T(8,128)(2,1)}, bf16[97,32,128]{2,1,0:T(8,128)(2,1)}, bf16[97,32,128]{2,1,0:T(8,128)(2,1)}) custom-call(s32[2304]{0:T(1024)S(1)} %add.111.inverse_ref, s32[768]{0:T(1024)S(1)} %reshape.141.row_ref, s32[768]{0:T(1024)S(1)} %reshape.142.lane_ref, ...), custom_call_target="tpu_custom_call" | custom-call | flops 149999992832 | bytes 1048576 | tf_op jit(solution)/shard_map/expert_1/pallas_call | solution.py:376
  115.8 3.3 %all-to-all-done.2.rest_0_ = bf16[32,16,2048]{2,1,0:T(8,128)(2,1)} async-done(((bf16[32,16,2048]{2,1,0:T(8,128)(2,1)}), bf16[32,16,2048]{2,1,0:T(8,128)(2,1)}, u32[]{:S(2)}, u32[]{:S(2)}) %all-to-all-start.2) | async-done | bytes 2097184 | tf_op jit(solution)/shard_map/all_to_all | solution.py:512
  119.1 4.7 %all-to-all-start.3 = ((bf16[32,16,2048]{2,1,0:T(8,128)(2,1)}), bf16[32,16,2048]{2,1,0:T(8,128)(2,1)S(1)}, u32[]{:S(2)}, u32[]{:S(2)}) async-start(bf16[32,16,2048]{2,1,0:T(8,128)(2,1)} %get-tuple-element.100), calls=%async_computation.3 | async-start | bytes 4194304 | tf_op jit(solution)/shard_map/all_to_all | solution.py:512
  123.8 3.0 %collective-permute-start.13 = (bf16[97,32,128]{2,1,0:T(8,128)(2,1)}, bf16[97,32,128]{2,1,0:T(8,128)(2,1)S(1)}, u32[]{:S(2)}, u32[]{:S(2)}) collective-permute-start(bf16[97,32,128]{2,1,0:T(8,128)(2,1)} %get-tuple-element.86), channel_id=1, source_target_pairs={{0,96},{32,0},{64,32},{96,64},{1,97},{33,1},{65,33},{97,65},{2,98}... | collective-permute-start | bytes 2383880 | tf_op jit(solution)/shard_map/ppermute | solution.py:478
  126.8 1.3 add.117
  128.2 0.1 collective-permute-start.17
  128.2 0.1 collective-permute-start.12
  128.3 15.6 %collective-permute-done.13 = bf16[97,32,128]{2,1,0:T(8,128)(2,1)S(1)} collective-permute-done((bf16[97,32,128]{2,1,0:T(8,128)(2,1)}, bf16[97,32,128]{2,1,0:T(8,128)(2,1)S(1)}, u32[]{:S(2)}, u32[]{:S(2)}) %collective-permute-start.13) | collective-permute-done | bytes 794656 | tf_op jit(solution)/shard_map/ppermute | solution.py:478
  143.9 1.1 add.116
  145.0 3.3 %collective-permute-start.14 = (bf16[97,32,128]{2,1,0:T(8,128)(2,1)}, bf16[97,32,128]{2,1,0:T(8,128)(2,1)}, u32[]{:S(2)}, u32[]{:S(2)}) collective-permute-start(bf16[97,32,128]{2,1,0:T(8,128)(2,1)} %add.116), channel_id=1, source_target_pairs={{0,96},{32,0},{64,32},{96,64},{1,97},{33,1},{65,33},{97,65},{2,98}... | collective-permute-start | bytes 2383880 | tf_op jit(solution)/shard_map/ppermute | solution.py:478
  148.3 0.6 broadcast_in_dim.52.router_ref
  148.9 0.3 copy-done.3
  149.2 3.6 %update_0.1 = (f32[192,4096]{1,0:T(8,128)}, f32[3,2,32]{2,1,0:T(2,128)}, f32[2,512]{1,0:T(2,128)}) custom-call(bf16[97,32,128]{2,1,0:T(8,128)(2,1)} %get-tuple-element.93.own_ref.own_last_ref, bf16[97,32,128]{2,1,0:T(8,128)(2,1)} %collective-permute-done.16.first_ref.first_last_ref, bf16[97,32,128]{2,1,0:T(8,128)(2,1)} %copy-done.3, ...), custom_call_target="tpu_custom_call" | custom-call | bytes 1048576 | tf_op jit(solution)/shard_map/update_0/pallas_call | solution.py:416
  152.9 5.0 %combine.1 = (bf16[256,2048]{1,0:T(8,128)(2,1)}, bf16[256,2048]{1,0:T(8,128)(2,1)}) custom-call(s32[8,64]{1,0:T(8,128)S(1)} %bitcast.13, bf16[32,16,2048]{2,1,0:T(8,128)(2,1)} %all-to-all-done.2.rest_0_, bf16[32,16,2048]{2,1,0:T(8,128)(2,1)S(1)} %all-to-all-done.3.rest_1_), custom_call_target="tpu_custom_call" | custom-call | flops 149999992832 | bytes 1048576 | tf_op jit(solution)/shard_map/combine/pallas_call | solution.py:441
  157.9 7.3 %collective-permute-done.12.first_ref.first_last_ref = bf16[97,32,128]{2,1,0:T(8,128)(2,1)} collective-permute-done((bf16[97,32,128]{2,1,0:T(8,128)(2,1)}, bf16[97,32,128]{2,1,0:T(8,128)(2,1)}, u32[]{:S(2)}, u32[]{:S(2)}) %collective-permute-start.12) | collective-permute-done | bytes 794656 | tf_op jit(solution)/shard_map/ppermute | solution.py:478
  165.2 3.6 %update_1.1 = (f32[192,4096]{1,0:T(8,128)}, f32[3,2,32]{2,1,0:T(2,128)}, f32[2,512]{1,0:T(2,128)}) custom-call(bf16[97,32,128]{2,1,0:T(8,128)(2,1)} %get-tuple-element.104.own_ref.own_last_ref, bf16[97,32,128]{2,1,0:T(8,128)(2,1)} %collective-permute-done.12.first_ref.first_last_ref, ...), custom_call_target="tpu_custom_call", output_to_operand_aliasing={{0}: (9, {})} | custom-call | bytes 1048576 | tf_op jit(solution)/shard_map/update_1/pallas_call | solution.py:416
  (46 shorter events, 0.2 us)
Async XLA Ops:
  6.3 38.0 %all-to-all-start = ((bf16[32,16,2048]{2,1,0:T(8,128)(2,1)}), bf16[32,16,2048]{2,1,0:T(8,128)(2,1)}, u32[]{:S(2)}, u32[]{:S(2)}) async-start(bf16[32,16,2048]{2,1,0:T(8,128)(2,1)} %get-tuple-element.71), calls=%async_computation | async-start | bytes 4194304 | tf_op jit(solution)/shard_map/all_to_all | solution.py:512
  18.5 7.7 %copy-start.6 = (s32[2,3,128]{2,0,1:T(2,128)S(1)}, s32[2,3,128]{2,0,1:T(2,128)}, u32[]{:S(2)}) copy-start(s32[2,3,128]{2,0,1:T(2,128)} %param.12) | copy-start | bytes 9220
  18.5 7.7 %copy-start.8 = (s32[3]{0:T(128)S(1)}, s32[3]{0:T(128)}, u32[]{:S(2)}) copy-start(s32[3]{0:T(128)} %constant.90.clone) | copy-start | bytes 40
  18.5 8.5 %copy-start.7 = (bf16[2048,2]{0,1:T(2,128)(2,1)S(1)}, bf16[2048,2]{0,1:T(2,128)(2,1)}, u32[]{:S(2)}) copy-start(bf16[2048,2]{0,1:T(2,128)(2,1)} %param.11) | copy-start | bytes 24580
  18.5 22.6 %collective-permute-start.1 = (bf16[48,32,128]{2,1,0:T(8,128)(2,1)}, bf16[48,32,128]{2,1,0:T(8,128)(2,1)S(1)}, u32[]{:S(2)}, u32[]{:S(2)}) collective-permute-start(bf16[48,32,128]{2,1,0:T(8,128)(2,1)} %get-tuple-element.62.rest_1_), channel_id=1, source_target_pairs={{0,96},{32,0},{64,32},{96,64},{1,97},{33,1},{65,33},{97,65},{2,98}... | collective-permute-start | bytes 1179656 | tf_op jit(solution)/shard_map/ppermute | solution.py:478
  21.0 31.9 %collective-permute-start.2 = (bf16[48,32,128]{2,1,0:T(8,128)(2,1)}, bf16[48,32,128]{2,1,0:T(8,128)(2,1)S(1)}, u32[]{:S(2)}, u32[]{:S(2)}) collective-permute-start(bf16[48,32,128]{2,1,0:T(8,128)(2,1)} %get-tuple-element.62.rest_1_), channel_id=1, source_target_pairs={{0,32},{32,64},{64,96},{96,0},{1,33},{33,65},{65,97},{97,1},{2,34}... | collective-permute-start | bytes 1179656 | tf_op jit(solution)/shard_map/ppermute | solution.py:478
  21.0 20.0 %collective-permute-start = (bf16[48,32,128]{2,1,0:T(8,128)(2,1)}, bf16[48,32,128]{2,1,0:T(8,128)(2,1)S(1)}, u32[]{:S(2)}, u32[]{:S(2)}) collective-permute-start(bf16[48,32,128]{2,1,0:T(8,128)(2,1)} %get-tuple-element.61.rest_0_), channel_id=1, source_target_pairs={{0,32},{32,64},{64,96},{96,0},{1,33},{33,65},{65,97},{97,1},{2,34}... | collective-permute-start | bytes 1179656 | tf_op jit(solution)/shard_map/ppermute | solution.py:478
  21.2 33.5 %collective-permute-start.3 = (bf16[48,32,128]{2,1,0:T(8,128)(2,1)}, bf16[48,32,128]{2,1,0:T(8,128)(2,1)S(1)}, u32[]{:S(2)}, u32[]{:S(2)}) collective-permute-start(bf16[48,32,128]{2,1,0:T(8,128)(2,1)} %get-tuple-element.61.rest_0_), channel_id=1, source_target_pairs={{0,96},{32,0},{64,32},{96,64},{1,97},{33,1},{65,33},{97,65},{2,98}... | collective-permute-start | bytes 1179656 | tf_op jit(solution)/shard_map/ppermute | solution.py:478
  41.0 13.7 %collective-permute-start.4 = (bf16[48,32,128]{2,1,0:T(8,128)(2,1)S(1)}, bf16[48,32,128]{2,1,0:T(8,128)(2,1)S(1)}, u32[]{:S(2)}, u32[]{:S(2)}) collective-permute-start(bf16[48,32,128]{2,1,0:T(8,128)(2,1)S(1)} %collective-permute-done.rest_2_), channel_id=1, source_target_pairs={{0,32},{32,64},{64,96},{96,0},{1,33},{33,65},{65,97},{97,1},{2,34}... | collective-permute-start | bytes 1179656 | tf_op jit(solution)/shard_map/ppermute | solution.py:478
  41.0 16.3 %collective-permute-start.5 = (bf16[48,32,128]{2,1,0:T(8,128)(2,1)S(1)}, bf16[48,32,128]{2,1,0:T(8,128)(2,1)S(1)}, u32[]{:S(2)}, u32[]{:S(2)}) collective-permute-start(bf16[48,32,128]{2,1,0:T(8,128)(2,1)S(1)} %collective-permute-done.1.rest_5_), channel_id=1, source_target_pairs={{0,96},{32,0},{64,32},{96,64},{1,97},{33,1},{65,33},{97,65},{2,98}... | collective-permute-start | bytes 1179656 | tf_op jit(solution)/shard_map/ppermute | solution.py:478
  43.7 35.4 %collective-permute-start.7 = (bf16[48,32,128]{2,1,0:T(8,128)(2,1)}, bf16[48,32,128]{2,1,0:T(8,128)(2,1)}, u32[]{:S(2)}, u32[]{:S(2)}) collective-permute-start(bf16[48,32,128]{2,1,0:T(8,128)(2,1)} %get-tuple-element.79.rest_1_), channel_id=1, source_target_pairs={{0,96},{32,0},{64,32},{96,64},{1,97},{33,1},{65,33},{97,65},{2,98}... | collective-permute-start | bytes 1179656 | tf_op jit(solution)/shard_map/ppermute | solution.py:478
  44.3 13.8 %copy-start.1 = (bf16[48,32,128]{2,1,0:T(8,128)(2,1)S(1)}, bf16[48,32,128]{2,1,0:T(8,128)(2,1)}, u32[]{:S(2)}) copy-start(bf16[48,32,128]{2,1,0:T(8,128)(2,1)} %get-tuple-element.61.rest_0_) | copy-start | bytes 1179652
  44.3 13.8 %copy-start.2 = (bf16[48,32,128]{2,1,0:T(8,128)(2,1)S(1)}, bf16[48,32,128]{2,1,0:T(8,128)(2,1)}, u32[]{:S(2)}) copy-start(bf16[48,32,128]{2,1,0:T(8,128)(2,1)} %get-tuple-element.62.rest_1_) | copy-start | bytes 1179652
  44.4 36.9 %all-to-all-start.1 = ((bf16[32,16,2048]{2,1,0:T(8,128)(2,1)}), bf16[32,16,2048]{2,1,0:T(8,128)(2,1)}, u32[]{:S(2)}, u32[]{:S(2)}) async-start(bf16[32,16,2048]{2,1,0:T(8,128)(2,1)} %get-tuple-element.72), calls=%async_computation.1 | async-start | bytes 4194304 | tf_op jit(solution)/shard_map/all_to_all | solution.py:512
  52.9 37.9 %collective-permute-start.8 = (bf16[48,32,128]{2,1,0:T(8,128)(2,1)}, bf16[48,32,128]{2,1,0:T(8,128)(2,1)}, u32[]{:S(2)}, u32[]{:S(2)}) collective-permute-start(bf16[48,32,128]{2,1,0:T(8,128)(2,1)} %get-tuple-element.79.rest_1_), channel_id=1, source_target_pairs={{0,32},{32,64},{64,96},{96,0},{1,33},{33,65},{65,97},{97,1},{2,34}... | collective-permute-start | bytes 1179656 | tf_op jit(solution)/shard_map/ppermute | solution.py:478
  54.7 24.5 %collective-permute-start.6 = (bf16[48,32,128]{2,1,0:T(8,128)(2,1)}, bf16[48,32,128]{2,1,0:T(8,128)(2,1)}, u32[]{:S(2)}, u32[]{:S(2)}) collective-permute-start(bf16[48,32,128]{2,1,0:T(8,128)(2,1)} %get-tuple-element.78.rest_0_), channel_id=1, source_target_pairs={{0,32},{32,64},{64,96},{96,0},{1,33},{33,65},{65,97},{97,1},{2,34}... | collective-permute-start | bytes 1179656 | tf_op jit(solution)/shard_map/ppermute | solution.py:478
  54.8 39.2 %collective-permute-start.9 = (bf16[48,32,128]{2,1,0:T(8,128)(2,1)}, bf16[48,32,128]{2,1,0:T(8,128)(2,1)}, u32[]{:S(2)}, u32[]{:S(2)}) collective-permute-start(bf16[48,32,128]{2,1,0:T(8,128)(2,1)} %get-tuple-element.78.rest_0_), channel_id=1, source_target_pairs={{0,96},{32,0},{64,32},{96,64},{1,97},{33,1},{65,33},{97,65},{2,98}... | collective-permute-start | bytes 1179656 | tf_op jit(solution)/shard_map/ppermute | solution.py:478
  57.4 0.8 copy-start.9
  81.2 12.8 %collective-permute-start.10 = (bf16[48,32,128]{2,1,0:T(8,128)(2,1)}, bf16[48,32,128]{2,1,0:T(8,128)(2,1)S(1)}, u32[]{:S(2)}, u32[]{:S(2)}) collective-permute-start(bf16[48,32,128]{2,1,0:T(8,128)(2,1)} %collective-permute-done.6.rest_2_), channel_id=1, source_target_pairs={{0,32},{32,64},{64,96},{96,0},{1,33},{33,65},{65,97},{97,1},{2,34}... | collective-permute-start | bytes 1179656 | tf_op jit(solution)/shard_map/ppermute | solution.py:478
  82.9 11.1 %collective-permute-start.11 = (bf16[48,32,128]{2,1,0:T(8,128)(2,1)}, bf16[48,32,128]{2,1,0:T(8,128)(2,1)S(1)}, u32[]{:S(2)}, u32[]{:S(2)}) collective-permute-start(bf16[48,32,128]{2,1,0:T(8,128)(2,1)} %collective-permute-done.7.rest_5_), channel_id=1, source_target_pairs={{0,96},{32,0},{64,32},{96,64},{1,97},{33,1},{65,33},{97,65},{2,98}... | collective-permute-start | bytes 1179656 | tf_op jit(solution)/shard_map/ppermute | solution.py:478
  83.9 31.9 %collective-permute-start.15 = (bf16[97,32,128]{2,1,0:T(8,128)(2,1)}, bf16[97,32,128]{2,1,0:T(8,128)(2,1)}, u32[]{:S(2)}, u32[]{:S(2)}) collective-permute-start(bf16[97,32,128]{2,1,0:T(8,128)(2,1)} %get-tuple-element.91), channel_id=1, source_target_pairs={{0,32},{32,64},{64,96},{96,0},{1,33},{33,65},{65,97},{97,1},{2,34}... | collective-permute-start | bytes 2383880 | tf_op jit(solution)/shard_map/ppermute | solution.py:478
  84.4 34.7 %all-to-all-start.2 = ((bf16[32,16,2048]{2,1,0:T(8,128)(2,1)}), bf16[32,16,2048]{2,1,0:T(8,128)(2,1)}, u32[]{:S(2)}, u32[]{:S(2)}) async-start(bf16[32,16,2048]{2,1,0:T(8,128)(2,1)} %get-tuple-element.88), calls=%async_computation.2 | async-start | bytes 4194304 | tf_op jit(solution)/shard_map/all_to_all | solution.py:512
  90.8 25.1 %collective-permute-start.16 = (bf16[97,32,128]{2,1,0:T(8,128)(2,1)}, bf16[97,32,128]{2,1,0:T(8,128)(2,1)}, u32[]{:S(2)}, u32[]{:S(2)}) collective-permute-start(bf16[97,32,128]{2,1,0:T(8,128)(2,1)} %get-tuple-element.92), channel_id=1, source_target_pairs={{0,96},{32,0},{64,32},{96,64},{1,97},{33,1},{65,33},{97,65},{2,98}... | collective-permute-start | bytes 2383880 | tf_op jit(solution)/shard_map/ppermute | solution.py:478
  94.0 0.7 copy-start.10
  119.1 7.7 %copy-start.4 = (bf16[97,32,128]{2,1,0:T(8,128)(2,1)S(1)}, bf16[97,32,128]{2,1,0:T(8,128)(2,1)}, u32[]{:S(2)}) copy-start(bf16[97,32,128]{2,1,0:T(8,128)(2,1)} %get-tuple-element.95) | copy-start | bytes 2383876
  119.1 33.7 %all-to-all-start.3 = ((bf16[32,16,2048]{2,1,0:T(8,128)(2,1)}), bf16[32,16,2048]{2,1,0:T(8,128)(2,1)S(1)}, u32[]{:S(2)}, u32[]{:S(2)}) async-start(bf16[32,16,2048]{2,1,0:T(8,128)(2,1)} %get-tuple-element.100), calls=%async_computation.3 | async-start | bytes 4194304 | tf_op jit(solution)/shard_map/all_to_all | solution.py:512
  123.8 20.1 %copy-start.5 = (bf16[97,32,128]{2,1,0:T(8,128)(2,1)S(1)}, bf16[97,32,128]{2,1,0:T(8,128)(2,1)}, u32[]{:S(2)}) copy-start(bf16[97,32,128]{2,1,0:T(8,128)(2,1)} %get-tuple-element.85) | copy-start | bytes 2383876
  123.8 20.1 %collective-permute-start.13 = (bf16[97,32,128]{2,1,0:T(8,128)(2,1)}, bf16[97,32,128]{2,1,0:T(8,128)(2,1)S(1)}, u32[]{:S(2)}, u32[]{:S(2)}) collective-permute-start(bf16[97,32,128]{2,1,0:T(8,128)(2,1)} %get-tuple-element.86), channel_id=1, source_target_pairs={{0,96},{32,0},{64,32},{96,64},{1,97},{33,1},{65,33},{97,65},{2,98}... | collective-permute-start | bytes 2383880 | tf_op jit(solution)/shard_map/ppermute | solution.py:478
  128.2 20.1 %collective-permute-start.17 = (bf16[97,32,128]{2,1,0:T(8,128)(2,1)S(1)}, bf16[97,32,128]{2,1,0:T(8,128)(2,1)S(1)}, u32[]{:S(2)}, u32[]{:S(2)}) collective-permute-start(bf16[97,32,128]{2,1,0:T(8,128)(2,1)S(1)} %add.117), channel_id=1, source_target_pairs={{0,32},{32,64},{64,96},{96,0},{1,33},{33,65},{65,97},{97,1},{2,34}... | collective-permute-start | bytes 2383880 | tf_op jit(solution)/shard_map/ppermute | solution.py:478
  128.2 37.0 %collective-permute-start.12 = (bf16[97,32,128]{2,1,0:T(8,128)(2,1)}, bf16[97,32,128]{2,1,0:T(8,128)(2,1)}, u32[]{:S(2)}, u32[]{:S(2)}) collective-permute-start(bf16[97,32,128]{2,1,0:T(8,128)(2,1)} %get-tuple-element.84), channel_id=1, source_target_pairs={{0,32},{32,64},{64,96},{96,0},{1,33},{33,65},{65,97},{97,1},{2,34}... | collective-permute-start | bytes 2383880 | tf_op jit(solution)/shard_map/ppermute | solution.py:478
  145.0 20.2 %collective-permute-start.14 = (bf16[97,32,128]{2,1,0:T(8,128)(2,1)}, bf16[97,32,128]{2,1,0:T(8,128)(2,1)}, u32[]{:S(2)}, u32[]{:S(2)}) collective-permute-start(bf16[97,32,128]{2,1,0:T(8,128)(2,1)} %add.116), channel_id=1, source_target_pairs={{0,96},{32,0},{64,32},{96,64},{1,97},{33,1},{65,33},{97,65},{2,98}... | collective-permute-start | bytes 2383880 | tf_op jit(solution)/shard_map/ppermute | solution.py:478
  148.3 0.9 copy-start.3
  149.2 3.7 %copy-start = (s32[1,64,8]{1,2,0:T(8,128)S(1)}, s32[1,64,8]{1,2,0:T(8,128)}, u32[]{:S(2)}) copy-start(s32[1,64,8]{1,2,0:T(8,128)} %param.10) | copy-start | bytes 6148
